TPU v7x, 32 devices: a whole 2x2x4 slice. The times are simulated.
32 devices in a mesh: dp: 8 (over z, y), shard: 4 (over x, core).
Axes of the slice: x: 2, y: 2, z: 4, core: 2. Of those that a mesh axis runs over, the one named last changes fastest.
Arguments:
- tokens: bfloat16 [16384, 768], P(('dp', 'shard')), may hold values from -6 to 6
- cotangent: bfloat16 [16384, 768], P(('dp', 'shard')), may hold values from -6 to 6
- lengths: int32 [8, 2], P('dp'), may hold values from 1 to 2047, as said below
- counts: int32 [8, 4], P('dp'), may hold values from 384 to 512, as said below
- attn_w: float32 [768, 3072], P('shard')
- attn_m: float32 [768, 3072], P('shard'), may hold values from -0.00061035156 to 0.00061035156
- attn_v: float32 [768, 3072], P('shard'), may hold values from 1.4110135e-10 to 5.644054e-10
- mlp_w: float32 [2, 768, 3072], P(None, 'shard')
- mlp_m: float32 [2, 768, 3072], P(None, 'shard'), may hold values from -0.00061035156 to 0.00061035156
- mlp_v: float32 [2, 768, 3072], P(None, 'shard'), may hold values from 1.4110135e-10 to 5.644054e-10
- vec_w: float32 [12, 768], P(None, 'shard')
- vec_m: float32 [12, 768], P(None, 'shard'), may hold values from -0.0024414062 to 0.0024414062
- vec_v: float32 [12, 768], P(None, 'shard'), may hold values from 2.2576216e-09 to 9.030487e-09
Outputs:
- block_out: bfloat16 [16384, 768], P(('dp', 'shard'))
- grad_in: bfloat16 [16384, 768], P(('dp', 'shard'))
- attn_grad: float32 [768, 3072], P('shard')
- mlp_grad: float32 [2, 768, 3072], P(None, 'shard')
- vec_grad: float32 [12, 768], P(None, 'shard')
- attn_w_new: float32 [768, 3072], P('shard')
- attn_m_new: float32 [768, 3072], P('shard')
- attn_v_new: float32 [768, 3072], P('shard')
- mlp_w_new: float32 [2, 768, 3072], P(None, 'shard')
- mlp_m_new: float32 [2, 768, 3072], P(None, 'shard')
- mlp_v_new: float32 [2, 768, 3072], P(None, 'shard')
- vec_w_new: float32 [12, 768], P(None, 'shard')
- vec_m_new: float32 [12, 768], P(None, 'shard')
- vec_v_new: float32 [12, 768], P(None, 'shard')
- clip_norm: float32 [1], replicated
Inputs may be any that keep to these rules, and one draw needn't show every extreme that they name: `counts`: in every group one device holds exactly 512 tokens. A group's lengths sum to the sum of its counts; one of its sequences holds tokens of the group's first device and of its last. In some group every device is full and its first sequence is a single token.
All inputs are finite; a program needn't handle non-finite values.
Results may differ from a plain program's by a relative error of at most 0.015.
The roundings to bfloat16 on the way count: a program that leaves them out, or rounds other values in their place, can miss the bound.
Values may be sent and summed in bfloat16 or wider, within the bound.
No kernel may reach another device: no remote copies, remote signals or barrier semaphores. Data moves between devices by JAX's collectives and lax.ppermute only.
A program may use at most 320 MiB of HBM per device.

v0:
```python
import jax
import jax.numpy as jnp
from jax import lax
from jax.sharding import PartitionSpec as P

HEADS = 12
STEP = 10


NORM_EPSILON = 1e-05
BETA_FIRST = 0.9
BETA_SECOND = 0.999
ADAM_EPSILON = 1e-08
RATE_MATRIX = 0.1
RATE_VECTOR = 0.2
DECAY_MATRIX = 0.1
CLIP_LIMIT = 1.0
MASKED_SCORE = -1e30


def layer_norm(features, norm_gain, norm_bias):
    centered = features - jnp.mean(features, axis=-1, keepdims=True)
    variance = jnp.mean(centered * centered, axis=-1, keepdims=True)
    return centered * lax.rsqrt(variance + NORM_EPSILON) * norm_gain + norm_bias


def gelu_tanh(features):
    return jax.nn.gelu(features, approximate=True)


def group_layout(length_row, count_row, slots):
    starts = jnp.cumsum(count_row) - count_row
    within = jnp.arange(slots, dtype=jnp.int32)
    position = (starts[:, None] + within[None, :]).reshape(-1)
    live_rows = (within[None, :] < count_row[:, None]).reshape(-1)
    boundary = jnp.cumsum(length_row)
    segment = jnp.sum((position[:, None] >= boundary[None, :]).astype(jnp.int32), axis=1)
    buffer_slot = jnp.arange(position.shape[0], dtype=jnp.int32)
    segment = jnp.where(live_rows, segment, -1 - buffer_slot)
    return (segment, position, live_rows)


def adam_update(master, first, second, gradient, factor, rate, decay):
    clipped = gradient * factor
    first_new = BETA_FIRST * first + (1.0 - BETA_FIRST) * clipped
    second_new = BETA_SECOND * second + (1.0 - BETA_SECOND) * clipped * clipped
    first_hat = first_new / (1.0 - BETA_FIRST**STEP)
    second_hat = second_new / (1.0 - BETA_SECOND**STEP)
    master_new = master - rate * (
        first_hat / (jnp.sqrt(second_hat) + ADAM_EPSILON) + decay * master
    )
    return (clipped, master_new, first_new, second_new)


def on_device(
    tokens,
    cotangent,
    lengths,
    counts,
    attn_w,
    attn_m,
    attn_v,
    mlp_w,
    mlp_m,
    mlp_v,
    vec_w,
    vec_m,
    vec_v,
):
    attn_round, mlp_round, vec_round = (
        lax.all_gather(attn_w.astype(jnp.bfloat16), "shard", axis=0, tiled=True),
        lax.all_gather(mlp_w.astype(jnp.bfloat16), "shard", axis=1, tiled=True),
        lax.all_gather(vec_w.astype(jnp.bfloat16), "shard", axis=1, tiled=True),
    )
    width = attn_round.shape[0]
    hidden = mlp_round.shape[2]
    slots = tokens.shape[0]
    heads = HEADS
    head_size = width // heads
    scale = head_size ** (-0.5)
    fc_rows = hidden // width
    vectors = vec_round.astype(jnp.float32)
    w_qkv = attn_round[:, : 3 * width]
    w_out = attn_round[:, 3 * width :]
    w_fc = mlp_round[0]
    w_proj = mlp_round[1]
    segment, position, live_rows = group_layout(lengths[0], counts[0], slots)
    first_slot = lax.axis_index("shard") * slots
    seg_own = lax.dynamic_slice_in_dim(segment, first_slot, slots)
    pos_own = lax.dynamic_slice_in_dim(position, first_slot, slots)
    live_own = lax.dynamic_slice_in_dim(live_rows, first_slot, slots)
    inputs = tokens.astype(jnp.float32)
    normed_first, norm_first_back = jax.vjp(layer_norm, inputs, vectors[0], vectors[1])
    acts_first = normed_first.astype(jnp.bfloat16)
    qkv_bias = jnp.concatenate([vectors[2], jnp.zeros((width,), jnp.float32), vectors[3]])
    projected = (jnp.dot(acts_first, w_qkv, preferred_element_type=jnp.float32) + qkv_bias).astype(
        jnp.bfloat16
    )
    queries = projected[:, :width].reshape(slots, heads, head_size)
    keyval_own = projected[:, width:]
    keyval_group = lax.all_gather(keyval_own, "shard", axis=0, tiled=True)

    def scored(keyval):
        keys_all = keyval[:, :width].reshape(-1, heads, head_size)
        scores = (
            jnp.einsum("qhd,khd->hqk", queries, keys_all, preferred_element_type=jnp.float32)
            * scale
        )
        allowed = (seg_own[:, None] == segment[None, :]) & (position[None, :] <= pos_own[:, None])
        return jnp.where(allowed[None], scores, MASKED_SCORE)

    scores = scored(keyval_group)
    highest = jnp.max(scores, axis=-1, keepdims=True)
    log_total = highest + jnp.log(jnp.sum(jnp.exp(scores - highest), axis=-1, keepdims=True))
    weights_low = jnp.exp(scores - log_total).astype(jnp.bfloat16)
    values_group = keyval_group[:, width:].reshape(-1, heads, head_size)
    mixed = jnp.einsum(
        "hqk,khd->qhd", weights_low, values_group, preferred_element_type=jnp.float32
    )
    mixed_low = mixed.reshape(slots, width).astype(jnp.bfloat16)
    attn_out = jnp.dot(mixed_low, w_out, preferred_element_type=jnp.float32) + vectors[4]
    resid = inputs + attn_out
    normed_second, norm_second_back = jax.vjp(layer_norm, resid, vectors[5], vectors[6])
    acts_second = normed_second.astype(jnp.bfloat16)
    fc_bias = vectors[7 : 7 + fc_rows].reshape(hidden)
    preact = jnp.dot(acts_second, w_fc, preferred_element_type=jnp.float32) + fc_bias
    activated, gelu_back = jax.vjp(gelu_tanh, preact)
    act_low = activated.astype(jnp.bfloat16)
    mlp_out = (
        jnp.einsum("tf,df->td", act_low, w_proj, preferred_element_type=jnp.float32)
        + vectors[7 + fc_rows]
    )
    output = resid + mlp_out
    block_out = jnp.where(live_own[:, None], output, 0.0).astype(jnp.bfloat16)
    upstream = jnp.where(live_own[:, None], cotangent.astype(jnp.float32), 0.0)
    up_low = upstream.astype(jnp.bfloat16)
    grad_proj_bias = jnp.sum(up_low.astype(jnp.float32), axis=0)
    grad_proj = jnp.einsum("td,tf->df", up_low, act_low, preferred_element_type=jnp.float32)
    grad_act = jnp.dot(up_low, w_proj, preferred_element_type=jnp.float32)
    grad_pre = gelu_back(grad_act)[0].astype(jnp.bfloat16)
    grad_fc_bias = jnp.sum(grad_pre.astype(jnp.float32), axis=0)
    grad_fc = jnp.einsum("td,tf->df", acts_second, grad_pre, preferred_element_type=jnp.float32)
    grad_acts_second = jnp.einsum("tf,df->td", grad_pre, w_fc, preferred_element_type=jnp.float32)
    grad_resid_norm, grad_gain_second, grad_bias_second = norm_second_back(grad_acts_second)
    grad_resid = upstream + grad_resid_norm
    resid_low = grad_resid.astype(jnp.bfloat16)
    grad_out_bias = jnp.sum(resid_low.astype(jnp.float32), axis=0)
    grad_out = jnp.einsum("tc,td->cd", mixed_low, resid_low, preferred_element_type=jnp.float32)
    grad_mixed = jnp.einsum("td,cd->tc", resid_low, w_out, preferred_element_type=jnp.float32)
    grad_mixed = grad_mixed.astype(jnp.bfloat16).reshape(slots, heads, head_size)
    group_rows = keyval_group.shape[0]
    keys_back = keyval_group[:, :width].reshape(group_rows, heads, head_size)
    values_back = keyval_group[:, width:].reshape(group_rows, heads, head_size)
    weights_back = jnp.exp(scored(keyval_group) - log_total)
    grad_weights = jnp.einsum(
        "qhd,khd->hqk", grad_mixed, values_back, preferred_element_type=jnp.float32
    )
    row_delta = jnp.sum(grad_weights * weights_back, axis=-1, keepdims=True)
    grad_scores = (weights_back * (grad_weights - row_delta)).astype(jnp.bfloat16)
    grad_queries = (
        jnp.einsum("hqk,khd->qhd", grad_scores, keys_back, preferred_element_type=jnp.float32)
        * scale
    )
    grad_keys = (
        jnp.einsum("hqk,qhd->khd", grad_scores, queries, preferred_element_type=jnp.float32) * scale
    )
    grad_values = jnp.einsum(
        "hqk,qhd->khd",
        weights_back.astype(jnp.bfloat16),
        grad_mixed,
        preferred_element_type=jnp.float32,
    )
    grad_keyval_group = jnp.concatenate(
        [grad_keys.reshape(group_rows, width), grad_values.reshape(group_rows, width)], axis=1
    )
    grad_keyval = lax.psum_scatter(
        grad_keyval_group.astype(jnp.bfloat16), "shard", scatter_dimension=0, tiled=True
    ).astype(jnp.float32)
    grad_projected = jnp.concatenate(
        [grad_queries.reshape(slots, width), grad_keyval], axis=1
    ).astype(jnp.bfloat16)
    grad_column_sums = jnp.sum(grad_projected.astype(jnp.float32), axis=0)
    grad_qkv = jnp.einsum(
        "tc,te->ce", acts_first, grad_projected, preferred_element_type=jnp.float32
    )
    grad_acts_first = jnp.einsum(
        "te,ce->tc", grad_projected, w_qkv, preferred_element_type=jnp.float32
    )
    grad_input_norm, grad_gain_first, grad_bias_first = norm_first_back(grad_acts_first)
    grad_input = grad_resid + grad_input_norm
    grad_in = jnp.where(live_own[:, None], grad_input, 0.0).astype(jnp.bfloat16)
    attn_grad_all = jnp.concatenate([grad_qkv, grad_out], axis=1)
    mlp_grad_all = jnp.stack([grad_fc, grad_proj])
    vec_grad_all = jnp.concatenate(
        [
            jnp.stack(
                [
                    grad_gain_first,
                    grad_bias_first,
                    grad_column_sums[:width],
                    grad_column_sums[2 * width :],
                    grad_out_bias,
                    grad_gain_second,
                    grad_bias_second,
                ]
            ),
            grad_fc_bias.reshape(fc_rows, width),
            grad_proj_bias[None],
        ],
        axis=0,
    )
    owned = (
        lax.psum_scatter(
            attn_grad_all.astype(jnp.bfloat16), "shard", scatter_dimension=0, tiled=True
        ).astype(jnp.float32),
        lax.psum_scatter(
            mlp_grad_all.astype(jnp.bfloat16), "shard", scatter_dimension=1, tiled=True
        ).astype(jnp.float32),
        lax.psum_scatter(
            vec_grad_all.astype(jnp.bfloat16), "shard", scatter_dimension=1, tiled=True
        ).astype(jnp.float32),
    )
    summed = lax.psum((owned[0], owned[1], owned[2]), "dp")
    summed_attn = summed[0]
    summed_mlp = summed[1]
    summed_vec = summed[2]
    squares = (
        jnp.sum(summed_attn * summed_attn)
        + jnp.sum(summed_mlp * summed_mlp)
        + jnp.sum(summed_vec * summed_vec)
    )
    norm_total = jnp.sqrt(lax.psum(squares, "shard"))
    factor = jnp.minimum(1.0, CLIP_LIMIT / (norm_total + 1e-06))
    attn_grad, attn_w_new, attn_m_new, attn_v_new = adam_update(
        attn_w, attn_m, attn_v, summed_attn, factor, RATE_MATRIX, DECAY_MATRIX
    )
    mlp_grad, mlp_w_new, mlp_m_new, mlp_v_new = adam_update(
        mlp_w, mlp_m, mlp_v, summed_mlp, factor, RATE_MATRIX, DECAY_MATRIX
    )
    vec_grad, vec_w_new, vec_m_new, vec_v_new = adam_update(
        vec_w, vec_m, vec_v, summed_vec, factor, RATE_VECTOR, 0.0
    )
    return (
        block_out,
        grad_in,
        attn_grad,
        mlp_grad,
        vec_grad,
        attn_w_new,
        attn_m_new,
        attn_v_new,
        mlp_w_new,
        mlp_m_new,
        mlp_v_new,
        vec_w_new,
        vec_m_new,
        vec_v_new,
        norm_total.reshape(1),
    )


def solution(mesh):
    placed = (
        P(("dp", "shard"), None),
        P(("dp", "shard"), None),
        P("dp", None),
        P("dp", None),
        P("shard", None),
        P("shard", None),
        P("shard", None),
        P(None, "shard", None),
        P(None, "shard", None),
        P(None, "shard", None),
        P(None, "shard"),
        P(None, "shard"),
        P(None, "shard"),
    )
    return jax.shard_map(
        on_device,
        mesh=mesh,
        in_specs=placed,
        out_specs=(
            P(("dp", "shard"), None),
            P(("dp", "shard"), None),
            P("shard", None),
            P(None, "shard", None),
            P(None, "shard"),
            P("shard", None),
            P("shard", None),
            P("shard", None),
            P(None, "shard", None),
            P(None, "shard", None),
            P(None, "shard", None),
            P(None, "shard"),
            P(None, "shard"),
            P(None, "shard"),
            P(),
        ),
        check_vma=False,
    )
```

profile of v0, /device:TPU:0, one launch (start us, length us, event | category | flops | bytes accessed | tf_op | source)
XLA Modules:
  0.0 873.2 jit_solution(11160697730208753510)
XLA Ops:
  7.2 2.9 convert_element_type.98
  10.2 6.2 all-gather
  16.5 0.6 slice_reduce_fusion.2
  17.4 0.4 fusion.30
  17.8 32.7 %all-gather.5.cloned.1.call-done = bf16[768,3072]{1,0:T(8,128)(2,1)} async-done(((bf16[192,3072]{1,0:T(8,128)(2,1)}), bf16[768,3072]{1,0:T(8,128)(2,1)}) %all-gather.5.cloned.1.call-update) | async-done | bytes 4718608 | tf_op jit(solution)/shard_map/all_gather | solution.py:71
  50.5 4.2 fusion.12
  54.7 1.4 copy-done.14
  56.1 1.3 slice.86
  57.5 4.1 convert_element_type.106
  62.5 0.9 compare_and_fusion
  63.5 0.3 copy.51
  63.8 40.2 %all-gather.7.cloned.1.call-done = bf16[2048,1536]{1,0:T(8,128)(2,1)} async-done(((bf16[512,1536]{1,0:T(8,128)(2,1)}), bf16[2048,1536]{1,0:T(8,128)(2,1)}) %all-gather.7.cloned.1.call-update) | async-done | bytes 6291472 | tf_op jit(solution)/shard_map/all_gather | solution.py:101
  104.0 5.9 fusion.63
  109.9 5.0 copy.52
  114.9 4.9 copy.50
  119.9 22.5 %fusion = (f32[12,512]{1,0:T(8,128)S(1)}, f32[12,512,2048]{2,1,0:T(8,128)}) fusion(pred[512,2048]{1,0:T(8,128)(4,1)S(1)} %compare_and_fusion, bf16[512,12,64]{0,2,1:T(8,128)(2,1)S(1)} %bitcast.82, bf16[2048,12,64]{0,2,1:T(8,128)(2,1)} %bitcast.75), kind=kOutput, calls=%fused_computation.5 | convolution fusion | flops 1648355328 | bytes 55336960 | tf_op jit(solution)/shard_map/qhd,khd->hqk/dot_general | solution.py:106
  142.3 22.0 %exponential_reduce_fusion = f32[12,512]{1,0:T(8,128)S(1)} fusion(f32[12,512,2048]{2,1,0:T(8,128)} %get-tuple-element.55, f32[12,512]{1,0:T(8,128)S(1)} %get-tuple-element.54, pred[512,2048]{1,0:T(8,128)(4,1)S(1)} %compare_and_fusion), kind=kLoop, calls=%fused_computation.3 | loop fusion | flops 50325504 | bytes 51429376 | tf_op jit(solution)/shard_map/reduce_sum | solution.py:114
  164.3 20.3 %convolution_convert_fusion.5 = bf16[12,64,512]{2,1,0:T(8,128)(2,1)S(1)} fusion(bf16[2048,12,64]{0,2,1:T(8,128)(2,1)} %bitcast.79, f32[12,512,2048]{2,1,0:T(8,128)} %get-tuple-element.55, f32[12,512]{1,0:T(8,128)S(1)} %log_add_fusion, pred[512,2048]{1,0:T(8,128)(4,1)S(1)} %compare_and_fusion), kind=kOutput, calls=%fused_computation.78 | convolution fusion | flops 1661337600 | bytes 55336960 | tf_op jit(solution)/shard_map/hqk,khd->qhd/dot_general | solution.py:117
  184.7 2.5 fusion.65
  187.2 0.3 multiply_reduce_fusion.5
  187.6 4.9 fusion.14
  192.5 0.6 copy-done.36
  193.1 7.0 fusion.66
  200.1 3.0 multiply_reduce_fusion.3
  203.1 0.6 fusion.62
  203.8 1.1 copy-done.1
  204.9 0.4 fusion.60
  205.4 0.9 copy-done.17
  206.3 3.0 convolution_convert_fusion.6
  209.2 1.4 copy.53
  210.6 22.3 %convolution_convert_fusion.3 = bf16[12,64,2048]{2,1,0:T(8,128)(2,1)} fusion(bf16[512,12,64]{0,2,1:T(8,128)(2,1)S(1)} %bitcast.87, f32[12,512,2048]{2,1,0:T(8,128)} %get-tuple-element.55, f32[12,512]{1,0:T(8,128)S(1)} %log_add_fusion, pred[512,2048]{1,0:T(8,128)(4,1)S(1)} %compare_and_fusion), kind=kOutput, calls=%fused_computation.41 | convolution fusion | flops 1662517248 | bytes 55336960 | tf_op jit(solution)/shard_map/hqk,qhd->khd/dot_general | solution.py:167
  232.9 37.2 %multiply_reduce_fusion = (f32[12,512]{1,0:T(8,128)S(1)}, f32[12,512,2048]{2,1,0:T(8,128)}) fusion(f32[12,512,2048]{2,1,0:T(8,128)} %get-tuple-element.55, f32[12,512]{1,0:T(8,128)S(1)} %log_add_fusion, pred[512,2048]{1,0:T(8,128)(4,1)S(1)} %compare_and_fusion, bf16[512,12,64]{0,2,1:T(8,128)(2,1)S(1)} %bitcast.88, bf16[2048,12,64]{0,2,1:T(8,128)(2,1)} %bitcast.80), kind=kOutput, calls=%fused_computation.1 | convolution fusion | flops 1673521152 | bytes 105693184 | tf_op jit(solution)/shard_map/qhd,khd->hqk/dot_general | solution.py:155
  270.1 40.4 %multiply_convert_fusion = bf16[12,512,2048]{2,1,0:T(8,128)(2,1)} fusion(f32[12,512,2048]{2,1,0:T(8,128)} %get-tuple-element.60, f32[12,512,2048]{2,1,0:T(8,128)} %get-tuple-element.55, f32[12,512]{1,0:T(8,128)S(1)} %get-tuple-element.59, f32[12,512]{1,0:T(8,128)S(1)} %log_add_fusion, pred[512,2048]{1,0:T(8,128)(4,1)S(1)} %compare_and_fusion), kind=kLoop, calls=%fused_computation | loop fusion | flops 75497472 | bytes 126926848 | tf_op jit(solution)/shard_map/convert_element_type | solution.py:159
  310.5 12.8 %multiply_convert_fusion.1 = bf16[12,64,2048]{2,1,0:T(8,128)(2,1)S(1)} fusion(bf16[512,12,64]{0,2,1:T(8,128)(2,1)S(1)} %bitcast.83, bf16[12,512,2048]{2,1,0:T(8,128)(2,1)} %multiply_convert_fusion), kind=kOutput, calls=%fused_computation.19 | convolution fusion | flops 1613758464 | bytes 29097984 | tf_op jit(solution)/shard_map/hqk,qhd->khd/dot_general | solution.py:165
  323.3 3.8 pad_maximum_fusion.1
  327.2 6.7 fusion.10
  333.9 9.5 %fusion.11 = bf16[1,768,3072]{2,1,0:T(8,128)(2,1)} fusion(bf16[512,768]{1,0:T(8,128)(2,1)S(1)} %copy-done.13, pred[512]{0:T(512)(128)(4,1)S(1)} %dynamic_slice.9, f32[512,3072]{1,0:T(8,128)} %copy-done.39, f32[3072]{0:T(1024)S(1)} %add.222), kind=kOutput, calls=%fused_computation.33 | convolution fusion | flops 2435186688 | bytes 11809280 | tf_op jit(solution)/shard_map/td,tf->df/dot_general | solution.py:138
  343.4 14.1 %multiply_convert_fusion.3 = bf16[12,64,512]{2,1,0:T(8,128)(2,1)} fusion(bf16[2048,12,64]{0,2,1:T(8,128)(2,1)S(1)} %bitcast.76, bf16[12,512,2048]{2,1,0:T(8,128)(2,1)} %multiply_convert_fusion), kind=kOutput, calls=%fused_computation.69 | convolution fusion | flops 1611399168 | bytes 29097984 | tf_op jit(solution)/shard_map/hqk,khd->qhd/dot_general | solution.py:161
  357.5 28.4 %reduce-scatter.7.cloned.1.call-done = bf16[512,1536]{0,1:T(8,128)(2,1)} async-done(((bf16[2048,1536]{0,1:T(8,128)(2,1)}), bf16[512,1536]{0,1:T(8,128)(2,1)}) %reduce-scatter.7.cloned.1.call-update) | async-done | bytes 1572880 | tf_op jit(solution)/shard_map/reduce_scatter | solution.py:176
  385.9 5.3 fusion.56
  391.3 1.1 copy-done.10
  392.4 0.8 fusion.29
  393.3 0.4 fusion.36
  393.7 0.2 concatenate.23
  393.9 0.8 copy.56
  394.7 0.4 reduce-scatter.11.cloned.1.call-start
  395.2 8.3 pad_maximum_fusion
  403.5 2.1 convolution_convert_fusion.4
  405.7 3.7 convolution_convert_fusion.2
  409.4 2.8 pad_maximum_fusion.2
  412.3 1.4 copy-done.9
  413.7 9.1 %select_convert_fusion.1 = bf16[512,768]{1,0:T(8,128)(2,1)} fusion(f32[512,768]{1,0:T(8,128)S(1)} %copy-done.9, bf16[2,768,3072]{2,1,0:T(8,128)(2,1)} %all-gather.9.cloned.1.call-done, f32[768]{0:T(1024)S(1)} %copy-done.32, pred[512]{0:T(512)(128)(4,1)S(1)} %dynamic_slice.9, f32[512,3072]{1,0:T(8,128)} %copy-done.39, f32[3072]{0:T(1024)S(1)} %add.222), kind=kOutput, calls=%fused_computation.74 | convolution fusion | flops 2433220608 | bytes 13385216 | tf_op jit(solution)/shard_map/tf,df->td/dot_general | solution.py:130
  422.8 0.9 copy.57
  423.7 72.0 %reduce-scatter.11.cloned.1.call-done = bf16[2,192,3072]{2,1,0:T(8,128)(2,1)} async-done(((bf16[2,768,3072]{2,1,0:T(8,128)(2,1)}), bf16[2,192,3072]{2,1,0:T(8,128)(2,1)}) %reduce-scatter.11.cloned.1.call-update) | async-done | bytes 2359312 | tf_op jit(solution)/shard_map/reduce_scatter | solution.py:216
  495.7 51.1 %reduce-scatter.9.cloned.1.call-done = bf16[192,3072]{1,0:T(8,128)(2,1)} async-done(((bf16[768,3072]{1,0:T(8,128)(2,1)}), bf16[192,3072]{1,0:T(8,128)(2,1)}) %reduce-scatter.9.cloned.1.call-update) | async-done | bytes 1179664 | tf_op jit(solution)/shard_map/reduce_scatter | solution.py:213
  546.9 279.0 %all-reduce.2 = (f32[192,3072]{1,0:T(8,128)}, f32[2,192,3072]{2,1,0:T(8,128)}, f32[12,192]{1,0:T(8,128)S(1)}) all-reduce(bf16[192,3072]{1,0:T(8,128)(2,1)} %reduce-scatter.9.cloned.1.call-done, bf16[2,192,3072]{2,1,0:T(8,128)(2,1)} %reduce-scatter.11.cloned.1.call-done, ...), channel_id=1, replica_groups=mesh['dp'=8,'shard'=4] {'dp'}, use_global_device_ids=true, to_apply=%region_16.17 | all-reduce | flops 1771776 | bytes 10630656 | tf_op jit(solution)/shard_map/psum | solution.py:223
  825.9 0.6 multiply_reduce_fusion.6
  826.5 4.3 multiply_reduce_fusion.1
  830.8 1.2 multiply_reduce_fusion.2
  834.0 3.0 select_convert_fusion
  837.0 6.6 psum.31
  844.4 0.6 multiply_subtract_fusion.2
  845.1 8.6 multiply_subtract_fusion.1
  853.7 11.3 %multiply_subtract_fusion = (f32[2,192,3072]{2,1,0:T(8,128)}, f32[2,192,3072]{2,1,0:T(8,128)}, f32[2,192,3072]{2,1,0:T(8,128)}, f32[2,192,3072]{2,1,0:T(8,128)}) fusion(f32[2,192,3072]{2,1,0:T(8,128)S(1)} %bitcast.78, f32[2,192,3072]{2,1,0:T(8,128)} %param.21, f32[2,192,3072]{2,1,0:T(8,128)} %param.22, f32[2,192,3072]{2,1,0:T(8,128)} %get-tuple-element.31, ...), kind=kLoop, calls=%fused_computation.29 | loop fusion | flops 18874368 | bytes 37748740 | tf_op jit(solution)/shard_map/sub | solution.py:49
  (137 shorter events, 1.9 us)
Async XLA Ops:
  7.2 3.1 copy-start.18
  7.2 10.0 %copy-start.3 = (bf16[512,768]{1,0:T(8,128)(2,1)S(1)}, bf16[512,768]{1,0:T(8,128)(2,1)}, u32[]{:S(2)}) copy-start(bf16[512,768]{1,0:T(8,128)(2,1)} %param.13) | copy-start | bytes 2359300
  7.2 43.3 %all-gather.5.cloned.1.call-start = ((), (), s32[]{:S(2)}) async-start(), calls=%async_computation.4 | async-start | bytes 5898240 | tf_op jit(solution)/shard_map/all_gather | solution.py:71
  10.2 93.8 %all-gather.7.cloned.1.call-start = ((), (), s32[]{:S(2)}) async-start(), calls=%async_computation.5 | async-start | bytes 7864320 | tf_op jit(solution)/shard_map/all_gather | solution.py:101
  17.2 37.5 %copy-start.20 = (f32[768]{0:T(1024)}, f32[768]{0:T(1024)S(1)}, u32[]{:S(2)}) copy-start(f32[768]{0:T(1024)S(1)} %get-tuple-element.29) | copy-start | bytes 9220
  17.2 37.5 %copy-start.33 = (f32[768]{0:T(1024)}, f32[768]{0:T(1024)S(1)}, u32[]{:S(2)}) copy-start(f32[768]{0:T(1024)S(1)} %get-tuple-element.28) | copy-start | bytes 9220
  17.4 37.3 %copy-start.22 = (f32[512]{0:T(512)}, f32[512]{0:T(512)S(1)}, u32[]{:S(2)}) copy-start(f32[512]{0:T(512)S(1)} %broadcast_multiply_fusion.4) | copy-start | bytes 6148
  17.8 36.9 %copy-start.26 = (f32[512]{0:T(512)}, f32[512]{0:T(512)S(1)}, u32[]{:S(2)}) copy-start(f32[512]{0:T(512)S(1)} %fusion.30) | copy-start | bytes 6148
  17.8 36.9 %copy-start.28 = (f32[512]{0:T(512)}, f32[512]{0:T(512)S(1)}, u32[]{:S(2)}) copy-start(f32[512]{0:T(512)S(1)} %fusion.42) | copy-start | bytes 6148
  54.7 1.4 copy-start.14
  57.4 4.3 copy-start.37
  57.4 4.4 copy-start.35
  57.4 130.1 %all-gather.9.cloned.1.call-start = ((), (), s32[]{:S(2)}) async-start(), calls=%async_computation.6 | async-start | bytes 11796480 | tf_op jit(solution)/shard_map/all_gather | solution.py:72
  61.6 1.9 slice-start.2
  61.6 324.3 %reduce-scatter.7.cloned.1.call-start = ((), (), s32[]{:S(2)}) async-start(), calls=%async_computation.7 | async-start | bytes 7864320 | tf_op jit(solution)/shard_map/reduce_scatter | solution.py:176
  63.8 56.1 %copy-start.6 = (bf16[512,768]{0,1:T(8,128)(2,1)}, bf16[512,768]{0,1:T(8,128)(2,1)S(1)}, u32[]{:S(2)}) copy-start(bf16[512,768]{0,1:T(8,128)(2,1)S(1)} %copy.51) | copy-start | bytes 2359300
  184.7 2.5 copy-start.38
  187.2 140.1 %copy-start.8 = (f32[512,768]{1,0:T(8,128)}, f32[512,768]{1,0:T(8,128)S(1)}, u32[]{:S(2)}) copy-start(f32[512,768]{1,0:T(8,128)S(1)} %get-tuple-element.57) | copy-start | bytes 4718596
  187.5 5.0 copy-start.12
  187.6 5.5 copy-start.36
  193.1 7.1 copy-start.39
  200.1 3.0 copy-start.40
  203.8 1.1 copy-start.1
  203.8 1.6 copy-start.24
  205.4 0.9 copy-start.17
  270.1 40.4 %copy-start.7 = (bf16[512,768]{0,1:T(8,128)(2,1)S(1)}, bf16[512,768]{0,1:T(8,128)(2,1)}, u32[]{:S(2)}) copy-start(bf16[512,768]{0,1:T(8,128)(2,1)} %copy-done.6) | copy-start | bytes 2359300
  310.5 12.8 %copy-start.15 = (bf16[12,64,2048]{2,1,0:T(8,128)(2,1)S(1)}, bf16[12,64,2048]{2,1,0:T(8,128)(2,1)}, u32[]{:S(2)}) copy-start(bf16[12,64,2048]{2,1,0:T(8,128)(2,1)} %convolution_convert_fusion.3) | copy-start | bytes 9437188
  327.1 95.7 %reduce-scatter.13.cloned.1.call-start = ((), (), s32[]{:S(2)}) async-start(), calls=%async_computation.10 | async-start | bytes 245760
  327.2 6.7 copy-start.13
  333.9 9.5 %copy-start = (bf16[2048,768]{0,1:T(8,128)(2,1)S(1)}, bf16[2048,768]{0,1:T(8,128)(2,1)}, u32[]{:S(2)}) copy-start(bf16[2048,768]{0,1:T(8,128)(2,1)} %copy.52) | copy-start | bytes 9437188
  343.4 42.5 %copy-start.21 = (f32[768]{0:T(1024)S(1)}, f32[768]{0:T(1024)}, u32[]{:S(2)}) copy-start(f32[768]{0:T(1024)} %copy-done.20) | copy-start | bytes 9220
  343.4 42.5 %copy-start.23 = (f32[512]{0:T(512)S(1)}, f32[512]{0:T(512)}, u32[]{:S(2)}) copy-start(f32[512]{0:T(512)} %copy-done.22) | copy-start | bytes 6148
  385.9 5.4 copy-start.27
  385.9 6.5 copy-start.4
  385.9 6.5 copy-start.29
  385.9 7.3 copy-start.11
  385.9 7.3 copy-start.16
  391.3 1.1 copy-start.10
  394.7 101.0 %reduce-scatter.11.cloned.1.call-start = ((), (), s32[]{:S(2)}) async-start(), calls=%async_computation.9 | async-start | bytes 11796480 | tf_op jit(solution)/shard_map/reduce_scatter | solution.py:216
  403.5 2.2 copy-start.34
  403.5 143.4 %reduce-scatter.9.cloned.1.call-start = ((), (), s32[]{:S(2)}) async-start(), calls=%async_computation.8 | async-start | bytes 5898240 | tf_op jit(solution)/shard_map/reduce_scatter | solution.py:213
  412.3 1.4 copy-start.9
  412.3 1.4 copy-start.32
  825.9 4.9 copy-start.5
  826.5 7.5 copy-start.2
  826.5 7.5 copy-start.25
  830.8 13.6 %copy-start.19 = (f32[12,192]{1,0:T(8,128)S(1)}, f32[12,192]{1,0:T(8,128)}, u32[]{:S(2)}) copy-start(f32[12,192]{1,0:T(8,128)} %param.23) | copy-start | bytes 27652
  830.8 13.6 %copy-start.30 = (f32[12,192]{1,0:T(8,128)S(1)}, f32[12,192]{1,0:T(8,128)}, u32[]{:S(2)}) copy-start(f32[12,192]{1,0:T(8,128)} %param.24) | copy-start | bytes 27652
  830.8 13.6 %copy-start.31 = (f32[12,192]{1,0:T(8,128)S(1)}, f32[12,192]{1,0:T(8,128)}, u32[]{:S(2)}) copy-start(f32[12,192]{1,0:T(8,128)} %param.25) | copy-start | bytes 27652
  834.0 19.7 %slice-start = ((s8[4718592]{0:T(1024)(128)(4,1)}), s8[524288]{0:T(1024)(128)(4,1)S(1)}, s32[]{:S(2)}) async-start(s8[4718592]{0:T(1024)(128)(4,1)} %bitcast.77), calls=%async_computation.11 | async-start | bytes 1048576
  845.1 8.6 slice-start.1
Sparse Core Ops, SparseCore 0:
  10.3 40.1 all-gather.4
  57.5 46.4 all-gather.6
  106.1 64.2 all-gather.8
  327.2 58.5 reduce-scatter.6
  394.9 19.6 reduce-scatter.12
  417.2 78.4 reduce-scatter.10
  499.0 47.8 reduce-scatter.8
where the time goes:
time: 879 us; the launch traced here: 873 us
  blocking collectives  292 us (33%)
  waiting for transfers between devices  225 us (26%)
  matrix products  190 us (22%)
  other arithmetic  119 us (14%)
  local copies, waits for them, and re-layouts  28.4 us (3%)
  between operations  18.8 us (2%)
    psum x1, blocking collectives, on_device(): summed = lax.psum((owned[0], owned[1], owned[2]), 'dp')  279 us
    reduce_scatter x1, waiting for transfers between devices, on_device(): lax.psum_scatter(mlp_grad_all.astype(jnp.bfloat16), 'shard', scatter_dime...  72 us
    reduce_scatter x1, waiting for transfers between devices, on_device(): lax.psum_scatter(attn_grad_all.astype(jnp.bfloat16), 'shard', scatter_dim...  51.1 us
    convert_element_type x1, other arithmetic, on_device(): (weights_back * (grad_weights - row_delta)).astype(jnp.bfloat16)  40.4 us
    all_gather x1, waiting for transfers between devices, on_device(): keyval_group = lax.all_gather(keyval_own, 'shard', axis=0, tiled=True)  40.2 us
    dot_general x1, matrix products, on_device(): jnp.einsum('qhd,khd->hqk', grad_mixed, values_back, preferred_element_typ...  37.2 us
    all_gather x1, waiting for transfers between devices, on_device(): lax.all_gather(attn_w.astype(jnp.bfloat16), 'shard', axis=0, tiled=True)  32.7 us
    reduce_scatter x1, waiting for transfers between devices, on_device(): lax.psum_scatter(grad_keyval_group.astype(jnp.bfloat16), 'shard', scatter...  28.4 us
  transfers between devices with their start and end apart: 7, of which 5 were waited for; matrix products, arithmetic and copies ran while one was open for 17% of the time, Pallas kernels for 0%

commit v1 on v0

v1 whole, which is shorter than its diff:
```python
import functools

import jax
import jax.numpy as jnp
from jax import lax
from jax.experimental import pallas as pl
from jax.experimental.pallas import tpu as pltpu
from jax.sharding import PartitionSpec as P

HEADS = 12
STEP = 10
NORM_EPSILON = 1e-05
BETA_FIRST = 0.9
BETA_SECOND = 0.999
ADAM_EPSILON = 1e-08
RATE_MATRIX = 0.1
RATE_VECTOR = 0.2
DECAY_MATRIX = 0.1
CLIP_LIMIT = 1.0
MASKED_SCORE = -1e30
QUERY_BLOCK = 256
VMEM_LIMIT = 50 * 1024 * 1024
LOW = jnp.bfloat16
HIGH = jnp.float32


def dot_nn(a, b):
    return lax.dot_general(a, b, (((1,), (0,)), ((), ())), preferred_element_type=HIGH)


def dot_nt(a, b):
    return lax.dot_general(a, b, (((1,), (1,)), ((), ())), preferred_element_type=HIGH)


def low_t(a):
    return a.astype(HIGH).T.astype(LOW)


def normalize(features):
    centered = features - jnp.mean(features, axis=-1, keepdims=True)
    variance = jnp.mean(centered * centered, axis=-1, keepdims=True)
    inverse = lax.rsqrt(variance + NORM_EPSILON)
    return centered * inverse, inverse


def normalize_back(unit, inverse, grad_unit):
    first = jnp.mean(grad_unit, axis=-1, keepdims=True)
    second = jnp.mean(grad_unit * unit, axis=-1, keepdims=True)
    return inverse * (grad_unit - first - unit * second)


def cut_kernel(place, w_ref, vec_ref, *out_refs):
    parts = len(out_refs)
    rows, columns = w_ref.shape
    width = columns // 3
    cols = width // parts
    vec = vec_ref[...]
    tail = [
        jnp.concatenate([vec[3 * k + m : 3 * k + m + 1, :] for m in range(3)], axis=1)
        for k in range(vec.shape[0] // 3)
    ]
    tail.append(jnp.zeros((16 - len(tail), 3 * cols), HIGH))
    tail = jnp.concatenate(tail, axis=0).astype(LOW)
    for r in range(parts):
        starts = [k * width + r * cols for k in range(3)]
        piece = jnp.concatenate([w_ref[:, c : c + cols] for c in starts], axis=1).astype(LOW)
        for j in range(parts):

            @pl.when((place[0] ^ j) == r)
            def _():
                out_refs[j][:rows, :] = piece
                out_refs[j][rows:, :] = tail


def widen_kernel(half, out_ref, mlp_ref, wide_ref, *half_refs):
    rows, width = out_ref.shape
    start = pl.multiple_of(half[0] * (rows // 2), 16)
    near = pl.ds(start, rows // 2)
    sources = [(out_ref[...], out_ref[near, :])]
    for f in range(mlp_ref.shape[2] // width):
        span = slice(f * width, (f + 1) * width)
        sources += [(mlp_ref[n, :, span], mlp_ref[n, near, span]) for n in range(2)]
    split = half_refs[0].shape[1] // width
    for n, (block, part) in enumerate(sources):
        wide_ref[:, n * width : (n + 1) * width] = block.astype(LOW)
        k = int(n >= split)
        at = (n - k * split) * width
        half_refs[k][:, at : at + width] = part.astype(LOW)


def project_kernel(parts, place, *refs):
    x_refs, w_refs, refs = refs[:parts], refs[parts : 2 * parts], refs[2 * parts :]
    bias_ref, a1_ref, qkv_ref, wt_ref, vec_ref, w_scr, x_scr, sems = refs
    step = pl.program_id(0)
    rows = vec_ref.shape[1] // parts

    def copy(j):
        return pltpu.make_async_copy(x_refs[j], x_scr.at[j], sems.at[j])

    @pl.when(step == 0)
    def _():
        for j in range(parts):
            copy(j).start()
        vec_ref[...] = jnp.zeros_like(vec_ref)
        for j in range(parts):
            start = pl.multiple_of((place[0] ^ j) * rows, 16)
            w_scr[pl.ds(start, rows), :] = w_refs[j][:rows, :].astype(HIGH)
            tail = w_refs[j][rows:, :].astype(HIGH)
            for r in range(parts):

                @pl.when((place[0] ^ j) == r)
                def _():
                    for n in range(12):
                        piece = tail[n // 3 : n // 3 + 1, n % 3 * rows : (n % 3 + 1) * rows]
                        vec_ref[n : n + 1, r * rows : (r + 1) * rows] = piece

        wt_ref[...] = w_scr[...].T.astype(LOW)

    for j in range(parts):

        @pl.when(step == j)
        def _():
            copy(j).wait()

    unit, _ = normalize(x_scr[step].astype(HIGH))
    a1 = (unit * vec_ref[0:1, :] + vec_ref[1:2, :]).astype(LOW)
    a1_ref[...] = a1
    qkv_ref[...] = (dot_nt(wt_ref[...], a1) + bias_ref[...]).astype(LOW)


def masked_scores(q, kt, seg_q, seg_k, start):
    block = q.shape[0]
    out = []
    if start:
        s = dot_nn(q, kt[:, :start])
        out.append(jnp.where(seg_q == seg_k[:, :start], s, MASKED_SCORE))
    s = dot_nn(q, kt[:, start : start + block])
    row = lax.broadcasted_iota(jnp.int32, (block, block), 0)
    col = lax.broadcasted_iota(jnp.int32, (block, block), 1)
    allowed = (seg_q == seg_k[:, start : start + block]) & (col <= row)
    out.append(jnp.where(allowed, s, MASKED_SCORE))
    return out


def attend_kernel(scale, place, qt_ref, kt_ref, vt_ref, segc_ref, segr_ref, o_ref, lse_ref, v_scr):
    total = qt_ref.shape[1]
    per_part = o_ref.shape[2]
    block = min(QUERY_BLOCK, per_part)
    v_scr[...] = low_t(vt_ref[...])
    for start in range(0, total, block):
        span = slice(start, start + block)
        q = (qt_ref[:, span].astype(HIGH) * scale).T.astype(LOW)
        pieces = masked_scores(q, kt_ref, segc_ref[span, :], segr_ref, start)
        top = functools.reduce(jnp.maximum, [jnp.max(s, axis=1, keepdims=True) for s in pieces])
        weights = [jnp.exp(s - top) for s in pieces]
        mass = sum(jnp.sum(w, axis=1, keepdims=True) for w in weights)
        lse_ref[0, span, :] = top + jnp.log(mass)
        inverse = 1.0 / mass
        mixed = dot_nn((weights[-1] * inverse).astype(LOW), v_scr[span, :])
        if start:
            mixed += dot_nn((weights[0] * inverse).astype(LOW), v_scr[:start, :])
        inner = start % per_part
        o_ref[place[0] ^ (start // per_part), :, inner : inner + block] = mixed.T.astype(LOW)


def attend_back_kernel(
    scale, place, qt_ref, kt_ref, vt_ref, segc_ref, segr_ref, lse_ref, *refs
):
    *do_refs, out_ref, k_scr, do_scr, dk_scr, dv_scr = refs
    total = qt_ref.shape[1]
    parts, per_part = len(do_refs), do_refs[0].shape[1]
    block = min(QUERY_BLOCK, per_part)
    k_scr[...] = low_t(kt_ref[...])
    for j in range(parts):
        do_scr[place[0] ^ j] = do_refs[j][...]
    dk_scr[...] = jnp.zeros_like(dk_scr)
    dv_scr[...] = jnp.zeros_like(dv_scr)
    for start in range(0, total, block):
        span = slice(start, start + block)
        inner = start % per_part
        qt = qt_ref[:, span].astype(HIGH) * scale
        dot_ = do_scr[start // per_part, :, inner : inner + block]
        q = qt.T.astype(LOW)
        qt = qt.astype(LOW)
        do = low_t(dot_)
        pieces = masked_scores(q, kt_ref, segc_ref[span, :], segr_ref, start)
        spans = [slice(0, start), span] if start else [span]
        lse = lse_ref[0, span, :]
        weights = [jnp.exp(s - lse) for s in pieces]
        grads = [dot_nn(do, vt_ref[:, at]) for at in spans]
        delta = sum(jnp.sum(g * w, axis=1, keepdims=True) for g, w in zip(grads, weights))
        dq = None
        for at, w, g in zip(spans, weights, grads):
            ds = (w * (g - delta)).astype(LOW)
            term = dot_nn(ds, k_scr[at, :])
            dq = term if dq is None else dq + term
            dk_scr[:, at] += dot_nn(qt, ds)
            dv_scr[:, at] += dot_nn(dot_, w.astype(LOW))
        out_ref[0, :, span] = (dq * scale).T.astype(LOW)
    out_ref[1] = dk_scr[...].astype(LOW)
    out_ref[2] = dv_scr[...].astype(LOW)


def projection_back_kernel(heads, parts, place, half, *refs):
    x_refs, (a1_ref, *refs) = refs[:parts], refs[parts:]
    head_refs, refs = refs[:heads], refs[heads:]
    wt_ref, vec_ref, grads_ref, keep_ref, send_ref, qkeep_ref, qsend_ref, *scratch = refs
    g_scr, vec_scr, sums_scr, ext_scr, all_scr, x_scr, sems = scratch
    step = pl.program_id(0)
    cols = g_scr.shape[0] // 3
    extra = grads_ref.shape[0]
    count = qkeep_ref.shape[2] - 3 * cols

    def copy(j):
        return pltpu.make_async_copy(x_refs[j], x_scr.at[j], sems.at[j])

    @pl.when(step == 0)
    def _():
        for j in range(parts):
            copy(j).start()
        g_scr[...] = jnp.zeros_like(g_scr)
        vec_scr[...] = grads_ref[...]
        sums_scr[...] = jnp.zeros_like(sums_scr)

    for j in range(parts):

        @pl.when(step == j)
        def _():
            copy(j).wait()

    dqkv = jnp.concatenate([ref[k] for k in range(3) for ref in head_refs], axis=0)
    da1 = dot_nn(low_t(dqkv), wt_ref[...])

    @pl.when(step % 2 == 0)
    def _():
        keep_ref[0] = da1.astype(LOW)

    @pl.when(step % 2 == 1)
    def _():
        send_ref[0] = da1.astype(LOW)

    g_scr[...] += dot_nn(dqkv, a1_ref[...])
    unit, _ = normalize(x_scr[step].astype(HIGH))
    vec_scr[0:1, :] += jnp.sum(da1 * unit, axis=0, keepdims=True)
    vec_scr[1:2, :] += jnp.sum(da1, axis=0, keepdims=True)
    sums_scr[...] += jnp.sum(dqkv.astype(HIGH), axis=1, keepdims=True)

    @pl.when(step == pl.num_programs(0) - 1)
    def _():
        ext_scr[...] = vec_scr[...].T
        own = pl.ds(pl.multiple_of(place[0] * cols, 16), cols)
        ext_scr[own, 2:3] = sums_scr[:cols, :]
        ext_scr[own, 3:4] = sums_scr[2 * cols :, :]
        all_scr[:, : 3 * cols] = g_scr[...].T
        all_scr[:, 3 * cols : 3 * cols + extra] = ext_scr[...]
        rows = all_scr.shape[0] // parts
        for r in range(parts):
            for ref, side in ((qkeep_ref, half[0]), (qsend_ref, 1 - half[0])):
                start = pl.multiple_of(r * rows + side * (rows // 2), 16)
                ref[r] = all_scr[pl.ds(start, rows // 2), : 3 * cols + count].astype(LOW)


GELU_C = 0.7978845608028654
GELU_A = 0.044715


def mlp_kernel(
    parts, first_blocks, place, half, live_ref, x_ref, cot_ref, vec_ref, *refs
):
    o_refs, refs = refs[:parts], refs[parts:]
    own_ref, core_ref, *wide_refs = refs[:10]
    out_ref, *grad_refs = refs[10:15]
    dr1_ref, vecg_ref, *refs = refs[15:]
    do_refs, scratch = refs[:parts], refs[parts:]
    wide, ot_scr, r1_scr, a2_scr, a2t_scr, dy_scr, dyt_scr, y_scr, da2_scr, act_scr, sems = scratch
    step = pl.program_id(0)
    rows = o_refs[0].shape[0]
    slots, width = x_ref.shape
    bo, gain, shift, bp = (vec_ref[r : r + 1, :] for r in (4, 5, 6, 11))
    split = wide_refs[0].shape[1]
    live = lax.broadcasted_iota(jnp.int32, (slots, 1), 0) < live_ref[0]

    def copies(k):
        half_rows = rows // 2
        near, far = half[0] * half_rows, (1 - half[0]) * half_rows
        span = slice(0, split) if k == 0 else slice(split, wide.shape[1])
        sources = [(own_ref.at[:, span], 0, 0), (core_ref.at[:, span], 1, 0)]
        spots = [(2, near), (2, far), (3, near), (3, far)]
        sources += [(wide_refs[4 * k + n], *spot) for n, spot in enumerate(spots)]
        for n, (source, j, offset) in enumerate(sources):
            start = pl.multiple_of((place[0] ^ j) * rows + offset, 16)
            target = wide.at[pl.ds(start, source.shape[0]), span]
            yield pltpu.make_async_copy(source, target, sems.at[k, n])

    def block(n):
        return wide[:, pl.ds(pl.multiple_of(n * width, 128), width)]

    def permuted(scratch, value):
        for j in range(parts):
            scratch[j * rows : (j + 1) * rows, :] = value(pl.multiple_of((place[0] ^ j) * rows, 16))

    def put(value):
        value = value.astype(LOW)
        for k in range(2):

            @pl.when((step >= first_blocks) == bool(k))
            def _():
                keep, send = grad_refs[2 * k : 2 * k + 2]
                for j in range(parts):
                    (send if j % 2 else keep)[j // 2] = value[j * rows : (j + 1) * rows, :]

    @pl.when(step == 0)
    def _():
        for k in range(2):
            for copy in copies(k):
                copy.start()
        for j in range(parts):
            start = pl.multiple_of((place[0] ^ j) * rows, 16)
            ot_scr[pl.ds(start, rows), :] = o_refs[j][...]
        mixed = low_t(ot_scr[...])
        dy = jnp.where(live, cot_ref[...].astype(HIGH), 0.0)
        dy_scr[...] = dy.astype(LOW)
        ot_scr[...] = dy.T.astype(LOW)
        permuted(dyt_scr, lambda start: ot_scr[pl.ds(start, rows), :])
        for copy in copies(0):
            copy.wait()
        r1 = x_ref[...].astype(HIGH) + dot_nn(mixed, wide[:, :width]) + bo
        r1_scr[...] = r1
        unit, _ = normalize(r1)
        a2 = unit * gain + shift
        a2_scr[...] = a2.astype(LOW)
        ot_scr[...] = a2.T.astype(LOW)
        permuted(a2t_scr, lambda start: ot_scr[pl.ds(start, rows), :])
        vecg_ref[...] = jnp.zeros_like(vecg_ref)
        vecg_ref[11:12, :] = jnp.sum(dy, axis=0, keepdims=True)
        y_scr[...] = r1 + bp
        da2_scr[...] = jnp.zeros_like(da2_scr)

    @pl.when(step == first_blocks)
    def _():
        for copy in copies(1):
            copy.wait()

    last = pl.num_programs(0) - 1

    @pl.when((step < last) & (step % 2 == 0))
    def _():
        w_fc, w_pt = block(1 + step), block(2 + step)
        u = dot_nn(a2_scr[...], w_fc) + vec_ref[pl.ds(7 + step // 2, 1), :]
        square = u * u
        t = jnp.tanh(GELU_C * (u + GELU_A * (square * u)))
        grown = 0.5 * (1.0 + t)
        act = (u * grown).astype(LOW)
        act_scr[...] = act
        y_scr[...] += dot_nt(act, w_pt)
        slope = grown + 0.5 * u * (1.0 - t * t) * (GELU_C + (3.0 * GELU_C * GELU_A) * square)
        du = (dot_nn(dy_scr[...], w_pt) * slope).astype(LOW)
        vecg_ref[pl.ds(7 + step // 2, 1), :] = jnp.sum(du.astype(HIGH), axis=0, keepdims=True)
        da2_scr[...] += dot_nt(du, w_fc)
        put(dot_nn(a2t_scr[...], du))

    @pl.when((step < last) & (step % 2 == 1))
    def _():
        put(dot_nn(dyt_scr[...], act_scr[...]))

    @pl.when(step == last)
    def _():
        out_ref[...] = jnp.where(live, y_scr[...], 0.0).astype(LOW)
        unit, inverse = normalize(r1_scr[...])
        da2 = da2_scr[...]
        vecg_ref[5:6, :] = jnp.sum(da2 * unit, axis=0, keepdims=True)
        vecg_ref[6:7, :] = jnp.sum(da2, axis=0, keepdims=True)
        dr1 = dy_scr[...].astype(HIGH) + normalize_back(unit, inverse, da2 * gain)
        dr1_ref[...] = dr1
        low = dr1.astype(LOW)
        vecg_ref[4:5, :] = jnp.sum(low.astype(HIGH), axis=0, keepdims=True)
        put(dot_nn(jnp.concatenate([ref[...] for ref in o_refs], axis=0), low))
        for j in range(parts):
            start = pl.multiple_of((place[0] ^ j) * rows, 16)
            do_refs[j][...] = dot_nt(wide[pl.ds(start, rows), :width], low).astype(LOW)


def group_layout(length_row, count_row, slots):
    starts = jnp.cumsum(count_row) - count_row
    within = jnp.arange(slots, dtype=jnp.int32)
    position = (starts[:, None] + within[None, :]).reshape(-1)
    live_rows = (within[None, :] < count_row[:, None]).reshape(-1)
    boundary = jnp.cumsum(length_row)
    segment = jnp.sum((position[:, None] >= boundary[None, :]).astype(jnp.int32), axis=1)
    buffer_slot = jnp.arange(position.shape[0], dtype=jnp.int32)
    return jnp.where(live_rows, segment, -1 - buffer_slot)


def adam_update(master, first, second, gradient, factor, rate, decay):
    clipped = gradient * factor
    first_new = BETA_FIRST * first + (1.0 - BETA_FIRST) * clipped
    second_new = BETA_SECOND * second + (1.0 - BETA_SECOND) * clipped * clipped
    first_hat = first_new / (1.0 - BETA_FIRST**STEP)
    second_hat = second_new / (1.0 - BETA_SECOND**STEP)
    master_new = master - rate * (
        first_hat / (jnp.sqrt(second_hat) + ADAM_EPSILON) + decay * master
    )
    return (clipped, master_new, first_new, second_new)


def adam_kernel(fc_rows, factor_ref, _, *refs):
    grads, states, outs = refs[:4], refs[4:10], refs[10:]
    near = pl.program_id(0) < pl.num_programs(0) // 2
    first, second = grads[0][0], grads[1][0]
    factor = factor_ref[0]
    width = outs[0].shape[-1] // fc_rows
    qkv = jnp.where(near, grads[2][0], grads[3][0])[:, : 3 * width]

    def update(gradient, at, base):
        results = adam_update(
            *[states[base + n][at] for n in range(3)],
            gradient.astype(HIGH), factor, RATE_MATRIX, DECAY_MATRIX,
        )
        for n, result in enumerate(results):
            outs[base // 3 * 4 + n][at] = result

    blocks = [first[:, n : n + width] for n in range(0, first.shape[1], width)]
    blocks += [second[:, n : n + width] for n in range(0, second.shape[1], width)]
    for f in range(fc_rows):
        span = slice(f * width, (f + 1) * width)
        for n in range(2):
            update(blocks[2 * f + n], (n, 0, slice(None), span), 3)
    update(qkv, (0, slice(None), slice(0, 3 * width)), 0)
    update(blocks[-1], (0, slice(None), slice(3 * width, 4 * width)), 0)


def swap(array, axis, bit, count):
    return lax.ppermute(array, axis, [(i, i ^ bit) for i in range(count)])


def pick(array, index):
    return lax.dynamic_index_in_dim(array, index, 0, keepdims=False)


def deal(pieces, parts):
    return list(pieces[:1]) + [swap(pieces[j], "shard", j, parts) for j in range(1, parts)]


def in_order(relative, place, parts):
    relative = jnp.stack(relative)
    return jnp.stack([pick(relative, place ^ r) for r in range(parts)])


def collect(own, parts):
    have = [own]
    bit = parts // 2
    slots = [0]
    while bit:
        have = have + [swap(piece, "shard", bit, parts) for piece in have]
        slots = slots + [s ^ bit for s in slots]
        bit //= 2
    return [have[slots.index(j)] for j in range(parts)]


def after(value, *others):
    return lax.optimization_barrier((value, *others))[0]


def add_low(a, b):
    return (a.astype(HIGH) + b.astype(HIGH)).astype(LOW)


def bits_of(count):
    return [1 << n for n in range(count.bit_length() - 1)]


def halve(array, upper, dim):
    length = array.shape[dim] // 2
    keep = lax.dynamic_slice_in_dim(array, upper * length, length, dim)
    return keep, lax.dynamic_slice_in_dim(array, (1 - upper) * length, length, dim)


def scatter_half(array, dim, bit, replica, replicas):
    keep, send = halve(array, (replica // bit) % 2, dim)
    return keep, swap(send, "dp", bit, replicas)


def params(*semantics):
    return pltpu.CompilerParams(dimension_semantics=semantics, vmem_limit_bytes=VMEM_LIMIT)


def cost(flops, moved, special=0):
    return pl.CostEstimate(flops=int(flops), bytes_accessed=int(moved), transcendentals=int(special))


def whole(*shape):
    zeros = (0,) * len(shape)
    return pl.BlockSpec(shape, lambda *_: zeros)


def make_on_device(parts, replicas):
    def on_device(
        tokens, cotangent, lengths, counts,
        attn_w, attn_m, attn_v, mlp_w, mlp_m, mlp_v, vec_w, vec_m, vec_v,
    ):
        slots, width = tokens.shape
        rows = attn_w.shape[0]
        hidden = mlp_w.shape[2]
        fc_rows = hidden // width
        total = parts * slots
        head_size = width // HEADS
        own_heads = HEADS // parts
        own_cols = own_heads * head_size
        scale = head_size ** (-0.5)
        place = lax.axis_index("shard")
        replica = lax.axis_index("dp")
        prefetch = place.reshape(1).astype(jnp.int32)

        half = replica % 2
        side = half.reshape(1).astype(jnp.int32)

        x_all = collect(tokens, parts)
        w_pieces = pl.pallas_call(
            cut_kernel,
            grid_spec=pltpu.PrefetchScalarGridSpec(
                num_scalar_prefetch=1,
                grid=(1,),
                in_specs=[whole(rows, 3 * width), whole(vec_w.shape[0], rows)],
                out_specs=[whole(rows + 16, 3 * own_cols)] * parts,
            ),
            out_shape=[jax.ShapeDtypeStruct((rows + 16, 3 * own_cols), LOW)] * parts,
            compiler_params=params("arbitrary"),
            cost_estimate=cost(0, 4e6),
            name="cut",
        )(prefetch, attn_w, vec_w)
        w_local = deal(w_pieces, parts)

        blocks = 2 * fc_rows + 1
        split = (fc_rows // 2 * 2 + 1) * width
        wide_own, *wide_half = pl.pallas_call(
            widen_kernel,
            grid_spec=pltpu.PrefetchScalarGridSpec(
                num_scalar_prefetch=1,
                grid=(1,),
                in_specs=[
                    pl.BlockSpec((rows, width), lambda *_: (0, 3)),
                    whole(2, rows, hidden),
                ],
                out_specs=[
                    whole(rows, blocks * width),
                    whole(rows // 2, split),
                    whole(rows // 2, blocks * width - split),
                ],
            ),
            out_shape=[
                jax.ShapeDtypeStruct((rows, blocks * width), LOW),
                jax.ShapeDtypeStruct((rows // 2, split), LOW),
                jax.ShapeDtypeStruct((rows // 2, blocks * width - split), LOW),
            ],
            compiler_params=params("arbitrary"),
            cost_estimate=cost(0, 12e6),
            name="widen",
        )(side, attn_w, mlp_w)
        wide_own, *wide_half = lax.optimization_barrier((wide_own, *wide_half, *w_local, *x_all))[:3]
        near = [swap(mine, "shard", parts // 2, parts) for mine in wide_half]
        wide_core = swap(wide_own, "shard", 1, parts)

        segment = group_layout(lengths[0], counts[0], slots)
        seg_col = segment[:, None]
        seg_row = segment[None, :]
        own_vec = vec_w.astype(LOW).astype(HIGH)
        bias_local = jnp.concatenate(
            [own_vec[2], jnp.zeros((own_cols,), HIGH), own_vec[3]]
        )[:, None]

        a1, qkv, w_t, vectors = pl.pallas_call(
            functools.partial(project_kernel, parts),
            grid_spec=pltpu.PrefetchScalarGridSpec(
                num_scalar_prefetch=1,
                grid=(parts,),
                in_specs=[
                    *[pl.BlockSpec(memory_space=pl.ANY)] * parts,
                    *[whole(rows + 16, 3 * own_cols)] * parts,
                    whole(3 * own_cols, 1),
                ],
                out_specs=[
                    pl.BlockSpec((slots, width), lambda i, p: (p[0] ^ i, 0)),
                    pl.BlockSpec((3 * own_cols, slots), lambda i, p: (0, p[0] ^ i)),
                    whole(3 * own_cols, width),
                    whole(16, width),
                ],
                scratch_shapes=[
                    pltpu.VMEM((width, 3 * own_cols), HIGH),
                    pltpu.VMEM((parts, slots, width), LOW),
                    pltpu.SemaphoreType.DMA((parts,)),
                ],
            ),
            out_shape=[
                jax.ShapeDtypeStruct((total, width), LOW),
                jax.ShapeDtypeStruct((3 * own_cols, total), LOW),
                jax.ShapeDtypeStruct((3 * own_cols, width), LOW),
                jax.ShapeDtypeStruct((16, width), HIGH),
            ],
            compiler_params=params("arbitrary"),
            cost_estimate=cost(2 * total * width * 3 * own_cols * 3, 12e6),
            name="project",
        )(prefetch, *x_all, *w_local, bias_local)

        pair_flops = 2 * total * total * head_size * 4 // 2

        def head_specs(h):
            return [
                pl.BlockSpec((head_size, total), functools.partial(lambda k, *_: (k * own_heads + h, 0), k))
                for k in range(3)
            ]

        def attend(h, qkv):
            return pl.pallas_call(
                functools.partial(attend_kernel, scale),
                grid_spec=pltpu.PrefetchScalarGridSpec(
                    num_scalar_prefetch=1,
                    grid=(1,),
                    in_specs=head_specs(h) + [whole(total, 1), whole(1, total)],
                    out_specs=[whole(parts, head_size, slots), whole(1, total, 1)],
                    scratch_shapes=[pltpu.VMEM((total, head_size), LOW)],
                ),
                out_shape=[
                    jax.ShapeDtypeStruct((parts, head_size, slots), LOW),
                    jax.ShapeDtypeStruct((1, total, 1), HIGH),
                ],
                compiler_params=params("arbitrary"),
                cost_estimate=cost(2 * pair_flops, 4e6, total * total // 2),
                name="attend",
            )(prefetch, qkv, qkv, qkv, seg_col, seg_row)

        mixed, lse = [], []
        for h in range(own_heads):
            if h == 1:
                qkv, near[0] = lax.optimization_barrier((qkv, near[0]))
                far = [swap(near[0], "dp", 1, replicas)]
                turned = [swap(near[0], "shard", 1, parts)]
            head_mixed, head_lse = attend(h, qkv)
            mixed.append(head_mixed)
            lse.append(head_lse)
        near[1] = after(near[1], mixed[-1])
        far.append(swap(near[1], "dp", 1, replicas))
        mixed_own = deal(
            [jnp.concatenate([head[j] for head in mixed], axis=0) for j in range(parts)], parts
        )
        turned.append(swap(near[1], "shard", 1, parts))
        wide = [wide_own, wide_core]
        for k in range(2):
            wide += [near[k], far[k], turned[k], swap(far[k], "shard", 1, parts)]

        steps = blocks
        live_own = lax.dynamic_index_in_dim(counts[0], place, 0, keepdims=True)
        first_blocks = fc_rows // 2 * 2

        def grad_spec(k):
            first, last = ((0, first_blocks - 1), (first_blocks, steps - 1))[k]
            return pl.BlockSpec(
                (parts // 2, rows, width), lambda i, *_: (0, 0, jnp.clip(i, first, last) - first)
            )

        grad_columns = [first_blocks * width, (steps - first_blocks) * width]

        in_hbm = pl.BlockSpec(memory_space=pltpu.HBM)
        out = pl.pallas_call(
            functools.partial(mlp_kernel, parts, first_blocks),
            grid_spec=pltpu.PrefetchScalarGridSpec(
                num_scalar_prefetch=3,
                grid=(steps,),
                in_specs=[whole(slots, width), whole(slots, width), whole(16, width)]
                + [whole(own_cols, slots)] * parts
                + [in_hbm] * len(wide),
                out_specs=[whole(slots, width)]
                + [grad_spec(k) for k in range(2) for _ in range(2)]
                + [whole(slots, width), whole(16, width)]
                + [whole(own_cols, slots)] * parts,
                scratch_shapes=[
                    pltpu.VMEM((width, blocks * width), LOW),
                    pltpu.VMEM((width, slots), LOW),
                    pltpu.VMEM((slots, width), HIGH),
                    pltpu.VMEM((slots, width), LOW),
                    pltpu.VMEM((width, slots), LOW),
                    pltpu.VMEM((slots, width), LOW),
                    pltpu.VMEM((width, slots), LOW),
                    pltpu.VMEM((slots, width), HIGH),
                    pltpu.VMEM((slots, width), HIGH),
                    pltpu.VMEM((slots, width), LOW),
                    pltpu.SemaphoreType.DMA((2, 6)),
                ],
            ),
            out_shape=[jax.ShapeDtypeStruct((slots, width), LOW)]
            + [jax.ShapeDtypeStruct((parts // 2, rows, c), LOW) for c in grad_columns for _ in range(2)]
            + [jax.ShapeDtypeStruct((slots, width), HIGH), jax.ShapeDtypeStruct((16, width), HIGH)]
            + [jax.ShapeDtypeStruct((own_cols, slots), LOW)] * parts,
            compiler_params=params("arbitrary"),
            cost_estimate=cost(2 * slots * width * (6 * hidden + 3 * width), 30e6, slots * hidden),
            name="mlp",
        )(prefetch, side, live_own, tokens, cotangent, vectors, *mixed_own, *wide)
        block_out, keep_a, send_a, keep_b, send_b, grad_resid, mid_grads, *do_pieces = out

        do_own = deal(do_pieces, parts)
        got_a = swap(send_a, "shard", 1, parts)
        got_b = swap(send_b, "shard", 1, parts)
        own_a, other_a = [add_low(keep_a[n], got_a[n]) for n in range(2)]
        own_b, other_b = halve(add_low(keep_b, got_b), half, 1)
        *do_own, own_a, other_a, own_b, other_b = lax.optimization_barrier(
            (*do_own, own_a, other_a, own_b, other_b)
        )
        got_a = swap(other_a, "shard", parts // 2, parts)
        got_b = swap(other_b, "dp", 1, replicas)

        def attend_back(h, qkv):
            return pl.pallas_call(
                functools.partial(attend_back_kernel, scale),
                grid_spec=pltpu.PrefetchScalarGridSpec(
                    num_scalar_prefetch=1,
                    grid=(1,),
                    in_specs=head_specs(h)
                    + [whole(total, 1), whole(1, total), whole(1, total, 1)]
                    + [pl.BlockSpec((head_size, slots), lambda *_: (h, 0))] * parts,
                    out_specs=whole(3, head_size, total),
                    scratch_shapes=[
                        pltpu.VMEM((total, head_size), LOW),
                        pltpu.VMEM((parts, head_size, slots), LOW),
                        pltpu.VMEM((head_size, total), HIGH),
                        pltpu.VMEM((head_size, total), HIGH),
                    ],
                ),
                out_shape=jax.ShapeDtypeStruct((3, head_size, total), LOW),
                compiler_params=params("arbitrary"),
                cost_estimate=cost(
                    5 * pair_flops, 4e6, total * total // 2
                ),
                name="attend_back",
            )(prefetch, qkv, qkv, qkv, seg_col, seg_row, lse[h], *do_own)

        dqkv = [attend_back(h, qkv) for h in range(own_heads)]
        *dqkv, got_a = lax.optimization_barrier((*dqkv, got_a))
        own_a, other_a = halve(add_low(own_a, got_a), half, 0)
        dqkv[0] = after(dqkv[0], other_a)
        got_a = swap(other_a, "dp", 1, replicas)

        q_cols = 3 * own_cols
        extra = vec_w.shape[0]
        half_rows = rows // 2
        da1_keep, da1_send, own_q, other_q = pl.pallas_call(
            functools.partial(projection_back_kernel, own_heads, parts),
            grid_spec=pltpu.PrefetchScalarGridSpec(
                num_scalar_prefetch=2,
                grid=(parts,),
                in_specs=[
                    *[pl.BlockSpec(memory_space=pl.ANY)] * parts,
                    pl.BlockSpec((slots, width), lambda i, p, _: (p[0] ^ i, 0)),
                ]
                + [pl.BlockSpec((3, head_size, slots), lambda i, p, _: (0, 0, p[0] ^ i))] * own_heads
                + [whole(q_cols, width), whole(16, width), whole(16, width)],
                out_specs=[pl.BlockSpec((1, slots, width), lambda i, *_: (i // 2, 0, 0))] * 2
                + [whole(parts, half_rows, q_cols + extra)] * 2,
                scratch_shapes=[
                    pltpu.VMEM((q_cols, width), HIGH),
                    pltpu.VMEM((16, width), HIGH),
                    pltpu.VMEM((q_cols, 1), HIGH),
                    pltpu.VMEM((width, 16), HIGH),
                    pltpu.VMEM((width, q_cols + 64), HIGH),
                    pltpu.VMEM((parts, slots, width), LOW),
                    pltpu.SemaphoreType.DMA((parts,)),
                ],
            ),
            out_shape=[jax.ShapeDtypeStruct((parts // 2, slots, width), LOW)] * 2
            + [jax.ShapeDtypeStruct((parts, half_rows, q_cols + extra), LOW)] * 2,
            compiler_params=params("arbitrary"),
            cost_estimate=cost(4 * total * width * 3 * own_cols * 2, 16e6),
            name="projection_back",
        )(prefetch, side, *x_all, a1, *dqkv, w_t, vectors, mid_grads)

        share = rows // replicas
        z_bits = [bit for bit in (1 << n for n in range(1, 20)) if bit < replicas]
        got_q = swap(other_q, "dp", 1, replicas)
        got_b = after(got_b, own_q)
        sum_b = add_low(own_b, got_b)
        got_b = swap(sum_b[1], "shard", parts // 2, parts)
        da1_got = swap(da1_send, "shard", 1, parts)

        got_a = after(got_a, sum_b)
        sum_a = add_low(own_a, got_a)
        states = {"a": sum_a}
        dims = {"a": 0, "q": 1, "b": 0}
        pending = {"q": (own_q, got_q), "b": (sum_b[0], got_b)}
        last = sum_a
        pending["a"] = scatter_half(sum_a, 0, z_bits[0], replica, replicas)
        for name in ("q", "b"):
            keep, got = pending[name]
            last = add_low(keep, after(got, last))
            pending[name] = scatter_half(last, dims[name], z_bits[0], replica, replicas)
        parts_done = {}
        for bit in z_bits[1:]:
            for name in ("a", "q", "b"):
                keep, got = pending[name]
                last = add_low(keep, after(got, last))
                pending[name] = scatter_half(last, dims[name], bit, replica, replicas)
        for name in ("a", "q", "b"):
            keep, got = pending[name]
            last = add_low(keep, after(got, last))
            parts_done[name] = last
        part_a, part_q, part_b = (parts_done[name] for name in ("a", "q", "b"))
        all_a = lax.all_gather(part_a, "dp", axis=0)
        all_b = lax.all_gather(part_b, "dp", axis=0)

        def as_pair(value):
            high = lax.reduce_precision(value, 8, 7)
            return jnp.stack([high, value - high]).astype(LOW)

        main = part_q[:, :, :q_cols]
        squares = sum(jnp.sum(jnp.square(p.astype(HIGH))) for p in (part_a, part_b, main))
        vec_parts = part_q[:, :, q_cols:].transpose(1, 0, 2).reshape(1, share, parts * extra)
        shared = jnp.concatenate(
            [vec_parts, jnp.broadcast_to(as_pair(squares), (1, share, 2))], axis=2
        )
        pieces = jnp.concatenate([main, jnp.broadcast_to(shared, (parts,) + shared.shape[1:])], axis=2)
        dealt = in_order(deal([pick(pieces, place ^ j) for j in range(parts)], parts), place, parts)
        q_rows = (
            dealt[:, :, :q_cols]
            .reshape(parts, share, 3, own_cols)
            .transpose(1, 2, 0, 3)
            .reshape(share, 3 * width)
        )
        summed = jnp.sum(dealt[:, :, q_cols:].astype(HIGH), axis=0)
        vec_parts = summed[:, : parts * extra].reshape(share, parts, extra).astype(LOW)
        squares = jnp.sum(summed[0, parts * extra :]) + jnp.sum(jnp.square(vec_parts.astype(HIGH)))
        vec_own = lax.dynamic_index_in_dim(vec_parts, place, 1, keepdims=False)
        near_q = jnp.concatenate(
            [q_rows, vec_own, jnp.broadcast_to(as_pair(squares), (share, 2))], axis=1
        )[None]
        for bit in z_bits[::-1]:
            near_q = jnp.concatenate([near_q, swap(near_q, "dp", bit, replicas)], axis=0)
        far_q = swap(near_q, "dp", 1, replicas)

        def block_of(index):
            block = index % 2
            for bit in z_bits:
                block = block * 2 + index // bit % 2
            return block

        def index_of(block):
            index = 0
            for bit in z_bits[::-1]:
                index = index + block % 2 * bit
                block = block // 2
            return index + block

        turn = block_of(replica)
        small = jnp.concatenate([near_q[:, :, 3 * width :], far_q[:, :, 3 * width :]], axis=0)
        small = jnp.stack([pick(small, turn ^ r) for r in range(replicas)]).astype(HIGH)
        summed_vec = small[:, :, :extra].reshape(rows, extra).T
        squares = jnp.sum(small[:, 0, extra:])

        own_da1 = da1_keep[0].astype(HIGH) + da1_got[0].astype(HIGH)
        da1 = own_da1 + swap(add_low(da1_keep[1], da1_got[1]), "shard", 2, parts).astype(HIGH)
        unit, inverse = normalize(tokens.astype(HIGH))
        grad_input = grad_resid + normalize_back(unit, inverse, da1 * vectors[0:1])
        live_rows = jnp.arange(slots, dtype=jnp.int32) < live_own[0]
        grad_in = jnp.where(live_rows[:, None], grad_input, 0.0).astype(LOW)

        norm_total = jnp.sqrt(squares)
        factor = jnp.minimum(1.0, CLIP_LIMIT / (norm_total + 1e-06))
        near_count = replicas // 2
        q_block = (1,) + near_q.shape[1:]

        def gathered_spec(array):
            return pl.BlockSpec((1,) + array.shape[1:], lambda i, _, p: (index_of(i ^ p[0]), 0, 0))

        attn_shape = (replicas, share, 4 * width)
        mlp_shape = (2, replicas, share, hidden)
        attn_spec = pl.BlockSpec((1, share, 4 * width), lambda i, _, p: (i ^ p[0], 0, 0))
        mlp_spec = pl.BlockSpec((2, 1, share, hidden), lambda i, _, p: (0, i ^ p[0], 0, 0))
        updated = pl.pallas_call(
            functools.partial(adam_kernel, fc_rows),
            grid_spec=pltpu.PrefetchScalarGridSpec(
                num_scalar_prefetch=2,
                grid=(replicas,),
                in_specs=[gathered_spec(all_a), gathered_spec(all_b)]
                + [
                    pl.BlockSpec(q_block, lambda i, *_: (jnp.minimum(i, near_count - 1), 0, 0)),
                    pl.BlockSpec(q_block, lambda i, *_: (jnp.maximum(i - near_count, 0), 0, 0)),
                ]
                + [attn_spec] * 3
                + [mlp_spec] * 3,
                out_specs=[attn_spec] * 4 + [mlp_spec] * 4,
            ),
            out_shape=[jax.ShapeDtypeStruct(attn_shape, HIGH)] * 4
            + [jax.ShapeDtypeStruct(mlp_shape, HIGH)] * 4,
            compiler_params=params("arbitrary"),
            cost_estimate=cost(30 * 9 * rows * width, 54e6),
            name="adam",
        )(
            factor.reshape(1),
            turn.reshape(1).astype(jnp.int32),
            all_a,
            all_b,
            near_q,
            far_q,
            *[array.reshape(attn_shape) for array in (attn_w, attn_m, attn_v)],
            *[array.reshape(mlp_shape) for array in (mlp_w, mlp_m, mlp_v)],
        )
        attn_grad, attn_w_new, attn_m_new, attn_v_new = [u.reshape(attn_w.shape) for u in updated[:4]]
        mlp_grad, mlp_w_new, mlp_m_new, mlp_v_new = [u.reshape(mlp_w.shape) for u in updated[4:]]
        vec_grad, vec_w_new, vec_m_new, vec_v_new = adam_update(
            vec_w, vec_m, vec_v, summed_vec, factor, RATE_VECTOR, 0.0
        )
        return (
            block_out, grad_in, attn_grad, mlp_grad, vec_grad,
            attn_w_new, attn_m_new, attn_v_new, mlp_w_new, mlp_m_new, mlp_v_new,
            vec_w_new, vec_m_new, vec_v_new, norm_total.reshape(1),
        )

    return on_device


def solution(mesh):
    tokens = P(("dp", "shard"), None)
    groups = P("dp", None)
    attn = P("shard", None)
    mlp = P(None, "shard", None)
    vec = P(None, "shard")
    return jax.shard_map(
        make_on_device(mesh.shape["shard"], mesh.shape["dp"]),
        mesh=mesh,
        in_specs=(tokens, tokens, groups, groups) + (attn,) * 3 + (mlp,) * 3 + (vec,) * 3,
        out_specs=(tokens, tokens, attn, mlp, vec) + (attn,) * 3 + (mlp,) * 3 + (vec,) * 3 + (P(),),
        check_vma=False,
    )
```

time: 879 us -> 366 us (0.42)
  blocking collectives: 292 us -> 0 us
  matrix products: 190 us -> 0 us
  Pallas kernels: 0 us -> 128 us
  waiting for transfers between devices: 225 us -> 123 us
  other arithmetic: 119 us -> 23.7 us
  starting transfers between devices: 0.69 us -> 36.2 us
    psum x2 -> x0, blocking collectives: 286 us -> none  [the longest x1 279 us: on_device(): summed = lax.psum((owned[0], owned[1], owned[2]), 'dp')]
    dot_general x18 -> x0, matrix products: 190 us -> none  [the longest x1 37.2 us: on_device(): jnp.einsum('qhd,khd->hqk', grad_mixed, values_back, preferred_element_typ...]
    reduce_scatter x3 -> x0, waiting for transfers between devices: 152 us -> none  [the longest x1 72 us: on_device(): lax.psum_scatter(mlp_grad_all.astype(jnp.bfloat16), 'shard', scatter_dime...]
    pallas_call x0 -> x12, Pallas kernels: none -> 128 us  [the longest x1 33 us: on_device(): pl.pallas_call(functools.partial(mlp_kernel, parts, first_blocks), grid_s...]
    ppermute x0 -> x42, waiting for transfers between devices: none -> 87.5 us  [swap(): return lax.ppermute(array, axis, [(i, i ^ bit) for i in range(count)])]
    convert_element_type x4 -> x15, other arithmetic: 50.4 us -> 12.7 us  [the longest x12 9.86 us: add_low(): return (a.astype(HIGH) + b.astype(HIGH)).astype(LOW)]
    all_gather x3 -> x2, waiting for transfers between devices: 72.9 us -> 35.9 us  [the longest x1 35.8 us: on_device(): all_b = lax.all_gather(part_b, 'dp', axis=0)]
    ppermute x0 -> x42, starting transfers between devices: none -> 36.1 us  [swap(): return lax.ppermute(array, axis, [(i, i ^ bit) for i in range(count)])]
  transfers between devices with their start and end apart: 7 -> 44, of which waited for: 5 -> 21; matrix products, arithmetic and copies ran while one was open for 17% -> 8% of each run, Pallas kernels for 0% -> 21%
where the time goes in v1:
time: 366 us; the launch traced here: 361 us
  Pallas kernels  128 us (35%)
  waiting for transfers between devices  123 us (34%)
  starting transfers between devices  36.2 us (10%)
  local copies, waits for them, and re-layouts  25.6 us (7%)
  between operations  23.9 us (7%)
  other arithmetic  23.7 us (6%)
    ppermute x42, waiting for transfers between devices, swap(): return lax.ppermute(array, axis, [(i, i ^ bit) for i in range(count)])  87.5 us
    ppermute x42, starting transfers between devices, swap(): return lax.ppermute(array, axis, [(i, i ^ bit) for i in range(count)])  36.1 us
    all_gather x1, waiting for transfers between devices, on_device(): all_b = lax.all_gather(part_b, 'dp', axis=0)  35.8 us
    pallas_call x1, Pallas kernels, on_device(): pl.pallas_call(functools.partial(mlp_kernel, parts, first_blocks), grid_s...  33 us
    pallas_call x3, Pallas kernels, attend_back(): pl.pallas_call(functools.partial(attend_back_kernel, scale), grid_spec=pl...  27.5 us
    pallas_call x3, Pallas kernels, attend(): pl.pallas_call(functools.partial(attend_kernel, scale), grid_spec=pltpu.P...  22.8 us
    unnamed x95, local copies, waits for them, and re-layouts  20.9 us
    pallas_call x1, Pallas kernels, on_device(): pl.pallas_call(functools.partial(adam_kernel, fc_rows), grid_spec=pltpu.P...  19.1 us
  transfers between devices with their start and end apart: 44, of which 21 were waited for; matrix products, arithmetic and copies ran while one was open for 8% of the time, Pallas kernels for 21%

profile of v1, /device:TPU:0, one launch (start us, length us, event | category | flops | bytes accessed | tf_op | source)
XLA Modules:
  0.0 361.2 jit_solution(3804122116350994114)
XLA Ops:
  7.2 3.0 collective-permute-start.1
  10.3 1.7 copy-done
  12.6 1.5 cut.1
  15.4 1.3 collective-permute-start.5
  17.5 1.3 copy.49
  19.0 1.1 copy.59
  20.0 4.4 %widen.1 = (bf16[192,6912]{1,0:T(8,128)(2,1)}, bf16[96,3840]{1,0:T(8,128)(2,1)S(1)}, bf16[96,3072]{1,0:T(8,128)(2,1)S(1)}) custom-call(s32[1]{0:T(128)} %bitcast.1.half, f32[192,3072]{1,0:T(8,128)S(1)} %copy-done.1, f32[2,192,3072]{2,1,0:T(8,128)} %mlp_ref.1), custom_call_target="tpu_custom_call" | custom-call | bytes 12000000 | tf_op jit(solution)/shard_map/widen/pallas_call | solution.py:535
  24.4 4.4 %collective-permute-done.1.refs_2_ = bf16[512,768]{1,0:T(8,128)(2,1)S(1)} collective-permute-done((bf16[512,768]{1,0:T(8,128)(2,1)}, bf16[512,768]{1,0:T(8,128)(2,1)S(1)}, u32[]{:S(2)}, u32[]{:S(2)}) %collective-permute-start.1) | collective-permute-done | bytes 786464 | tf_op jit(solution)/shard_map/ppermute | solution.py:433
  29.1 5.6 %collective-permute-done.4.refs_6_ = bf16[208,576]{1,0:T(8,128)(2,1)} collective-permute-done((bf16[208,576]{1,0:T(8,128)(2,1)}, bf16[208,576]{1,0:T(8,128)(2,1)}, u32[]{:S(2)}, u32[]{:S(2)}) %collective-permute-start.4) | collective-permute-done | bytes 239648 | tf_op jit(solution)/shard_map/ppermute | solution.py:433
  34.6 4.1 %collective-permute-done.5.refs_7_ = bf16[208,576]{1,0:T(8,128)(2,1)} collective-permute-done((bf16[208,576]{1,0:T(8,128)(2,1)}, bf16[208,576]{1,0:T(8,128)(2,1)}, u32[]{:S(2)}, u32[]{:S(2)}) %collective-permute-start.5) | collective-permute-done | bytes 239648 | tf_op jit(solution)/shard_map/ppermute | solution.py:433
  38.8 1.4 collective-permute-start.6
  41.0 7.3 %project.1 = (bf16[2048,768]{1,0:T(8,128)(2,1)}, bf16[576,2048]{1,0:T(8,128)(2,1)}, bf16[576,768]{1,0:T(8,128)(2,1)}, f32[16,768]{1,0:T(8,128)S(1)}) custom-call(s32[1]{0:T(128)} %bitcast.place, bf16[512,768]{1,0:T(8,128)(2,1)S(1)} %copy-done.2, bf16[512,768]{1,0:T(8,128)(2,1)} %collective-permute-done.refs_1_, ...), custom_call_target="tpu_custom_call" | custom-call | flops 5435817984 | bytes 12000000 | tf_op jit(solution)/shard_map/project/pallas_call | solution.py:571
  48.3 7.5 %attend.3 = (bf16[4,64,512]{2,1,0:T(8,128)(2,1)S(1)}, f32[1,2048,1]{2,1,0:T(8,128)S(1)}) custom-call(s32[1]{0:T(128)} %bitcast.place, bf16[576,2048]{1,0:T(8,128)(2,1)} %get-tuple-element.95.qt_ref.kt_ref.vt_ref, bf16[576,2048]{1,0:T(8,128)(2,1)} %get-tuple-element.95.qt_ref.kt_ref.vt_ref, bf16[576,2048]{1,0:T(8,128)(2,1)} %get-tuple-element.95.qt_ref.kt_ref.vt_ref, ...), custom_call_target="tpu_custom_call" | custom-call | flops 2147483648 | bytes 4000000 | tf_op jit(solution)/shard_map/attend/pallas_call | solution.py:613
  55.8 1.0 copy-done.8
  56.8 1.4 collective-permute-done.6.refs_6_
  58.2 1.6 collective-permute-start.11
  59.8 7.5 %attend.5 = (bf16[4,64,512]{2,1,0:T(8,128)(2,1)S(1)}, f32[1,2048,1]{2,1,0:T(8,128)S(1)}) custom-call(s32[1]{0:T(128)} %bitcast.place, bf16[576,2048]{1,0:T(8,128)(2,1)} %get-tuple-element.95.qt_ref.kt_ref.vt_ref, bf16[576,2048]{1,0:T(8,128)(2,1)} %get-tuple-element.95.qt_ref.kt_ref.vt_ref, bf16[576,2048]{1,0:T(8,128)(2,1)} %get-tuple-element.95.qt_ref.kt_ref.vt_ref, ...), custom_call_target="tpu_custom_call" | custom-call | flops 2147483648 | bytes 4000000 | tf_op jit(solution)/shard_map/attend/pallas_call | solution.py:613
  67.4 1.0 copy-done.10
  68.4 7.8 %attend.4 = (bf16[4,64,512]{2,1,0:T(8,128)(2,1)S(1)}, f32[1,2048,1]{2,1,0:T(8,128)S(1)}) custom-call(s32[1]{0:T(128)} %bitcast.place, bf16[576,2048]{1,0:T(8,128)(2,1)} %get-tuple-element.95.qt_ref.kt_ref.vt_ref, bf16[576,2048]{1,0:T(8,128)(2,1)} %get-tuple-element.95.qt_ref.kt_ref.vt_ref, bf16[576,2048]{1,0:T(8,128)(2,1)} %get-tuple-element.95.qt_ref.kt_ref.vt_ref, ...), custom_call_target="tpu_custom_call" | custom-call | flops 2147483648 | bytes 4000000 | tf_op jit(solution)/shard_map/attend/pallas_call | solution.py:613
  78.7 5.7 %collective-permute-done.9.refs_3_ = bf16[192,512]{1,0:T(8,128)(2,1)S(1)} collective-permute-done((bf16[192,512]{1,0:T(8,128)(2,1)S(1)}, bf16[192,512]{1,0:T(8,128)(2,1)S(1)}, u32[]{:S(2)}, u32[]{:S(2)}) %collective-permute-start.9) | collective-permute-done | bytes 196640 | tf_op jit(solution)/shard_map/ppermute | solution.py:433
  85.1 3.3 collective-permute-done.8.refs_2_
  91.8 2.3 collective-permute-done.16.refs_12_
  94.9 1.1 copy-done.15
  96.0 0.9 copy-done.25
  96.9 0.9 copy-done.27
  98.8 33.0 %mlp.1 = (bf16[512,768]{1,0:T(8,128)(2,1)}, bf16[2,192,3072]{2,1,0:T(8,128)(2,1)}, bf16[2,192,3072]{2,1,0:T(8,128)(2,1)}, bf16[2,192,3840]{2,1,0:T(8,128)(2,1)},...) custom-call(s32[1]{0:T(128)} %bitcast.place, ...), custom_call_target="tpu_custom_call" | custom-call | flops 16307453952 | bytes 30000000 | tf_op jit(solution)/shard_map/mlp/pallas_call | solution.py:663
  137.5 1.9 collective-permute-done.21
  139.4 3.4 fusion.14
  142.7 1.1 collective-permute-done.22
  143.9 2.6 add_convert_fusion
  146.5 1.3 constant_dynamic-slice_fusion.12
  148.7 1.5 collective-permute-start.28
  150.3 9.0 %attend_back.5.refs_7_ = bf16[3,64,2048]{2,1,0:T(8,128)(2,1)S(1)} custom-call(s32[1]{0:T(128)} %bitcast.place, bf16[576,2048]{1,0:T(8,128)(2,1)} %get-tuple-element.95.qt_ref.kt_ref.vt_ref, bf16[576,2048]{1,0:T(8,128)(2,1)} %get-tuple-element.95.qt_ref.kt_ref.vt_ref, bf16[576,2048]{1,0:T(8,128)(2,1)} %get-tuple-element.95.qt_ref.kt_ref.vt_ref, ...), custom_call_target="tpu_custom_call" | custom-call | flops 5368709120 | bytes 4000000 | tf_op jit(solution)/shard_map/attend_back/pallas_call | solution.py:711
  160.2 9.3 %attend_back.4.refs_6_ = bf16[3,64,2048]{2,1,0:T(8,128)(2,1)S(1)} custom-call(s32[1]{0:T(128)} %bitcast.place, bf16[576,2048]{1,0:T(8,128)(2,1)} %get-tuple-element.95.qt_ref.kt_ref.vt_ref, bf16[576,2048]{1,0:T(8,128)(2,1)} %get-tuple-element.95.qt_ref.kt_ref.vt_ref, bf16[576,2048]{1,0:T(8,128)(2,1)} %get-tuple-element.95.qt_ref.kt_ref.vt_ref, ...), custom_call_target="tpu_custom_call" | custom-call | flops 5368709120 | bytes 4000000 | tf_op jit(solution)/shard_map/attend_back/pallas_call | solution.py:711
  170.4 9.2 %attend_back.3.refs_5_ = bf16[3,64,2048]{2,1,0:T(8,128)(2,1)S(1)} custom-call(s32[1]{0:T(128)} %bitcast.place, bf16[576,2048]{1,0:T(8,128)(2,1)} %get-tuple-element.95.qt_ref.kt_ref.vt_ref, bf16[576,2048]{1,0:T(8,128)(2,1)} %get-tuple-element.95.qt_ref.kt_ref.vt_ref, bf16[576,2048]{1,0:T(8,128)(2,1)} %get-tuple-element.95.qt_ref.kt_ref.vt_ref, ...), custom_call_target="tpu_custom_call" | custom-call | flops 5368709120 | bytes 4000000 | tf_op jit(solution)/shard_map/attend_back/pallas_call | solution.py:711
  181.1 12.8 %projection_back.1 = (bf16[2,512,768]{2,1,0:T(8,128)(2,1)}, bf16[2,512,768]{2,1,0:T(8,128)(2,1)}, bf16[4,96,588]{2,1,0:T(8,128)(2,1)S(1)}, bf16[4,96,588]{2,1,0:T(8,128)(2,1)S(1)}) custom-call(s32[1]{0:T(128)} %bitcast.place, s32[1]{0:T(128)} %bitcast.1.half, bf16[512,768]{1,0:T(8,128)(2,1)S(1)} %copy-done.3, bf16[512,768]{1,0:T(8,128)(2,1)} %collective-permute-done.refs_1_, ...), custom_call_target="tpu_custom_call" | custom-call | flops 7247757312 | bytes 16000000 | tf_op jit(solution)/shard_map/projection_back/pallas_call | solution.py:744
  193.9 1.6 collective-permute-start.26
  195.9 1.0 collective-permute-start.31
  197.1 9.3 %collective-permute-done.26 = bf16[4,96,588]{2,1,0:T(8,128)(2,1)S(1)} collective-permute-done((bf16[4,96,588]{2,1,0:T(8,128)(2,1)S(1)}, bf16[4,96,588]{2,1,0:T(8,128)(2,1)S(1)}, u32[]{:S(2)}, u32[]{:S(2)}) %collective-permute-start.26) | collective-permute-done | bytes 451616 | tf_op jit(solution)/shard_map/ppermute | solution.py:433
  206.4 1.6 collective-permute-start.30
  208.7 6.1 %collective-permute-done.31 = bf16[96,3840]{1,0:T(8,128)(2,1)S(1)} collective-permute-done((bf16[96,3840]{1,0:T(8,128)(2,1)S(1)}, bf16[96,3840]{1,0:T(8,128)(2,1)S(1)}, u32[]{:S(2)}, u32[]{:S(2)}) %collective-permute-start.31) | collective-permute-done | bytes 737312 | tf_op jit(solution)/shard_map/ppermute | solution.py:433
  215.1 1.6 collective-permute-start.34
  216.8 3.8 %collective-permute-done.29 = bf16[4,48,588]{2,1,0:T(8,128)(2,1)S(1)} collective-permute-done((bf16[4,48,588]{2,1,0:T(8,128)(2,1)S(1)}, bf16[4,48,588]{2,1,0:T(8,128)(2,1)S(1)}, u32[]{:S(2)}, u32[]{:S(2)}) %collective-permute-start.29) | collective-permute-done | bytes 225824 | tf_op jit(solution)/shard_map/ppermute | solution.py:433
  220.6 6.4 %collective-permute-start.33 = (bf16[24,3072]{1,0:T(8,128)(2,1)S(1)}, bf16[24,3072]{1,0:T(8,128)(2,1)S(1)}, u32[]{:S(2)}, u32[]{:S(2)}) collective-permute-start(bf16[24,3072]{1,0:T(8,128)(2,1)S(1)} %constant_dynamic-slice_fusion.7), channel_id=1, source_target_pairs={{0,16},{4,20},{8,24},{12,28},{16,0},{20,4},{24,8},{28,12},{1,17},{... | collective-permute-start | bytes 442376 | tf_op jit(solution)/shard_map/ppermute | solution.py:433
  227.3 3.9 %collective-permute-done.34 = bf16[48,3840]{1,0:T(8,128)(2,1)S(1)} collective-permute-done((bf16[48,3840]{1,0:T(8,128)(2,1)S(1)}, bf16[48,3840]{1,0:T(8,128)(2,1)S(1)}, u32[]{:S(2)}, u32[]{:S(2)}) %collective-permute-start.34) | collective-permute-done | bytes 368672 | tf_op jit(solution)/shard_map/ppermute | solution.py:433
  231.2 1.6 collective-permute-start.35
  232.9 1.3 multiply_reduce_fusion.1
  234.2 7.6 %collective-permute-done.32 = bf16[4,24,588]{2,1,0:T(8,128)(2,1)S(1)} collective-permute-done((bf16[4,24,588]{2,1,0:T(8,128)(2,1)S(1)}, bf16[4,24,588]{2,1,0:T(8,128)(2,1)S(1)}, u32[]{:S(2)}, u32[]{:S(2)}) %collective-permute-start.32) | collective-permute-done | bytes 112928 | tf_op jit(solution)/shard_map/ppermute | solution.py:433
  242.7 2.0 collective-permute-done.35
  244.7 1.3 multiply_reduce_fusion
  250.7 1.2 collective-permute-start.38
  252.0 2.4 collective-permute-done.37
  259.8 2.4 fusion.15
  262.2 1.1 collective-permute-start.25
  263.4 5.0 %collective-permute-done.39 = bf16[1,24,2318]{2,1,0:T(8,128)(2,1)S(1)} collective-permute-done((bf16[1,24,2318]{2,1,0:T(8,128)(2,1)S(1)}, bf16[1,24,2318]{2,1,0:T(8,128)(2,1)S(1)}, u32[]{:S(2)}, u32[]{:S(2)}) %collective-permute-start.39) | collective-permute-done | bytes 111296 | tf_op jit(solution)/shard_map/ppermute | solution.py:433
  269.2 11.3 %collective-permute-done.40 = bf16[2,24,2318]{2,1,0:T(8,128)(2,1)S(1)} collective-permute-done((bf16[2,24,2318]{2,1,0:T(8,128)(2,1)S(1)}, bf16[2,24,2318]{2,1,0:T(8,128)(2,1)S(1)}, u32[]{:S(2)}, u32[]{:S(2)}) %collective-permute-start.40) | collective-permute-done | bytes 222560 | tf_op jit(solution)/shard_map/ppermute | solution.py:433
  280.6 1.6 collective-permute-start.41
  282.3 2.3 fusion.34
  284.6 2.8 fusion.9
  287.4 5.3 %collective-permute-done.41.refs_3_ = bf16[4,24,2318]{2,1,0:T(8,128)(2,1)S(1)} collective-permute-done((bf16[4,24,2318]{2,1,0:T(8,128)(2,1)S(1)}, bf16[4,24,2318]{2,1,0:T(8,128)(2,1)S(1)}, u32[]{:S(2)}, u32[]{:S(2)}) %collective-permute-start.41) | collective-permute-done | bytes 445088 | tf_op jit(solution)/shard_map/ppermute | solution.py:433
  295.2 35.8 %all-gather.7.cloned.1.call-done = bf16[192,3840]{1,0:T(8,128)(2,1)} async-done(((bf16[24,3840]{1,0:T(8,128)(2,1)}), bf16[192,3840]{1,0:T(8,128)(2,1)}) %all-gather.7.cloned.1.call-update) | async-done | bytes 1474576 | tf_op jit(solution)/shard_map/all_gather | solution.py:805
  331.0 1.4 copy-done.4
  332.4 1.3 copy-done.5
  333.7 19.1 %adam.1 = (f32[8,24,3072]{2,1,0:T(8,128)}, f32[8,24,3072]{2,1,0:T(8,128)}, f32[8,24,3072]{2,1,0:T(8,128)}, f32[8,24,3072]{2,1,0:T(8,128)}, f32[2,8,24,3072]{3,2,...) custom-call(f32[1]{0:T(128)} %bitcast.46.factor_ref, ...), custom_call_target="tpu_custom_call" | custom-call | flops 39813120 | bytes 54000000 | tf_op jit(solution)/shard_map/adam/pallas_call | solution.py:874
  (228 shorter events, 30.5 us)
Async XLA Ops:
  7.2 9.8 %copy-start.43 = (s32[1,4]{1,0:T(1,128)S(1)}, s32[1,4]{1,0:T(1,128)}, u32[]{:S(2)}) copy-start(s32[1,4]{1,0:T(1,128)} %param.16) | copy-start | bytes 52
  7.2 10.0 %copy-start.45 = (s32[1,2]{1,0:T(1,128)S(1)}, s32[1,2]{1,0:T(1,128)}, u32[]{:S(2)}) copy-start(s32[1,2]{1,0:T(1,128)} %param.15) | copy-start | bytes 28
  7.2 288.0 %all-gather.5.cloned.1.call-start = ((), (), s32[]{:S(2)}) async-start(), calls=%async_computation | async-start | bytes 1327104 | tf_op jit(solution)/shard_map/all_gather | solution.py:804
  7.2 21.6 %collective-permute-start.1 = (bf16[512,768]{1,0:T(8,128)(2,1)}, bf16[512,768]{1,0:T(8,128)(2,1)S(1)}, u32[]{:S(2)}, u32[]{:S(2)}) collective-permute-start(bf16[512,768]{1,0:T(8,128)(2,1)} %refs_0_.3), channel_id=1, source_target_pairs={{0,2},{1,3},{2,0},{3,1},{4,6},{5,7},{6,4},{7,5},{8,10},{9,11},{10,... | collective-permute-start | bytes 2359304 | tf_op jit(solution)/shard_map/ppermute | solution.py:433
  10.2 28.5 %collective-permute-start = (bf16[512,768]{1,0:T(8,128)(2,1)}, bf16[512,768]{1,0:T(8,128)(2,1)}, u32[]{:S(2)}, u32[]{:S(2)}) collective-permute-start(bf16[512,768]{1,0:T(8,128)(2,1)} %refs_0_.3), channel_id=1, source_target_pairs={{0,1},{1,0},{2,3},{3,2},{4,5},{5,4},{6,7},{7,6},{8,9},{9,8},{10,11... | collective-permute-start | bytes 2359304 | tf_op jit(solution)/shard_map/ppermute | solution.py:433
  12.6 4.1 %copy-start.7 = (f32[12,192]{1,0:T(8,128)S(1)}, f32[12,192]{1,0:T(8,128)}, u32[]{:S(2)}) copy-start(f32[12,192]{1,0:T(8,128)} %vec_ref.1) | copy-start | bytes 27652
  12.6 7.4 %copy-start.1 = (f32[192,3072]{1,0:T(8,128)S(1)}, f32[192,3072]{1,0:T(8,128)}, u32[]{:S(2)}) copy-start(f32[192,3072]{1,0:T(8,128)} %out_ref.1) | copy-start | bytes 7077892
  14.9 14.2 %collective-permute-start.3 = (bf16[208,576]{1,0:T(8,128)(2,1)}, bf16[208,576]{1,0:T(8,128)(2,1)}, u32[]{:S(2)}, u32[]{:S(2)}) collective-permute-start(bf16[208,576]{1,0:T(8,128)(2,1)} %get-tuple-element.85), channel_id=1, source_target_pairs={{0,1},{1,0},{2,3},{3,2},{4,5},{5,4},{6,7},{7,6},{8,9},{9,8},{10,11... | collective-permute-start | bytes 718856 | tf_op jit(solution)/shard_map/ppermute | solution.py:433
  15.4 19.3 %collective-permute-start.4 = (bf16[208,576]{1,0:T(8,128)(2,1)}, bf16[208,576]{1,0:T(8,128)(2,1)}, u32[]{:S(2)}, u32[]{:S(2)}) collective-permute-start(bf16[208,576]{1,0:T(8,128)(2,1)} %get-tuple-element.86), channel_id=1, source_target_pairs={{0,2},{1,3},{2,0},{3,1},{4,6},{5,7},{6,4},{7,5},{8,10},{9,11},{10,... | collective-permute-start | bytes 718856 | tf_op jit(solution)/shard_map/ppermute | solution.py:433
  15.4 23.3 %collective-permute-start.5 = (bf16[208,576]{1,0:T(8,128)(2,1)}, bf16[208,576]{1,0:T(8,128)(2,1)}, u32[]{:S(2)}, u32[]{:S(2)}) collective-permute-start(bf16[208,576]{1,0:T(8,128)(2,1)} %get-tuple-element.87), channel_id=1, source_target_pairs={{0,3},{1,2},{2,1},{3,0},{4,7},{5,6},{6,5},{7,4},{8,11},{9,10},{10,... | collective-permute-start | bytes 718856 | tf_op jit(solution)/shard_map/ppermute | solution.py:433
  20.0 8.8 %copy-start.35 = (s32[2048,1]{1,0:T(8,128)S(1)}, s32[2048,1]{1,0:T(8,128)}, u32[]{:S(2)}) copy-start(s32[2048,1]{1,0:T(8,128)} %copy.49) | copy-start | bytes 24580
  20.0 8.8 %copy-start.39 = (pred[1,2048]{0,1:T(8,128)(4,1)S(1)}, pred[1,2048]{0,1:T(8,128)(4,1)}, u32[]{:S(2)}) copy-start(pred[1,2048]{0,1:T(8,128)(4,1)} %copy.59) | copy-start | bytes 6148
  24.4 16.6 %copy-start.2 = (bf16[512,768]{1,0:T(8,128)(2,1)S(1)}, bf16[512,768]{1,0:T(8,128)(2,1)}, u32[]{:S(2)}) copy-start(bf16[512,768]{1,0:T(8,128)(2,1)} %refs_0_.3) | copy-start | bytes 2359300
  24.4 16.6 %copy-start.17 = (bf16[208,576]{1,0:T(8,128)(2,1)S(1)}, bf16[208,576]{1,0:T(8,128)(2,1)}, u32[]{:S(2)}) copy-start(bf16[208,576]{1,0:T(8,128)(2,1)} %copy-done.16) | copy-start | bytes 718852
  28.8 10.0 %collective-permute-start.2 = (bf16[512,768]{1,0:T(8,128)(2,1)S(1)}, bf16[512,768]{1,0:T(8,128)(2,1)S(1)}, u32[]{:S(2)}, u32[]{:S(2)}) collective-permute-start(bf16[512,768]{1,0:T(8,128)(2,1)S(1)} %collective-permute-done.1.refs_2_), channel_id=1, source_target_pairs={{0,1},{1,0},{2,3},{3,2},{4,5},{5,4},{6,7},{7,6},{8,9},{9,8},{10,11... | collective-permute-start | bytes 2359304 | tf_op jit(solution)/shard_map/ppermute | solution.py:433
  38.8 2.2 copy-start.44
  38.8 19.4 %collective-permute-start.6 = (bf16[96,3840]{1,0:T(8,128)(2,1)S(1)}, bf16[96,3840]{1,0:T(8,128)(2,1)}, u32[]{:S(2)}, u32[]{:S(2)}) collective-permute-start(bf16[96,3840]{1,0:T(8,128)(2,1)S(1)} %get-tuple-element.94), channel_id=1, source_target_pairs={{0,2},{1,3},{2,0},{3,1},{4,6},{5,7},{6,4},{7,5},{8,10},{9,11},{10,... | collective-permute-start | bytes 2211848 | tf_op jit(solution)/shard_map/ppermute | solution.py:433
  40.2 36.0 %collective-permute-start.14 = (bf16[96,3072]{1,0:T(8,128)(2,1)S(1)}, bf16[96,3072]{1,0:T(8,128)(2,1)}, u32[]{:S(2)}, u32[]{:S(2)}) collective-permute-start(bf16[96,3072]{1,0:T(8,128)(2,1)S(1)} %get-tuple-element.100), channel_id=1, source_target_pairs={{0,2},{1,3},{2,0},{3,1},{4,6},{5,7},{6,4},{7,5},{8,10},{9,11},{10,... | collective-permute-start | bytes 1769480 | tf_op jit(solution)/shard_map/ppermute | solution.py:433
  40.9 54.0 %collective-permute-start.10 = (bf16[192,6912]{1,0:T(8,128)(2,1)}, bf16[192,6912]{1,0:T(8,128)(2,1)}, u32[]{:S(2)}, u32[]{:S(2)}) collective-permute-start(bf16[192,6912]{1,0:T(8,128)(2,1)} %get-tuple-element.98.refs_4_), channel_id=1, source_target_pairs={{0,1},{1,0},{2,3},{3,2},{4,5},{5,4},{6,7},{7,6},{8,9},{9,8},{10,11... | collective-permute-start | bytes 7962632 | tf_op jit(solution)/shard_map/ppermute | solution.py:433
  58.2 31.1 %collective-permute-start.11 = (bf16[96,3840]{1,0:T(8,128)(2,1)}, bf16[96,3840]{1,0:T(8,128)(2,1)}, u32[]{:S(2)}, u32[]{:S(2)}) collective-permute-start(bf16[96,3840]{1,0:T(8,128)(2,1)} %collective-permute-done.6.refs_6_), channel_id=1, source_target_pairs={{0,4},{4,0},{8,12},{12,8},{16,20},{20,16},{24,28},{28,24},{1,5},{5... | collective-permute-start | bytes 2211848 | tf_op jit(solution)/shard_map/ppermute | solution.py:433
  76.1 15.0 %collective-permute-start.15 = (bf16[96,3072]{1,0:T(8,128)(2,1)}, bf16[96,3072]{1,0:T(8,128)(2,1)S(1)}, u32[]{:S(2)}, u32[]{:S(2)}) collective-permute-start(bf16[96,3072]{1,0:T(8,128)(2,1)} %collective-permute-done.14.refs_10_), channel_id=1, source_target_pairs={{0,4},{4,0},{8,12},{12,8},{16,20},{20,16},{24,28},{28,24},{1,5},{5... | collective-permute-start | bytes 1769480 | tf_op jit(solution)/shard_map/ppermute | solution.py:433
  77.1 7.3 %collective-permute-start.9 = (bf16[192,512]{1,0:T(8,128)(2,1)S(1)}, bf16[192,512]{1,0:T(8,128)(2,1)S(1)}, u32[]{:S(2)}, u32[]{:S(2)}) collective-permute-start(bf16[192,512]{1,0:T(8,128)(2,1)S(1)} %pad_maximum_fusion.5), channel_id=1, source_target_pairs={{0,3},{1,2},{2,1},{3,0},{4,7},{5,6},{6,5},{7,4},{8,11},{9,10},{10,... | collective-permute-start | bytes 589832 | tf_op jit(solution)/shard_map/ppermute | solution.py:433
  78.0 10.4 %collective-permute-start.8 = (bf16[192,512]{1,0:T(8,128)(2,1)S(1)}, bf16[192,512]{1,0:T(8,128)(2,1)S(1)}, u32[]{:S(2)}, u32[]{:S(2)}) collective-permute-start(bf16[192,512]{1,0:T(8,128)(2,1)S(1)} %pad_maximum_fusion.4), channel_id=1, source_target_pairs={{0,2},{1,3},{2,0},{3,1},{4,6},{5,7},{6,4},{7,5},{8,10},{9,11},{10,... | collective-permute-start | bytes 589832 | tf_op jit(solution)/shard_map/ppermute | solution.py:433
  85.1 4.5 %collective-permute-start.7 = (bf16[192,512]{1,0:T(8,128)(2,1)S(1)}, bf16[192,512]{1,0:T(8,128)(2,1)S(1)}, u32[]{:S(2)}, u32[]{:S(2)}) collective-permute-start(bf16[192,512]{1,0:T(8,128)(2,1)S(1)} %pad_maximum_fusion.3), channel_id=1, source_target_pairs={{0,1},{1,0},{2,3},{3,2},{4,5},{5,4},{6,7},{7,6},{8,9},{9,8},{10,11... | collective-permute-start | bytes 589832 | tf_op jit(solution)/shard_map/ppermute | solution.py:433
  89.1 5.8 %collective-permute-start.12 = (bf16[96,3840]{1,0:T(8,128)(2,1)}, bf16[96,3840]{1,0:T(8,128)(2,1)}, u32[]{:S(2)}, u32[]{:S(2)}) collective-permute-start(bf16[96,3840]{1,0:T(8,128)(2,1)} %collective-permute-done.6.refs_6_), channel_id=1, source_target_pairs={{0,1},{1,0},{2,3},{3,2},{4,5},{5,4},{6,7},{7,6},{8,9},{9,8},{10,11... | collective-permute-start | bytes 2211848 | tf_op jit(solution)/shard_map/ppermute | solution.py:433
  89.3 5.6 %collective-permute-start.13 = (bf16[96,3840]{1,0:T(8,128)(2,1)}, bf16[96,3840]{1,0:T(8,128)(2,1)}, u32[]{:S(2)}, u32[]{:S(2)}) collective-permute-start(bf16[96,3840]{1,0:T(8,128)(2,1)} %collective-permute-done.11.refs_7_), channel_id=1, source_target_pairs={{0,1},{1,0},{2,3},{3,2},{4,5},{5,4},{6,7},{7,6},{8,9},{9,8},{10,11... | collective-permute-start | bytes 2211848 | tf_op jit(solution)/shard_map/ppermute | solution.py:433
  90.3 3.8 %collective-permute-start.16 = (bf16[96,3072]{1,0:T(8,128)(2,1)}, bf16[96,3072]{1,0:T(8,128)(2,1)S(1)}, u32[]{:S(2)}, u32[]{:S(2)}) collective-permute-start(bf16[96,3072]{1,0:T(8,128)(2,1)} %collective-permute-done.14.refs_10_), channel_id=1, source_target_pairs={{0,1},{1,0},{2,3},{3,2},{4,5},{5,4},{6,7},{7,6},{8,9},{9,8},{10,11... | collective-permute-start | bytes 1769480 | tf_op jit(solution)/shard_map/ppermute | solution.py:433
  91.2 3.7 %collective-permute-start.17 = (bf16[96,3072]{1,0:T(8,128)(2,1)S(1)}, bf16[96,3072]{1,0:T(8,128)(2,1)}, u32[]{:S(2)}, u32[]{:S(2)}) collective-permute-start(bf16[96,3072]{1,0:T(8,128)(2,1)S(1)} %collective-permute-done.15.refs_11_), channel_id=1, source_target_pairs={{0,1},{1,0},{2,3},{3,2},{4,5},{5,4},{6,7},{7,6},{8,9},{9,8},{10,11... | collective-permute-start | bytes 1769480 | tf_op jit(solution)/shard_map/ppermute | solution.py:433
  98.8 36.2 %copy-start.3 = (bf16[512,768]{1,0:T(8,128)(2,1)S(1)}, bf16[512,768]{1,0:T(8,128)(2,1)}, u32[]{:S(2)}) copy-start(bf16[512,768]{1,0:T(8,128)(2,1)} %refs_0_.3) | copy-start | bytes 2359300
  134.5 4.9 %collective-permute-start.21 = (bf16[2,192,3072]{2,1,0:T(8,128)(2,1)}, bf16[2,192,3072]{2,1,0:T(8,128)(2,1)}, u32[]{:S(2)}, u32[]{:S(2)}) collective-permute-start(bf16[2,192,3072]{2,1,0:T(8,128)(2,1)} %get-tuple-element.111), channel_id=1, source_target_pairs={{0,1},{1,0},{2,3},{3,2},{4,5},{5,4},{6,7},{7,6},{8,9},{9,8},{10,11... | collective-permute-start | bytes 7077896 | tf_op jit(solution)/shard_map/ppermute | solution.py:433
  134.9 9.0 %collective-permute-start.22 = (bf16[2,192,3840]{2,1,0:T(8,128)(2,1)}, bf16[2,192,3840]{2,1,0:T(8,128)(2,1)}, u32[]{:S(2)}, u32[]{:S(2)}) collective-permute-start(bf16[2,192,3840]{2,1,0:T(8,128)(2,1)} %get-tuple-element.113), channel_id=1, source_target_pairs={{0,1},{1,0},{2,3},{3,2},{4,5},{5,4},{6,7},{7,6},{8,9},{9,8},{10,11... | collective-permute-start | bytes 8847368 | tf_op jit(solution)/shard_map/ppermute | solution.py:433
  135.5 12.3 %collective-permute-start.18 = (bf16[192,512]{1,0:T(8,128)(2,1)S(1)}, bf16[192,512]{1,0:T(8,128)(2,1)S(1)}, u32[]{:S(2)}, u32[]{:S(2)}) collective-permute-start(bf16[192,512]{1,0:T(8,128)(2,1)S(1)} %copy-done.23), channel_id=1, source_target_pairs={{0,1},{1,0},{2,3},{3,2},{4,5},{5,4},{6,7},{7,6},{8,9},{9,8},{10,11... | collective-permute-start | bytes 589832 | tf_op jit(solution)/shard_map/ppermute | solution.py:433
  136.0 11.8 %collective-permute-start.19 = (bf16[192,512]{1,0:T(8,128)(2,1)S(1)}, bf16[192,512]{1,0:T(8,128)(2,1)S(1)}, u32[]{:S(2)}, u32[]{:S(2)}) collective-permute-start(bf16[192,512]{1,0:T(8,128)(2,1)S(1)} %copy-done.21), channel_id=1, source_target_pairs={{0,2},{1,3},{2,0},{3,1},{4,6},{5,7},{6,4},{7,5},{8,10},{9,11},{10,... | collective-permute-start | bytes 589832 | tf_op jit(solution)/shard_map/ppermute | solution.py:433
  136.6 11.2 %collective-permute-start.20 = (bf16[192,512]{1,0:T(8,128)(2,1)S(1)}, bf16[192,512]{1,0:T(8,128)(2,1)S(1)}, u32[]{:S(2)}, u32[]{:S(2)}) collective-permute-start(bf16[192,512]{1,0:T(8,128)(2,1)S(1)} %copy-done.19), channel_id=1, source_target_pairs={{0,3},{1,2},{2,1},{3,0},{4,7},{5,6},{6,5},{7,4},{8,11},{9,10},{10,... | collective-permute-start | bytes 589832 | tf_op jit(solution)/shard_map/ppermute | solution.py:433
  139.4 4.5 %copy-start.37 = (bf16[2,192,3840]{2,1,0:T(8,128)(2,1)S(1)}, bf16[2,192,3840]{2,1,0:T(8,128)(2,1)}, u32[]{:S(2)}) copy-start(bf16[2,192,3840]{2,1,0:T(8,128)(2,1)} %get-tuple-element.112) | copy-start | bytes 8847364
  146.5 3.8 %copy-start.11 = (f32[1,2048,1]{2,1,0:T(8,128)S(1)}, f32[1,2048,1]{2,1,0:T(8,128)}, u32[]{:S(2)}) copy-start(f32[1,2048,1]{2,1,0:T(8,128)} %copy-done.10) | copy-start | bytes 24580
  146.5 3.8 %copy-start.34 = (bf16[192,512]{1,0:T(8,128)(2,1)S(1)}, bf16[192,512]{1,0:T(8,128)(2,1)}, u32[]{:S(2)}) copy-start(bf16[192,512]{1,0:T(8,128)(2,1)} %copy-done.33) | copy-start | bytes 589828
  147.8 31.8 %collective-permute-start.23 = (bf16[192,3072]{1,0:T(8,128)(2,1)S(1)}, bf16[192,3072]{1,0:T(8,128)(2,1)S(1)}, u32[]{:S(2)}, u32[]{:S(2)}) collective-permute-start(bf16[192,3072]{1,0:T(8,128)(2,1)S(1)} %get-tuple-element.120), channel_id=1, source_target_pairs={{0,2},{1,3},{2,0},{3,1},{4,6},{5,7},{6,4},{7,5},{8,10},{9,11},{10,... | collective-permute-start | bytes 3538952 | tf_op jit(solution)/shard_map/ppermute | solution.py:433
  148.7 46.7 %collective-permute-start.28 = (bf16[2,96,3840]{2,1,0:T(8,128)(2,1)}, bf16[2,96,3840]{2,1,0:T(8,128)(2,1)S(1)}, u32[]{:S(2)}, u32[]{:S(2)}) collective-permute-start(bf16[2,96,3840]{2,1,0:T(8,128)(2,1)} %get-tuple-element.134), channel_id=1, source_target_pairs={{0,4},{4,0},{8,12},{12,8},{16,20},{20,16},{24,28},{28,24},{1,5},{5... | collective-permute-start | bytes 4423688 | tf_op jit(solution)/shard_map/ppermute | solution.py:433
  150.3 9.9 %copy-start.13 = (f32[1,2048,1]{2,1,0:T(8,128)S(1)}, f32[1,2048,1]{2,1,0:T(8,128)}, u32[]{:S(2)}) copy-start(f32[1,2048,1]{2,1,0:T(8,128)} %copy-done.12) | copy-start | bytes 24580
  160.2 10.2 %copy-start.9 = (f32[1,2048,1]{2,1,0:T(8,128)S(1)}, f32[1,2048,1]{2,1,0:T(8,128)}, u32[]{:S(2)}) copy-start(f32[1,2048,1]{2,1,0:T(8,128)} %copy-done.8) | copy-start | bytes 24580
  180.5 16.4 %collective-permute-start.27 = (bf16[96,3072]{1,0:T(8,128)(2,1)S(1)}, bf16[96,3072]{1,0:T(8,128)(2,1)S(1)}, u32[]{:S(2)}, u32[]{:S(2)}) collective-permute-start(bf16[96,3072]{1,0:T(8,128)(2,1)S(1)} %constant_dynamic-slice_fusion.11), channel_id=1, source_target_pairs={{0,4},{4,0},{8,12},{12,8},{16,20},{20,16},{24,28},{28,24},{1,5},{5... | collective-permute-start | bytes 1769480 | tf_op jit(solution)/shard_map/ppermute | solution.py:433
  193.9 12.5 %collective-permute-start.26 = (bf16[4,96,588]{2,1,0:T(8,128)(2,1)S(1)}, bf16[4,96,588]{2,1,0:T(8,128)(2,1)S(1)}, u32[]{:S(2)}, u32[]{:S(2)}) collective-permute-start(bf16[4,96,588]{2,1,0:T(8,128)(2,1)S(1)} %get-tuple-element.132), channel_id=1, source_target_pairs={{0,4},{4,0},{8,12},{12,8},{16,20},{20,16},{24,28},{28,24},{1,5},{5... | collective-permute-start | bytes 1354760 | tf_op jit(solution)/shard_map/ppermute | solution.py:433
  195.5 64.3 %collective-permute-start.24 = (bf16[2,512,768]{2,1,0:T(8,128)(2,1)}, bf16[2,512,768]{2,1,0:T(8,128)(2,1)}, u32[]{:S(2)}, u32[]{:S(2)}) collective-permute-start(bf16[2,512,768]{2,1,0:T(8,128)(2,1)} %get-tuple-element.130), channel_id=1, source_target_pairs={{0,1},{1,0},{2,3},{3,2},{4,5},{5,4},{6,7},{7,6},{8,9},{9,8},{10,11... | collective-permute-start | bytes 4718600 | tf_op jit(solution)/shard_map/ppermute | solution.py:433
  195.9 19.0 %collective-permute-start.31 = (bf16[96,3840]{1,0:T(8,128)(2,1)S(1)}, bf16[96,3840]{1,0:T(8,128)(2,1)S(1)}, u32[]{:S(2)}, u32[]{:S(2)}) collective-permute-start(bf16[96,3840]{1,0:T(8,128)(2,1)S(1)} %slice_bitcast_fusion), channel_id=1, source_target_pairs={{0,2},{1,3},{2,0},{3,1},{4,6},{5,7},{6,4},{7,5},{8,10},{9,11},{10,... | collective-permute-start | bytes 2211848 | tf_op jit(solution)/shard_map/ppermute | solution.py:433
  206.4 10.3 %collective-permute-start.30 = (bf16[48,3072]{1,0:T(8,128)(2,1)S(1)}, bf16[48,3072]{1,0:T(8,128)(2,1)S(1)}, u32[]{:S(2)}, u32[]{:S(2)}) collective-permute-start(bf16[48,3072]{1,0:T(8,128)(2,1)S(1)} %constant_dynamic-slice_fusion.9), channel_id=1, source_target_pairs={{0,8},{4,12},{8,0},{12,4},{16,24},{20,28},{24,16},{28,20},{1,9},{5... | collective-permute-start | bytes 884744 | tf_op jit(solution)/shard_map/ppermute | solution.py:433
  208.2 12.4 %collective-permute-start.29 = (bf16[4,48,588]{2,1,0:T(8,128)(2,1)S(1)}, bf16[4,48,588]{2,1,0:T(8,128)(2,1)S(1)}, u32[]{:S(2)}, u32[]{:S(2)}) collective-permute-start(bf16[4,48,588]{2,1,0:T(8,128)(2,1)S(1)} %constant_dynamic-slice_fusion.10), channel_id=1, source_target_pairs={{0,8},{4,12},{8,0},{12,4},{16,24},{20,28},{24,16},{28,20},{1,9},{5... | collective-permute-start | bytes 677384 | tf_op jit(solution)/shard_map/ppermute | solution.py:433
  215.1 16.1 %collective-permute-start.34 = (bf16[48,3840]{1,0:T(8,128)(2,1)S(1)}, bf16[48,3840]{1,0:T(8,128)(2,1)S(1)}, u32[]{:S(2)}, u32[]{:S(2)}) collective-permute-start(bf16[48,3840]{1,0:T(8,128)(2,1)S(1)} %constant_dynamic-slice_fusion.6), channel_id=1, source_target_pairs={{0,8},{4,12},{8,0},{12,4},{16,24},{20,28},{24,16},{28,20},{1,9},{5... | collective-permute-start | bytes 1105928 | tf_op jit(solution)/shard_map/ppermute | solution.py:433
  220.6 12.2 %collective-permute-start.33 = (bf16[24,3072]{1,0:T(8,128)(2,1)S(1)}, bf16[24,3072]{1,0:T(8,128)(2,1)S(1)}, u32[]{:S(2)}, u32[]{:S(2)}) collective-permute-start(bf16[24,3072]{1,0:T(8,128)(2,1)S(1)} %constant_dynamic-slice_fusion.7), channel_id=1, source_target_pairs={{0,16},{4,20},{8,24},{12,28},{16,0},{20,4},{24,8},{28,12},{1,17},{... | collective-permute-start | bytes 442376 | tf_op jit(solution)/shard_map/ppermute | solution.py:433
  227.2 14.7 %collective-permute-start.32 = (bf16[4,24,588]{2,1,0:T(8,128)(2,1)S(1)}, bf16[4,24,588]{2,1,0:T(8,128)(2,1)S(1)}, u32[]{:S(2)}, u32[]{:S(2)}) collective-permute-start(bf16[4,24,588]{2,1,0:T(8,128)(2,1)S(1)} %constant_dynamic-slice_fusion.8), channel_id=1, source_target_pairs={{0,16},{4,20},{8,24},{12,28},{16,0},{20,4},{24,8},{28,12},{1,17},{... | collective-permute-start | bytes 338696 | tf_op jit(solution)/shard_map/ppermute | solution.py:433
  231.2 13.5 %collective-permute-start.35 = (bf16[24,3840]{1,0:T(8,128)(2,1)S(1)}, bf16[24,3840]{1,0:T(8,128)(2,1)S(1)}, u32[]{:S(2)}, u32[]{:S(2)}) collective-permute-start(bf16[24,3840]{1,0:T(8,128)(2,1)S(1)} %constant_dynamic-slice_fusion.5), channel_id=1, source_target_pairs={{0,16},{4,20},{8,24},{12,28},{16,0},{20,4},{24,8},{28,12},{1,17},{... | collective-permute-start | bytes 552968 | tf_op jit(solution)/shard_map/ppermute | solution.py:433
  234.2 96.8 %all-gather.7.cloned.1.call-start = ((), (), s32[]{:S(2)}) async-start(), calls=%async_computation.1 | async-start | bytes 1658880 | tf_op jit(solution)/shard_map/all_gather | solution.py:805
  250.0 1.9 collective-permute-start.36
  250.1 4.3 %collective-permute-start.37 = (bf16[24,626]{1,0:T(8,128)(2,1)S(1)}, bf16[24,626]{1,0:T(8,128)(2,1)S(1)}, u32[]{:S(2)}, u32[]{:S(2)}) collective-permute-start(bf16[24,626]{1,0:T(8,128)(2,1)S(1)} %get-tuple-element.182), channel_id=1, source_target_pairs={{0,2},{1,3},{2,0},{3,1},{4,6},{5,7},{6,4},{7,5},{8,10},{9,11},{10,... | collective-permute-start | bytes 90152 | tf_op jit(solution)/shard_map/ppermute | solution.py:433
  250.7 3.6 %collective-permute-start.38 = (bf16[24,626]{1,0:T(8,128)(2,1)S(1)}, bf16[24,626]{1,0:T(8,128)(2,1)S(1)}, u32[]{:S(2)}, u32[]{:S(2)}) collective-permute-start(bf16[24,626]{1,0:T(8,128)(2,1)S(1)} %get-tuple-element.183), channel_id=1, source_target_pairs={{0,3},{1,2},{2,1},{3,0},{4,7},{5,6},{6,5},{7,4},{8,11},{9,10},{10,... | collective-permute-start | bytes 90152 | tf_op jit(solution)/shard_map/ppermute | solution.py:433
  259.8 8.6 %collective-permute-start.39 = (bf16[1,24,2318]{2,1,0:T(8,128)(2,1)S(1)}, bf16[1,24,2318]{2,1,0:T(8,128)(2,1)S(1)}, u32[]{:S(2)}, u32[]{:S(2)}) collective-permute-start(bf16[1,24,2318]{2,1,0:T(8,128)(2,1)S(1)} %bitcast.129), channel_id=1, source_target_pairs={{0,16},{4,20},{8,24},{12,28},{16,0},{20,4},{24,8},{28,12},{1,17},{... | collective-permute-start | bytes 333800 | tf_op jit(solution)/shard_map/ppermute | solution.py:433
  262.2 20.0 %collective-permute-start.25 = (bf16[512,768]{1,0:T(8,128)(2,1)}, bf16[512,768]{1,0:T(8,128)(2,1)S(1)}, u32[]{:S(2)}, u32[]{:S(2)}) collective-permute-start(bf16[512,768]{1,0:T(8,128)(2,1)} %fusion.15), channel_id=1, source_target_pairs={{0,2},{1,3},{2,0},{3,1},{4,6},{5,7},{6,4},{7,5},{8,10},{9,11},{10,... | collective-permute-start | bytes 2359304 | tf_op jit(solution)/shard_map/ppermute | solution.py:433
  268.5 12.1 %collective-permute-start.40 = (bf16[2,24,2318]{2,1,0:T(8,128)(2,1)S(1)}, bf16[2,24,2318]{2,1,0:T(8,128)(2,1)S(1)}, u32[]{:S(2)}, u32[]{:S(2)}) collective-permute-start(bf16[2,24,2318]{2,1,0:T(8,128)(2,1)S(1)} %pad_maximum_fusion.1), channel_id=1, source_target_pairs={{0,8},{4,12},{8,0},{12,4},{16,24},{20,28},{24,16},{28,20},{1,9},{5... | collective-permute-start | bytes 667592 | tf_op jit(solution)/shard_map/ppermute | solution.py:433
  280.6 12.1 %collective-permute-start.41 = (bf16[4,24,2318]{2,1,0:T(8,128)(2,1)S(1)}, bf16[4,24,2318]{2,1,0:T(8,128)(2,1)S(1)}, u32[]{:S(2)}, u32[]{:S(2)}) collective-permute-start(bf16[4,24,2318]{2,1,0:T(8,128)(2,1)S(1)} %pad_maximum_fusion.refs_2_), channel_id=1, source_target_pairs={{0,4},{4,0},{8,12},{12,8},{16,20},{20,16},{24,28},{28,24},{1,5},{5... | collective-permute-start | bytes 1335176 | tf_op jit(solution)/shard_map/ppermute | solution.py:433
  282.2 2.3 copy-start.36
  282.3 2.4 copy-start.38
  284.6 9.9 %copy-start.41 = (f32[12,192]{1,0:T(8,128)S(1)}, f32[12,192]{1,0:T(8,128)}, u32[]{:S(2)}) copy-start(f32[12,192]{1,0:T(8,128)} %param.24) | copy-start | bytes 27652
  284.6 9.9 %copy-start.42 = (f32[12,192]{1,0:T(8,128)S(1)}, f32[12,192]{1,0:T(8,128)}, u32[]{:S(2)}) copy-start(f32[12,192]{1,0:T(8,128)} %param.25) | copy-start | bytes 27652
  294.5 58.3 %copy-start.40 = (f32[192,12]{0,1:T(8,128)}, f32[192,12]{0,1:T(8,128)S(1)}, u32[]{:S(2)}) copy-start(f32[192,12]{0,1:T(8,128)S(1)} %copy.55) | copy-start | bytes 27652
  (26 other events, 25.5 us)
Sparse Core Ops, SparseCore 0:
  234.3 51.0 all-gather.4
  288.1 42.8 all-gather.6

commit v2 on v1

--- a/solution.py
+++ b/solution.py
@@ -19,7 +19,7 @@
 CLIP_LIMIT = 1.0
 MASKED_SCORE = -1e30
 QUERY_BLOCK = 256
-VMEM_LIMIT = 50 * 1024 * 1024
+VMEM_LIMIT = 60 * 1024 * 1024
 LOW = jnp.bfloat16
 HIGH = jnp.float32
 
@@ -404,12 +404,12 @@
 
 
 def adam_kernel(fc_rows, factor_ref, _, *refs):
-    grads, states, outs = refs[:4], refs[4:10], refs[10:]
+    grads, states, outs = refs[:5], refs[5:11], refs[11:]
     near = pl.program_id(0) < pl.num_programs(0) // 2
-    first, second = grads[0][0], grads[1][0]
+    first, second = grads[0][0], jnp.where(near, grads[1][0], grads[2][0])
     factor = factor_ref[0]
     width = outs[0].shape[-1] // fc_rows
-    qkv = jnp.where(near, grads[2][0], grads[3][0])[:, : 3 * width]
+    qkv = jnp.where(near, grads[3][0], grads[4][0])[:, : 3 * width]
 
     def update(gradient, at, base):
         results = adam_update(
@@ -773,65 +773,86 @@
 
         share = rows // replicas
         z_bits = [bit for bit in (1 << n for n in range(1, 20)) if bit < replicas]
+        tokens_seen = [own_q]
+
+        def seen(*values):
+            *values, _ = lax.optimization_barrier((*values, tokens_seen[-1]))
+            return values[0] if len(values) == 1 else values
+
+        def event(value):
+            tokens_seen.append(value)
+            return value
+
+        def scatter_on(name, keep, got, bit):
+            array = event(add_low(keep, seen(got)))
+            return scatter_half(array, {"q": 1}.get(name, 0), bit, replica, replicas)
+
+        last_bit = z_bits[-1]
+
+        def scatter_rest(name, state):
+            for bit in z_bits[1:]:
+                state = scatter_on(name, *state, bit)
+            return state
+
         got_q = swap(other_q, "dp", 1, replicas)
-        got_b = after(got_b, own_q)
-        sum_b = add_low(own_b, got_b)
+        sum_b = event(add_low(own_b, seen(got_b)))
         got_b = swap(sum_b[1], "shard", parts // 2, parts)
         da1_got = swap(da1_send, "shard", 1, parts)
-
-        got_a = after(got_a, sum_b)
-        sum_a = add_low(own_a, got_a)
-        states = {"a": sum_a}
-        dims = {"a": 0, "q": 1, "b": 0}
-        pending = {"q": (own_q, got_q), "b": (sum_b[0], got_b)}
-        last = sum_a
-        pending["a"] = scatter_half(sum_a, 0, z_bits[0], replica, replicas)
-        for name in ("q", "b"):
-            keep, got = pending[name]
-            last = add_low(keep, after(got, last))
-            pending[name] = scatter_half(last, dims[name], z_bits[0], replica, replicas)
-        parts_done = {}
-        for bit in z_bits[1:]:
-            for name in ("a", "q", "b"):
-                keep, got = pending[name]
-                last = add_low(keep, after(got, last))
-                pending[name] = scatter_half(last, dims[name], bit, replica, replicas)
-        for name in ("a", "q", "b"):
-            keep, got = pending[name]
-            last = add_low(keep, after(got, last))
-            parts_done[name] = last
-        part_a, part_q, part_b = (parts_done[name] for name in ("a", "q", "b"))
+        state_a = scatter_on("a", own_a, got_a, z_bits[0])
+        state_a = scatter_rest("a", state_a)
+        state_q = scatter_on("q", own_q, got_q, z_bits[0])
+        state_b = scatter_on("b", sum_b[0], got_b, z_bits[0])
+        part_a = event(add_low(state_a[0], seen(state_a[1])))
         all_a = lax.all_gather(part_a, "dp", axis=0)
-        all_b = lax.all_gather(part_b, "dp", axis=0)
-
-        def as_pair(value):
-            high = lax.reduce_precision(value, 8, 7)
-            return jnp.stack([high, value - high]).astype(LOW)
+        state_q = scatter_rest("q", state_q)
+        state_b = scatter_rest("b", state_b)
+        part_q = event(add_low(state_q[0], seen(state_q[1])))
 
         main = part_q[:, :, :q_cols]
-        squares = sum(jnp.sum(jnp.square(p.astype(HIGH))) for p in (part_a, part_b, main))
         vec_parts = part_q[:, :, q_cols:].transpose(1, 0, 2).reshape(1, share, parts * extra)
-        shared = jnp.concatenate(
-            [vec_parts, jnp.broadcast_to(as_pair(squares), (1, share, 2))], axis=2
-        )
-        pieces = jnp.concatenate([main, jnp.broadcast_to(shared, (parts,) + shared.shape[1:])], axis=2)
-        dealt = in_order(deal([pick(pieces, place ^ j) for j in range(parts)], parts), place, parts)
+        vec_parts = jnp.broadcast_to(vec_parts, (parts,) + vec_parts.shape[1:])
+        pieces = jnp.concatenate([main, vec_parts], axis=2)
+        dealt = deal([pick(pieces, place ^ j) for j in range(parts)], parts)
+        dealt = in_order(seen(*dealt), place, parts)
         q_rows = (
             dealt[:, :, :q_cols]
             .reshape(parts, share, 3, own_cols)
             .transpose(1, 2, 0, 3)
             .reshape(share, 3 * width)
         )
-        summed = jnp.sum(dealt[:, :, q_cols:].astype(HIGH), axis=0)
-        vec_parts = summed[:, : parts * extra].reshape(share, parts, extra).astype(LOW)
-        squares = jnp.sum(summed[0, parts * extra :]) + jnp.sum(jnp.square(vec_parts.astype(HIGH)))
-        vec_own = lax.dynamic_index_in_dim(vec_parts, place, 1, keepdims=False)
-        near_q = jnp.concatenate(
-            [q_rows, vec_own, jnp.broadcast_to(as_pair(squares), (share, 2))], axis=1
-        )[None]
-        for bit in z_bits[::-1]:
-            near_q = jnp.concatenate([near_q, swap(near_q, "dp", bit, replicas)], axis=0)
-        far_q = swap(near_q, "dp", 1, replicas)
+        vec_parts = jnp.sum(dealt[:, :, q_cols:].astype(HIGH), axis=0).astype(LOW)
+        vec_own = lax.dynamic_index_in_dim(
+            vec_parts.reshape(share, parts, extra), place, 1, keepdims=False
+        )
+        near_q = event(jnp.concatenate([q_rows, vec_own], axis=1)[None])
+        got_q = swap(near_q, "dp", last_bit, replicas)
+        near_b = event(add_low(state_b[0], seen(state_b[1])))[None]
+        got_b = swap(near_b, "dp", last_bit, replicas)
+        squares = sum(jnp.sum(jnp.square(p.astype(HIGH))) for p in (part_a, near_b, main))
+        squares += jnp.where(place == 0, jnp.sum(jnp.square(vec_parts.astype(HIGH))), 0.0)
+        squares = squares.reshape(1, 1)
+        hops = [("shard", bit, parts) for bit in (1 << n for n in range(20)) if bit < parts]
+        hops += [("dp", bit, replicas) for bit in (1 << n for n in range(20)) if bit < replicas]
+        hops = iter(hops)
+        pending = swap(squares, *next(hops))
+
+        def norm_hop():
+            nonlocal squares, pending
+            if pending is None:
+                return
+            squares = event(squares + seen(pending))
+            hop = next(hops, None)
+            pending = None if hop is None else swap(squares, *hop)
+
+        for bit in z_bits[-2::-1] + [1]:
+            near_q = event(jnp.concatenate([near_q, seen(got_q)], axis=0))
+            got_q = swap(near_q, "dp", bit, replicas)
+            near_b = event(jnp.concatenate([near_b, seen(got_b)], axis=0))
+            got_b = swap(near_b, "dp", bit, replicas)
+            norm_hop()
+        while pending is not None:
+            norm_hop()
+        far_q, far_b = seen(got_q, got_b)
 
         def block_of(index):
             block = index % 2
@@ -850,7 +871,6 @@
         small = jnp.concatenate([near_q[:, :, 3 * width :], far_q[:, :, 3 * width :]], axis=0)
         small = jnp.stack([pick(small, turn ^ r) for r in range(replicas)]).astype(HIGH)
         summed_vec = small[:, :, :extra].reshape(rows, extra).T
-        squares = jnp.sum(small[:, 0, extra:])
 
         own_da1 = da1_keep[0].astype(HIGH) + da1_got[0].astype(HIGH)
         da1 = own_da1 + swap(add_low(da1_keep[1], da1_got[1]), "shard", 2, parts).astype(HIGH)
@@ -859,10 +879,16 @@
         live_rows = jnp.arange(slots, dtype=jnp.int32) < live_own[0]
         grad_in = jnp.where(live_rows[:, None], grad_input, 0.0).astype(LOW)
 
-        norm_total = jnp.sqrt(squares)
+        norm_total = jnp.sqrt(squares[0, 0])
         factor = jnp.minimum(1.0, CLIP_LIMIT / (norm_total + 1e-06))
         near_count = replicas // 2
-        q_block = (1,) + near_q.shape[1:]
+        def near_spec(array):
+            block = (1,) + array.shape[1:]
+            return pl.BlockSpec(block, lambda i, *_: (jnp.minimum(i, near_count - 1), 0, 0))
+
+        def far_spec(array):
+            block = (1,) + array.shape[1:]
+            return pl.BlockSpec(block, lambda i, *_: (jnp.maximum(i - near_count, 0), 0, 0))
 
         def gathered_spec(array):
             return pl.BlockSpec((1,) + array.shape[1:], lambda i, _, p: (index_of(i ^ p[0]), 0, 0))
@@ -876,11 +902,8 @@
             grid_spec=pltpu.PrefetchScalarGridSpec(
                 num_scalar_prefetch=2,
                 grid=(replicas,),
-                in_specs=[gathered_spec(all_a), gathered_spec(all_b)]
-                + [
-                    pl.BlockSpec(q_block, lambda i, *_: (jnp.minimum(i, near_count - 1), 0, 0)),
-                    pl.BlockSpec(q_block, lambda i, *_: (jnp.maximum(i - near_count, 0), 0, 0)),
-                ]
+                in_specs=[gathered_spec(all_a)]
+                + [near_spec(near_b), far_spec(far_b), near_spec(near_q), far_spec(far_q)]
                 + [attn_spec] * 3
                 + [mlp_spec] * 3,
                 out_specs=[attn_spec] * 4 + [mlp_spec] * 4,
@@ -894,7 +917,8 @@
             factor.reshape(1),
             turn.reshape(1).astype(jnp.int32),
             all_a,
-            all_b,
+            near_b,
+            far_b,
             near_q,
             far_q,
             *[array.reshape(attn_shape) for array in (attn_w, attn_m, attn_v)],

time: 366 us -> 373 us (1.019)
  starting transfers between devices: 36.2 us -> 83.3 us
  waiting for transfers between devices: 123 us -> 82 us
  local copies, waits for them, and re-layouts: 25.6 us -> 11 us
  Pallas kernels: 128 us -> 141 us
  other arithmetic: 23.7 us -> 29.7 us
    ppermute x42 -> x50, starting transfers between devices: 36.1 us -> 83.2 us  [swap(): return lax.ppermute(array, axis, [(i, i ^ bit) for i in range(count)])]
    all_gather x1 -> x0, waiting for transfers between devices: 35.8 us -> none  [on_device(): all_b = lax.all_gather(part_b, 'dp', axis=0)]
    unnamed x95 -> x73, local copies, waits for them, and re-layouts: 20.9 us -> 3.91 us
    ppermute x42 -> x50, waiting for transfers between devices: 87.5 us -> 82 us  [swap(): return lax.ppermute(array, axis, [(i, i ^ bit) for i in range(count)])]
    pallas_call x3, Pallas kernels: 27.5 us -> 32 us  [attend_back(): pl.pallas_call(functools.partial(attend_back_kernel, scale), grid_spec=pl...]
  transfers between devices with their start and end apart: 44 -> 51, of which waited for: 21 -> 21; matrix products, arithmetic and copies ran while one was open for 8% -> 10% of each run, Pallas kernels for 21% -> 24%
where the time goes in v2:
time: 373 us; the launch traced here: 369 us
  Pallas kernels  141 us (38%)
  starting transfers between devices  83.3 us (22%)
  waiting for transfers between devices  82 us (22%)
  other arithmetic  29.7 us (8%)
  between operations  21.9 us (6%)
  local copies, waits for them, and re-layouts  11 us (3%)
    ppermute x50, starting transfers between devices, swap(): return lax.ppermute(array, axis, [(i, i ^ bit) for i in range(count)])  83.2 us
    ppermute x50, waiting for transfers between devices, swap(): return lax.ppermute(array, axis, [(i, i ^ bit) for i in range(count)])  82 us
    pallas_call x1, Pallas kernels, on_device(): pl.pallas_call(functools.partial(mlp_kernel, parts, first_blocks), grid_s...  33.6 us
    pallas_call x3, Pallas kernels, attend_back(): pl.pallas_call(functools.partial(attend_back_kernel, scale), grid_spec=pl...  32 us
    pallas_call x3, Pallas kernels, attend(): pl.pallas_call(functools.partial(attend_kernel, scale), grid_spec=pltpu.P...  25.9 us
    pallas_call x1, Pallas kernels, on_device(): pl.pallas_call(functools.partial(adam_kernel, fc_rows), grid_spec=pltpu.P...  19.9 us
    pallas_call x1, Pallas kernels, on_device(): pl.pallas_call(functools.partial(projection_back_kernel, own_heads, parts...  14.2 us
    convert_element_type x12, other arithmetic, add_low(): return (a.astype(HIGH) + b.astype(HIGH)).astype(LOW)  12.3 us
  transfers between devices with their start and end apart: 51, of which 21 were waited for; matrix products, arithmetic and copies ran while one was open for 10% of the time, Pallas kernels for 24%

profile of v2, /device:TPU:0, one launch (start us, length us, event | category | flops | bytes accessed | tf_op | source)
XLA Modules:
  0.0 368.6 jit_solution(5685781178568472865)
XLA Ops:
  7.3 3.0 collective-permute-start.1
  10.3 3.1 cut.1
  13.9 1.3 collective-permute-start.5
  17.6 4.6 %widen.1 = (bf16[192,6912]{1,0:T(8,128)(2,1)}, bf16[96,3840]{1,0:T(8,128)(2,1)}, bf16[96,3072]{1,0:T(8,128)(2,1)}) custom-call(s32[1]{0:T(128)} %bitcast.1.half, f32[192,3072]{1,0:T(8,128)} %out_ref.1, f32[2,192,3072]{2,1,0:T(8,128)} %mlp_ref.1), custom_call_target="tpu_custom_call" | custom-call | bytes 12000000 | tf_op jit(solution)/shard_map/widen/pallas_call | solution.py:535
  22.3 6.6 %collective-permute-done.1.refs_2_ = bf16[512,768]{1,0:T(8,128)(2,1)S(1)} collective-permute-done((bf16[512,768]{1,0:T(8,128)(2,1)}, bf16[512,768]{1,0:T(8,128)(2,1)S(1)}, u32[]{:S(2)}, u32[]{:S(2)}) %collective-permute-start.1) | collective-permute-done | bytes 786464 | tf_op jit(solution)/shard_map/ppermute | solution.py:433
  28.8 1.3 subtract_select_fusion.segc_ref
  30.7 3.8 %collective-permute-done.4.refs_6_ = bf16[208,576]{1,0:T(8,128)(2,1)S(1)} collective-permute-done((bf16[208,576]{1,0:T(8,128)(2,1)}, bf16[208,576]{1,0:T(8,128)(2,1)S(1)}, u32[]{:S(2)}, u32[]{:S(2)}) %collective-permute-start.4) | collective-permute-done | bytes 239648 | tf_op jit(solution)/shard_map/ppermute | solution.py:433
  34.5 4.2 %collective-permute-done.5.refs_7_ = bf16[208,576]{1,0:T(8,128)(2,1)} collective-permute-done((bf16[208,576]{1,0:T(8,128)(2,1)}, bf16[208,576]{1,0:T(8,128)(2,1)}, u32[]{:S(2)}, u32[]{:S(2)}) %collective-permute-start.5) | collective-permute-done | bytes 239648 | tf_op jit(solution)/shard_map/ppermute | solution.py:433
  39.7 1.3 collective-permute-start.6
  41.8 7.6 %project.1 = (bf16[2048,768]{1,0:T(8,128)(2,1)}, bf16[576,2048]{1,0:T(8,128)(2,1)}, bf16[576,768]{1,0:T(8,128)(2,1)}, f32[16,768]{1,0:T(8,128)}) custom-call(s32[1]{0:T(128)} %bitcast.place, bf16[512,768]{1,0:T(8,128)(2,1)} %refs_0_.3, bf16[512,768]{1,0:T(8,128)(2,1)} %copy-done.20, bf16[512,768]{1,0:T(8,128)(2,1)} %copy-done.19, ...), custom_call_target="tpu_custom_call" | custom-call | flops 5435817984 | bytes 12000000 | tf_op jit(solution)/shard_map/project/pallas_call | solution.py:571
  49.5 8.6 %attend.3 = (bf16[4,64,512]{2,1,0:T(8,128)(2,1)}, f32[1,2048,1]{2,1,0:T(8,128)}) custom-call(s32[1]{0:T(128)} %bitcast.place, bf16[576,2048]{1,0:T(8,128)(2,1)} %get-tuple-element.110.qt_ref.kt_ref.vt_ref, bf16[576,2048]{1,0:T(8,128)(2,1)} %get-tuple-element.110.qt_ref.kt_ref.vt_ref, bf16[576,2048]{1,0:T(8,128)(2,1)} %get-tuple-element.110.qt_ref.kt_ref.vt_ref, ...), custom_call_target="tpu_custom_call" | custom-call | flops 2147483648 | bytes 4000000 | tf_op jit(solution)/shard_map/attend/pallas_call | solution.py:613
  59.2 1.6 collective-permute-start.11
  60.8 8.6 %attend.5 = (bf16[4,64,512]{2,1,0:T(8,128)(2,1)}, f32[1,2048,1]{2,1,0:T(8,128)}) custom-call(s32[1]{0:T(128)} %bitcast.place, bf16[576,2048]{1,0:T(8,128)(2,1)} %get-tuple-element.110.qt_ref.kt_ref.vt_ref, bf16[576,2048]{1,0:T(8,128)(2,1)} %get-tuple-element.110.qt_ref.kt_ref.vt_ref, bf16[576,2048]{1,0:T(8,128)(2,1)} %get-tuple-element.110.qt_ref.kt_ref.vt_ref, ...), custom_call_target="tpu_custom_call" | custom-call | flops 2147483648 | bytes 4000000 | tf_op jit(solution)/shard_map/attend/pallas_call | solution.py:613
  69.4 8.8 %attend.4 = (bf16[4,64,512]{2,1,0:T(8,128)(2,1)}, f32[1,2048,1]{2,1,0:T(8,128)}) custom-call(s32[1]{0:T(128)} %bitcast.place, bf16[576,2048]{1,0:T(8,128)(2,1)} %get-tuple-element.110.qt_ref.kt_ref.vt_ref, bf16[576,2048]{1,0:T(8,128)(2,1)} %get-tuple-element.110.qt_ref.kt_ref.vt_ref, bf16[576,2048]{1,0:T(8,128)(2,1)} %get-tuple-element.110.qt_ref.kt_ref.vt_ref, ...), custom_call_target="tpu_custom_call" | custom-call | flops 2147483648 | bytes 4000000 | tf_op jit(solution)/shard_map/attend/pallas_call | solution.py:613
  78.6 1.0 slice_bitcast_fusion.2
  81.3 5.5 %collective-permute-done.9.refs_3_ = bf16[192,512]{1,0:T(8,128)(2,1)S(1)} collective-permute-done((bf16[192,512]{1,0:T(8,128)(2,1)S(1)}, bf16[192,512]{1,0:T(8,128)(2,1)S(1)}, u32[]{:S(2)}, u32[]{:S(2)}) %collective-permute-start.9) | collective-permute-done | bytes 196640 | tf_op jit(solution)/shard_map/ppermute | solution.py:433
  87.1 4.0 %collective-permute-done.8.refs_2_ = bf16[192,512]{1,0:T(8,128)(2,1)S(1)} collective-permute-done((bf16[192,512]{1,0:T(8,128)(2,1)S(1)}, bf16[192,512]{1,0:T(8,128)(2,1)S(1)}, u32[]{:S(2)}, u32[]{:S(2)}) %collective-permute-start.8) | collective-permute-done | bytes 196640 | tf_op jit(solution)/shard_map/ppermute | solution.py:433
  91.7 1.9 collective-permute-done.15.refs_11_
  96.4 33.6 %mlp.1 = (bf16[512,768]{1,0:T(8,128)(2,1)}, bf16[2,192,3072]{2,1,0:T(8,128)(2,1)}, bf16[2,192,3072]{2,1,0:T(8,128)(2,1)}, bf16[2,192,3840]{2,1,0:T(8,128)(2,1)},...) custom-call(s32[1]{0:T(128)} %bitcast.place, ...), custom_call_target="tpu_custom_call" | custom-call | flops 16307453952 | bytes 30000000 | tf_op jit(solution)/shard_map/mlp/pallas_call | solution.py:663
  132.8 1.1 collective-permute-start.19
  134.5 2.3 collective-permute-done.21
  136.8 1.4 copy-done.5
  138.2 3.4 fusion.14
  141.6 2.6 add_convert_fusion
  144.2 1.3 constant_dynamic-slice_fusion.12
  145.5 1.0 collective-permute-start.23
  146.6 1.5 collective-permute-start.27
  148.1 10.4 %attend_back.5.refs_7_ = bf16[3,64,2048]{2,1,0:T(8,128)(2,1)} custom-call(s32[1]{0:T(128)} %bitcast.place, bf16[576,2048]{1,0:T(8,128)(2,1)} %get-tuple-element.110.qt_ref.kt_ref.vt_ref, bf16[576,2048]{1,0:T(8,128)(2,1)} %get-tuple-element.110.qt_ref.kt_ref.vt_ref, bf16[576,2048]{1,0:T(8,128)(2,1)} %get-tuple-element.110.qt_ref.kt_ref.vt_ref, ...), custom_call_target="tpu_custom_call" | custom-call | flops 5368709120 | bytes 4000000 | tf_op jit(solution)/shard_map/attend_back/pallas_call | solution.py:711
  158.6 10.9 %attend_back.4.refs_6_ = bf16[3,64,2048]{2,1,0:T(8,128)(2,1)} custom-call(s32[1]{0:T(128)} %bitcast.place, bf16[576,2048]{1,0:T(8,128)(2,1)} %get-tuple-element.110.qt_ref.kt_ref.vt_ref, bf16[576,2048]{1,0:T(8,128)(2,1)} %get-tuple-element.110.qt_ref.kt_ref.vt_ref, bf16[576,2048]{1,0:T(8,128)(2,1)} %get-tuple-element.110.qt_ref.kt_ref.vt_ref, ...), custom_call_target="tpu_custom_call" | custom-call | flops 5368709120 | bytes 4000000 | tf_op jit(solution)/shard_map/attend_back/pallas_call | solution.py:711
  169.4 10.6 %attend_back.3.refs_5_ = bf16[3,64,2048]{2,1,0:T(8,128)(2,1)} custom-call(s32[1]{0:T(128)} %bitcast.place, bf16[576,2048]{1,0:T(8,128)(2,1)} %get-tuple-element.110.qt_ref.kt_ref.vt_ref, bf16[576,2048]{1,0:T(8,128)(2,1)} %get-tuple-element.110.qt_ref.kt_ref.vt_ref, bf16[576,2048]{1,0:T(8,128)(2,1)} %get-tuple-element.110.qt_ref.kt_ref.vt_ref, ...), custom_call_target="tpu_custom_call" | custom-call | flops 5368709120 | bytes 4000000 | tf_op jit(solution)/shard_map/attend_back/pallas_call | solution.py:711
  180.1 1.7 add_convert_fusion.2
  182.4 14.2 %projection_back.1 = (bf16[2,512,768]{2,1,0:T(8,128)(2,1)}, bf16[2,512,768]{2,1,0:T(8,128)(2,1)}, bf16[4,96,588]{2,1,0:T(8,128)(2,1)}, bf16[4,96,588]{2,1,0:T(8,128)(2,1)}) custom-call(s32[1]{0:T(128)} %bitcast.place, s32[1]{0:T(128)} %bitcast.1.half, bf16[512,768]{1,0:T(8,128)(2,1)} %refs_0_.3, bf16[512,768]{1,0:T(8,128)(2,1)} %copy-done.20, ...), custom_call_target="tpu_custom_call" | custom-call | flops 7247757312 | bytes 16000000 | tf_op jit(solution)/shard_map/projection_back/pallas_call | solution.py:744
  196.5 1.6 collective-permute-start.31
  198.1 1.7 add_convert_fusion.1
  200.1 1.6 collective-permute-start.28
  201.8 1.1 collective-permute-start.30
  202.9 6.7 %collective-permute-done.28 = bf16[48,3072]{1,0:T(8,128)(2,1)S(1)} collective-permute-done((bf16[48,3072]{1,0:T(8,128)(2,1)S(1)}, bf16[48,3072]{1,0:T(8,128)(2,1)S(1)}, u32[]{:S(2)}, u32[]{:S(2)}) %collective-permute-start.28) | collective-permute-done | bytes 294944 | tf_op jit(solution)/shard_map/ppermute | solution.py:433
  209.8 1.6 collective-permute-start.33
  211.5 2.7 collective-permute-start.29
  214.1 6.3 %collective-permute-done.30 = bf16[96,3840]{1,0:T(8,128)(2,1)S(1)} collective-permute-done((bf16[96,3840]{1,0:T(8,128)(2,1)S(1)}, bf16[96,3840]{1,0:T(8,128)(2,1)S(1)}, u32[]{:S(2)}, u32[]{:S(2)}) %collective-permute-start.30) | collective-permute-done | bytes 737312 | tf_op jit(solution)/shard_map/ppermute | solution.py:433
  220.7 2.5 collective-permute-start.32
  223.2 1.3 multiply_reduce_fusion.1
  225.3 8.5 %collective-permute-done.32 = bf16[48,3840]{1,0:T(8,128)(2,1)S(1)} collective-permute-done((bf16[48,3840]{1,0:T(8,128)(2,1)S(1)}, bf16[48,3840]{1,0:T(8,128)(2,1)S(1)}, u32[]{:S(2)}, u32[]{:S(2)}) %collective-permute-start.32) | collective-permute-done | bytes 368672 | tf_op jit(solution)/shard_map/ppermute | solution.py:433
  234.7 1.1 collective-permute-start.37
  237.2 3.4 collective-permute-start.34
  241.5 1.8 collective-permute-start.41
  244.6 8.7 %collective-permute-done.34 = bf16[24,3840]{1,0:T(8,128)(2,1)S(1)} collective-permute-done((bf16[24,3840]{1,0:T(8,128)(2,1)S(1)}, bf16[24,3840]{1,0:T(8,128)(2,1)S(1)}, u32[]{:S(2)}, u32[]{:S(2)}) %collective-permute-start.34) | collective-permute-done | bytes 184352 | tf_op jit(solution)/shard_map/ppermute | solution.py:433
  254.0 1.6 collective-permute-done.41
  256.4 2.5 collective-permute-start.44
  258.9 15.1 %collective-permute-done.40 = bf16[1,24,3840]{2,1,0:T(8,128)(2,1)S(1)} collective-permute-done((bf16[1,24,3840]{2,1,0:T(8,128)(2,1)S(1)}, bf16[1,24,3840]{2,1,0:T(8,128)(2,1)S(1)}, u32[]{:S(2)}, u32[]{:S(2)}) %collective-permute-start.40) | collective-permute-done | bytes 184352 | tf_op jit(solution)/shard_map/ppermute | solution.py:433
  274.9 2.2 fusion.15
  279.3 1.0 collective-permute-start.39
  281.3 13.4 %collective-permute-start.42 = (f32[1,1]{1,0:T(1,128)}, f32[1,1]{1,0:T(1,128)}, u32[]{:S(2)}, u32[]{:S(2)}) collective-permute-start(f32[1,1]{1,0:T(1,128)} %add.271), channel_id=1, source_target_pairs={{0,2},{1,3},{2,0},{3,1},{4,6},{5,7},{6,4},{7,5},{8,10},{9,11},{10,... | collective-permute-start | bytes 20 | tf_op jit(solution)/shard_map/ppermute | solution.py:433
  294.7 1.1 pad_maximum_fusion.1.refs_3_
  296.6 1.1 pad_maximum_fusion.refs_1_
  297.7 1.3 collective-permute-start.49
  299.7 22.1 %collective-permute-start.45 = (f32[1,1]{1,0:T(1,128)}, f32[1,1]{1,0:T(1,128)}, u32[]{:S(2)}, u32[]{:S(2)}) collective-permute-start(f32[1,1]{1,0:T(1,128)} %add.272), channel_id=1, source_target_pairs={{0,4},{4,0},{8,12},{12,8},{16,20},{20,16},{24,28},{28,24},{1,5},{5... | collective-permute-start | bytes 20 | tf_op jit(solution)/shard_map/ppermute | solution.py:433
  321.8 1.8 collective-permute-done.45
  324.2 2.8 collective-permute-start.46
  328.6 2.8 collective-permute-start.47
  331.4 1.8 collective-permute-done.47
  333.9 2.0 fusion.35
  336.0 2.8 fusion.9
  340.6 19.9 %adam.1 = (f32[8,24,3072]{2,1,0:T(8,128)}, f32[8,24,3072]{2,1,0:T(8,128)}, f32[8,24,3072]{2,1,0:T(8,128)}, f32[8,24,3072]{2,1,0:T(8,128)}, f32[2,8,24,3072]{3,2,...) custom-call(f32[1]{0:T(128)} %bitcast.45.factor_ref, ...), custom_call_target="tpu_custom_call" | custom-call | flops 39813120 | bytes 54000000 | tf_op jit(solution)/shard_map/adam/pallas_call | solution.py:900
  (214 shorter events, 27.9 us)
Async XLA Ops:
  7.2 333.4 %all-gather.3.cloned.1.call-start = ((), (), s32[]{:S(2)}) async-start(), calls=%async_computation | async-start | bytes 1327104 | tf_op jit(solution)/shard_map/all_gather | solution.py:806
  7.3 21.6 %collective-permute-start.1 = (bf16[512,768]{1,0:T(8,128)(2,1)}, bf16[512,768]{1,0:T(8,128)(2,1)S(1)}, u32[]{:S(2)}, u32[]{:S(2)}) collective-permute-start(bf16[512,768]{1,0:T(8,128)(2,1)} %refs_0_.3), channel_id=1, source_target_pairs={{0,2},{1,3},{2,0},{3,1},{4,6},{5,7},{6,4},{7,5},{8,10},{9,11},{10,... | collective-permute-start | bytes 2359304 | tf_op jit(solution)/shard_map/ppermute | solution.py:433
  10.3 28.5 %collective-permute-start = (bf16[512,768]{1,0:T(8,128)(2,1)}, bf16[512,768]{1,0:T(8,128)(2,1)S(1)}, u32[]{:S(2)}, u32[]{:S(2)}) collective-permute-start(bf16[512,768]{1,0:T(8,128)(2,1)} %refs_0_.3), channel_id=1, source_target_pairs={{0,1},{1,0},{2,3},{3,2},{4,5},{5,4},{6,7},{7,6},{8,9},{9,8},{10,11... | collective-permute-start | bytes 2359304 | tf_op jit(solution)/shard_map/ppermute | solution.py:433
  13.3 17.4 %collective-permute-start.3 = (bf16[208,576]{1,0:T(8,128)(2,1)}, bf16[208,576]{1,0:T(8,128)(2,1)S(1)}, u32[]{:S(2)}, u32[]{:S(2)}) collective-permute-start(bf16[208,576]{1,0:T(8,128)(2,1)} %get-tuple-element.100), channel_id=1, source_target_pairs={{0,1},{1,0},{2,3},{3,2},{4,5},{5,4},{6,7},{7,6},{8,9},{9,8},{10,11... | collective-permute-start | bytes 718856 | tf_op jit(solution)/shard_map/ppermute | solution.py:433
  13.8 20.7 %collective-permute-start.4 = (bf16[208,576]{1,0:T(8,128)(2,1)}, bf16[208,576]{1,0:T(8,128)(2,1)S(1)}, u32[]{:S(2)}, u32[]{:S(2)}) collective-permute-start(bf16[208,576]{1,0:T(8,128)(2,1)} %get-tuple-element.101), channel_id=1, source_target_pairs={{0,2},{1,3},{2,0},{3,1},{4,6},{5,7},{6,4},{7,5},{8,10},{9,11},{10,... | collective-permute-start | bytes 718856 | tf_op jit(solution)/shard_map/ppermute | solution.py:433
  13.9 24.9 %collective-permute-start.5 = (bf16[208,576]{1,0:T(8,128)(2,1)}, bf16[208,576]{1,0:T(8,128)(2,1)}, u32[]{:S(2)}, u32[]{:S(2)}) collective-permute-start(bf16[208,576]{1,0:T(8,128)(2,1)} %get-tuple-element.102), channel_id=1, source_target_pairs={{0,3},{1,2},{2,1},{3,0},{4,7},{5,6},{6,5},{7,4},{8,11},{9,10},{10,... | collective-permute-start | bytes 718856 | tf_op jit(solution)/shard_map/ppermute | solution.py:433
  28.8 13.0 %copy-start.19 = (bf16[512,768]{1,0:T(8,128)(2,1)}, bf16[512,768]{1,0:T(8,128)(2,1)S(1)}, u32[]{:S(2)}) copy-start(bf16[512,768]{1,0:T(8,128)(2,1)S(1)} %collective-permute-done.1.refs_2_) | copy-start | bytes 2359300
  28.8 10.0 %collective-permute-start.2 = (bf16[512,768]{1,0:T(8,128)(2,1)S(1)}, bf16[512,768]{1,0:T(8,128)(2,1)S(1)}, u32[]{:S(2)}, u32[]{:S(2)}) collective-permute-start(bf16[512,768]{1,0:T(8,128)(2,1)S(1)} %collective-permute-done.1.refs_2_), channel_id=1, source_target_pairs={{0,1},{1,0},{2,3},{3,2},{4,5},{5,4},{6,7},{7,6},{8,9},{9,8},{10,11... | collective-permute-start | bytes 2359304 | tf_op jit(solution)/shard_map/ppermute | solution.py:433
  30.7 11.1 %copy-start.26 = (bf16[208,576]{1,0:T(8,128)(2,1)}, bf16[208,576]{1,0:T(8,128)(2,1)S(1)}, u32[]{:S(2)}) copy-start(bf16[208,576]{1,0:T(8,128)(2,1)S(1)} %collective-permute-done.3.refs_5_) | copy-start | bytes 718852
  39.7 19.5 %collective-permute-start.6 = (bf16[96,3840]{1,0:T(8,128)(2,1)}, bf16[96,3840]{1,0:T(8,128)(2,1)S(1)}, u32[]{:S(2)}, u32[]{:S(2)}) collective-permute-start(bf16[96,3840]{1,0:T(8,128)(2,1)} %get-tuple-element.109), channel_id=1, source_target_pairs={{0,2},{1,3},{2,0},{3,1},{4,6},{5,7},{6,4},{7,5},{8,10},{9,11},{10,... | collective-permute-start | bytes 2211848 | tf_op jit(solution)/shard_map/ppermute | solution.py:433
  41.1 37.1 %collective-permute-start.14 = (bf16[96,3072]{1,0:T(8,128)(2,1)}, bf16[96,3072]{1,0:T(8,128)(2,1)}, u32[]{:S(2)}, u32[]{:S(2)}) collective-permute-start(bf16[96,3072]{1,0:T(8,128)(2,1)} %get-tuple-element.115), channel_id=1, source_target_pairs={{0,2},{1,3},{2,0},{3,1},{4,6},{5,7},{6,4},{7,5},{8,10},{9,11},{10,... | collective-permute-start | bytes 1769480 | tf_op jit(solution)/shard_map/ppermute | solution.py:433
  41.8 54.4 %collective-permute-start.10 = (bf16[192,6912]{1,0:T(8,128)(2,1)}, bf16[192,6912]{1,0:T(8,128)(2,1)}, u32[]{:S(2)}, u32[]{:S(2)}) collective-permute-start(bf16[192,6912]{1,0:T(8,128)(2,1)} %get-tuple-element.113.refs_4_), channel_id=1, source_target_pairs={{0,1},{1,0},{2,3},{3,2},{4,5},{5,4},{6,7},{7,6},{8,9},{9,8},{10,11... | collective-permute-start | bytes 7962632 | tf_op jit(solution)/shard_map/ppermute | solution.py:433
  59.2 31.9 %copy-start.22 = (bf16[96,3840]{1,0:T(8,128)(2,1)}, bf16[96,3840]{1,0:T(8,128)(2,1)S(1)}, u32[]{:S(2)}) copy-start(bf16[96,3840]{1,0:T(8,128)(2,1)S(1)} %collective-permute-done.6.refs_6_) | copy-start | bytes 2211844
  59.2 31.9 %collective-permute-start.11 = (bf16[96,3840]{1,0:T(8,128)(2,1)S(1)}, bf16[96,3840]{1,0:T(8,128)(2,1)S(1)}, u32[]{:S(2)}, u32[]{:S(2)}) collective-permute-start(bf16[96,3840]{1,0:T(8,128)(2,1)S(1)} %collective-permute-done.6.refs_6_), channel_id=1, source_target_pairs={{0,4},{4,0},{8,12},{12,8},{16,20},{20,16},{24,28},{28,24},{1,5},{5... | collective-permute-start | bytes 2211848 | tf_op jit(solution)/shard_map/ppermute | solution.py:433
  69.4 9.2 %copy-start.13 = (bf16[4,64,512]{2,1,0:T(8,128)(2,1)S(1)}, bf16[4,64,512]{2,1,0:T(8,128)(2,1)}, u32[]{:S(2)}) copy-start(bf16[4,64,512]{2,1,0:T(8,128)(2,1)} %get-tuple-element.112) | copy-start | bytes 786436
  78.2 15.4 %collective-permute-start.15 = (bf16[96,3072]{1,0:T(8,128)(2,1)}, bf16[96,3072]{1,0:T(8,128)(2,1)S(1)}, u32[]{:S(2)}, u32[]{:S(2)}) collective-permute-start(bf16[96,3072]{1,0:T(8,128)(2,1)} %collective-permute-done.14.refs_10_), channel_id=1, source_target_pairs={{0,4},{4,0},{8,12},{12,8},{16,20},{20,16},{24,28},{28,24},{1,5},{5... | collective-permute-start | bytes 1769480 | tf_op jit(solution)/shard_map/ppermute | solution.py:433
  79.6 7.2 %collective-permute-start.9 = (bf16[192,512]{1,0:T(8,128)(2,1)S(1)}, bf16[192,512]{1,0:T(8,128)(2,1)S(1)}, u32[]{:S(2)}, u32[]{:S(2)}) collective-permute-start(bf16[192,512]{1,0:T(8,128)(2,1)S(1)} %pad_maximum_fusion.7), channel_id=1, source_target_pairs={{0,3},{1,2},{2,1},{3,0},{4,7},{5,6},{6,5},{7,4},{8,11},{9,10},{10,... | collective-permute-start | bytes 589832 | tf_op jit(solution)/shard_map/ppermute | solution.py:433
  80.4 10.7 %collective-permute-start.8 = (bf16[192,512]{1,0:T(8,128)(2,1)S(1)}, bf16[192,512]{1,0:T(8,128)(2,1)S(1)}, u32[]{:S(2)}, u32[]{:S(2)}) collective-permute-start(bf16[192,512]{1,0:T(8,128)(2,1)S(1)} %pad_maximum_fusion.6), channel_id=1, source_target_pairs={{0,2},{1,3},{2,0},{3,1},{4,6},{5,7},{6,4},{7,5},{8,10},{9,11},{10,... | collective-permute-start | bytes 589832 | tf_op jit(solution)/shard_map/ppermute | solution.py:433
  86.8 9.6 %copy-start.28 = (bf16[192,512]{1,0:T(8,128)(2,1)}, bf16[192,512]{1,0:T(8,128)(2,1)S(1)}, u32[]{:S(2)}) copy-start(bf16[192,512]{1,0:T(8,128)(2,1)S(1)} %collective-permute-done.9.refs_3_) | copy-start | bytes 589828
  86.8 4.8 %collective-permute-start.7 = (bf16[192,512]{1,0:T(8,128)(2,1)S(1)}, bf16[192,512]{1,0:T(8,128)(2,1)S(1)}, u32[]{:S(2)}, u32[]{:S(2)}) collective-permute-start(bf16[192,512]{1,0:T(8,128)(2,1)S(1)} %pad_maximum_fusion.5), channel_id=1, source_target_pairs={{0,1},{1,0},{2,3},{3,2},{4,5},{5,4},{6,7},{7,6},{8,9},{9,8},{10,11... | collective-permute-start | bytes 589832 | tf_op jit(solution)/shard_map/ppermute | solution.py:433
  91.1 4.4 %collective-permute-start.12 = (bf16[96,3840]{1,0:T(8,128)(2,1)S(1)}, bf16[96,3840]{1,0:T(8,128)(2,1)S(1)}, u32[]{:S(2)}, u32[]{:S(2)}) collective-permute-start(bf16[96,3840]{1,0:T(8,128)(2,1)S(1)} %collective-permute-done.6.refs_6_), channel_id=1, source_target_pairs={{0,1},{1,0},{2,3},{3,2},{4,5},{5,4},{6,7},{7,6},{8,9},{9,8},{10,11... | collective-permute-start | bytes 2211848 | tf_op jit(solution)/shard_map/ppermute | solution.py:433
  91.1 5.1 %collective-permute-start.13 = (bf16[96,3840]{1,0:T(8,128)(2,1)S(1)}, bf16[96,3840]{1,0:T(8,128)(2,1)}, u32[]{:S(2)}, u32[]{:S(2)}) collective-permute-start(bf16[96,3840]{1,0:T(8,128)(2,1)S(1)} %collective-permute-done.11.refs_7_), channel_id=1, source_target_pairs={{0,1},{1,0},{2,3},{3,2},{4,5},{5,4},{6,7},{7,6},{8,9},{9,8},{10,11... | collective-permute-start | bytes 2211848 | tf_op jit(solution)/shard_map/ppermute | solution.py:433
  91.6 3.9 %collective-permute-start.16 = (bf16[96,3072]{1,0:T(8,128)(2,1)}, bf16[96,3072]{1,0:T(8,128)(2,1)}, u32[]{:S(2)}, u32[]{:S(2)}) collective-permute-start(bf16[96,3072]{1,0:T(8,128)(2,1)} %collective-permute-done.14.refs_10_), channel_id=1, source_target_pairs={{0,1},{1,0},{2,3},{3,2},{4,5},{5,4},{6,7},{7,6},{8,9},{9,8},{10,11... | collective-permute-start | bytes 1769480 | tf_op jit(solution)/shard_map/ppermute | solution.py:433
  93.6 2.6 collective-permute-start.17
  96.4 34.9 %copy-start = (bf16[512,768]{1,0:T(8,128)(2,1)S(1)}, bf16[512,768]{1,0:T(8,128)(2,1)}, u32[]{:S(2)}) copy-start(bf16[512,768]{1,0:T(8,128)(2,1)} %refs_0_.3) | copy-start | bytes 2359300
  130.0 6.8 %collective-permute-start.21 = (bf16[2,192,3072]{2,1,0:T(8,128)(2,1)}, bf16[2,192,3072]{2,1,0:T(8,128)(2,1)S(1)}, u32[]{:S(2)}, u32[]{:S(2)}) collective-permute-start(bf16[2,192,3072]{2,1,0:T(8,128)(2,1)} %get-tuple-element.126), channel_id=1, source_target_pairs={{0,1},{1,0},{2,3},{3,2},{4,5},{5,4},{6,7},{7,6},{8,9},{9,8},{10,11... | collective-permute-start | bytes 7077896 | tf_op jit(solution)/shard_map/ppermute | solution.py:433
  130.2 11.4 %collective-permute-start.22 = (bf16[2,192,3840]{2,1,0:T(8,128)(2,1)}, bf16[2,192,3840]{2,1,0:T(8,128)(2,1)}, u32[]{:S(2)}, u32[]{:S(2)}) collective-permute-start(bf16[2,192,3840]{2,1,0:T(8,128)(2,1)} %get-tuple-element.128), channel_id=1, source_target_pairs={{0,1},{1,0},{2,3},{3,2},{4,5},{5,4},{6,7},{7,6},{8,9},{9,8},{10,11... | collective-permute-start | bytes 8847368 | tf_op jit(solution)/shard_map/ppermute | solution.py:433
  132.6 12.9 %collective-permute-start.18 = (bf16[192,512]{1,0:T(8,128)(2,1)}, bf16[192,512]{1,0:T(8,128)(2,1)S(1)}, u32[]{:S(2)}, u32[]{:S(2)}) collective-permute-start(bf16[192,512]{1,0:T(8,128)(2,1)} %get-tuple-element.122), channel_id=1, source_target_pairs={{0,1},{1,0},{2,3},{3,2},{4,5},{5,4},{6,7},{7,6},{8,9},{9,8},{10,11... | collective-permute-start | bytes 589832 | tf_op jit(solution)/shard_map/ppermute | solution.py:433
  132.8 12.7 %collective-permute-start.19 = (bf16[192,512]{1,0:T(8,128)(2,1)}, bf16[192,512]{1,0:T(8,128)(2,1)S(1)}, u32[]{:S(2)}, u32[]{:S(2)}) collective-permute-start(bf16[192,512]{1,0:T(8,128)(2,1)} %get-tuple-element.123), channel_id=1, source_target_pairs={{0,2},{1,3},{2,0},{3,1},{4,6},{5,7},{6,4},{7,5},{8,10},{9,11},{10,... | collective-permute-start | bytes 589832 | tf_op jit(solution)/shard_map/ppermute | solution.py:433
  133.9 11.6 %collective-permute-start.20 = (bf16[192,512]{1,0:T(8,128)(2,1)}, bf16[192,512]{1,0:T(8,128)(2,1)S(1)}, u32[]{:S(2)}, u32[]{:S(2)}) collective-permute-start(bf16[192,512]{1,0:T(8,128)(2,1)} %get-tuple-element.124), channel_id=1, source_target_pairs={{0,3},{1,2},{2,1},{3,0},{4,7},{5,6},{6,5},{7,4},{8,11},{9,10},{10,... | collective-permute-start | bytes 589832 | tf_op jit(solution)/shard_map/ppermute | solution.py:433
  145.5 34.5 %collective-permute-start.23 = (bf16[192,3072]{1,0:T(8,128)(2,1)S(1)}, bf16[192,3072]{1,0:T(8,128)(2,1)}, u32[]{:S(2)}, u32[]{:S(2)}) collective-permute-start(bf16[192,3072]{1,0:T(8,128)(2,1)S(1)} %get-tuple-element.135), channel_id=1, source_target_pairs={{0,2},{1,3},{2,0},{3,1},{4,6},{5,7},{6,4},{7,5},{8,10},{9,11},{10,... | collective-permute-start | bytes 3538952 | tf_op jit(solution)/shard_map/ppermute | solution.py:433
  146.6 51.6 %collective-permute-start.27 = (bf16[2,96,3840]{2,1,0:T(8,128)(2,1)}, bf16[2,96,3840]{2,1,0:T(8,128)(2,1)}, u32[]{:S(2)}, u32[]{:S(2)}) collective-permute-start(bf16[2,96,3840]{2,1,0:T(8,128)(2,1)} %get-tuple-element.147), channel_id=1, source_target_pairs={{0,4},{4,0},{8,12},{12,8},{16,20},{20,16},{24,28},{28,24},{1,5},{5... | collective-permute-start | bytes 4423688 | tf_op jit(solution)/shard_map/ppermute | solution.py:433
  181.8 18.0 %collective-permute-start.26 = (bf16[96,3072]{1,0:T(8,128)(2,1)S(1)}, bf16[96,3072]{1,0:T(8,128)(2,1)S(1)}, u32[]{:S(2)}, u32[]{:S(2)}) collective-permute-start(bf16[96,3072]{1,0:T(8,128)(2,1)S(1)} %constant_dynamic-slice_fusion.11), channel_id=1, source_target_pairs={{0,4},{4,0},{8,12},{12,8},{16,20},{20,16},{24,28},{28,24},{1,5},{5... | collective-permute-start | bytes 1769480 | tf_op jit(solution)/shard_map/ppermute | solution.py:433
  196.5 13.1 %collective-permute-start.31 = (bf16[4,96,588]{2,1,0:T(8,128)(2,1)}, bf16[4,96,588]{2,1,0:T(8,128)(2,1)S(1)}, u32[]{:S(2)}, u32[]{:S(2)}) collective-permute-start(bf16[4,96,588]{2,1,0:T(8,128)(2,1)} %get-tuple-element.152), channel_id=1, source_target_pairs={{0,4},{4,0},{8,12},{12,8},{16,20},{20,16},{24,28},{28,24},{1,5},{5... | collective-permute-start | bytes 1354760 | tf_op jit(solution)/shard_map/ppermute | solution.py:433
  198.1 76.7 %collective-permute-start.24 = (bf16[2,512,768]{2,1,0:T(8,128)(2,1)}, bf16[2,512,768]{2,1,0:T(8,128)(2,1)}, u32[]{:S(2)}, u32[]{:S(2)}) collective-permute-start(bf16[2,512,768]{2,1,0:T(8,128)(2,1)} %get-tuple-element.145), channel_id=1, source_target_pairs={{0,1},{1,0},{2,3},{3,2},{4,5},{5,4},{6,7},{7,6},{8,9},{9,8},{10,11... | collective-permute-start | bytes 4718600 | tf_op jit(solution)/shard_map/ppermute | solution.py:433
  200.0 9.6 %copy-start.11 = (bf16[4,96,588]{2,1,0:T(8,128)(2,1)S(1)}, bf16[4,96,588]{2,1,0:T(8,128)(2,1)}, u32[]{:S(2)}) copy-start(bf16[4,96,588]{2,1,0:T(8,128)(2,1)} %get-tuple-element.148) | copy-start | bytes 1354756
  200.1 9.5 %collective-permute-start.28 = (bf16[48,3072]{1,0:T(8,128)(2,1)S(1)}, bf16[48,3072]{1,0:T(8,128)(2,1)S(1)}, u32[]{:S(2)}, u32[]{:S(2)}) collective-permute-start(bf16[48,3072]{1,0:T(8,128)(2,1)S(1)} %constant_dynamic-slice_fusion.10), channel_id=1, source_target_pairs={{0,8},{4,12},{8,0},{12,4},{16,24},{20,28},{24,16},{28,20},{1,9},{5... | collective-permute-start | bytes 884744 | tf_op jit(solution)/shard_map/ppermute | solution.py:433
  201.8 18.7 %collective-permute-start.30 = (bf16[96,3840]{1,0:T(8,128)(2,1)S(1)}, bf16[96,3840]{1,0:T(8,128)(2,1)S(1)}, u32[]{:S(2)}, u32[]{:S(2)}) collective-permute-start(bf16[96,3840]{1,0:T(8,128)(2,1)S(1)} %slice_bitcast_fusion), channel_id=1, source_target_pairs={{0,2},{1,3},{2,0},{3,1},{4,6},{5,7},{6,4},{7,5},{8,10},{9,11},{10,... | collective-permute-start | bytes 2211848 | tf_op jit(solution)/shard_map/ppermute | solution.py:433
  209.8 14.7 %collective-permute-start.33 = (bf16[4,48,588]{2,1,0:T(8,128)(2,1)S(1)}, bf16[4,48,588]{2,1,0:T(8,128)(2,1)S(1)}, u32[]{:S(2)}, u32[]{:S(2)}) collective-permute-start(bf16[4,48,588]{2,1,0:T(8,128)(2,1)S(1)} %constant_dynamic-slice_fusion.7), channel_id=1, source_target_pairs={{0,8},{4,12},{8,0},{12,4},{16,24},{20,28},{24,16},{28,20},{1,9},{5... | collective-permute-start | bytes 677384 | tf_op jit(solution)/shard_map/ppermute | solution.py:433
  211.5 9.2 %collective-permute-start.29 = (bf16[24,3072]{1,0:T(8,128)(2,1)S(1)}, bf16[24,3072]{1,0:T(8,128)(2,1)S(1)}, u32[]{:S(2)}, u32[]{:S(2)}) collective-permute-start(bf16[24,3072]{1,0:T(8,128)(2,1)S(1)} %constant_dynamic-slice_fusion.9), channel_id=1, source_target_pairs={{0,16},{4,20},{8,24},{12,28},{16,0},{20,4},{24,8},{28,12},{1,17},{... | collective-permute-start | bytes 442376 | tf_op jit(solution)/shard_map/ppermute | solution.py:433
  220.7 13.2 %collective-permute-start.32 = (bf16[48,3840]{1,0:T(8,128)(2,1)S(1)}, bf16[48,3840]{1,0:T(8,128)(2,1)S(1)}, u32[]{:S(2)}, u32[]{:S(2)}) collective-permute-start(bf16[48,3840]{1,0:T(8,128)(2,1)S(1)} %constant_dynamic-slice_fusion.8), channel_id=1, source_target_pairs={{0,8},{4,12},{8,0},{12,4},{16,24},{20,28},{24,16},{28,20},{1,9},{5... | collective-permute-start | bytes 1105928 | tf_op jit(solution)/shard_map/ppermute | solution.py:433
  224.7 9.6 %collective-permute-start.35 = (bf16[4,24,588]{2,1,0:T(8,128)(2,1)S(1)}, bf16[4,24,588]{2,1,0:T(8,128)(2,1)S(1)}, u32[]{:S(2)}, u32[]{:S(2)}) collective-permute-start(bf16[4,24,588]{2,1,0:T(8,128)(2,1)S(1)} %constant_dynamic-slice_fusion.5), channel_id=1, source_target_pairs={{0,16},{4,20},{8,24},{12,28},{16,0},{20,4},{24,8},{28,12},{1,17},{... | collective-permute-start | bytes 338696 | tf_op jit(solution)/shard_map/ppermute | solution.py:433
  234.6 6.0 %collective-permute-start.36 = (bf16[24,624]{1,0:T(8,128)(2,1)S(1)}, bf16[24,624]{1,0:T(8,128)(2,1)S(1)}, u32[]{:S(2)}, u32[]{:S(2)}) collective-permute-start(bf16[24,624]{1,0:T(8,128)(2,1)S(1)} %get-tuple-element.210), channel_id=1, source_target_pairs={{0,1},{1,0},{2,3},{3,2},{4,5},{5,4},{6,7},{7,6},{8,9},{9,8},{10,11... | collective-permute-start | bytes 89864 | tf_op jit(solution)/shard_map/ppermute | solution.py:433
  234.7 6.0 %collective-permute-start.37 = (bf16[24,624]{1,0:T(8,128)(2,1)S(1)}, bf16[24,624]{1,0:T(8,128)(2,1)S(1)}, u32[]{:S(2)}, u32[]{:S(2)}) collective-permute-start(bf16[24,624]{1,0:T(8,128)(2,1)S(1)} %get-tuple-element.211), channel_id=1, source_target_pairs={{0,2},{1,3},{2,0},{3,1},{4,6},{5,7},{6,4},{7,5},{8,10},{9,11},{10,... | collective-permute-start | bytes 89864 | tf_op jit(solution)/shard_map/ppermute | solution.py:433
  235.7 4.9 %collective-permute-start.38 = (bf16[24,624]{1,0:T(8,128)(2,1)S(1)}, bf16[24,624]{1,0:T(8,128)(2,1)S(1)}, u32[]{:S(2)}, u32[]{:S(2)}) collective-permute-start(bf16[24,624]{1,0:T(8,128)(2,1)S(1)} %get-tuple-element.208), channel_id=1, source_target_pairs={{0,3},{1,2},{2,1},{3,0},{4,7},{5,6},{6,5},{7,4},{8,11},{9,10},{10,... | collective-permute-start | bytes 89864 | tf_op jit(solution)/shard_map/ppermute | solution.py:433
  237.2 16.1 %collective-permute-start.34 = (bf16[24,3840]{1,0:T(8,128)(2,1)S(1)}, bf16[24,3840]{1,0:T(8,128)(2,1)S(1)}, u32[]{:S(2)}, u32[]{:S(2)}) collective-permute-start(bf16[24,3840]{1,0:T(8,128)(2,1)S(1)} %constant_dynamic-slice_fusion.6), channel_id=1, source_target_pairs={{0,16},{4,20},{8,24},{12,28},{16,0},{20,4},{24,8},{28,12},{1,17},{... | collective-permute-start | bytes 552968 | tf_op jit(solution)/shard_map/ppermute | solution.py:433
  240.8 34.1 %copy-start.2 = (bf16[2,512,768]{2,1,0:T(8,128)(2,1)S(1)}, bf16[2,512,768]{2,1,0:T(8,128)(2,1)}, u32[]{:S(2)}) copy-start(bf16[2,512,768]{2,1,0:T(8,128)(2,1)} %get-tuple-element.144) | copy-start | bytes 4718596
  241.5 14.1 %collective-permute-start.41 = (bf16[1,24,2316]{2,1,0:T(8,128)(2,1)S(1)}, bf16[1,24,2316]{2,1,0:T(8,128)(2,1)S(1)}, u32[]{:S(2)}, u32[]{:S(2)}) collective-permute-start(bf16[1,24,2316]{2,1,0:T(8,128)(2,1)S(1)} %maximum_bitcast_fusion), channel_id=1, source_target_pairs={{0,16},{4,20},{8,24},{12,28},{16,0},{20,4},{24,8},{28,12},{1,17},{... | collective-permute-start | bytes 333512 | tf_op jit(solution)/shard_map/ppermute | solution.py:433
  255.6 19.2 %copy-start.12 = (bf16[1,24,2316]{2,1,0:T(8,128)(2,1)}, bf16[1,24,2316]{2,1,0:T(8,128)(2,1)S(1)}, u32[]{:S(2)}) copy-start(bf16[1,24,2316]{2,1,0:T(8,128)(2,1)S(1)} %collective-permute-done.41) | copy-start | bytes 333508
  255.6 18.4 %collective-permute-start.40 = (bf16[1,24,3840]{2,1,0:T(8,128)(2,1)S(1)}, bf16[1,24,3840]{2,1,0:T(8,128)(2,1)S(1)}, u32[]{:S(2)}, u32[]{:S(2)}) collective-permute-start(bf16[1,24,3840]{2,1,0:T(8,128)(2,1)S(1)} %bitcast.126), channel_id=1, source_target_pairs={{0,16},{4,20},{8,24},{12,28},{16,0},{20,4},{24,8},{28,12},{1,17},{... | collective-permute-start | bytes 552968 | tf_op jit(solution)/shard_map/ppermute | solution.py:433
  256.4 38.3 %collective-permute-start.44 = (bf16[2,24,2316]{2,1,0:T(8,128)(2,1)}, bf16[2,24,2316]{2,1,0:T(8,128)(2,1)}, u32[]{:S(2)}, u32[]{:S(2)}) collective-permute-start(bf16[2,24,2316]{2,1,0:T(8,128)(2,1)} %pad_maximum_fusion.3), channel_id=1, source_target_pairs={{0,8},{4,12},{8,0},{12,4},{16,24},{20,28},{24,16},{28,20},{1,9},{5... | collective-permute-start | bytes 667016 | tf_op jit(solution)/shard_map/ppermute | solution.py:433
  274.8 21.7 %collective-permute-start.43 = (bf16[2,24,3840]{2,1,0:T(8,128)(2,1)}, bf16[2,24,3840]{2,1,0:T(8,128)(2,1)}, u32[]{:S(2)}, u32[]{:S(2)}) collective-permute-start(bf16[2,24,3840]{2,1,0:T(8,128)(2,1)} %pad_maximum_fusion.2), channel_id=1, source_target_pairs={{0,8},{4,12},{8,0},{12,4},{16,24},{20,28},{24,16},{28,20},{1,9},{5... | collective-permute-start | bytes 1105928 | tf_op jit(solution)/shard_map/ppermute | solution.py:433
  277.1 56.9 %copy-start.1 = (bf16[512,768]{1,0:T(8,128)(2,1)S(1)}, bf16[512,768]{1,0:T(8,128)(2,1)}, u32[]{:S(2)}) copy-start(bf16[512,768]{1,0:T(8,128)(2,1)} %refs_0_.3) | copy-start | bytes 2359300
  277.1 56.8 %collective-permute-start.25 = (bf16[512,768]{1,0:T(8,128)(2,1)}, bf16[512,768]{1,0:T(8,128)(2,1)S(1)}, u32[]{:S(2)}, u32[]{:S(2)}) collective-permute-start(bf16[512,768]{1,0:T(8,128)(2,1)} %fusion.15), channel_id=1, source_target_pairs={{0,2},{1,3},{2,0},{3,1},{4,6},{5,7},{6,4},{7,5},{8,10},{9,11},{10,... | collective-permute-start | bytes 2359304 | tf_op jit(solution)/shard_map/ppermute | solution.py:433
  279.3 1.3 collective-permute-start.39
  281.3 17.8 %collective-permute-start.42 = (f32[1,1]{1,0:T(1,128)}, f32[1,1]{1,0:T(1,128)}, u32[]{:S(2)}, u32[]{:S(2)}) collective-permute-start(f32[1,1]{1,0:T(1,128)} %add.271), channel_id=1, source_target_pairs={{0,2},{1,3},{2,0},{3,1},{4,6},{5,7},{6,4},{7,5},{8,10},{9,11},{10,... | collective-permute-start | bytes 20 | tf_op jit(solution)/shard_map/ppermute | solution.py:433
  295.8 40.2 %copy-start.6 = (bf16[4,24,2316]{2,1,0:T(8,128)(2,1)}, bf16[4,24,2316]{2,1,0:T(8,128)(2,1)S(1)}, u32[]{:S(2)}) copy-start(bf16[4,24,2316]{2,1,0:T(8,128)(2,1)S(1)} %pad_maximum_fusion.1.refs_3_) | copy-start | bytes 1334020
  295.8 43.0 %collective-permute-start.48 = (bf16[4,24,2316]{2,1,0:T(8,128)(2,1)S(1)}, bf16[4,24,2316]{2,1,0:T(8,128)(2,1)S(1)}, u32[]{:S(2)}, u32[]{:S(2)}) collective-permute-start(bf16[4,24,2316]{2,1,0:T(8,128)(2,1)S(1)} %pad_maximum_fusion.1.refs_3_), channel_id=1, source_target_pairs={{0,4},{4,0},{8,12},{12,8},{16,20},{20,16},{24,28},{28,24},{1,5},{5... | collective-permute-start | bytes 1334024 | tf_op jit(solution)/shard_map/ppermute | solution.py:433
  297.7 38.3 %copy-start.4 = (bf16[4,24,3840]{2,1,0:T(8,128)(2,1)}, bf16[4,24,3840]{2,1,0:T(8,128)(2,1)S(1)}, u32[]{:S(2)}) copy-start(bf16[4,24,3840]{2,1,0:T(8,128)(2,1)S(1)} %pad_maximum_fusion.refs_1_) | copy-start | bytes 2211844
  297.7 41.1 %collective-permute-start.49 = (bf16[4,24,3840]{2,1,0:T(8,128)(2,1)S(1)}, bf16[4,24,3840]{2,1,0:T(8,128)(2,1)S(1)}, u32[]{:S(2)}, u32[]{:S(2)}) collective-permute-start(bf16[4,24,3840]{2,1,0:T(8,128)(2,1)S(1)} %pad_maximum_fusion.refs_1_), channel_id=1, source_target_pairs={{0,4},{4,0},{8,12},{12,8},{16,20},{20,16},{24,28},{28,24},{1,5},{5... | collective-permute-start | bytes 2211848 | tf_op jit(solution)/shard_map/ppermute | solution.py:433
  299.7 23.9 %collective-permute-start.45 = (f32[1,1]{1,0:T(1,128)}, f32[1,1]{1,0:T(1,128)}, u32[]{:S(2)}, u32[]{:S(2)}) collective-permute-start(f32[1,1]{1,0:T(1,128)} %add.272), channel_id=1, source_target_pairs={{0,4},{4,0},{8,12},{12,8},{16,20},{20,16},{24,28},{28,24},{1,5},{5... | collective-permute-start | bytes 20 | tf_op jit(solution)/shard_map/ppermute | solution.py:433
  324.2 3.7 %collective-permute-start.46 = (f32[1,1]{1,0:T(1,128)}, f32[1,1]{1,0:T(1,128)}, u32[]{:S(2)}, u32[]{:S(2)}) collective-permute-start(f32[1,1]{1,0:T(1,128)} %add.273), channel_id=1, source_target_pairs={{0,8},{4,12},{8,0},{12,4},{16,24},{20,28},{24,16},{28,20},{1,9},{5... | collective-permute-start | bytes 20 | tf_op jit(solution)/shard_map/ppermute | solution.py:433
  328.6 4.6 %collective-permute-start.47 = (f32[1,1]{1,0:T(1,128)}, f32[1,1]{1,0:T(1,128)}, u32[]{:S(2)}, u32[]{:S(2)}) collective-permute-start(f32[1,1]{1,0:T(1,128)} %add.274), channel_id=1, source_target_pairs={{0,16},{4,20},{8,24},{12,28},{16,0},{20,4},{24,8},{28,12},{1,17},{... | collective-permute-start | bytes 20 | tf_op jit(solution)/shard_map/ppermute | solution.py:433
  340.0 20.5 %copy-start.15 = (f32[192,12]{0,1:T(8,128)}, f32[192,12]{0,1:T(8,128)S(1)}, u32[]{:S(2)}) copy-start(f32[192,12]{0,1:T(8,128)S(1)} %copy.54) | copy-start | bytes 27652
  (22 other events, 77.2 us)
Sparse Core Ops, SparseCore 0:
  224.7 50.9 all-gather.2

commit v3 on v2

--- a/solution.py
+++ b/solution.py
@@ -19,7 +19,7 @@
 CLIP_LIMIT = 1.0
 MASKED_SCORE = -1e30
 QUERY_BLOCK = 256
-VMEM_LIMIT = 60 * 1024 * 1024
+VMEM_LIMIT = 50 * 1024 * 1024
 LOW = jnp.bfloat16
 HIGH = jnp.float32
 
@@ -264,50 +264,58 @@
 GELU_A = 0.044715
 
 
-def mlp_kernel(
-    parts, first_blocks, place, half, live_ref, x_ref, cot_ref, vec_ref, *refs
-):
-    o_refs, refs = refs[:parts], refs[parts:]
-    own_ref, core_ref, *wide_refs = refs[:10]
-    out_ref, *grad_refs = refs[10:15]
-    dr1_ref, vecg_ref, *refs = refs[15:]
-    do_refs, scratch = refs[:parts], refs[parts:]
-    wide, ot_scr, r1_scr, a2_scr, a2t_scr, dy_scr, dyt_scr, y_scr, da2_scr, act_scr, sems = scratch
+def weight_copies(place, half, sources, wide, span, offset, sems):
+    rows = sources[0].shape[0]
+    near, far = half[0] * (rows // 2), (1 - half[0]) * (rows // 2)
+    spots = [(0, 0), (1, 0), (2, near), (2, far), (3, near), (3, far)]
+    for n, ((j, inner), source) in enumerate(zip(spots, sources)):
+        base = offset if n < 2 else 0
+        start = pl.multiple_of((place[0] ^ j) * rows + inner, 16)
+        source = source.at[:, base + span[0] : base + span[1]]
+        target = wide.at[pl.ds(start, source.shape[0]), span[0] : span[1]]
+        yield pltpu.make_async_copy(source, target, sems.at[n])
+
+
+def put(keep, send, value):
+    parts = 2 * keep.shape[0]
+    rows = value.shape[0] // parts
+    value = value.astype(LOW)
+    for j in range(parts):
+        (send if j % 2 else keep)[j // 2] = value[j * rows : (j + 1) * rows, :]
+
+
+def mlp_chunk(a2, a2t, dy, w_fc, w_pt, bias, y_ref, da2_ref, act_scr, keep, send):
+    u = dot_nn(a2[...], w_fc) + bias
+    square = u * u
+    t = jnp.tanh(GELU_C * (u + GELU_A * (square * u)))
+    grown = 0.5 * (1.0 + t)
+    act = (u * grown).astype(LOW)
+    act_scr[...] = act
+    y_ref[...] += dot_nt(act, w_pt)
+    slope = grown + 0.5 * u * (1.0 - t * t) * (GELU_C + (3.0 * GELU_C * GELU_A) * square)
+    du = (dot_nn(dy[...], w_pt) * slope).astype(LOW)
+    da2_ref[...] += dot_nt(du, w_fc)
+    put(keep, send, dot_nn(a2t[...], du))
+    return jnp.sum(du.astype(HIGH), axis=0, keepdims=True)
+
+
+def mlp_first_kernel(parts, place, half, live_ref, x_ref, cot_ref, vec_ref, *refs):
+    o_refs, sources, refs = refs[:parts], refs[parts : parts + 6], refs[parts + 6 :]
+    keep, send, r1_ref, a2_ref, a2t_ref, dy_ref, dyt_ref, y_ref, da2_ref, wout_ref, vecg_ref = refs[:11]
+    wide, ot_scr, act_scr, sems = refs[11:]
     step = pl.program_id(0)
     rows = o_refs[0].shape[0]
     slots, width = x_ref.shape
     bo, gain, shift, bp = (vec_ref[r : r + 1, :] for r in (4, 5, 6, 11))
-    split = wide_refs[0].shape[1]
-    live = lax.broadcasted_iota(jnp.int32, (slots, 1), 0) < live_ref[0]
 
     def copies(k):
-        half_rows = rows // 2
-        near, far = half[0] * half_rows, (1 - half[0]) * half_rows
-        span = slice(0, split) if k == 0 else slice(split, wide.shape[1])
-        sources = [(own_ref.at[:, span], 0, 0), (core_ref.at[:, span], 1, 0)]
-        spots = [(2, near), (2, far), (3, near), (3, far)]
-        sources += [(wide_refs[4 * k + n], *spot) for n, spot in enumerate(spots)]
-        for n, (source, j, offset) in enumerate(sources):
-            start = pl.multiple_of((place[0] ^ j) * rows + offset, 16)
-            target = wide.at[pl.ds(start, source.shape[0]), span]
-            yield pltpu.make_async_copy(source, target, sems.at[k, n])
-
-    def block(n):
-        return wide[:, pl.ds(pl.multiple_of(n * width, 128), width)]
-
-    def permuted(scratch, value):
+        span = ((0, width), (width, wide.shape[1]))[k]
+        return weight_copies(place, half, sources, wide, span, 0, sems.at[k])
+
+    def permuted(ref):
         for j in range(parts):
-            scratch[j * rows : (j + 1) * rows, :] = value(pl.multiple_of((place[0] ^ j) * rows, 16))
-
-    def put(value):
-        value = value.astype(LOW)
-        for k in range(2):
-
-            @pl.when((step >= first_blocks) == bool(k))
-            def _():
-                keep, send = grad_refs[2 * k : 2 * k + 2]
-                for j in range(parts):
-                    (send if j % 2 else keep)[j // 2] = value[j * rows : (j + 1) * rows, :]
+            start = pl.multiple_of((place[0] ^ j) * rows, 16)
+            ref[j * rows : (j + 1) * rows, :] = ot_scr[pl.ds(start, rows), :]
 
     @pl.when(step == 0)
     def _():
@@ -318,66 +326,107 @@
             start = pl.multiple_of((place[0] ^ j) * rows, 16)
             ot_scr[pl.ds(start, rows), :] = o_refs[j][...]
         mixed = low_t(ot_scr[...])
+        live = lax.broadcasted_iota(jnp.int32, (slots, 1), 0) < live_ref[0]
         dy = jnp.where(live, cot_ref[...].astype(HIGH), 0.0)
-        dy_scr[...] = dy.astype(LOW)
+        dy_ref[...] = dy.astype(LOW)
         ot_scr[...] = dy.T.astype(LOW)
-        permuted(dyt_scr, lambda start: ot_scr[pl.ds(start, rows), :])
+        permuted(dyt_ref)
         for copy in copies(0):
             copy.wait()
-        r1 = x_ref[...].astype(HIGH) + dot_nn(mixed, wide[:, :width]) + bo
-        r1_scr[...] = r1
+        w_out = wide[:, :width]
+        wout_ref[...] = w_out
+        r1 = x_ref[...].astype(HIGH) + dot_nn(mixed, w_out) + bo
+        r1_ref[...] = r1
         unit, _ = normalize(r1)
         a2 = unit * gain + shift
-        a2_scr[...] = a2.astype(LOW)
+        a2_ref[...] = a2.astype(LOW)
         ot_scr[...] = a2.T.astype(LOW)
-        permuted(a2t_scr, lambda start: ot_scr[pl.ds(start, rows), :])
+        permuted(a2t_ref)
         vecg_ref[...] = jnp.zeros_like(vecg_ref)
         vecg_ref[11:12, :] = jnp.sum(dy, axis=0, keepdims=True)
-        y_scr[...] = r1 + bp
-        da2_scr[...] = jnp.zeros_like(da2_scr)
-
-    @pl.when(step == first_blocks)
-    def _():
+        y_ref[...] = r1 + bp
+        da2_ref[...] = jnp.zeros_like(da2_ref)
         for copy in copies(1):
             copy.wait()
 
+    def block(n):
+        return wide[:, pl.ds(pl.multiple_of(n * width, 128), width)]
+
+    @pl.when(step % 2 == 0)
+    def _():
+        row = pl.ds(7 + step // 2, 1)
+        vecg_ref[row, :] = mlp_chunk(
+            a2_ref, a2t_ref, dy_ref, block(1 + step), block(2 + step), vec_ref[row, :],
+            y_ref, da2_ref, act_scr, keep, send,
+        )
+
+    @pl.when(step % 2 == 1)
+    def _():
+        put(keep, send, dot_nn(dyt_ref[...], act_scr[...]))
+
+
+def mlp_last_kernel(parts, done, place, half, live_ref, vec_ref, *refs):
+    r1_ref, a2_ref, a2t_ref, dy_ref, dyt_ref, y_ref, da2_ref, wout_ref, vecg_in, *refs = refs
+    o_refs, sources, refs = refs[:parts], refs[parts : parts + 6], refs[parts + 6 :]
+    out_ref, keep, send, dr1_ref, vecg_ref = refs[:5]
+    do_refs, (wide, act_scr, y_scr, da2_scr, sems) = refs[5 : 5 + parts], refs[5 + parts :]
+    step = pl.program_id(0)
     last = pl.num_programs(0) - 1
+    rows = o_refs[0].shape[0]
+    slots, width = r1_ref.shape
+    split = 2 * width
+
+    def copies(k):
+        span = ((0, split), (split, wide.shape[1]))[k]
+        return weight_copies(place, half, sources, wide, span, (1 + 2 * done) * width, sems.at[k])
+
+    def block(n):
+        return wide[:, pl.ds(pl.multiple_of(n * width, 128), width)]
+
+    @pl.when(step == 0)
+    def _():
+        for k in range(2):
+            for copy in copies(k):
+                copy.start()
+        y_scr[...] = y_ref[...]
+        da2_scr[...] = da2_ref[...]
+        vecg_ref[...] = vecg_in[...]
+        for copy in copies(0):
+            copy.wait()
+
+    @pl.when(step == 2)
+    def _():
+        for copy in copies(1):
+            copy.wait()
 
     @pl.when((step < last) & (step % 2 == 0))
     def _():
-        w_fc, w_pt = block(1 + step), block(2 + step)
-        u = dot_nn(a2_scr[...], w_fc) + vec_ref[pl.ds(7 + step // 2, 1), :]
-        square = u * u
-        t = jnp.tanh(GELU_C * (u + GELU_A * (square * u)))
-        grown = 0.5 * (1.0 + t)
-        act = (u * grown).astype(LOW)
-        act_scr[...] = act
-        y_scr[...] += dot_nt(act, w_pt)
-        slope = grown + 0.5 * u * (1.0 - t * t) * (GELU_C + (3.0 * GELU_C * GELU_A) * square)
-        du = (dot_nn(dy_scr[...], w_pt) * slope).astype(LOW)
-        vecg_ref[pl.ds(7 + step // 2, 1), :] = jnp.sum(du.astype(HIGH), axis=0, keepdims=True)
-        da2_scr[...] += dot_nt(du, w_fc)
-        put(dot_nn(a2t_scr[...], du))
+        row = pl.ds(7 + done + step // 2, 1)
+        vecg_ref[row, :] = mlp_chunk(
+            a2_ref, a2t_ref, dy_ref, block(step), block(1 + step), vec_ref[row, :],
+            y_scr, da2_scr, act_scr, keep, send,
+        )
 
     @pl.when((step < last) & (step % 2 == 1))
     def _():
-        put(dot_nn(dyt_scr[...], act_scr[...]))
+        put(keep, send, dot_nn(dyt_ref[...], act_scr[...]))
 
     @pl.when(step == last)
     def _():
+        live = lax.broadcasted_iota(jnp.int32, (slots, 1), 0) < live_ref[0]
         out_ref[...] = jnp.where(live, y_scr[...], 0.0).astype(LOW)
-        unit, inverse = normalize(r1_scr[...])
+        unit, inverse = normalize(r1_ref[...])
         da2 = da2_scr[...]
         vecg_ref[5:6, :] = jnp.sum(da2 * unit, axis=0, keepdims=True)
         vecg_ref[6:7, :] = jnp.sum(da2, axis=0, keepdims=True)
-        dr1 = dy_scr[...].astype(HIGH) + normalize_back(unit, inverse, da2 * gain)
+        dr1 = dy_ref[...].astype(HIGH) + normalize_back(unit, inverse, da2 * vec_ref[5:6, :])
         dr1_ref[...] = dr1
         low = dr1.astype(LOW)
         vecg_ref[4:5, :] = jnp.sum(low.astype(HIGH), axis=0, keepdims=True)
-        put(dot_nn(jnp.concatenate([ref[...] for ref in o_refs], axis=0), low))
         for j in range(parts):
             start = pl.multiple_of((place[0] ^ j) * rows, 16)
-            do_refs[j][...] = dot_nt(wide[pl.ds(start, rows), :width], low).astype(LOW)
+            do_refs[j][...] = dot_nt(wout_ref[pl.ds(start, rows), :], low).astype(LOW)
+        put(keep, send, dot_nn(jnp.concatenate([ref[...] for ref in o_refs], axis=0), low))
 
 
 def group_layout(length_row, count_row, slots):
@@ -643,68 +692,91 @@
             [jnp.concatenate([head[j] for head in mixed], axis=0) for j in range(parts)], parts
         )
         turned.append(swap(near[1], "shard", 1, parts))
-        wide = [wide_own, wide_core]
-        for k in range(2):
-            wide += [near[k], far[k], turned[k], swap(far[k], "shard", 1, parts)]
-
-        steps = blocks
+        far[1], mixed_own[0] = lax.optimization_barrier((far[1], mixed_own[0]))
+        wide = [
+            [wide_own, wide_core, near[k], far[k], turned[k], swap(far[k], "shard", 1, parts)]
+            for k in range(2)
+        ]
         live_own = lax.dynamic_index_in_dim(counts[0], place, 0, keepdims=True)
-        first_blocks = fc_rows // 2 * 2
-
-        def grad_spec(k):
-            first, last = ((0, first_blocks - 1), (first_blocks, steps - 1))[k]
-            return pl.BlockSpec(
-                (parts // 2, rows, width), lambda i, *_: (0, 0, jnp.clip(i, first, last) - first)
-            )
-
-        grad_columns = [first_blocks * width, (steps - first_blocks) * width]
-
+        scalars = (prefetch, side, live_own)
         in_hbm = pl.BlockSpec(memory_space=pltpu.HBM)
-        out = pl.pallas_call(
-            functools.partial(mlp_kernel, parts, first_blocks),
+        done = fc_rows // 2
+
+        def grad_outs(steps):
+            spec = pl.BlockSpec((parts // 2, rows, width), lambda i, *_: (0, 0, i))
+            shape = jax.ShapeDtypeStruct((parts // 2, rows, steps * width), LOW)
+            return [spec] * 2, [shape] * 2
+
+        def mlp_cost(steps):
+            return cost(6 * slots * width * width * (steps + 1), 20e6, slots * hidden // 2)
+
+        by_slot, by_width = (slots, width), (width, slots)
+        kept = [by_slot, by_slot, by_width, by_slot, by_width, by_slot, by_slot, (width, width), (16, width)]
+        kept_types = [HIGH, LOW, LOW, LOW, LOW, HIGH, HIGH, LOW, HIGH]
+        specs, shapes = grad_outs(2 * done)
+        keep_a, send_a, *state = pl.pallas_call(
+            functools.partial(mlp_first_kernel, parts),
             grid_spec=pltpu.PrefetchScalarGridSpec(
                 num_scalar_prefetch=3,
-                grid=(steps,),
+                grid=(2 * done,),
                 in_specs=[whole(slots, width), whole(slots, width), whole(16, width)]
                 + [whole(own_cols, slots)] * parts
-                + [in_hbm] * len(wide),
-                out_specs=[whole(slots, width)]
-                + [grad_spec(k) for k in range(2) for _ in range(2)]
-                + [whole(slots, width), whole(16, width)]
-                + [whole(own_cols, slots)] * parts,
+                + [in_hbm] * 6,
+                out_specs=specs + [whole(*shape) for shape in kept],
                 scratch_shapes=[
-                    pltpu.VMEM((width, blocks * width), LOW),
+                    pltpu.VMEM((width, split), LOW),
                     pltpu.VMEM((width, slots), LOW),
-                    pltpu.VMEM((slots, width), HIGH),
-                    pltpu.VMEM((slots, width), LOW),
-                    pltpu.VMEM((width, slots), LOW),
-                    pltpu.VMEM((slots, width), LOW),
-                    pltpu.VMEM((width, slots), LOW),
-                    pltpu.VMEM((slots, width), HIGH),
-                    pltpu.VMEM((slots, width), HIGH),
                     pltpu.VMEM((slots, width), LOW),
                     pltpu.SemaphoreType.DMA((2, 6)),
                 ],
             ),
+            out_shape=shapes
+            + [jax.ShapeDtypeStruct(shape, kind) for shape, kind in zip(kept, kept_types)],
+            compiler_params=params("arbitrary"),
+            cost_estimate=mlp_cost(2 * done),
+            name="mlp_first",
+        )(*scalars, tokens, cotangent, vectors, *mixed_own, *wide[0])
+        got_a = swap(send_a, "shard", 1, parts)
+
+        specs, shapes = grad_outs(blocks - 2 * done)
+        block_out, keep_b, send_b, grad_resid, mid_grads, *do_pieces = pl.pallas_call(
+            functools.partial(mlp_last_kernel, parts, done),
+            grid_spec=pltpu.PrefetchScalarGridSpec(
+                num_scalar_prefetch=3,
+                grid=(blocks - 2 * done,),
+                in_specs=[whole(16, width)]
+                + [whole(*shape) for shape in kept]
+                + [whole(own_cols, slots)] * parts
+                + [in_hbm] * 6,
+                out_specs=[whole(slots, width)]
+                + specs
+                + [whole(slots, width), whole(16, width)]
+                + [whole(own_cols, slots)] * parts,
+                scratch_shapes=[
+                    pltpu.VMEM((width, blocks * width - split), LOW),
+                    pltpu.VMEM((slots, width), LOW),
+                    pltpu.VMEM((slots, width), HIGH),
+                    pltpu.VMEM((slots, width), HIGH),
+                    pltpu.SemaphoreType.DMA((2, 6)),
+                ],
+            ),
             out_shape=[jax.ShapeDtypeStruct((slots, width), LOW)]
-            + [jax.ShapeDtypeStruct((parts // 2, rows, c), LOW) for c in grad_columns for _ in range(2)]
+            + shapes
             + [jax.ShapeDtypeStruct((slots, width), HIGH), jax.ShapeDtypeStruct((16, width), HIGH)]
             + [jax.ShapeDtypeStruct((own_cols, slots), LOW)] * parts,
             compiler_params=params("arbitrary"),
-            cost_estimate=cost(2 * slots * width * (6 * hidden + 3 * width), 30e6, slots * hidden),
-            name="mlp",
-        )(prefetch, side, live_own, tokens, cotangent, vectors, *mixed_own, *wide)
-        block_out, keep_a, send_a, keep_b, send_b, grad_resid, mid_grads, *do_pieces = out
+            cost_estimate=mlp_cost(blocks - 2 * done),
+            name="mlp_last",
+        )(*scalars, vectors, *state, *mixed_own, *wide[1])
 
         do_own = deal(do_pieces, parts)
-        got_a = swap(send_a, "shard", 1, parts)
         got_b = swap(send_b, "shard", 1, parts)
+        got_a = after(got_a, grad_resid)
         own_a, other_a = [add_low(keep_a[n], got_a[n]) for n in range(2)]
+        got_a = swap(other_a, "shard", parts // 2, parts)
+        got_b = after(got_b, other_a)
         own_b, other_b = halve(add_low(keep_b, got_b), half, 1)
-        *do_own, own_a, other_a, own_b, other_b = lax.optimization_barrier(
-            (*do_own, own_a, other_a, own_b, other_b)
-        )
-        got_a = swap(other_a, "shard", parts // 2, parts)
+        *do_own, own_a, own_b, other_b = lax.optimization_barrier((*do_own, own_a, own_b, other_b))
         got_b = swap(other_b, "dp", 1, replicas)
 
         def attend_back(h, qkv):
@@ -732,11 +804,20 @@
                 name="attend_back",
             )(prefetch, qkv, qkv, qkv, seg_col, seg_row, lse[h], *do_own)
 
-        dqkv = [attend_back(h, qkv) for h in range(own_heads)]
-        *dqkv, got_a = lax.optimization_barrier((*dqkv, got_a))
-        own_a, other_a = halve(add_low(own_a, got_a), half, 0)
-        dqkv[0] = after(dqkv[0], other_a)
-        got_a = swap(other_a, "dp", 1, replicas)
+        dqkv = []
+        for h in range(own_heads):
+            if h == own_heads - 1:
+                got_a, *dqkv = lax.optimization_barrier((got_a, *dqkv))
+                own_a, other_a = halve(add_low(own_a, got_a), half, 0)
+                qkv = after(qkv, other_a)
+                got_a = swap(other_a, "dp", 1, replicas)
+            dqkv.append(attend_back(h, qkv))
+        z_bits = [bit for bit in (1 << n for n in range(1, 20)) if bit < replicas]
+        got_a, got_b, dqkv[-1] = lax.optimization_barrier((got_a, got_b, dqkv[-1]))
+        own_b, other_b = [add_low(own_b[n], got_b[n]) for n in range(2)]
+        got_b = swap(other_b, "shard", parts // 2, parts)
+        state_a = scatter_half(add_low(own_a, got_a), 0, z_bits[0], replica, replicas)
+        dqkv[0] = after(dqkv[0], own_b, other_b, state_a[0])
 
         q_cols = 3 * own_cols
         extra = vec_w.shape[0]
@@ -772,7 +853,6 @@
         )(prefetch, side, *x_all, a1, *dqkv, w_t, vectors, mid_grads)
 
         share = rows // replicas
-        z_bits = [bit for bit in (1 << n for n in range(1, 20)) if bit < replicas]
         tokens_seen = [own_q]
 
         def seen(*values):
@@ -795,17 +875,14 @@
             return state
 
         got_q = swap(other_q, "dp", 1, replicas)
-        sum_b = event(add_low(own_b, seen(got_b)))
-        got_b = swap(sum_b[1], "shard", parts // 2, parts)
         da1_got = swap(da1_send, "shard", 1, parts)
-        state_a = scatter_on("a", own_a, got_a, z_bits[0])
         state_a = scatter_rest("a", state_a)
+        state_b = scatter_on("b", own_b, got_b, z_bits[0])
         state_q = scatter_on("q", own_q, got_q, z_bits[0])
-        state_b = scatter_on("b", sum_b[0], got_b, z_bits[0])
         part_a = event(add_low(state_a[0], seen(state_a[1])))
         all_a = lax.all_gather(part_a, "dp", axis=0)
+        state_b = scatter_rest("b", state_b)
         state_q = scatter_rest("q", state_q)
-        state_b = scatter_rest("b", state_b)
         part_q = event(add_low(state_q[0], seen(state_q[1])))
 
         main = part_q[:, :, :q_cols]

time: 373 us -> 377 us (1.011)
  waiting for transfers between devices: 82 us -> 104 us
  starting transfers between devices: 83.3 us -> 69.7 us
  Pallas kernels: 141 us -> 135 us
  local copies, waits for them, and re-layouts: 11 us -> 15.4 us
    ppermute x50, waiting for transfers between devices: 82 us -> 104 us  [swap(): return lax.ppermute(array, axis, [(i, i ^ bit) for i in range(count)])]
    ppermute x50, starting transfers between devices: 83.2 us -> 69.7 us  [swap(): return lax.ppermute(array, axis, [(i, i ^ bit) for i in range(count)])]
    unnamed x73 -> x75, local copies, waits for them, and re-layouts: 3.91 us -> 10.8 us
    pallas_call x1 -> x2, Pallas kernels: 33.6 us -> 39.7 us  [the longest x1 21 us: on_device(): pl.pallas_call(functools.partial(mlp_last_kernel, parts, done), grid_spec...]
    pallas_call x3, Pallas kernels: 32 us -> 27.6 us  [attend_back(): pl.pallas_call(functools.partial(attend_back_kernel, scale), grid_spec=pl...]
  transfers between devices with their start and end apart: 51 -> 51, of which waited for: 21 -> 19; matrix products, arithmetic and copies ran while one was open for 10% -> 8% of each run, Pallas kernels for 24% -> 31%
where the time goes in v3:
time: 377 us; the launch traced here: 372 us
  Pallas kernels  135 us (36%)
  waiting for transfers between devices  104 us (28%)
  starting transfers between devices  69.7 us (18%)
  other arithmetic  26.1 us (7%)
  between operations  22 us (6%)
  local copies, waits for them, and re-layouts  15.4 us (4%)
    ppermute x50, waiting for transfers between devices, swap(): return lax.ppermute(array, axis, [(i, i ^ bit) for i in range(count)])  104 us
    ppermute x50, starting transfers between devices, swap(): return lax.ppermute(array, axis, [(i, i ^ bit) for i in range(count)])  69.7 us
    pallas_call x3, Pallas kernels, attend_back(): pl.pallas_call(functools.partial(attend_back_kernel, scale), grid_spec=pl...  27.6 us
    pallas_call x3, Pallas kernels, attend(): pl.pallas_call(functools.partial(attend_kernel, scale), grid_spec=pltpu.P...  22.8 us
    pallas_call x1, Pallas kernels, on_device(): pl.pallas_call(functools.partial(mlp_last_kernel, parts, done), grid_spec...  21 us
    pallas_call x1, Pallas kernels, on_device(): pl.pallas_call(functools.partial(adam_kernel, fc_rows), grid_spec=pltpu.P...  19.2 us
    pallas_call x1, Pallas kernels, on_device(): pl.pallas_call(functools.partial(mlp_first_kernel, parts), grid_spec=pltp...  18.7 us
    pallas_call x1, Pallas kernels, on_device(): pl.pallas_call(functools.partial(projection_back_kernel, own_heads, parts...  12.7 us
  transfers between devices with their start and end apart: 51, of which 19 were waited for; matrix products, arithmetic and copies ran while one was open for 8% of the time, Pallas kernels for 31%

profile of v3, /device:TPU:0, one launch (start us, length us, event | category | flops | bytes accessed | tf_op | source)
XLA Modules:
  0.0 372.1 jit_solution(17451348895022766816)
XLA Ops:
  7.2 3.0 collective-permute-start.1
  10.3 1.7 copy-done
  12.6 1.5 cut.1
  17.3 1.3 copy.48
  19.8 9.2 %collective-permute-done.1.refs_2_ = bf16[512,768]{1,0:T(8,128)(2,1)} collective-permute-done((bf16[512,768]{1,0:T(8,128)(2,1)}, bf16[512,768]{1,0:T(8,128)(2,1)}, u32[]{:S(2)}, u32[]{:S(2)}) %collective-permute-start.1) | collective-permute-done | bytes 786464 | tf_op jit(solution)/shard_map/ppermute | solution.py:482
  28.9 1.4 subtract_select_fusion.segc_ref
  30.5 4.3 %widen.1 = (bf16[192,6912]{1,0:T(8,128)(2,1)}, bf16[96,3840]{1,0:T(8,128)(2,1)S(1)}, bf16[96,3072]{1,0:T(8,128)(2,1)S(1)}) custom-call(s32[1]{0:T(128)} %bitcast.1.half, f32[192,3072]{1,0:T(8,128)S(1)} %copy-done.1, f32[2,192,3072]{2,1,0:T(8,128)} %mlp_ref.1), custom_call_target="tpu_custom_call" | custom-call | bytes 12000000 | tf_op jit(solution)/shard_map/widen/pallas_call | solution.py:584
  34.8 4.0 %collective-permute-done.5.refs_7_ = bf16[208,576]{1,0:T(8,128)(2,1)} collective-permute-done((bf16[208,576]{1,0:T(8,128)(2,1)}, bf16[208,576]{1,0:T(8,128)(2,1)}, u32[]{:S(2)}, u32[]{:S(2)}) %collective-permute-start.5) | collective-permute-done | bytes 239648 | tf_op jit(solution)/shard_map/ppermute | solution.py:482
  39.6 1.8 collective-permute-start.7
  41.8 7.2 %project.1 = (bf16[2048,768]{1,0:T(8,128)(2,1)}, bf16[576,2048]{1,0:T(8,128)(2,1)}, bf16[576,768]{1,0:T(8,128)(2,1)}, f32[16,768]{1,0:T(8,128)S(1)}) custom-call(s32[1]{0:T(128)} %bitcast.place, bf16[512,768]{1,0:T(8,128)(2,1)S(1)} %copy-done.2, bf16[512,768]{1,0:T(8,128)(2,1)} %collective-permute-done.refs_1_, ...), custom_call_target="tpu_custom_call" | custom-call | flops 5435817984 | bytes 12000000 | tf_op jit(solution)/shard_map/project/pallas_call | solution.py:620
  49.0 10.0 %collective-permute-done.7.refs_6_ = bf16[96,3840]{1,0:T(8,128)(2,1)S(1)} collective-permute-done((bf16[96,3840]{1,0:T(8,128)(2,1)S(1)}, bf16[96,3840]{1,0:T(8,128)(2,1)S(1)}, u32[]{:S(2)}, u32[]{:S(2)}) %collective-permute-start.7) | collective-permute-done | bytes 737312 | tf_op jit(solution)/shard_map/ppermute | solution.py:482
  59.0 1.8 collective-permute-start.13
  60.8 7.5 %attend.4 = (bf16[4,64,512]{2,1,0:T(8,128)(2,1)S(1)}, f32[1,2048,1]{2,1,0:T(8,128)S(1)}) custom-call(s32[1]{0:T(128)} %bitcast.place, bf16[576,2048]{1,0:T(8,128)(2,1)} %get-tuple-element.165.qt_ref.kt_ref.vt_ref, bf16[576,2048]{1,0:T(8,128)(2,1)} %get-tuple-element.165.qt_ref.kt_ref.vt_ref, bf16[576,2048]{1,0:T(8,128)(2,1)} %get-tuple-element.165.qt_ref.kt_ref.vt_ref, ...), custom_call_target="tpu_custom_call" | custom-call | flops 2147483648 | bytes 4000000 | tf_op jit(solution)/shard_map/attend/pallas_call | solution.py:662
  69.3 7.5 %attend.3 = (bf16[4,64,512]{2,1,0:T(8,128)(2,1)S(1)}, f32[1,2048,1]{2,1,0:T(8,128)S(1)}) custom-call(s32[1]{0:T(128)} %bitcast.place, bf16[576,2048]{1,0:T(8,128)(2,1)} %get-tuple-element.165.qt_ref.kt_ref.vt_ref, bf16[576,2048]{1,0:T(8,128)(2,1)} %get-tuple-element.165.qt_ref.kt_ref.vt_ref, bf16[576,2048]{1,0:T(8,128)(2,1)} %get-tuple-element.165.qt_ref.kt_ref.vt_ref, ...), custom_call_target="tpu_custom_call" | custom-call | flops 2147483648 | bytes 4000000 | tf_op jit(solution)/shard_map/attend/pallas_call | solution.py:662
  77.2 7.7 %attend.5 = (bf16[4,64,512]{2,1,0:T(8,128)(2,1)S(1)}, f32[1,2048,1]{2,1,0:T(8,128)S(1)}) custom-call(s32[1]{0:T(128)} %bitcast.place, bf16[576,2048]{1,0:T(8,128)(2,1)} %get-tuple-element.165.qt_ref.kt_ref.vt_ref, bf16[576,2048]{1,0:T(8,128)(2,1)} %get-tuple-element.165.qt_ref.kt_ref.vt_ref, bf16[576,2048]{1,0:T(8,128)(2,1)} %get-tuple-element.165.qt_ref.kt_ref.vt_ref, ...), custom_call_target="tpu_custom_call" | custom-call | flops 2147483648 | bytes 4000000 | tf_op jit(solution)/shard_map/attend/pallas_call | solution.py:662
  86.0 1.6 collective-permute-start.11
  89.0 3.8 %collective-permute-done.11.refs_3_.refs_12_ = bf16[192,512]{1,0:T(8,128)(2,1)S(1)} collective-permute-done((bf16[192,512]{1,0:T(8,128)(2,1)S(1)}, bf16[192,512]{1,0:T(8,128)(2,1)S(1)}, u32[]{:S(2)}, u32[]{:S(2)}) %collective-permute-start.11) | collective-permute-done | bytes 196640 | tf_op jit(solution)/shard_map/ppermute | solution.py:482
  92.8 1.9 collective-permute-start.10
  95.2 4.9 %collective-permute-done.10.refs_2_.refs_11_ = bf16[192,512]{1,0:T(8,128)(2,1)} collective-permute-done((bf16[192,512]{1,0:T(8,128)(2,1)}, bf16[192,512]{1,0:T(8,128)(2,1)}, u32[]{:S(2)}, u32[]{:S(2)}) %collective-permute-start.10) | collective-permute-done | bytes 196640 | tf_op jit(solution)/shard_map/ppermute | solution.py:482
  100.7 18.7 %mlp_first.1 = (bf16[2,192,3072]{2,1,0:T(8,128)(2,1)}, bf16[2,192,3072]{2,1,0:T(8,128)(2,1)}, f32[512,768]{1,0:T(8,128)}, bf16[512,768]{1,0:T(8,128)(2,1)}, bf16...) custom-call(s32[1]{0:T(128)} %bitcast.place, ...), custom_call_target="tpu_custom_call" | custom-call | flops 9059696640 | bytes 20000000 | tf_op jit(solution)/shard_map/mlp_first/pallas_call | solution.py:717
  120.5 21.0 %mlp_last.1 = (bf16[512,768]{1,0:T(8,128)(2,1)}, bf16[2,192,3840]{2,1,0:T(8,128)(2,1)}, bf16[2,192,3840]{2,1,0:T(8,128)(2,1)}, f32[512,768]{1,0:T(8,128)}, f32[1...) custom-call(s32[1]{0:T(128)} %bitcast.place, ...), custom_call_target="tpu_custom_call" | custom-call | flops 10871635968 | bytes 20000000 | tf_op jit(solution)/shard_map/mlp_last/pallas_call | solution.py:742
  145.5 1.8 collective-permute-start.21
  147.3 3.4 fusion.13
  150.7 1.8 collective-permute-start.19
  152.5 2.6 add_convert_fusion
  155.1 1.3 constant_dynamic-slice_fusion.13
  156.7 1.6 collective-permute-start.25
  158.3 9.0 %attend_back.4.refs_6_ = bf16[3,64,2048]{2,1,0:T(8,128)(2,1)S(1)} custom-call(s32[1]{0:T(128)} %bitcast.place, bf16[576,2048]{1,0:T(8,128)(2,1)} %get-tuple-element.165.qt_ref.kt_ref.vt_ref, bf16[576,2048]{1,0:T(8,128)(2,1)} %get-tuple-element.165.qt_ref.kt_ref.vt_ref, bf16[576,2048]{1,0:T(8,128)(2,1)} %get-tuple-element.165.qt_ref.kt_ref.vt_ref, ...), custom_call_target="tpu_custom_call" | custom-call | flops 5368709120 | bytes 4000000 | tf_op jit(solution)/shard_map/attend_back/pallas_call | solution.py:783
  168.2 9.4 %attend_back.3.refs_5_ = bf16[3,64,2048]{2,1,0:T(8,128)(2,1)S(1)} custom-call(s32[1]{0:T(128)} %bitcast.place, bf16[576,2048]{1,0:T(8,128)(2,1)} %get-tuple-element.165.qt_ref.kt_ref.vt_ref, bf16[576,2048]{1,0:T(8,128)(2,1)} %get-tuple-element.165.qt_ref.kt_ref.vt_ref, bf16[576,2048]{1,0:T(8,128)(2,1)} %get-tuple-element.165.qt_ref.kt_ref.vt_ref, ...), custom_call_target="tpu_custom_call" | custom-call | flops 5368709120 | bytes 4000000 | tf_op jit(solution)/shard_map/attend_back/pallas_call | solution.py:783
  177.6 4.7 %collective-permute-done.19 = bf16[192,3072]{1,0:T(8,128)(2,1)} collective-permute-done((bf16[192,3072]{1,0:T(8,128)(2,1)S(1)}, bf16[192,3072]{1,0:T(8,128)(2,1)}, u32[]{:S(2)}, u32[]{:S(2)}) %collective-permute-start.19) | collective-permute-done | bytes 1179680 | tf_op jit(solution)/shard_map/ppermute | solution.py:482
  182.3 1.7 add_convert_fusion.1
  184.1 1.8 collective-permute-start.24
  185.9 9.1 %attend_back.5.refs_7_ = bf16[3,64,2048]{2,1,0:T(8,128)(2,1)S(1)} custom-call(s32[1]{0:T(128)} %bitcast.place, bf16[576,2048]{1,0:T(8,128)(2,1)} %get-tuple-element.165.qt_ref.kt_ref.vt_ref, bf16[576,2048]{1,0:T(8,128)(2,1)} %get-tuple-element.165.qt_ref.kt_ref.vt_ref, bf16[576,2048]{1,0:T(8,128)(2,1)} %get-tuple-element.165.qt_ref.kt_ref.vt_ref, ...), custom_call_target="tpu_custom_call" | custom-call | flops 5368709120 | bytes 4000000 | tf_op jit(solution)/shard_map/attend_back/pallas_call | solution.py:783
  195.1 9.2 %collective-permute-done.24 = bf16[96,3072]{1,0:T(8,128)(2,1)S(1)} collective-permute-done((bf16[96,3072]{1,0:T(8,128)(2,1)S(1)}, bf16[96,3072]{1,0:T(8,128)(2,1)S(1)}, u32[]{:S(2)}, u32[]{:S(2)}) %collective-permute-start.24) | collective-permute-done | bytes 589856 | tf_op jit(solution)/shard_map/ppermute | solution.py:482
  204.8 1.8 collective-permute-start.31
  206.6 1.7 collective-permute-start.28
  208.3 12.7 %projection_back.1 = (bf16[2,512,768]{2,1,0:T(8,128)(2,1)}, bf16[2,512,768]{2,1,0:T(8,128)(2,1)}, bf16[4,96,588]{2,1,0:T(8,128)(2,1)S(1)}, bf16[4,96,588]{2,1,0:T(8,128)(2,1)S(1)}) custom-call(s32[1]{0:T(128)} %bitcast.place, s32[1]{0:T(128)} %bitcast.1.half, bf16[512,768]{1,0:T(8,128)(2,1)S(1)} %copy-done.3, bf16[512,768]{1,0:T(8,128)(2,1)} %collective-permute-done.refs_1_, ...), custom_call_target="tpu_custom_call" | custom-call | flops 7247757312 | bytes 16000000 | tf_op jit(solution)/shard_map/projection_back/pallas_call | solution.py:825
  221.0 1.6 collective-permute-start.30
  222.7 2.7 collective-permute-start.29
  225.6 8.0 %collective-permute-done.30 = bf16[4,96,588]{2,1,0:T(8,128)(2,1)S(1)} collective-permute-done((bf16[4,96,588]{2,1,0:T(8,128)(2,1)S(1)}, bf16[4,96,588]{2,1,0:T(8,128)(2,1)S(1)}, u32[]{:S(2)}, u32[]{:S(2)}) %collective-permute-start.30) | collective-permute-done | bytes 451616 | tf_op jit(solution)/shard_map/ppermute | solution.py:482
  234.1 1.7 collective-permute-start.34
  235.8 1.3 multiply_reduce_fusion.1
  237.2 7.9 %collective-permute-done.32 = bf16[48,3840]{1,0:T(8,128)(2,1)S(1)} collective-permute-done((bf16[48,3840]{1,0:T(8,128)(2,1)S(1)}, bf16[48,3840]{1,0:T(8,128)(2,1)S(1)}, u32[]{:S(2)}, u32[]{:S(2)}) %collective-permute-start.32) | collective-permute-done | bytes 368672 | tf_op jit(solution)/shard_map/ppermute | solution.py:482
  245.2 4.2 %collective-permute-done.34 = bf16[4,48,588]{2,1,0:T(8,128)(2,1)} collective-permute-done((bf16[4,48,588]{2,1,0:T(8,128)(2,1)S(1)}, bf16[4,48,588]{2,1,0:T(8,128)(2,1)}, u32[]{:S(2)}, u32[]{:S(2)}) %collective-permute-start.34) | collective-permute-done | bytes 225824 | tf_op jit(solution)/shard_map/ppermute | solution.py:482
  250.4 2.7 collective-permute-start.35
  253.5 10.2 %collective-permute-done.35 = bf16[4,24,588]{2,1,0:T(8,128)(2,1)S(1)} collective-permute-done((bf16[4,24,588]{2,1,0:T(8,128)(2,1)S(1)}, bf16[4,24,588]{2,1,0:T(8,128)(2,1)S(1)}, u32[]{:S(2)}, u32[]{:S(2)}) %collective-permute-start.35) | collective-permute-done | bytes 112928 | tf_op jit(solution)/shard_map/ppermute | solution.py:482
  264.6 1.3 collective-permute-start.38
  266.6 1.6 collective-permute-done.37
  270.5 1.6 multiply_reduce_fusion
  272.1 2.9 collective-permute-start.40
  278.0 9.8 %collective-permute-done.41 = bf16[1,24,2316]{2,1,0:T(8,128)(2,1)S(1)} collective-permute-done((bf16[1,24,2316]{2,1,0:T(8,128)(2,1)S(1)}, bf16[1,24,2316]{2,1,0:T(8,128)(2,1)S(1)}, u32[]{:S(2)}, u32[]{:S(2)}) %collective-permute-start.41) | collective-permute-done | bytes 111200 | tf_op jit(solution)/shard_map/ppermute | solution.py:482
  287.9 5.7 %collective-permute-done.40 = bf16[1,24,3840]{2,1,0:T(8,128)(2,1)S(1)} collective-permute-done((bf16[1,24,3840]{2,1,0:T(8,128)(2,1)S(1)}, bf16[1,24,3840]{2,1,0:T(8,128)(2,1)S(1)}, u32[]{:S(2)}, u32[]{:S(2)}) %collective-permute-start.40) | collective-permute-done | bytes 184352 | tf_op jit(solution)/shard_map/ppermute | solution.py:482
  294.4 2.8 collective-permute-start.42
  297.2 1.3 fusion.14
  299.3 1.5 collective-permute-start.48
  300.8 5.7 %collective-permute-done.43 = bf16[2,24,3840]{2,1,0:T(8,128)(2,1)S(1)} collective-permute-done((bf16[2,24,3840]{2,1,0:T(8,128)(2,1)S(1)}, bf16[2,24,3840]{2,1,0:T(8,128)(2,1)S(1)}, u32[]{:S(2)}, u32[]{:S(2)}) %collective-permute-start.43) | collective-permute-done | bytes 368672 | tf_op jit(solution)/shard_map/ppermute | solution.py:482
  306.5 1.5 collective-permute-start.49
  308.7 17.4 %collective-permute-start.45 = (f32[1,1]{1,0:T(1,128)}, f32[1,1]{1,0:T(1,128)}, u32[]{:S(2)}, u32[]{:S(2)}) collective-permute-start(f32[1,1]{1,0:T(1,128)} %add.278), channel_id=1, source_target_pairs={{0,4},{4,0},{8,12},{12,8},{16,20},{20,16},{24,28},{28,24},{1,5},{5... | collective-permute-start | bytes 20 | tf_op jit(solution)/shard_map/ppermute | solution.py:482
  327.9 2.6 collective-permute-start.46
  332.2 2.4 collective-permute-start.47
  334.6 2.2 collective-permute-done.47
  337.6 2.0 fusion.36
  339.7 2.8 fusion.9
  344.8 19.2 %adam.1 = (f32[8,24,3072]{2,1,0:T(8,128)}, f32[8,24,3072]{2,1,0:T(8,128)}, f32[8,24,3072]{2,1,0:T(8,128)}, f32[8,24,3072]{2,1,0:T(8,128)}, f32[2,8,24,3072]{3,2,...) custom-call(f32[1]{0:T(128)} %bitcast.45.factor_ref, ...), custom_call_target="tpu_custom_call" | custom-call | flops 39813120 | bytes 54000000 | tf_op jit(solution)/shard_map/adam/pallas_call | solution.py:977
  (216 shorter events, 29.9 us)
Async XLA Ops:
  7.2 9.8 %copy-start.35 = (s32[1,2]{1,0:T(1,128)S(1)}, s32[1,2]{1,0:T(1,128)}, u32[]{:S(2)}) copy-start(s32[1,2]{1,0:T(1,128)} %param.15) | copy-start | bytes 28
  7.2 336.3 %all-gather.3.cloned.1.call-start = ((), (), s32[]{:S(2)}) async-start(), calls=%async_computation | async-start | bytes 1327104 | tf_op jit(solution)/shard_map/all_gather | solution.py:883
  7.2 21.7 %collective-permute-start.1 = (bf16[512,768]{1,0:T(8,128)(2,1)}, bf16[512,768]{1,0:T(8,128)(2,1)}, u32[]{:S(2)}, u32[]{:S(2)}) collective-permute-start(bf16[512,768]{1,0:T(8,128)(2,1)} %refs_0_.3), channel_id=1, source_target_pairs={{0,2},{1,3},{2,0},{3,1},{4,6},{5,7},{6,4},{7,5},{8,10},{9,11},{10,... | collective-permute-start | bytes 2359304 | tf_op jit(solution)/shard_map/ppermute | solution.py:482
  10.3 28.5 %collective-permute-start = (bf16[512,768]{1,0:T(8,128)(2,1)}, bf16[512,768]{1,0:T(8,128)(2,1)}, u32[]{:S(2)}, u32[]{:S(2)}) collective-permute-start(bf16[512,768]{1,0:T(8,128)(2,1)} %refs_0_.3), channel_id=1, source_target_pairs={{0,1},{1,0},{2,3},{3,2},{4,5},{5,4},{6,7},{7,6},{8,9},{9,8},{10,11... | collective-permute-start | bytes 2359304 | tf_op jit(solution)/shard_map/ppermute | solution.py:482
  14.9 19.9 %collective-permute-start.3 = (bf16[208,576]{1,0:T(8,128)(2,1)}, bf16[208,576]{1,0:T(8,128)(2,1)}, u32[]{:S(2)}, u32[]{:S(2)}) collective-permute-start(bf16[208,576]{1,0:T(8,128)(2,1)} %get-tuple-element.113), channel_id=1, source_target_pairs={{0,1},{1,0},{2,3},{3,2},{4,5},{5,4},{6,7},{7,6},{8,9},{9,8},{10,11... | collective-permute-start | bytes 718856 | tf_op jit(solution)/shard_map/ppermute | solution.py:482
  15.4 19.4 %collective-permute-start.4 = (bf16[208,576]{1,0:T(8,128)(2,1)}, bf16[208,576]{1,0:T(8,128)(2,1)}, u32[]{:S(2)}, u32[]{:S(2)}) collective-permute-start(bf16[208,576]{1,0:T(8,128)(2,1)} %get-tuple-element.114), channel_id=1, source_target_pairs={{0,2},{1,3},{2,0},{3,1},{4,6},{5,7},{6,4},{7,5},{8,10},{9,11},{10,... | collective-permute-start | bytes 718856 | tf_op jit(solution)/shard_map/ppermute | solution.py:482
  15.4 23.3 %collective-permute-start.5 = (bf16[208,576]{1,0:T(8,128)(2,1)}, bf16[208,576]{1,0:T(8,128)(2,1)}, u32[]{:S(2)}, u32[]{:S(2)}) collective-permute-start(bf16[208,576]{1,0:T(8,128)(2,1)} %get-tuple-element.115), channel_id=1, source_target_pairs={{0,3},{1,2},{2,1},{3,0},{4,7},{5,6},{6,5},{7,4},{8,11},{9,10},{10,... | collective-permute-start | bytes 718856 | tf_op jit(solution)/shard_map/ppermute | solution.py:482
  18.6 11.8 %copy-start.6 = (f32[12,192]{1,0:T(8,128)S(1)}, f32[12,192]{1,0:T(8,128)}, u32[]{:S(2)}) copy-start(f32[12,192]{1,0:T(8,128)} %vec_ref.1) | copy-start | bytes 27652
  18.6 11.8 %copy-start.1 = (f32[192,3072]{1,0:T(8,128)S(1)}, f32[192,3072]{1,0:T(8,128)}, u32[]{:S(2)}) copy-start(f32[192,3072]{1,0:T(8,128)} %out_ref.1) | copy-start | bytes 7077892
  28.9 9.8 %collective-permute-start.2 = (bf16[512,768]{1,0:T(8,128)(2,1)}, bf16[512,768]{1,0:T(8,128)(2,1)}, u32[]{:S(2)}, u32[]{:S(2)}) collective-permute-start(bf16[512,768]{1,0:T(8,128)(2,1)} %collective-permute-done.1.refs_2_), channel_id=1, source_target_pairs={{0,1},{1,0},{2,3},{3,2},{4,5},{5,4},{6,7},{7,6},{8,9},{9,8},{10,11... | collective-permute-start | bytes 2359304 | tf_op jit(solution)/shard_map/ppermute | solution.py:482
  30.4 11.3 %copy-start.2 = (bf16[512,768]{1,0:T(8,128)(2,1)S(1)}, bf16[512,768]{1,0:T(8,128)(2,1)}, u32[]{:S(2)}) copy-start(bf16[512,768]{1,0:T(8,128)(2,1)} %refs_0_.3) | copy-start | bytes 2359300
  30.4 11.3 %copy-start.14 = (bf16[208,576]{1,0:T(8,128)(2,1)S(1)}, bf16[208,576]{1,0:T(8,128)(2,1)}, u32[]{:S(2)}) copy-start(bf16[208,576]{1,0:T(8,128)(2,1)} %copy-done.13) | copy-start | bytes 718852
  38.8 61.9 %collective-permute-start.12 = (bf16[192,6912]{1,0:T(8,128)(2,1)}, bf16[192,6912]{1,0:T(8,128)(2,1)}, u32[]{:S(2)}, u32[]{:S(2)}) collective-permute-start(bf16[192,6912]{1,0:T(8,128)(2,1)} %get-tuple-element.129.refs_4_.refs_13_), channel_id=1, source_target_pairs={{0,1},{1,0},{2,3},{3,2},{4,5},{5,4},{6,7},{7,6},{8,9},{9,8},{10,11... | collective-permute-start | bytes 7962632 | tf_op jit(solution)/shard_map/ppermute | solution.py:482
  39.6 19.4 %collective-permute-start.7 = (bf16[96,3840]{1,0:T(8,128)(2,1)S(1)}, bf16[96,3840]{1,0:T(8,128)(2,1)S(1)}, u32[]{:S(2)}, u32[]{:S(2)}) collective-permute-start(bf16[96,3840]{1,0:T(8,128)(2,1)S(1)} %get-tuple-element.122), channel_id=1, source_target_pairs={{0,2},{1,3},{2,0},{3,1},{4,6},{5,7},{6,4},{7,5},{8,10},{9,11},{10,... | collective-permute-start | bytes 2211848 | tf_op jit(solution)/shard_map/ppermute | solution.py:482
  41.4 35.5 %collective-permute-start.6 = (bf16[96,3072]{1,0:T(8,128)(2,1)S(1)}, bf16[96,3072]{1,0:T(8,128)(2,1)S(1)}, u32[]{:S(2)}, u32[]{:S(2)}) collective-permute-start(bf16[96,3072]{1,0:T(8,128)(2,1)S(1)} %get-tuple-element.120), channel_id=1, source_target_pairs={{0,2},{1,3},{2,0},{3,1},{4,6},{5,7},{6,4},{7,5},{8,10},{9,11},{10,... | collective-permute-start | bytes 1769480 | tf_op jit(solution)/shard_map/ppermute | solution.py:482
  59.0 26.0 %collective-permute-start.13 = (bf16[96,3840]{1,0:T(8,128)(2,1)S(1)}, bf16[96,3840]{1,0:T(8,128)(2,1)}, u32[]{:S(2)}, u32[]{:S(2)}) collective-permute-start(bf16[96,3840]{1,0:T(8,128)(2,1)S(1)} %collective-permute-done.7.refs_6_), channel_id=1, source_target_pairs={{0,4},{4,0},{8,12},{12,8},{16,20},{20,16},{24,28},{28,24},{1,5},{5... | collective-permute-start | bytes 2211848 | tf_op jit(solution)/shard_map/ppermute | solution.py:482
  69.3 31.4 %collective-permute-start.14 = (bf16[96,3840]{1,0:T(8,128)(2,1)S(1)}, bf16[96,3840]{1,0:T(8,128)(2,1)}, u32[]{:S(2)}, u32[]{:S(2)}) collective-permute-start(bf16[96,3840]{1,0:T(8,128)(2,1)S(1)} %collective-permute-done.7.refs_6_), channel_id=1, source_target_pairs={{0,1},{1,0},{2,3},{3,2},{4,5},{5,4},{6,7},{7,6},{8,9},{9,8},{10,11... | collective-permute-start | bytes 2211848 | tf_op jit(solution)/shard_map/ppermute | solution.py:482
  76.9 17.7 %collective-permute-start.8 = (bf16[96,3072]{1,0:T(8,128)(2,1)S(1)}, bf16[96,3072]{1,0:T(8,128)(2,1)}, u32[]{:S(2)}, u32[]{:S(2)}) collective-permute-start(bf16[96,3072]{1,0:T(8,128)(2,1)S(1)} %collective-permute-done.6.refs_15_), channel_id=1, source_target_pairs={{0,4},{4,0},{8,12},{12,8},{16,20},{20,16},{24,28},{28,24},{1,5},{5... | collective-permute-start | bytes 1769480 | tf_op jit(solution)/shard_map/ppermute | solution.py:482
  85.0 15.7 %collective-permute-start.15 = (bf16[96,3840]{1,0:T(8,128)(2,1)}, bf16[96,3840]{1,0:T(8,128)(2,1)}, u32[]{:S(2)}, u32[]{:S(2)}) collective-permute-start(bf16[96,3840]{1,0:T(8,128)(2,1)} %collective-permute-done.13.refs_7_), channel_id=1, source_target_pairs={{0,1},{1,0},{2,3},{3,2},{4,5},{5,4},{6,7},{7,6},{8,9},{9,8},{10,11... | collective-permute-start | bytes 2211848 | tf_op jit(solution)/shard_map/ppermute | solution.py:482
  86.0 6.8 %collective-permute-start.11 = (bf16[192,512]{1,0:T(8,128)(2,1)S(1)}, bf16[192,512]{1,0:T(8,128)(2,1)S(1)}, u32[]{:S(2)}, u32[]{:S(2)}) collective-permute-start(bf16[192,512]{1,0:T(8,128)(2,1)S(1)} %pad_maximum_fusion.7), channel_id=1, source_target_pairs={{0,3},{1,2},{2,1},{3,0},{4,7},{5,6},{6,5},{7,4},{8,11},{9,10},{10,... | collective-permute-start | bytes 589832 | tf_op jit(solution)/shard_map/ppermute | solution.py:482
  92.8 26.7 %copy-start.19 = (bf16[192,512]{1,0:T(8,128)(2,1)}, bf16[192,512]{1,0:T(8,128)(2,1)S(1)}, u32[]{:S(2)}) copy-start(bf16[192,512]{1,0:T(8,128)(2,1)S(1)} %collective-permute-done.11.refs_3_.refs_12_) | copy-start | bytes 589828
  92.8 7.4 %collective-permute-start.10 = (bf16[192,512]{1,0:T(8,128)(2,1)}, bf16[192,512]{1,0:T(8,128)(2,1)}, u32[]{:S(2)}, u32[]{:S(2)}) collective-permute-start(bf16[192,512]{1,0:T(8,128)(2,1)} %pad_maximum_fusion.6), channel_id=1, source_target_pairs={{0,2},{1,3},{2,0},{3,1},{4,6},{5,7},{6,4},{7,5},{8,10},{9,11},{10,... | collective-permute-start | bytes 589832 | tf_op jit(solution)/shard_map/ppermute | solution.py:482
  94.6 5.6 %collective-permute-start.9 = (bf16[192,512]{1,0:T(8,128)(2,1)}, bf16[192,512]{1,0:T(8,128)(2,1)}, u32[]{:S(2)}, u32[]{:S(2)}) collective-permute-start(bf16[192,512]{1,0:T(8,128)(2,1)} %pad_maximum_fusion.5), channel_id=1, source_target_pairs={{0,1},{1,0},{2,3},{3,2},{4,5},{5,4},{6,7},{7,6},{8,9},{9,8},{10,11... | collective-permute-start | bytes 589832 | tf_op jit(solution)/shard_map/ppermute | solution.py:482
  100.2 19.3 %collective-permute-start.16 = (bf16[96,3072]{1,0:T(8,128)(2,1)}, bf16[96,3072]{1,0:T(8,128)(2,1)S(1)}, u32[]{:S(2)}, u32[]{:S(2)}) collective-permute-start(bf16[96,3072]{1,0:T(8,128)(2,1)} %copy-done.11), channel_id=1, source_target_pairs={{0,1},{1,0},{2,3},{3,2},{4,5},{5,4},{6,7},{7,6},{8,9},{9,8},{10,11... | collective-permute-start | bytes 1769480 | tf_op jit(solution)/shard_map/ppermute | solution.py:482
  100.2 19.3 %collective-permute-start.17 = (bf16[96,3072]{1,0:T(8,128)(2,1)}, bf16[96,3072]{1,0:T(8,128)(2,1)S(1)}, u32[]{:S(2)}, u32[]{:S(2)}) collective-permute-start(bf16[96,3072]{1,0:T(8,128)(2,1)} %collective-permute-done.8.refs_16_), channel_id=1, source_target_pairs={{0,1},{1,0},{2,3},{3,2},{4,5},{5,4},{6,7},{7,6},{8,9},{9,8},{10,11... | collective-permute-start | bytes 1769480 | tf_op jit(solution)/shard_map/ppermute | solution.py:482
  100.7 18.8 %copy-start.12 = (bf16[96,3072]{1,0:T(8,128)(2,1)S(1)}, bf16[96,3072]{1,0:T(8,128)(2,1)}, u32[]{:S(2)}) copy-start(bf16[96,3072]{1,0:T(8,128)(2,1)} %copy-done.11) | copy-start | bytes 1769476
  119.5 27.8 %collective-permute-start.18 = (bf16[2,192,3072]{2,1,0:T(8,128)(2,1)}, bf16[2,192,3072]{2,1,0:T(8,128)(2,1)}, u32[]{:S(2)}, u32[]{:S(2)}) collective-permute-start(bf16[2,192,3072]{2,1,0:T(8,128)(2,1)} %get-tuple-element.145), channel_id=1, source_target_pairs={{0,1},{1,0},{2,3},{3,2},{4,5},{5,4},{6,7},{7,6},{8,9},{9,8},{10,11... | collective-permute-start | bytes 7077896 | tf_op jit(solution)/shard_map/ppermute | solution.py:482
  120.5 24.3 %copy-start.3 = (bf16[512,768]{1,0:T(8,128)(2,1)S(1)}, bf16[512,768]{1,0:T(8,128)(2,1)}, u32[]{:S(2)}) copy-start(bf16[512,768]{1,0:T(8,128)(2,1)} %refs_0_.3) | copy-start | bytes 2359300
  143.6 8.9 %collective-permute-start.23 = (bf16[2,192,3840]{2,1,0:T(8,128)(2,1)}, bf16[2,192,3840]{2,1,0:T(8,128)(2,1)}, u32[]{:S(2)}, u32[]{:S(2)}) collective-permute-start(bf16[2,192,3840]{2,1,0:T(8,128)(2,1)} %get-tuple-element.153), channel_id=1, source_target_pairs={{0,1},{1,0},{2,3},{3,2},{4,5},{5,4},{6,7},{7,6},{8,9},{9,8},{10,11... | collective-permute-start | bytes 8847368 | tf_op jit(solution)/shard_map/ppermute | solution.py:482
  145.3 11.1 %collective-permute-start.20 = (bf16[192,512]{1,0:T(8,128)(2,1)S(1)}, bf16[192,512]{1,0:T(8,128)(2,1)S(1)}, u32[]{:S(2)}, u32[]{:S(2)}) collective-permute-start(bf16[192,512]{1,0:T(8,128)(2,1)S(1)} %copy-done.18), channel_id=1, source_target_pairs={{0,1},{1,0},{2,3},{3,2},{4,5},{5,4},{6,7},{7,6},{8,9},{9,8},{10,11... | collective-permute-start | bytes 589832 | tf_op jit(solution)/shard_map/ppermute | solution.py:482
  145.5 10.9 %collective-permute-start.21 = (bf16[192,512]{1,0:T(8,128)(2,1)S(1)}, bf16[192,512]{1,0:T(8,128)(2,1)S(1)}, u32[]{:S(2)}, u32[]{:S(2)}) collective-permute-start(bf16[192,512]{1,0:T(8,128)(2,1)S(1)} %copy-done.16), channel_id=1, source_target_pairs={{0,2},{1,3},{2,0},{3,1},{4,6},{5,7},{6,4},{7,5},{8,10},{9,11},{10,... | collective-permute-start | bytes 589832 | tf_op jit(solution)/shard_map/ppermute | solution.py:482
  147.2 9.4 %collective-permute-start.22 = (bf16[192,512]{1,0:T(8,128)(2,1)S(1)}, bf16[192,512]{1,0:T(8,128)(2,1)S(1)}, u32[]{:S(2)}, u32[]{:S(2)}) collective-permute-start(bf16[192,512]{1,0:T(8,128)(2,1)S(1)} %get-tuple-element.151), channel_id=1, source_target_pairs={{0,3},{1,2},{2,1},{3,0},{4,7},{5,6},{6,5},{7,4},{8,11},{9,10},{10,... | collective-permute-start | bytes 589832 | tf_op jit(solution)/shard_map/ppermute | solution.py:482
  150.7 31.7 %collective-permute-start.19 = (bf16[192,3072]{1,0:T(8,128)(2,1)S(1)}, bf16[192,3072]{1,0:T(8,128)(2,1)}, u32[]{:S(2)}, u32[]{:S(2)}) collective-permute-start(bf16[192,3072]{1,0:T(8,128)(2,1)S(1)} %get-tuple-element.219), channel_id=1, source_target_pairs={{0,2},{1,3},{2,0},{3,1},{4,6},{5,7},{6,4},{7,5},{8,10},{9,11},{10,... | collective-permute-start | bytes 3538952 | tf_op jit(solution)/shard_map/ppermute | solution.py:482
  156.7 47.6 %collective-permute-start.25 = (bf16[2,96,3840]{2,1,0:T(8,128)(2,1)}, bf16[2,96,3840]{2,1,0:T(8,128)(2,1)S(1)}, u32[]{:S(2)}, u32[]{:S(2)}) collective-permute-start(bf16[2,96,3840]{2,1,0:T(8,128)(2,1)} %get-tuple-element.164), channel_id=1, source_target_pairs={{0,4},{4,0},{8,12},{12,8},{16,20},{20,16},{24,28},{28,24},{1,5},{5... | collective-permute-start | bytes 4423688 | tf_op jit(solution)/shard_map/ppermute | solution.py:482
  158.3 9.9 %copy-start.8 = (f32[1,2048,1]{2,1,0:T(8,128)S(1)}, f32[1,2048,1]{2,1,0:T(8,128)}, u32[]{:S(2)}) copy-start(f32[1,2048,1]{2,1,0:T(8,128)} %copy-done.7) | copy-start | bytes 24580
  184.1 20.2 %collective-permute-start.24 = (bf16[96,3072]{1,0:T(8,128)(2,1)S(1)}, bf16[96,3072]{1,0:T(8,128)(2,1)S(1)}, u32[]{:S(2)}, u32[]{:S(2)}) collective-permute-start(bf16[96,3072]{1,0:T(8,128)(2,1)S(1)} %constant_dynamic-slice_fusion.12), channel_id=1, source_target_pairs={{0,4},{4,0},{8,12},{12,8},{16,20},{20,16},{24,28},{28,24},{1,5},{5... | collective-permute-start | bytes 1769480 | tf_op jit(solution)/shard_map/ppermute | solution.py:482
  195.1 9.7 %copy-start.23 = (bf16[3,64,2048]{2,1,0:T(8,128)(2,1)}, bf16[3,64,2048]{2,1,0:T(8,128)(2,1)S(1)}, u32[]{:S(2)}) copy-start(bf16[3,64,2048]{2,1,0:T(8,128)(2,1)S(1)} %attend_back.5.refs_7_) | copy-start | bytes 2359300
  204.8 20.6 %collective-permute-start.31 = (bf16[96,3840]{1,0:T(8,128)(2,1)S(1)}, bf16[96,3840]{1,0:T(8,128)(2,1)S(1)}, u32[]{:S(2)}, u32[]{:S(2)}) collective-permute-start(bf16[96,3840]{1,0:T(8,128)(2,1)S(1)} %get-tuple-element.220), channel_id=1, source_target_pairs={{0,2},{1,3},{2,0},{3,1},{4,6},{5,7},{6,4},{7,5},{8,10},{9,11},{10,... | collective-permute-start | bytes 2211848 | tf_op jit(solution)/shard_map/ppermute | solution.py:482
  206.6 16.0 %collective-permute-start.28 = (bf16[48,3072]{1,0:T(8,128)(2,1)S(1)}, bf16[48,3072]{1,0:T(8,128)(2,1)S(1)}, u32[]{:S(2)}, u32[]{:S(2)}) collective-permute-start(bf16[48,3072]{1,0:T(8,128)(2,1)S(1)} %get-tuple-element.224), channel_id=1, source_target_pairs={{0,8},{4,12},{8,0},{12,4},{16,24},{20,28},{24,16},{28,20},{1,9},{5... | collective-permute-start | bytes 884744 | tf_op jit(solution)/shard_map/ppermute | solution.py:482
  221.0 12.5 %collective-permute-start.30 = (bf16[4,96,588]{2,1,0:T(8,128)(2,1)S(1)}, bf16[4,96,588]{2,1,0:T(8,128)(2,1)S(1)}, u32[]{:S(2)}, u32[]{:S(2)}) collective-permute-start(bf16[4,96,588]{2,1,0:T(8,128)(2,1)S(1)} %get-tuple-element.178), channel_id=1, source_target_pairs={{0,4},{4,0},{8,12},{12,8},{16,20},{20,16},{24,28},{28,24},{1,5},{5... | collective-permute-start | bytes 1354760 | tf_op jit(solution)/shard_map/ppermute | solution.py:482
  222.6 74.6 %collective-permute-start.26 = (bf16[2,512,768]{2,1,0:T(8,128)(2,1)}, bf16[2,512,768]{2,1,0:T(8,128)(2,1)}, u32[]{:S(2)}, u32[]{:S(2)}) collective-permute-start(bf16[2,512,768]{2,1,0:T(8,128)(2,1)} %get-tuple-element.175), channel_id=1, source_target_pairs={{0,1},{1,0},{2,3},{3,2},{4,5},{5,4},{6,7},{7,6},{8,9},{9,8},{10,11... | collective-permute-start | bytes 4718600 | tf_op jit(solution)/shard_map/ppermute | solution.py:482
  222.7 13.1 %collective-permute-start.29 = (bf16[24,3072]{1,0:T(8,128)(2,1)S(1)}, bf16[24,3072]{1,0:T(8,128)(2,1)S(1)}, u32[]{:S(2)}, u32[]{:S(2)}) collective-permute-start(bf16[24,3072]{1,0:T(8,128)(2,1)S(1)} %constant_dynamic-slice_fusion.9), channel_id=1, source_target_pairs={{0,16},{4,20},{8,24},{12,28},{16,0},{20,4},{24,8},{28,12},{1,17},{... | collective-permute-start | bytes 442376 | tf_op jit(solution)/shard_map/ppermute | solution.py:482
  233.6 11.5 %collective-permute-start.32 = (bf16[48,3840]{1,0:T(8,128)(2,1)S(1)}, bf16[48,3840]{1,0:T(8,128)(2,1)S(1)}, u32[]{:S(2)}, u32[]{:S(2)}) collective-permute-start(bf16[48,3840]{1,0:T(8,128)(2,1)S(1)} %constant_dynamic-slice_fusion.8), channel_id=1, source_target_pairs={{0,8},{4,12},{8,0},{12,4},{16,24},{20,28},{24,16},{28,20},{1,9},{5... | collective-permute-start | bytes 1105928 | tf_op jit(solution)/shard_map/ppermute | solution.py:482
  234.1 15.2 %collective-permute-start.34 = (bf16[4,48,588]{2,1,0:T(8,128)(2,1)S(1)}, bf16[4,48,588]{2,1,0:T(8,128)(2,1)}, u32[]{:S(2)}, u32[]{:S(2)}) collective-permute-start(bf16[4,48,588]{2,1,0:T(8,128)(2,1)S(1)} %constant_dynamic-slice_fusion.6), channel_id=1, source_target_pairs={{0,8},{4,12},{8,0},{12,4},{16,24},{20,28},{24,16},{28,20},{1,9},{5... | collective-permute-start | bytes 677384 | tf_op jit(solution)/shard_map/ppermute | solution.py:482
  250.4 13.3 %collective-permute-start.35 = (bf16[4,24,588]{2,1,0:T(8,128)(2,1)S(1)}, bf16[4,24,588]{2,1,0:T(8,128)(2,1)S(1)}, u32[]{:S(2)}, u32[]{:S(2)}) collective-permute-start(bf16[4,24,588]{2,1,0:T(8,128)(2,1)S(1)} %constant_dynamic-slice_fusion.5), channel_id=1, source_target_pairs={{0,16},{4,20},{8,24},{12,28},{16,0},{20,4},{24,8},{28,12},{1,17},{... | collective-permute-start | bytes 338696 | tf_op jit(solution)/shard_map/ppermute | solution.py:482
  253.2 17.3 %collective-permute-start.33 = (bf16[24,3840]{1,0:T(8,128)(2,1)S(1)}, bf16[24,3840]{1,0:T(8,128)(2,1)}, u32[]{:S(2)}, u32[]{:S(2)}) collective-permute-start(bf16[24,3840]{1,0:T(8,128)(2,1)S(1)} %constant_dynamic-slice_fusion.7), channel_id=1, source_target_pairs={{0,16},{4,20},{8,24},{12,28},{16,0},{20,4},{24,8},{28,12},{1,17},{... | collective-permute-start | bytes 552968 | tf_op jit(solution)/shard_map/ppermute | solution.py:482
  264.0 2.6 collective-permute-start.36
  264.1 4.2 %collective-permute-start.37 = (bf16[24,624]{1,0:T(8,128)(2,1)S(1)}, bf16[24,624]{1,0:T(8,128)(2,1)S(1)}, u32[]{:S(2)}, u32[]{:S(2)}) collective-permute-start(bf16[24,624]{1,0:T(8,128)(2,1)S(1)} %get-tuple-element.241), channel_id=1, source_target_pairs={{0,2},{1,3},{2,0},{3,1},{4,6},{5,7},{6,4},{7,5},{8,10},{9,11},{10,... | collective-permute-start | bytes 89864 | tf_op jit(solution)/shard_map/ppermute | solution.py:482
  264.6 3.6 collective-permute-start.38
  268.4 28.8 %copy-start.26 = (bf16[2,512,768]{2,1,0:T(8,128)(2,1)S(1)}, bf16[2,512,768]{2,1,0:T(8,128)(2,1)}, u32[]{:S(2)}) copy-start(bf16[2,512,768]{2,1,0:T(8,128)(2,1)} %get-tuple-element.174) | copy-start | bytes 4718596
  269.2 18.6 %collective-permute-start.41 = (bf16[1,24,2316]{2,1,0:T(8,128)(2,1)S(1)}, bf16[1,24,2316]{2,1,0:T(8,128)(2,1)S(1)}, u32[]{:S(2)}, u32[]{:S(2)}) collective-permute-start(bf16[1,24,2316]{2,1,0:T(8,128)(2,1)S(1)} %maximum_bitcast_fusion), channel_id=1, source_target_pairs={{0,16},{4,20},{8,24},{12,28},{16,0},{20,4},{24,8},{28,12},{1,17},{... | collective-permute-start | bytes 333512 | tf_op jit(solution)/shard_map/ppermute | solution.py:482
  272.1 21.5 %collective-permute-start.40 = (bf16[1,24,3840]{2,1,0:T(8,128)(2,1)S(1)}, bf16[1,24,3840]{2,1,0:T(8,128)(2,1)S(1)}, u32[]{:S(2)}, u32[]{:S(2)}) collective-permute-start(bf16[1,24,3840]{2,1,0:T(8,128)(2,1)S(1)} %bitcast.124), channel_id=1, source_target_pairs={{0,16},{4,20},{8,24},{12,28},{16,0},{20,4},{24,8},{28,12},{1,17},{... | collective-permute-start | bytes 552968 | tf_op jit(solution)/shard_map/ppermute | solution.py:482
  277.0 16.7 %collective-permute-start.39 = (f32[1,1]{1,0:T(1,128)}, f32[1,1]{1,0:T(1,128)}, u32[]{:S(2)}, u32[]{:S(2)}) collective-permute-start(f32[1,1]{1,0:T(1,128)} %bitcast.43), channel_id=1, source_target_pairs={{0,1},{1,0},{2,3},{3,2},{4,5},{5,4},{6,7},{7,6},{8,9},{9,8},{10,11... | collective-permute-start | bytes 20 | tf_op jit(solution)/shard_map/ppermute | solution.py:482
  287.8 11.3 %collective-permute-start.44 = (bf16[2,24,2316]{2,1,0:T(8,128)(2,1)S(1)}, bf16[2,24,2316]{2,1,0:T(8,128)(2,1)S(1)}, u32[]{:S(2)}, u32[]{:S(2)}) collective-permute-start(bf16[2,24,2316]{2,1,0:T(8,128)(2,1)S(1)} %pad_maximum_fusion.3), channel_id=1, source_target_pairs={{0,8},{4,12},{8,0},{12,4},{16,24},{20,28},{24,16},{28,20},{1,9},{5... | collective-permute-start | bytes 667016 | tf_op jit(solution)/shard_map/ppermute | solution.py:482
  293.7 12.8 %collective-permute-start.43 = (bf16[2,24,3840]{2,1,0:T(8,128)(2,1)S(1)}, bf16[2,24,3840]{2,1,0:T(8,128)(2,1)S(1)}, u32[]{:S(2)}, u32[]{:S(2)}) collective-permute-start(bf16[2,24,3840]{2,1,0:T(8,128)(2,1)S(1)} %pad_maximum_fusion.2), channel_id=1, source_target_pairs={{0,8},{4,12},{8,0},{12,4},{16,24},{20,28},{24,16},{28,20},{1,9},{5... | collective-permute-start | bytes 1105928 | tf_op jit(solution)/shard_map/ppermute | solution.py:482
  294.4 13.6 %collective-permute-start.42 = (f32[1,1]{1,0:T(1,128)}, f32[1,1]{1,0:T(1,128)}, u32[]{:S(2)}, u32[]{:S(2)}) collective-permute-start(f32[1,1]{1,0:T(1,128)} %add.277), channel_id=1, source_target_pairs={{0,2},{1,3},{2,0},{3,1},{4,6},{5,7},{6,4},{7,5},{8,10},{9,11},{10,... | collective-permute-start | bytes 20 | tf_op jit(solution)/shard_map/ppermute | solution.py:482
  298.5 39.1 %copy-start.27 = (bf16[2,512,768]{2,1,0:T(8,128)(2,1)S(1)}, bf16[2,512,768]{2,1,0:T(8,128)(2,1)}, u32[]{:S(2)}) copy-start(bf16[2,512,768]{2,1,0:T(8,128)(2,1)} %get-tuple-element.174) | copy-start | bytes 4718596
  298.5 39.1 %collective-permute-start.27 = (bf16[512,768]{1,0:T(8,128)(2,1)S(1)}, bf16[512,768]{1,0:T(8,128)(2,1)S(1)}, u32[]{:S(2)}, u32[]{:S(2)}) collective-permute-start(bf16[512,768]{1,0:T(8,128)(2,1)S(1)} %fusion.14), channel_id=1, source_target_pairs={{0,2},{1,3},{2,0},{3,1},{4,6},{5,7},{6,4},{7,5},{8,10},{9,11},{10,... | collective-permute-start | bytes 2359304 | tf_op jit(solution)/shard_map/ppermute | solution.py:482
  299.3 43.2 %collective-permute-start.48 = (bf16[4,24,2316]{2,1,0:T(8,128)(2,1)S(1)}, bf16[4,24,2316]{2,1,0:T(8,128)(2,1)S(1)}, u32[]{:S(2)}, u32[]{:S(2)}) collective-permute-start(bf16[4,24,2316]{2,1,0:T(8,128)(2,1)S(1)} %pad_maximum_fusion.1.refs_3_), channel_id=1, source_target_pairs={{0,4},{4,0},{8,12},{12,8},{16,20},{20,16},{24,28},{28,24},{1,5},{5... | collective-permute-start | bytes 1334024 | tf_op jit(solution)/shard_map/ppermute | solution.py:482
  306.5 36.0 %collective-permute-start.49 = (bf16[4,24,3840]{2,1,0:T(8,128)(2,1)S(1)}, bf16[4,24,3840]{2,1,0:T(8,128)(2,1)S(1)}, u32[]{:S(2)}, u32[]{:S(2)}) collective-permute-start(bf16[4,24,3840]{2,1,0:T(8,128)(2,1)S(1)} %pad_maximum_fusion.refs_1_), channel_id=1, source_target_pairs={{0,4},{4,0},{8,12},{12,8},{16,20},{20,16},{24,28},{28,24},{1,5},{5... | collective-permute-start | bytes 2211848 | tf_op jit(solution)/shard_map/ppermute | solution.py:482
  308.7 18.6 %collective-permute-start.45 = (f32[1,1]{1,0:T(1,128)}, f32[1,1]{1,0:T(1,128)}, u32[]{:S(2)}, u32[]{:S(2)}) collective-permute-start(f32[1,1]{1,0:T(1,128)} %add.278), channel_id=1, source_target_pairs={{0,4},{4,0},{8,12},{12,8},{16,20},{20,16},{24,28},{28,24},{1,5},{5... | collective-permute-start | bytes 20 | tf_op jit(solution)/shard_map/ppermute | solution.py:482
  327.9 3.7 collective-permute-start.46
  332.2 4.6 %collective-permute-start.47 = (f32[1,1]{1,0:T(1,128)}, f32[1,1]{1,0:T(1,128)}, u32[]{:S(2)}, u32[]{:S(2)}) collective-permute-start(f32[1,1]{1,0:T(1,128)} %add.280), channel_id=1, source_target_pairs={{0,16},{4,20},{8,24},{12,28},{16,0},{20,4},{24,8},{28,12},{1,17},{... | collective-permute-start | bytes 20 | tf_op jit(solution)/shard_map/ppermute | solution.py:482
  342.9 21.1 %copy-start.30 = (f32[192,12]{0,1:T(8,128)}, f32[192,12]{0,1:T(8,128)S(1)}, u32[]{:S(2)}) copy-start(f32[192,12]{0,1:T(8,128)S(1)} %copy.54) | copy-start | bytes 27652
  (23 other events, 68.0 us)
Sparse Core Ops, SparseCore 0:
  237.3 54.1 all-gather.2

commit v4 on v1

--- a/solution.py
+++ b/solution.py
@@ -404,12 +404,11 @@
 
 
 def adam_kernel(fc_rows, factor_ref, _, *refs):
-    grads, states, outs = refs[:4], refs[4:10], refs[10:]
+    grads, states, outs = refs[:3], refs[3:9], refs[9:]
     near = pl.program_id(0) < pl.num_programs(0) // 2
-    first, second = grads[0][0], grads[1][0]
     factor = factor_ref[0]
     width = outs[0].shape[-1] // fc_rows
-    qkv = jnp.where(near, grads[2][0], grads[3][0])[:, : 3 * width]
+    qkv = jnp.where(near, grads[1][0], grads[2][0])[:, : 3 * width]
 
     def update(gradient, at, base):
         results = adam_update(
@@ -419,8 +418,7 @@
         for n, result in enumerate(results):
             outs[base // 3 * 4 + n][at] = result
 
-    blocks = [first[:, n : n + width] for n in range(0, first.shape[1], width)]
-    blocks += [second[:, n : n + width] for n in range(0, second.shape[1], width)]
+    blocks = [grads[0][0, :, n : n + width] for n in range(0, grads[0].shape[2], width)]
     for f in range(fc_rows):
         span = slice(f * width, (f + 1) * width)
         for n in range(2):
@@ -733,10 +731,12 @@
             )(prefetch, qkv, qkv, qkv, seg_col, seg_row, lse[h], *do_own)
 
         dqkv = [attend_back(h, qkv) for h in range(own_heads)]
-        *dqkv, got_a = lax.optimization_barrier((*dqkv, got_a))
+        *dqkv, got_a, got_b = lax.optimization_barrier((*dqkv, got_a, got_b))
         own_a, other_a = halve(add_low(own_a, got_a), half, 0)
-        dqkv[0] = after(dqkv[0], other_a)
         got_a = swap(other_a, "dp", 1, replicas)
+        own_b, other_b = [add_low(own_b[n], got_b[n]) for n in range(2)]
+        got_b = swap(other_b, "shard", parts // 2, parts)
+        dqkv[0] = after(dqkv[0], other_a, own_b, other_b)
 
         q_cols = 3 * own_cols
         extra = vec_w.shape[0]
@@ -773,43 +773,42 @@
 
         share = rows // replicas
         z_bits = [bit for bit in (1 << n for n in range(1, 20)) if bit < replicas]
+        last_event = [own_q]
+
+        def seen(value):
+            return lax.optimization_barrier((value, last_event[0]))[0]
+
+        def event(value):
+            last_event[0] = value
+            return value
+
+        def next_half(keep, got, bit, dim):
+            array = event(add_low(keep, seen(got)))
+            return scatter_half(array, dim, bit, replica, replicas)
+
         got_q = swap(other_q, "dp", 1, replicas)
-        got_b = after(got_b, own_q)
-        sum_b = add_low(own_b, got_b)
-        got_b = swap(sum_b[1], "shard", parts // 2, parts)
         da1_got = swap(da1_send, "shard", 1, parts)
-
-        got_a = after(got_a, sum_b)
-        sum_a = add_low(own_a, got_a)
-        states = {"a": sum_a}
-        dims = {"a": 0, "q": 1, "b": 0}
-        pending = {"q": (own_q, got_q), "b": (sum_b[0], got_b)}
-        last = sum_a
-        pending["a"] = scatter_half(sum_a, 0, z_bits[0], replica, replicas)
-        for name in ("q", "b"):
-            keep, got = pending[name]
-            last = add_low(keep, after(got, last))
-            pending[name] = scatter_half(last, dims[name], z_bits[0], replica, replicas)
-        parts_done = {}
+        state_a = next_half(own_a, got_a, z_bits[0], 0)
+        state_b = next_half(own_b, got_b, z_bits[0], 0)
         for bit in z_bits[1:]:
-            for name in ("a", "q", "b"):
-                keep, got = pending[name]
-                last = add_low(keep, after(got, last))
-                pending[name] = scatter_half(last, dims[name], bit, replica, replicas)
-        for name in ("a", "q", "b"):
-            keep, got = pending[name]
-            last = add_low(keep, after(got, last))
-            parts_done[name] = last
-        part_a, part_q, part_b = (parts_done[name] for name in ("a", "q", "b"))
-        all_a = lax.all_gather(part_a, "dp", axis=0)
-        all_b = lax.all_gather(part_b, "dp", axis=0)
+            state_a = next_half(*state_a, bit, 0)
+        state_q = next_half(own_q, got_q, z_bits[0], 1)
+        for bit in z_bits[1:]:
+            state_b = next_half(*state_b, bit, 0)
+        part_a = event(add_low(state_a[0], seen(state_a[1])))
+        for bit in z_bits[1:]:
+            state_q = next_half(*state_q, bit, 1)
+        part_b = event(add_low(state_b[0], seen(state_b[1])))
+        part_ab = event(jnp.concatenate([part_a, part_b], axis=1))
+        all_ab = lax.all_gather(part_ab, "dp", axis=0)
+        part_q = event(add_low(state_q[0], seen(state_q[1])))
 
         def as_pair(value):
             high = lax.reduce_precision(value, 8, 7)
             return jnp.stack([high, value - high]).astype(LOW)
 
         main = part_q[:, :, :q_cols]
-        squares = sum(jnp.sum(jnp.square(p.astype(HIGH))) for p in (part_a, part_b, main))
+        squares = sum(jnp.sum(jnp.square(p.astype(HIGH))) for p in (part_ab, main))
         vec_parts = part_q[:, :, q_cols:].transpose(1, 0, 2).reshape(1, share, parts * extra)
         shared = jnp.concatenate(
             [vec_parts, jnp.broadcast_to(as_pair(squares), (1, share, 2))], axis=2
@@ -876,7 +875,7 @@
             grid_spec=pltpu.PrefetchScalarGridSpec(
                 num_scalar_prefetch=2,
                 grid=(replicas,),
-                in_specs=[gathered_spec(all_a), gathered_spec(all_b)]
+                in_specs=[gathered_spec(all_ab)]
                 + [
                     pl.BlockSpec(q_block, lambda i, *_: (jnp.minimum(i, near_count - 1), 0, 0)),
                     pl.BlockSpec(q_block, lambda i, *_: (jnp.maximum(i - near_count, 0), 0, 0)),
@@ -893,8 +892,7 @@
         )(
             factor.reshape(1),
             turn.reshape(1).astype(jnp.int32),
-            all_a,
-            all_b,
+            all_ab,
             near_q,
             far_q,
             *[array.reshape(attn_shape) for array in (attn_w, attn_m, attn_v)],

time: 366 us -> 345 us (0.943)
  waiting for transfers between devices: 123 us -> 97.2 us
  other arithmetic: 23.7 us -> 29 us
    all_gather x2 -> x1, waiting for transfers between devices: 35.9 us -> 5.79 us  [on_device(): all_ab = lax.all_gather(part_ab, 'dp', axis=0)]
    unnamed x95 -> x87, local copies, waits for them, and re-layouts: 20.9 us -> 15.5 us
    ppermute x42, waiting for transfers between devices: 87.5 us -> 91.4 us  [swap(): return lax.ppermute(array, axis, [(i, i ^ bit) for i in range(count)])]
    convert_element_type x12 -> x14, other arithmetic: 9.86 us -> 11.9 us  [add_low(): return (a.astype(HIGH) + b.astype(HIGH)).astype(LOW)]
  transfers between devices with their start and end apart: 44 -> 43, of which waited for: 21 -> 25; matrix products, arithmetic and copies ran while one was open for 8% -> 11% of each run, Pallas kernels for 21% -> 22%
where the time goes in v4:
time: 345 us; the launch traced here: 340 us
  Pallas kernels  128 us (37%)
  waiting for transfers between devices  97.2 us (28%)
  starting transfers between devices  37 us (11%)
  other arithmetic  29 us (8%)
  local copies, waits for them, and re-layouts  25.4 us (7%)
  between operations  23.3 us (7%)
    ppermute x42, waiting for transfers between devices, swap(): return lax.ppermute(array, axis, [(i, i ^ bit) for i in range(count)])  91.4 us
    ppermute x42, starting transfers between devices, swap(): return lax.ppermute(array, axis, [(i, i ^ bit) for i in range(count)])  37 us
    pallas_call x1, Pallas kernels, on_device(): pl.pallas_call(functools.partial(mlp_kernel, parts, first_blocks), grid_s...  32.9 us
    pallas_call x3, Pallas kernels, attend_back(): pl.pallas_call(functools.partial(attend_back_kernel, scale), grid_spec=pl...  27.4 us
    pallas_call x3, Pallas kernels, attend(): pl.pallas_call(functools.partial(attend_kernel, scale), grid_spec=pltpu.P...  22.8 us
    pallas_call x1, Pallas kernels, on_device(): pl.pallas_call(functools.partial(adam_kernel, fc_rows), grid_spec=pltpu.P...  19.3 us
    unnamed x87, local copies, waits for them, and re-layouts  15.5 us
    pallas_call x1, Pallas kernels, on_device(): pl.pallas_call(functools.partial(projection_back_kernel, own_heads, parts...  12.7 us
  transfers between devices with their start and end apart: 43, of which 25 were waited for; matrix products, arithmetic and copies ran while one was open for 11% of the time, Pallas kernels for 22%

profile of v4, /device:TPU:0, one launch (start us, length us, event | category | flops | bytes accessed | tf_op | source)
XLA Modules:
  0.0 340.2 jit_solution(13031027412116918564)
XLA Ops:
  7.2 3.0 collective-permute-start.1
  10.3 1.7 copy-done
  12.6 1.5 cut.1
  15.4 1.3 collective-permute-start.5
  18.2 1.3 copy.49
  19.7 1.1 copy.59
  20.8 4.4 %widen.1 = (bf16[192,6912]{1,0:T(8,128)(2,1)}, bf16[96,3840]{1,0:T(8,128)(2,1)S(1)}, bf16[96,3072]{1,0:T(8,128)(2,1)S(1)}) custom-call(s32[1]{0:T(128)} %bitcast.1.half, f32[192,3072]{1,0:T(8,128)S(1)} %copy-done.1, f32[2,192,3072]{2,1,0:T(8,128)} %mlp_ref.1), custom_call_target="tpu_custom_call" | custom-call | bytes 12000000 | tf_op jit(solution)/shard_map/widen/pallas_call | solution.py:533
  25.1 3.8 %collective-permute-done.1.refs_2_ = bf16[512,768]{1,0:T(8,128)(2,1)} collective-permute-done((bf16[512,768]{1,0:T(8,128)(2,1)}, bf16[512,768]{1,0:T(8,128)(2,1)}, u32[]{:S(2)}, u32[]{:S(2)}) %collective-permute-start.1) | collective-permute-done | bytes 786464 | tf_op jit(solution)/shard_map/ppermute | solution.py:431
  29.2 5.5 %collective-permute-done.4.refs_6_ = bf16[208,576]{1,0:T(8,128)(2,1)} collective-permute-done((bf16[208,576]{1,0:T(8,128)(2,1)}, bf16[208,576]{1,0:T(8,128)(2,1)}, u32[]{:S(2)}, u32[]{:S(2)}) %collective-permute-start.4) | collective-permute-done | bytes 239648 | tf_op jit(solution)/shard_map/ppermute | solution.py:431
  34.6 4.1 %collective-permute-done.5.refs_7_ = bf16[208,576]{1,0:T(8,128)(2,1)} collective-permute-done((bf16[208,576]{1,0:T(8,128)(2,1)}, bf16[208,576]{1,0:T(8,128)(2,1)}, u32[]{:S(2)}, u32[]{:S(2)}) %collective-permute-start.5) | collective-permute-done | bytes 239648 | tf_op jit(solution)/shard_map/ppermute | solution.py:431
  38.8 1.4 collective-permute-start.6
  41.0 7.2 %project.1 = (bf16[2048,768]{1,0:T(8,128)(2,1)}, bf16[576,2048]{1,0:T(8,128)(2,1)}, bf16[576,768]{1,0:T(8,128)(2,1)}, f32[16,768]{1,0:T(8,128)S(1)}) custom-call(s32[1]{0:T(128)} %bitcast.place, bf16[512,768]{1,0:T(8,128)(2,1)S(1)} %copy-done.2, bf16[512,768]{1,0:T(8,128)(2,1)} %collective-permute-done.refs_1_, ...), custom_call_target="tpu_custom_call" | custom-call | flops 5435817984 | bytes 12000000 | tf_op jit(solution)/shard_map/project/pallas_call | solution.py:569
  48.2 7.5 %attend.3 = (bf16[4,64,512]{2,1,0:T(8,128)(2,1)S(1)}, f32[1,2048,1]{2,1,0:T(8,128)S(1)}) custom-call(s32[1]{0:T(128)} %bitcast.place, bf16[576,2048]{1,0:T(8,128)(2,1)} %get-tuple-element.95.qt_ref.kt_ref.vt_ref, bf16[576,2048]{1,0:T(8,128)(2,1)} %get-tuple-element.95.qt_ref.kt_ref.vt_ref, bf16[576,2048]{1,0:T(8,128)(2,1)} %get-tuple-element.95.qt_ref.kt_ref.vt_ref, ...), custom_call_target="tpu_custom_call" | custom-call | flops 2147483648 | bytes 4000000 | tf_op jit(solution)/shard_map/attend/pallas_call | solution.py:611
  55.8 1.0 copy-done.7
  58.2 1.6 collective-permute-start.11
  59.8 7.5 %attend.5 = (bf16[4,64,512]{2,1,0:T(8,128)(2,1)S(1)}, f32[1,2048,1]{2,1,0:T(8,128)S(1)}) custom-call(s32[1]{0:T(128)} %bitcast.place, bf16[576,2048]{1,0:T(8,128)(2,1)} %get-tuple-element.95.qt_ref.kt_ref.vt_ref, bf16[576,2048]{1,0:T(8,128)(2,1)} %get-tuple-element.95.qt_ref.kt_ref.vt_ref, bf16[576,2048]{1,0:T(8,128)(2,1)} %get-tuple-element.95.qt_ref.kt_ref.vt_ref, ...), custom_call_target="tpu_custom_call" | custom-call | flops 2147483648 | bytes 4000000 | tf_op jit(solution)/shard_map/attend/pallas_call | solution.py:611
  67.4 1.0 copy-done.9
  68.3 7.8 %attend.4 = (bf16[4,64,512]{2,1,0:T(8,128)(2,1)S(1)}, f32[1,2048,1]{2,1,0:T(8,128)S(1)}) custom-call(s32[1]{0:T(128)} %bitcast.place, bf16[576,2048]{1,0:T(8,128)(2,1)} %get-tuple-element.95.qt_ref.kt_ref.vt_ref, bf16[576,2048]{1,0:T(8,128)(2,1)} %get-tuple-element.95.qt_ref.kt_ref.vt_ref, bf16[576,2048]{1,0:T(8,128)(2,1)} %get-tuple-element.95.qt_ref.kt_ref.vt_ref, ...), custom_call_target="tpu_custom_call" | custom-call | flops 2147483648 | bytes 4000000 | tf_op jit(solution)/shard_map/attend/pallas_call | solution.py:611
  78.9 5.7 %collective-permute-done.9.refs_3_ = bf16[192,512]{1,0:T(8,128)(2,1)S(1)} collective-permute-done((bf16[192,512]{1,0:T(8,128)(2,1)S(1)}, bf16[192,512]{1,0:T(8,128)(2,1)S(1)}, u32[]{:S(2)}, u32[]{:S(2)}) %collective-permute-start.9) | collective-permute-done | bytes 196640 | tf_op jit(solution)/shard_map/ppermute | solution.py:431
  85.4 3.3 collective-permute-done.8.refs_2_
  92.8 1.1 collective-permute-done.16.refs_12_
  94.7 0.9 copy-done.19
  97.5 32.9 %mlp.1 = (bf16[512,768]{1,0:T(8,128)(2,1)}, bf16[2,192,3072]{2,1,0:T(8,128)(2,1)}, bf16[2,192,3072]{2,1,0:T(8,128)(2,1)}, bf16[2,192,3840]{2,1,0:T(8,128)(2,1)},...) custom-call(s32[1]{0:T(128)} %bitcast.place, ...), custom_call_target="tpu_custom_call" | custom-call | flops 16307453952 | bytes 30000000 | tf_op jit(solution)/shard_map/mlp/pallas_call | solution.py:661
  133.7 1.3 convert_reduce_fusion
  135.3 1.2 collective-permute-start.19
  136.9 1.1 collective-permute-done.21
  138.0 4.3 %fusion.13 = (bf16[192,3072]{1,0:T(8,128)(2,1)}, bf16[192,3072]{1,0:T(8,128)(2,1)S(1)}) fusion(bf16[2,192,3072]{2,1,0:T(8,128)(2,1)} %collective-permute-done.21, bf16[2,192,3072]{2,1,0:T(8,128)(2,1)} %get-tuple-element.110), kind=kLoop, calls=%fused_computation.24 | loop fusion | flops 4718592 | bytes 7077888 | tf_op jit(solution)/shard_map/convert_element_type | solution.py:463
  142.5 2.6 add_convert_fusion
  146.1 1.3 collective-permute-start.24
  147.5 1.1 collective-permute-start.23
  148.6 9.0 %attend_back.5.refs_7_ = bf16[3,64,2048]{2,1,0:T(8,128)(2,1)S(1)} custom-call(s32[1]{0:T(128)} %bitcast.place, bf16[576,2048]{1,0:T(8,128)(2,1)} %get-tuple-element.95.qt_ref.kt_ref.vt_ref, bf16[576,2048]{1,0:T(8,128)(2,1)} %get-tuple-element.95.qt_ref.kt_ref.vt_ref, bf16[576,2048]{1,0:T(8,128)(2,1)} %get-tuple-element.95.qt_ref.kt_ref.vt_ref, ...), custom_call_target="tpu_custom_call" | custom-call | flops 5368709120 | bytes 4000000 | tf_op jit(solution)/shard_map/attend_back/pallas_call | solution.py:709
  158.5 9.2 %attend_back.4.refs_6_ = bf16[3,64,2048]{2,1,0:T(8,128)(2,1)S(1)} custom-call(s32[1]{0:T(128)} %bitcast.place, bf16[576,2048]{1,0:T(8,128)(2,1)} %get-tuple-element.95.qt_ref.kt_ref.vt_ref, bf16[576,2048]{1,0:T(8,128)(2,1)} %get-tuple-element.95.qt_ref.kt_ref.vt_ref, bf16[576,2048]{1,0:T(8,128)(2,1)} %get-tuple-element.95.qt_ref.kt_ref.vt_ref, ...), custom_call_target="tpu_custom_call" | custom-call | flops 5368709120 | bytes 4000000 | tf_op jit(solution)/shard_map/attend_back/pallas_call | solution.py:709
  168.6 9.2 %attend_back.3.refs_5_ = bf16[3,64,2048]{2,1,0:T(8,128)(2,1)S(1)} custom-call(s32[1]{0:T(128)} %bitcast.place, bf16[576,2048]{1,0:T(8,128)(2,1)} %get-tuple-element.95.qt_ref.kt_ref.vt_ref, bf16[576,2048]{1,0:T(8,128)(2,1)} %get-tuple-element.95.qt_ref.kt_ref.vt_ref, bf16[576,2048]{1,0:T(8,128)(2,1)} %get-tuple-element.95.qt_ref.kt_ref.vt_ref, ...), custom_call_target="tpu_custom_call" | custom-call | flops 5368709120 | bytes 4000000 | tf_op jit(solution)/shard_map/attend_back/pallas_call | solution.py:709
  177.8 3.0 collective-permute-done.24
  181.3 1.5 collective-permute-start.28
  183.1 1.2 collective-permute-start.30
  184.3 12.7 %projection_back.1 = (bf16[2,512,768]{2,1,0:T(8,128)(2,1)}, bf16[2,512,768]{2,1,0:T(8,128)(2,1)}, bf16[4,96,588]{2,1,0:T(8,128)(2,1)S(1)}, bf16[4,96,588]{2,1,0:T(8,128)(2,1)S(1)}) custom-call(s32[1]{0:T(128)} %bitcast.place, s32[1]{0:T(128)} %bitcast.1.half, bf16[512,768]{1,0:T(8,128)(2,1)S(1)} %copy-done.3, bf16[512,768]{1,0:T(8,128)(2,1)} %collective-permute-done.refs_1_, ...), custom_call_target="tpu_custom_call" | custom-call | flops 7247757312 | bytes 16000000 | tf_op jit(solution)/shard_map/projection_back/pallas_call | solution.py:744
  197.9 1.6 collective-permute-start.29
  199.5 1.6 collective-permute-done.30
  201.3 1.6 collective-permute-start.33
  203.0 4.9 %collective-permute-done.29 = bf16[48,3072]{1,0:T(8,128)(2,1)S(1)} collective-permute-done((bf16[48,3072]{1,0:T(8,128)(2,1)S(1)}, bf16[48,3072]{1,0:T(8,128)(2,1)S(1)}, u32[]{:S(2)}, u32[]{:S(2)}) %collective-permute-start.29) | collective-permute-done | bytes 294944 | tf_op jit(solution)/shard_map/ppermute | solution.py:431
  208.0 1.6 collective-permute-done.27
  209.6 2.7 collective-permute-start.32
  212.4 1.6 collective-permute-start.31
  214.0 6.8 %collective-permute-done.33 = bf16[48,3840]{1,0:T(8,128)(2,1)S(1)} collective-permute-done((bf16[48,3840]{1,0:T(8,128)(2,1)S(1)}, bf16[48,3840]{1,0:T(8,128)(2,1)S(1)}, u32[]{:S(2)}, u32[]{:S(2)}) %collective-permute-start.33) | collective-permute-done | bytes 368672 | tf_op jit(solution)/shard_map/ppermute | solution.py:431
  221.0 1.9 collective-permute-start.35
  222.9 1.2 collective-permute-done.31
  224.9 2.6 collective-permute-start.34
  227.5 6.1 %collective-permute-done.35 = bf16[24,3840]{1,0:T(8,128)(2,1)S(1)} collective-permute-done((bf16[24,3840]{1,0:T(8,128)(2,1)S(1)}, bf16[24,3840]{1,0:T(8,128)(2,1)S(1)}, u32[]{:S(2)}, u32[]{:S(2)}) %collective-permute-start.35) | collective-permute-done | bytes 184352 | tf_op jit(solution)/shard_map/ppermute | solution.py:431
  235.2 1.0 add_convert_fusion.15
  240.4 1.0 collective-permute-start.37
  243.3 1.1 collective-permute-done.37
  251.3 1.0 concatenate.45
  252.4 1.0 fusion.10
  253.4 14.0 %collective-permute-done.39 = bf16[1,24,2318]{2,1,0:T(8,128)(2,1)S(1)} collective-permute-done((bf16[1,24,2318]{2,1,0:T(8,128)(2,1)S(1)}, bf16[1,24,2318]{2,1,0:T(8,128)(2,1)S(1)}, u32[]{:S(2)}, u32[]{:S(2)}) %collective-permute-start.39) | collective-permute-done | bytes 111296 | tf_op jit(solution)/shard_map/ppermute | solution.py:431
  267.5 7.7 %collective-permute-done.40 = bf16[2,24,2318]{2,1,0:T(8,128)(2,1)S(1)} collective-permute-done((bf16[2,24,2318]{2,1,0:T(8,128)(2,1)S(1)}, bf16[2,24,2318]{2,1,0:T(8,128)(2,1)S(1)}, u32[]{:S(2)}, u32[]{:S(2)}) %collective-permute-start.40) | collective-permute-done | bytes 222560 | tf_op jit(solution)/shard_map/ppermute | solution.py:431
  276.1 1.3 collective-permute-start.41
  278.1 2.5 fusion.14
  280.6 1.6 collective-permute-start.26
  282.9 15.2 %collective-permute-done.41.refs_2_ = bf16[4,24,2318]{2,1,0:T(8,128)(2,1)} collective-permute-done((bf16[4,24,2318]{2,1,0:T(8,128)(2,1)}, bf16[4,24,2318]{2,1,0:T(8,128)(2,1)}, u32[]{:S(2)}, u32[]{:S(2)}) %collective-permute-start.41) | collective-permute-done | bytes 445088 | tf_op jit(solution)/shard_map/ppermute | solution.py:431
  301.2 2.5 fusion.35
  303.8 2.9 fusion.9
  306.7 5.8 %all-gather.3.cloned.1.call-done = bf16[192,6912]{1,0:T(8,128)(2,1)} async-done(((bf16[24,6912]{1,0:T(8,128)(2,1)}), bf16[192,6912]{1,0:T(8,128)(2,1)}) %all-gather.3.cloned.1.call-update) | async-done | bytes 2654224 | tf_op jit(solution)/shard_map/all_gather | solution.py:803
  312.5 19.3 %adam.1 = (f32[8,24,3072]{2,1,0:T(8,128)}, f32[8,24,3072]{2,1,0:T(8,128)}, f32[8,24,3072]{2,1,0:T(8,128)}, f32[8,24,3072]{2,1,0:T(8,128)}, f32[2,8,24,3072]{3,2,...) custom-call(f32[1]{0:T(128)} %bitcast.46.factor_ref, ...), custom_call_target="tpu_custom_call" | custom-call | flops 39813120 | bytes 54000000 | tf_op jit(solution)/shard_map/adam/pallas_call | solution.py:873
  (218 shorter events, 39.4 us)
Async XLA Ops:
  7.2 10.5 %copy-start.39 = (s32[1,4]{1,0:T(1,128)S(1)}, s32[1,4]{1,0:T(1,128)}, u32[]{:S(2)}) copy-start(s32[1,4]{1,0:T(1,128)} %param.16) | copy-start | bytes 52
  7.2 10.8 %copy-start.41 = (s32[1,2]{1,0:T(1,128)S(1)}, s32[1,2]{1,0:T(1,128)}, u32[]{:S(2)}) copy-start(s32[1,2]{1,0:T(1,128)} %param.15) | copy-start | bytes 28
  7.2 305.3 %all-gather.3.cloned.1.call-start = ((), (), s32[]{:S(2)}) async-start(), calls=%async_computation | async-start | bytes 2985984 | tf_op jit(solution)/shard_map/all_gather | solution.py:803
  7.2 21.7 %collective-permute-start.1 = (bf16[512,768]{1,0:T(8,128)(2,1)}, bf16[512,768]{1,0:T(8,128)(2,1)}, u32[]{:S(2)}, u32[]{:S(2)}) collective-permute-start(bf16[512,768]{1,0:T(8,128)(2,1)} %refs_0_.3), channel_id=1, source_target_pairs={{0,2},{1,3},{2,0},{3,1},{4,6},{5,7},{6,4},{7,5},{8,10},{9,11},{10,... | collective-permute-start | bytes 2359304 | tf_op jit(solution)/shard_map/ppermute | solution.py:431
  10.3 28.5 %collective-permute-start = (bf16[512,768]{1,0:T(8,128)(2,1)}, bf16[512,768]{1,0:T(8,128)(2,1)}, u32[]{:S(2)}, u32[]{:S(2)}) collective-permute-start(bf16[512,768]{1,0:T(8,128)(2,1)} %refs_0_.3), channel_id=1, source_target_pairs={{0,1},{1,0},{2,3},{3,2},{4,5},{5,4},{6,7},{7,6},{8,9},{9,8},{10,11... | collective-permute-start | bytes 2359304 | tf_op jit(solution)/shard_map/ppermute | solution.py:431
  12.6 4.1 %copy-start.6 = (f32[12,192]{1,0:T(8,128)S(1)}, f32[12,192]{1,0:T(8,128)}, u32[]{:S(2)}) copy-start(f32[12,192]{1,0:T(8,128)} %vec_ref.1) | copy-start | bytes 27652
  12.6 8.1 %copy-start.1 = (f32[192,3072]{1,0:T(8,128)S(1)}, f32[192,3072]{1,0:T(8,128)}, u32[]{:S(2)}) copy-start(f32[192,3072]{1,0:T(8,128)} %out_ref.1) | copy-start | bytes 7077892
  14.9 14.3 %collective-permute-start.3 = (bf16[208,576]{1,0:T(8,128)(2,1)}, bf16[208,576]{1,0:T(8,128)(2,1)}, u32[]{:S(2)}, u32[]{:S(2)}) collective-permute-start(bf16[208,576]{1,0:T(8,128)(2,1)} %get-tuple-element.85), channel_id=1, source_target_pairs={{0,1},{1,0},{2,3},{3,2},{4,5},{5,4},{6,7},{7,6},{8,9},{9,8},{10,11... | collective-permute-start | bytes 718856 | tf_op jit(solution)/shard_map/ppermute | solution.py:431
  15.4 19.3 %collective-permute-start.4 = (bf16[208,576]{1,0:T(8,128)(2,1)}, bf16[208,576]{1,0:T(8,128)(2,1)}, u32[]{:S(2)}, u32[]{:S(2)}) collective-permute-start(bf16[208,576]{1,0:T(8,128)(2,1)} %get-tuple-element.86), channel_id=1, source_target_pairs={{0,2},{1,3},{2,0},{3,1},{4,6},{5,7},{6,4},{7,5},{8,10},{9,11},{10,... | collective-permute-start | bytes 718856 | tf_op jit(solution)/shard_map/ppermute | solution.py:431
  15.4 23.3 %collective-permute-start.5 = (bf16[208,576]{1,0:T(8,128)(2,1)}, bf16[208,576]{1,0:T(8,128)(2,1)}, u32[]{:S(2)}, u32[]{:S(2)}) collective-permute-start(bf16[208,576]{1,0:T(8,128)(2,1)} %get-tuple-element.87), channel_id=1, source_target_pairs={{0,3},{1,2},{2,1},{3,0},{4,7},{5,6},{6,5},{7,4},{8,11},{9,10},{10,... | collective-permute-start | bytes 718856 | tf_op jit(solution)/shard_map/ppermute | solution.py:431
  20.8 8.2 %copy-start.29 = (s32[2048,1]{1,0:T(8,128)S(1)}, s32[2048,1]{1,0:T(8,128)}, u32[]{:S(2)}) copy-start(s32[2048,1]{1,0:T(8,128)} %copy.49) | copy-start | bytes 24580
  20.8 8.2 %copy-start.33 = (pred[1,2048]{0,1:T(8,128)(4,1)S(1)}, pred[1,2048]{0,1:T(8,128)(4,1)}, u32[]{:S(2)}) copy-start(pred[1,2048]{0,1:T(8,128)(4,1)} %copy.59) | copy-start | bytes 6148
  25.1 15.9 %copy-start.2 = (bf16[512,768]{1,0:T(8,128)(2,1)S(1)}, bf16[512,768]{1,0:T(8,128)(2,1)}, u32[]{:S(2)}) copy-start(bf16[512,768]{1,0:T(8,128)(2,1)} %refs_0_.3) | copy-start | bytes 2359300
  25.1 15.9 %copy-start.4 = (f32[576,1]{1,0:T(8,128)S(1)}, f32[576,1]{1,0:T(8,128)}, u32[]{:S(2)}) copy-start(f32[576,1]{1,0:T(8,128)} %broadcast_in_dim.54.refs_8_) | copy-start | bytes 6916
  25.1 15.9 %copy-start.14 = (bf16[208,576]{1,0:T(8,128)(2,1)S(1)}, bf16[208,576]{1,0:T(8,128)(2,1)}, u32[]{:S(2)}) copy-start(bf16[208,576]{1,0:T(8,128)(2,1)} %copy-done.13) | copy-start | bytes 718852
  28.9 9.8 %collective-permute-start.2 = (bf16[512,768]{1,0:T(8,128)(2,1)}, bf16[512,768]{1,0:T(8,128)(2,1)S(1)}, u32[]{:S(2)}, u32[]{:S(2)}) collective-permute-start(bf16[512,768]{1,0:T(8,128)(2,1)} %collective-permute-done.1.refs_2_), channel_id=1, source_target_pairs={{0,1},{1,0},{2,3},{3,2},{4,5},{5,4},{6,7},{7,6},{8,9},{9,8},{10,11... | collective-permute-start | bytes 2359304 | tf_op jit(solution)/shard_map/ppermute | solution.py:431
  38.8 19.4 %collective-permute-start.6 = (bf16[96,3840]{1,0:T(8,128)(2,1)S(1)}, bf16[96,3840]{1,0:T(8,128)(2,1)}, u32[]{:S(2)}, u32[]{:S(2)}) collective-permute-start(bf16[96,3840]{1,0:T(8,128)(2,1)S(1)} %get-tuple-element.94), channel_id=1, source_target_pairs={{0,2},{1,3},{2,0},{3,1},{4,6},{5,7},{6,4},{7,5},{8,10},{9,11},{10,... | collective-permute-start | bytes 2211848 | tf_op jit(solution)/shard_map/ppermute | solution.py:431
  40.2 35.9 %collective-permute-start.14 = (bf16[96,3072]{1,0:T(8,128)(2,1)S(1)}, bf16[96,3072]{1,0:T(8,128)(2,1)}, u32[]{:S(2)}, u32[]{:S(2)}) collective-permute-start(bf16[96,3072]{1,0:T(8,128)(2,1)S(1)} %get-tuple-element.100), channel_id=1, source_target_pairs={{0,2},{1,3},{2,0},{3,1},{4,6},{5,7},{6,4},{7,5},{8,10},{9,11},{10,... | collective-permute-start | bytes 1769480 | tf_op jit(solution)/shard_map/ppermute | solution.py:431
  40.9 53.8 %collective-permute-start.10 = (bf16[192,6912]{1,0:T(8,128)(2,1)}, bf16[192,6912]{1,0:T(8,128)(2,1)}, u32[]{:S(2)}, u32[]{:S(2)}) collective-permute-start(bf16[192,6912]{1,0:T(8,128)(2,1)} %get-tuple-element.98.refs_4_), channel_id=1, source_target_pairs={{0,1},{1,0},{2,3},{3,2},{4,5},{5,4},{6,7},{7,6},{8,9},{9,8},{10,11... | collective-permute-start | bytes 7962632 | tf_op jit(solution)/shard_map/ppermute | solution.py:431
  58.2 31.4 %collective-permute-start.11 = (bf16[96,3840]{1,0:T(8,128)(2,1)}, bf16[96,3840]{1,0:T(8,128)(2,1)}, u32[]{:S(2)}, u32[]{:S(2)}) collective-permute-start(bf16[96,3840]{1,0:T(8,128)(2,1)} %collective-permute-done.6.refs_6_), channel_id=1, source_target_pairs={{0,4},{4,0},{8,12},{12,8},{16,20},{20,16},{24,28},{28,24},{1,5},{5... | collective-permute-start | bytes 2211848 | tf_op jit(solution)/shard_map/ppermute | solution.py:431
  76.1 15.2 %collective-permute-start.15 = (bf16[96,3072]{1,0:T(8,128)(2,1)}, bf16[96,3072]{1,0:T(8,128)(2,1)}, u32[]{:S(2)}, u32[]{:S(2)}) collective-permute-start(bf16[96,3072]{1,0:T(8,128)(2,1)} %collective-permute-done.14.refs_10_), channel_id=1, source_target_pairs={{0,4},{4,0},{8,12},{12,8},{16,20},{20,16},{24,28},{28,24},{1,5},{5... | collective-permute-start | bytes 1769480 | tf_op jit(solution)/shard_map/ppermute | solution.py:431
  77.3 7.3 %collective-permute-start.9 = (bf16[192,512]{1,0:T(8,128)(2,1)S(1)}, bf16[192,512]{1,0:T(8,128)(2,1)S(1)}, u32[]{:S(2)}, u32[]{:S(2)}) collective-permute-start(bf16[192,512]{1,0:T(8,128)(2,1)S(1)} %pad_maximum_fusion.6), channel_id=1, source_target_pairs={{0,3},{1,2},{2,1},{3,0},{4,7},{5,6},{6,5},{7,4},{8,11},{9,10},{10,... | collective-permute-start | bytes 589832 | tf_op jit(solution)/shard_map/ppermute | solution.py:431
  78.0 10.7 %collective-permute-start.8 = (bf16[192,512]{1,0:T(8,128)(2,1)S(1)}, bf16[192,512]{1,0:T(8,128)(2,1)S(1)}, u32[]{:S(2)}, u32[]{:S(2)}) collective-permute-start(bf16[192,512]{1,0:T(8,128)(2,1)S(1)} %pad_maximum_fusion.5), channel_id=1, source_target_pairs={{0,2},{1,3},{2,0},{3,1},{4,6},{5,7},{6,4},{7,5},{8,10},{9,11},{10,... | collective-permute-start | bytes 589832 | tf_op jit(solution)/shard_map/ppermute | solution.py:431
  85.3 4.7 %collective-permute-start.7 = (bf16[192,512]{1,0:T(8,128)(2,1)S(1)}, bf16[192,512]{1,0:T(8,128)(2,1)S(1)}, u32[]{:S(2)}, u32[]{:S(2)}) collective-permute-start(bf16[192,512]{1,0:T(8,128)(2,1)S(1)} %pad_maximum_fusion.4), channel_id=1, source_target_pairs={{0,1},{1,0},{2,3},{3,2},{4,5},{5,4},{6,7},{7,6},{8,9},{9,8},{10,11... | collective-permute-start | bytes 589832 | tf_op jit(solution)/shard_map/ppermute | solution.py:431
  89.4 4.5 %collective-permute-start.12 = (bf16[96,3840]{1,0:T(8,128)(2,1)}, bf16[96,3840]{1,0:T(8,128)(2,1)}, u32[]{:S(2)}, u32[]{:S(2)}) collective-permute-start(bf16[96,3840]{1,0:T(8,128)(2,1)} %collective-permute-done.6.refs_6_), channel_id=1, source_target_pairs={{0,1},{1,0},{2,3},{3,2},{4,5},{5,4},{6,7},{7,6},{8,9},{9,8},{10,11... | collective-permute-start | bytes 2211848 | tf_op jit(solution)/shard_map/ppermute | solution.py:431
  89.7 5.1 %collective-permute-start.13 = (bf16[96,3840]{1,0:T(8,128)(2,1)}, bf16[96,3840]{1,0:T(8,128)(2,1)}, u32[]{:S(2)}, u32[]{:S(2)}) collective-permute-start(bf16[96,3840]{1,0:T(8,128)(2,1)} %collective-permute-done.11.refs_7_), channel_id=1, source_target_pairs={{0,1},{1,0},{2,3},{3,2},{4,5},{5,4},{6,7},{7,6},{8,9},{9,8},{10,11... | collective-permute-start | bytes 2211848 | tf_op jit(solution)/shard_map/ppermute | solution.py:431
  90.6 3.3 collective-permute-start.16
  91.3 3.4 %collective-permute-start.17 = (bf16[96,3072]{1,0:T(8,128)(2,1)}, bf16[96,3072]{1,0:T(8,128)(2,1)}, u32[]{:S(2)}, u32[]{:S(2)}) collective-permute-start(bf16[96,3072]{1,0:T(8,128)(2,1)} %collective-permute-done.15.refs_11_), channel_id=1, source_target_pairs={{0,1},{1,0},{2,3},{3,2},{4,5},{5,4},{6,7},{7,6},{8,9},{9,8},{10,11... | collective-permute-start | bytes 1769480 | tf_op jit(solution)/shard_map/ppermute | solution.py:431
  133.2 4.9 %collective-permute-start.21 = (bf16[2,192,3072]{2,1,0:T(8,128)(2,1)}, bf16[2,192,3072]{2,1,0:T(8,128)(2,1)}, u32[]{:S(2)}, u32[]{:S(2)}) collective-permute-start(bf16[2,192,3072]{2,1,0:T(8,128)(2,1)} %get-tuple-element.111), channel_id=1, source_target_pairs={{0,1},{1,0},{2,3},{3,2},{4,5},{5,4},{6,7},{7,6},{8,9},{9,8},{10,11... | collective-permute-start | bytes 7077896 | tf_op jit(solution)/shard_map/ppermute | solution.py:431
  133.4 9.1 %collective-permute-start.22 = (bf16[2,192,3840]{2,1,0:T(8,128)(2,1)}, bf16[2,192,3840]{2,1,0:T(8,128)(2,1)}, u32[]{:S(2)}, u32[]{:S(2)}) collective-permute-start(bf16[2,192,3840]{2,1,0:T(8,128)(2,1)} %get-tuple-element.113), channel_id=1, source_target_pairs={{0,1},{1,0},{2,3},{3,2},{4,5},{5,4},{6,7},{7,6},{8,9},{9,8},{10,11... | collective-permute-start | bytes 8847368 | tf_op jit(solution)/shard_map/ppermute | solution.py:431
  135.0 10.4 %collective-permute-start.18 = (bf16[192,512]{1,0:T(8,128)(2,1)}, bf16[192,512]{1,0:T(8,128)(2,1)S(1)}, u32[]{:S(2)}, u32[]{:S(2)}) collective-permute-start(bf16[192,512]{1,0:T(8,128)(2,1)} %copy-done.17), channel_id=1, source_target_pairs={{0,1},{1,0},{2,3},{3,2},{4,5},{5,4},{6,7},{7,6},{8,9},{9,8},{10,11... | collective-permute-start | bytes 589832 | tf_op jit(solution)/shard_map/ppermute | solution.py:431
  135.3 10.1 %collective-permute-start.19 = (bf16[192,512]{1,0:T(8,128)(2,1)}, bf16[192,512]{1,0:T(8,128)(2,1)S(1)}, u32[]{:S(2)}, u32[]{:S(2)}) collective-permute-start(bf16[192,512]{1,0:T(8,128)(2,1)} %copy-done.16), channel_id=1, source_target_pairs={{0,2},{1,3},{2,0},{3,1},{4,6},{5,7},{6,4},{7,5},{8,10},{9,11},{10,... | collective-permute-start | bytes 589832 | tf_op jit(solution)/shard_map/ppermute | solution.py:431
  136.5 9.6 %collective-permute-start.20 = (bf16[192,512]{1,0:T(8,128)(2,1)}, bf16[192,512]{1,0:T(8,128)(2,1)S(1)}, u32[]{:S(2)}, u32[]{:S(2)}) collective-permute-start(bf16[192,512]{1,0:T(8,128)(2,1)} %copy-done.15), channel_id=1, source_target_pairs={{0,3},{1,2},{2,1},{3,0},{4,7},{5,6},{6,5},{7,4},{8,11},{9,10},{10,... | collective-permute-start | bytes 589832 | tf_op jit(solution)/shard_map/ppermute | solution.py:431
  138.0 4.5 %copy-start.31 = (bf16[2,192,3840]{2,1,0:T(8,128)(2,1)S(1)}, bf16[2,192,3840]{2,1,0:T(8,128)(2,1)}, u32[]{:S(2)}) copy-start(bf16[2,192,3840]{2,1,0:T(8,128)(2,1)} %get-tuple-element.112) | copy-start | bytes 8847364
  145.1 3.4 %copy-start.10 = (f32[1,2048,1]{2,1,0:T(8,128)S(1)}, f32[1,2048,1]{2,1,0:T(8,128)}, u32[]{:S(2)}) copy-start(f32[1,2048,1]{2,1,0:T(8,128)} %copy-done.9) | copy-start | bytes 24580
  145.2 3.4 %copy-start.28 = (bf16[192,512]{1,0:T(8,128)(2,1)S(1)}, bf16[192,512]{1,0:T(8,128)(2,1)}, u32[]{:S(2)}) copy-start(bf16[192,512]{1,0:T(8,128)(2,1)} %copy-done.27) | copy-start | bytes 589828
  146.1 34.7 %collective-permute-start.24 = (bf16[2,96,3840]{2,1,0:T(8,128)(2,1)S(1)}, bf16[2,96,3840]{2,1,0:T(8,128)(2,1)S(1)}, u32[]{:S(2)}, u32[]{:S(2)}) collective-permute-start(bf16[2,96,3840]{2,1,0:T(8,128)(2,1)S(1)} %get-tuple-element.121), channel_id=1, source_target_pairs={{0,4},{4,0},{8,12},{12,8},{16,20},{20,16},{24,28},{28,24},{1,5},{5... | collective-permute-start | bytes 4423688 | tf_op jit(solution)/shard_map/ppermute | solution.py:431
  147.5 30.3 %collective-permute-start.23 = (bf16[192,3072]{1,0:T(8,128)(2,1)}, bf16[192,3072]{1,0:T(8,128)(2,1)S(1)}, u32[]{:S(2)}, u32[]{:S(2)}) collective-permute-start(bf16[192,3072]{1,0:T(8,128)(2,1)} %get-tuple-element.120), channel_id=1, source_target_pairs={{0,2},{1,3},{2,0},{3,1},{4,6},{5,7},{6,4},{7,5},{8,10},{9,11},{10,... | collective-permute-start | bytes 3538952 | tf_op jit(solution)/shard_map/ppermute | solution.py:431
  148.6 9.9 %copy-start.12 = (f32[1,2048,1]{2,1,0:T(8,128)S(1)}, f32[1,2048,1]{2,1,0:T(8,128)}, u32[]{:S(2)}) copy-start(f32[1,2048,1]{2,1,0:T(8,128)} %copy-done.11) | copy-start | bytes 24580
  158.5 10.1 %copy-start.8 = (f32[1,2048,1]{2,1,0:T(8,128)S(1)}, f32[1,2048,1]{2,1,0:T(8,128)}, u32[]{:S(2)}) copy-start(f32[1,2048,1]{2,1,0:T(8,128)} %copy-done.7) | copy-start | bytes 24580
  177.8 3.4 %copy-start.26 = (bf16[3,64,2048]{2,1,0:T(8,128)(2,1)}, bf16[3,64,2048]{2,1,0:T(8,128)(2,1)S(1)}, u32[]{:S(2)}) copy-start(bf16[3,64,2048]{2,1,0:T(8,128)(2,1)S(1)} %attend_back.3.refs_5_) | copy-start | bytes 2359300
  181.3 3.1 copy-start.3
  181.3 16.4 %collective-permute-start.28 = (bf16[96,3072]{1,0:T(8,128)(2,1)S(1)}, bf16[96,3072]{1,0:T(8,128)(2,1)S(1)}, u32[]{:S(2)}, u32[]{:S(2)}) collective-permute-start(bf16[96,3072]{1,0:T(8,128)(2,1)S(1)} %constant_dynamic-slice_fusion.11), channel_id=1, source_target_pairs={{0,4},{4,0},{8,12},{12,8},{16,20},{20,16},{24,28},{28,24},{1,5},{5... | collective-permute-start | bytes 1769480 | tf_op jit(solution)/shard_map/ppermute | solution.py:431
  183.1 18.0 %collective-permute-start.30 = (bf16[96,3840]{1,0:T(8,128)(2,1)S(1)}, bf16[96,3840]{1,0:T(8,128)(2,1)S(1)}, u32[]{:S(2)}, u32[]{:S(2)}) collective-permute-start(bf16[96,3840]{1,0:T(8,128)(2,1)S(1)} %get-tuple-element.162), channel_id=1, source_target_pairs={{0,2},{1,3},{2,0},{3,1},{4,6},{5,7},{6,4},{7,5},{8,10},{9,11},{10,... | collective-permute-start | bytes 2211848 | tf_op jit(solution)/shard_map/ppermute | solution.py:431
  197.1 12.5 %collective-permute-start.27 = (bf16[4,96,588]{2,1,0:T(8,128)(2,1)S(1)}, bf16[4,96,588]{2,1,0:T(8,128)(2,1)S(1)}, u32[]{:S(2)}, u32[]{:S(2)}) collective-permute-start(bf16[4,96,588]{2,1,0:T(8,128)(2,1)S(1)} %get-tuple-element.135), channel_id=1, source_target_pairs={{0,4},{4,0},{8,12},{12,8},{16,20},{20,16},{24,28},{28,24},{1,5},{5... | collective-permute-start | bytes 1354760 | tf_op jit(solution)/shard_map/ppermute | solution.py:431
  197.9 10.0 %collective-permute-start.29 = (bf16[48,3072]{1,0:T(8,128)(2,1)S(1)}, bf16[48,3072]{1,0:T(8,128)(2,1)S(1)}, u32[]{:S(2)}, u32[]{:S(2)}) collective-permute-start(bf16[48,3072]{1,0:T(8,128)(2,1)S(1)} %constant_dynamic-slice_fusion.10), channel_id=1, source_target_pairs={{0,8},{4,12},{8,0},{12,4},{16,24},{20,28},{24,16},{28,20},{1,9},{5... | collective-permute-start | bytes 884744 | tf_op jit(solution)/shard_map/ppermute | solution.py:431
  201.3 19.5 %collective-permute-start.33 = (bf16[48,3840]{1,0:T(8,128)(2,1)S(1)}, bf16[48,3840]{1,0:T(8,128)(2,1)S(1)}, u32[]{:S(2)}, u32[]{:S(2)}) collective-permute-start(bf16[48,3840]{1,0:T(8,128)(2,1)S(1)} %constant_dynamic-slice_fusion.7), channel_id=1, source_target_pairs={{0,8},{4,12},{8,0},{12,4},{16,24},{20,28},{24,16},{28,20},{1,9},{5... | collective-permute-start | bytes 1105928 | tf_op jit(solution)/shard_map/ppermute | solution.py:431
  209.6 13.2 %collective-permute-start.32 = (bf16[24,3072]{1,0:T(8,128)(2,1)S(1)}, bf16[24,3072]{1,0:T(8,128)(2,1)S(1)}, u32[]{:S(2)}, u32[]{:S(2)}) collective-permute-start(bf16[24,3072]{1,0:T(8,128)(2,1)S(1)} %constant_dynamic-slice_fusion.8), channel_id=1, source_target_pairs={{0,16},{4,20},{8,24},{12,28},{16,0},{20,4},{24,8},{28,12},{1,17},{... | collective-permute-start | bytes 442376 | tf_op jit(solution)/shard_map/ppermute | solution.py:431
  212.4 11.7 %collective-permute-start.31 = (bf16[4,48,588]{2,1,0:T(8,128)(2,1)S(1)}, bf16[4,48,588]{2,1,0:T(8,128)(2,1)S(1)}, u32[]{:S(2)}, u32[]{:S(2)}) collective-permute-start(bf16[4,48,588]{2,1,0:T(8,128)(2,1)S(1)} %constant_dynamic-slice_fusion.9), channel_id=1, source_target_pairs={{0,8},{4,12},{8,0},{12,4},{16,24},{20,28},{24,16},{28,20},{1,9},{5... | collective-permute-start | bytes 677384 | tf_op jit(solution)/shard_map/ppermute | solution.py:431
  221.0 12.7 %collective-permute-start.35 = (bf16[24,3840]{1,0:T(8,128)(2,1)S(1)}, bf16[24,3840]{1,0:T(8,128)(2,1)S(1)}, u32[]{:S(2)}, u32[]{:S(2)}) collective-permute-start(bf16[24,3840]{1,0:T(8,128)(2,1)S(1)} %constant_dynamic-slice_fusion.5), channel_id=1, source_target_pairs={{0,16},{4,20},{8,24},{12,28},{16,0},{20,4},{24,8},{28,12},{1,17},{... | collective-permute-start | bytes 552968 | tf_op jit(solution)/shard_map/ppermute | solution.py:431
  224.2 9.5 %copy-start.34 = (bf16[4,48,588]{2,1,0:T(8,128)(2,1)}, bf16[4,48,588]{2,1,0:T(8,128)(2,1)S(1)}, u32[]{:S(2)}) copy-start(bf16[4,48,588]{2,1,0:T(8,128)(2,1)S(1)} %add_convert_fusion.12) | copy-start | bytes 677380
  224.9 10.3 %collective-permute-start.34 = (bf16[4,24,588]{2,1,0:T(8,128)(2,1)}, bf16[4,24,588]{2,1,0:T(8,128)(2,1)}, u32[]{:S(2)}, u32[]{:S(2)}) collective-permute-start(bf16[4,24,588]{2,1,0:T(8,128)(2,1)} %constant_dynamic-slice_fusion.6), channel_id=1, source_target_pairs={{0,16},{4,20},{8,24},{12,28},{16,0},{20,4},{24,8},{28,12},{1,17},{... | collective-permute-start | bytes 338696 | tf_op jit(solution)/shard_map/ppermute | solution.py:431
  240.4 2.9 collective-permute-start.36
  240.4 4.0 %collective-permute-start.37 = (bf16[24,626]{1,0:T(8,128)(2,1)S(1)}, bf16[24,626]{1,0:T(8,128)(2,1)S(1)}, u32[]{:S(2)}, u32[]{:S(2)}) collective-permute-start(bf16[24,626]{1,0:T(8,128)(2,1)S(1)} %get-tuple-element.180), channel_id=1, source_target_pairs={{0,2},{1,3},{2,0},{3,1},{4,6},{5,7},{6,4},{7,5},{8,10},{9,11},{10,... | collective-permute-start | bytes 90152 | tf_op jit(solution)/shard_map/ppermute | solution.py:431
  241.5 3.3 collective-permute-start.38
  242.9 35.2 %collective-permute-start.25 = (bf16[2,512,768]{2,1,0:T(8,128)(2,1)}, bf16[2,512,768]{2,1,0:T(8,128)(2,1)}, u32[]{:S(2)}, u32[]{:S(2)}) collective-permute-start(bf16[2,512,768]{2,1,0:T(8,128)(2,1)} %get-tuple-element.133), channel_id=1, source_target_pairs={{0,1},{1,0},{2,3},{3,2},{4,5},{5,4},{6,7},{7,6},{8,9},{9,8},{10,11... | collective-permute-start | bytes 4718600 | tf_op jit(solution)/shard_map/ppermute | solution.py:431
  252.3 15.0 %collective-permute-start.39 = (bf16[1,24,2318]{2,1,0:T(8,128)(2,1)S(1)}, bf16[1,24,2318]{2,1,0:T(8,128)(2,1)S(1)}, u32[]{:S(2)}, u32[]{:S(2)}) collective-permute-start(bf16[1,24,2318]{2,1,0:T(8,128)(2,1)S(1)} %bitcast.124), channel_id=1, source_target_pairs={{0,16},{4,20},{8,24},{12,28},{16,0},{20,4},{24,8},{28,12},{1,17},{... | collective-permute-start | bytes 333800 | tf_op jit(solution)/shard_map/ppermute | solution.py:431
  267.4 7.8 %collective-permute-start.40 = (bf16[2,24,2318]{2,1,0:T(8,128)(2,1)S(1)}, bf16[2,24,2318]{2,1,0:T(8,128)(2,1)S(1)}, u32[]{:S(2)}, u32[]{:S(2)}) collective-permute-start(bf16[2,24,2318]{2,1,0:T(8,128)(2,1)S(1)} %pad_maximum_fusion.2), channel_id=1, source_target_pairs={{0,8},{4,12},{8,0},{12,4},{16,24},{20,28},{24,16},{28,20},{1,9},{5... | collective-permute-start | bytes 667592 | tf_op jit(solution)/shard_map/ppermute | solution.py:431
  276.1 22.0 %collective-permute-start.41 = (bf16[4,24,2318]{2,1,0:T(8,128)(2,1)}, bf16[4,24,2318]{2,1,0:T(8,128)(2,1)}, u32[]{:S(2)}, u32[]{:S(2)}) collective-permute-start(bf16[4,24,2318]{2,1,0:T(8,128)(2,1)} %pad_maximum_fusion.refs_1_), channel_id=1, source_target_pairs={{0,4},{4,0},{8,12},{12,8},{16,20},{20,16},{24,28},{28,24},{1,5},{5... | collective-permute-start | bytes 1335176 | tf_op jit(solution)/shard_map/ppermute | solution.py:431
  278.1 22.5 %copy-start.37 = (f32[12,192]{1,0:T(8,128)S(1)}, f32[12,192]{1,0:T(8,128)}, u32[]{:S(2)}) copy-start(f32[12,192]{1,0:T(8,128)} %param.24) | copy-start | bytes 27652
  278.1 22.5 %copy-start.38 = (f32[12,192]{1,0:T(8,128)S(1)}, f32[12,192]{1,0:T(8,128)}, u32[]{:S(2)}) copy-start(f32[12,192]{1,0:T(8,128)} %param.25) | copy-start | bytes 27652
  278.1 23.1 %copy-start.36 = (f32[512]{0:T(512)S(1)}, f32[512]{0:T(512)}, u32[]{:S(2)}) copy-start(f32[512]{0:T(512)} %broadcast_multiply_fusion.2) | copy-start | bytes 6148
  280.6 20.6 %collective-permute-start.26 = (bf16[512,768]{1,0:T(8,128)(2,1)}, bf16[512,768]{1,0:T(8,128)(2,1)}, u32[]{:S(2)}, u32[]{:S(2)}) collective-permute-start(bf16[512,768]{1,0:T(8,128)(2,1)} %fusion.14), channel_id=1, source_target_pairs={{0,2},{1,3},{2,0},{3,1},{4,6},{5,7},{6,4},{7,5},{8,10},{9,11},{10,... | collective-permute-start | bytes 2359304 | tf_op jit(solution)/shard_map/ppermute | solution.py:431
  300.6 3.2 copy-start.35
  (21 other events, 22.8 us)
Sparse Core Ops, SparseCore 0:
  243.4 69.0 all-gather.2

commit v5 on v4

--- a/solution.py
+++ b/solution.py
@@ -19,7 +19,6 @@
 CLIP_LIMIT = 1.0
 MASKED_SCORE = -1e30
 QUERY_BLOCK = 256
-VMEM_LIMIT = 50 * 1024 * 1024
 LOW = jnp.bfloat16
 HIGH = jnp.float32
 
@@ -478,8 +477,10 @@
     return keep, swap(send, "dp", bit, replicas)
 
 
-def params(*semantics):
-    return pltpu.CompilerParams(dimension_semantics=semantics, vmem_limit_bytes=VMEM_LIMIT)
+def params(mebibytes):
+    return pltpu.CompilerParams(
+        dimension_semantics=("arbitrary",), vmem_limit_bytes=mebibytes * 1024 * 1024
+    )
 
 
 def cost(flops, moved, special=0):
@@ -522,7 +523,7 @@
                 out_specs=[whole(rows + 16, 3 * own_cols)] * parts,
             ),
             out_shape=[jax.ShapeDtypeStruct((rows + 16, 3 * own_cols), LOW)] * parts,
-            compiler_params=params("arbitrary"),
+            compiler_params=params(12),
             cost_estimate=cost(0, 4e6),
             name="cut",
         )(prefetch, attn_w, vec_w)
@@ -550,7 +551,7 @@
                 jax.ShapeDtypeStruct((rows // 2, split), LOW),
                 jax.ShapeDtypeStruct((rows // 2, blocks * width - split), LOW),
             ],
-            compiler_params=params("arbitrary"),
+            compiler_params=params(28),
             cost_estimate=cost(0, 12e6),
             name="widen",
         )(side, attn_w, mlp_w)
@@ -594,7 +595,7 @@
                 jax.ShapeDtypeStruct((3 * own_cols, width), LOW),
                 jax.ShapeDtypeStruct((16, width), HIGH),
             ],
-            compiler_params=params("arbitrary"),
+            compiler_params=params(24),
             cost_estimate=cost(2 * total * width * 3 * own_cols * 3, 12e6),
             name="project",
         )(prefetch, *x_all, *w_local, bias_local)
@@ -621,7 +622,7 @@
                     jax.ShapeDtypeStruct((parts, head_size, slots), LOW),
                     jax.ShapeDtypeStruct((1, total, 1), HIGH),
                 ],
-                compiler_params=params("arbitrary"),
+                compiler_params=params(24),
                 cost_estimate=cost(2 * pair_flops, 4e6, total * total // 2),
                 name="attend",
             )(prefetch, qkv, qkv, qkv, seg_col, seg_row)
@@ -688,7 +689,7 @@
             + [jax.ShapeDtypeStruct((parts // 2, rows, c), LOW) for c in grad_columns for _ in range(2)]
             + [jax.ShapeDtypeStruct((slots, width), HIGH), jax.ShapeDtypeStruct((16, width), HIGH)]
             + [jax.ShapeDtypeStruct((own_cols, slots), LOW)] * parts,
-            compiler_params=params("arbitrary"),
+            compiler_params=params(50),
             cost_estimate=cost(2 * slots * width * (6 * hidden + 3 * width), 30e6, slots * hidden),
             name="mlp",
         )(prefetch, side, live_own, tokens, cotangent, vectors, *mixed_own, *wide)
@@ -723,7 +724,7 @@
                     ],
                 ),
                 out_shape=jax.ShapeDtypeStruct((3, head_size, total), LOW),
-                compiler_params=params("arbitrary"),
+                compiler_params=params(28),
                 cost_estimate=cost(
                     5 * pair_flops, 4e6, total * total // 2
                 ),
@@ -766,7 +767,7 @@
             ),
             out_shape=[jax.ShapeDtypeStruct((parts // 2, slots, width), LOW)] * 2
             + [jax.ShapeDtypeStruct((parts, half_rows, q_cols + extra), LOW)] * 2,
-            compiler_params=params("arbitrary"),
+            compiler_params=params(28),
             cost_estimate=cost(4 * total * width * 3 * own_cols * 2, 16e6),
             name="projection_back",
         )(prefetch, side, *x_all, a1, *dqkv, w_t, vectors, mid_grads)
@@ -886,7 +887,7 @@
             ),
             out_shape=[jax.ShapeDtypeStruct(attn_shape, HIGH)] * 4
             + [jax.ShapeDtypeStruct(mlp_shape, HIGH)] * 4,
-            compiler_params=params("arbitrary"),
+            compiler_params=params(20),
             cost_estimate=cost(30 * 9 * rows * width, 54e6),
             name="adam",
         )(

time: 345 us -> 345 us (level)
  Pallas kernels: 128 us -> 107 us
  local copies, waits for them, and re-layouts: 25.4 us -> 40.9 us
  waiting for transfers between devices: 97.2 us -> 104 us
    unnamed x87 -> x129, local copies, waits for them, and re-layouts: 15.5 us -> 34.7 us
    pallas_call x1, Pallas kernels: 19.3 us -> 10.7 us  [on_device(): pl.pallas_call(functools.partial(adam_kernel, fc_rows), grid_spec=pltpu.P...]
    ppermute x42, waiting for transfers between devices: 91.4 us -> 98.6 us  [swap(): return lax.ppermute(array, axis, [(i, i ^ bit) for i in range(count)])]
  transfers between devices with their start and end apart: 43 -> 43, of which waited for: 25 -> 28; matrix products, arithmetic and copies ran while one was open for 11% -> 9% of each run, Pallas kernels for 22% -> 19%
where the time goes in v5:
time: 345 us; the launch traced here: 340 us
  Pallas kernels  107 us (31%)
  waiting for transfers between devices  104 us (30%)
  local copies, waits for them, and re-layouts  40.9 us (12%)
  starting transfers between devices  37.7 us (11%)
  other arithmetic  26.5 us (8%)
  between operations  23.4 us (7%)
    ppermute x42, waiting for transfers between devices, swap(): return lax.ppermute(array, axis, [(i, i ^ bit) for i in range(count)])  98.6 us
    ppermute x42, starting transfers between devices, swap(): return lax.ppermute(array, axis, [(i, i ^ bit) for i in range(count)])  37.7 us
    unnamed x129, local copies, waits for them, and re-layouts  34.7 us
    pallas_call x1, Pallas kernels, on_device(): pl.pallas_call(functools.partial(mlp_kernel, parts, first_blocks), grid_s...  32.9 us
    pallas_call x3, Pallas kernels, attend_back(): pl.pallas_call(functools.partial(attend_back_kernel, scale), grid_spec=pl...  24.2 us
    pallas_call x3, Pallas kernels, attend(): pl.pallas_call(functools.partial(attend_kernel, scale), grid_spec=pltpu.P...  19.5 us
    pallas_call x1, Pallas kernels, on_device(): pl.pallas_call(functools.partial(adam_kernel, fc_rows), grid_spec=pltpu.P...  10.7 us
    pallas_call x1, Pallas kernels, on_device(): pl.pallas_call(functools.partial(projection_back_kernel, own_heads, parts...  10.1 us
  transfers between devices with their start and end apart: 43, of which 28 were waited for; matrix products, arithmetic and copies ran while one was open for 9% of the time, Pallas kernels for 19%

profile of v5, /device:TPU:0, one launch (start us, length us, event | category | flops | bytes accessed | tf_op | source)
XLA Modules:
  0.0 340.1 jit_solution(8792556771044910777)
XLA Ops:
  7.2 3.0 collective-permute-start.1
  10.3 1.7 copy-done
  12.6 1.5 cut.1
  15.4 1.3 collective-permute-start.5
  18.2 1.3 copy.49
  20.8 2.3 copy-done.3
  23.1 1.9 widen.1
  25.0 3.8 %collective-permute-done.1.refs_2_ = bf16[512,768]{1,0:T(8,128)(2,1)S(1)} collective-permute-done((bf16[512,768]{1,0:T(8,128)(2,1)}, bf16[512,768]{1,0:T(8,128)(2,1)S(1)}, u32[]{:S(2)}, u32[]{:S(2)}) %collective-permute-start.1) | collective-permute-done | bytes 786464 | tf_op jit(solution)/shard_map/ppermute | solution.py:430
  29.8 4.8 %collective-permute-done.4.refs_6_ = bf16[208,576]{1,0:T(8,128)(2,1)} collective-permute-done((bf16[208,576]{1,0:T(8,128)(2,1)}, bf16[208,576]{1,0:T(8,128)(2,1)}, u32[]{:S(2)}, u32[]{:S(2)}) %collective-permute-start.4) | collective-permute-done | bytes 239648 | tf_op jit(solution)/shard_map/ppermute | solution.py:430
  34.6 4.1 %collective-permute-done.5.refs_7_ = bf16[208,576]{1,0:T(8,128)(2,1)} collective-permute-done((bf16[208,576]{1,0:T(8,128)(2,1)}, bf16[208,576]{1,0:T(8,128)(2,1)}, u32[]{:S(2)}, u32[]{:S(2)}) %collective-permute-start.5) | collective-permute-done | bytes 239648 | tf_op jit(solution)/shard_map/ppermute | solution.py:430
  38.8 1.4 collective-permute-start.6
  43.1 6.5 %project.1 = (bf16[2048,768]{1,0:T(8,128)(2,1)S(1)}, bf16[576,2048]{1,0:T(8,128)(2,1)S(1)}, bf16[576,768]{1,0:T(8,128)(2,1)S(1)}, f32[16,768]{1,0:T(8,128)S(1)}) custom-call(s32[1]{0:T(128)} %bitcast.place, bf16[512,768]{1,0:T(8,128)(2,1)S(1)} %copy-done.5, bf16[512,768]{1,0:T(8,128)(2,1)} %collective-permute-done.refs_1_, bf16[512,768]{1,0:T(8,128)(2,1)S(1)} %copy-done.28, ...), custom_call_target="tpu_custom_call" | custom-call | flops 5435817984 | bytes 12000000 | tf_op jit(solution)/shard_map/project/pallas_call | solution.py:570
  49.6 1.7 copy-done.45
  51.2 6.4 %attend.3 = (bf16[4,64,512]{2,1,0:T(8,128)(2,1)S(1)}, f32[1,2048,1]{2,1,0:T(8,128)S(1)}) custom-call(s32[1]{0:T(128)} %bitcast.place, bf16[576,2048]{1,0:T(8,128)(2,1)S(1)} %get-tuple-element.95.qt_ref.kt_ref.vt_ref, bf16[576,2048]{1,0:T(8,128)(2,1)S(1)} %get-tuple-element.95.qt_ref.kt_ref.vt_ref, ...), custom_call_target="tpu_custom_call" | custom-call | flops 2147483648 | bytes 4000000 | tf_op jit(solution)/shard_map/attend/pallas_call | solution.py:612
  59.3 1.7 collective-permute-start.11
  61.0 6.4 %attend.5 = (bf16[4,64,512]{2,1,0:T(8,128)(2,1)S(1)}, f32[1,2048,1]{2,1,0:T(8,128)S(1)}) custom-call(s32[1]{0:T(128)} %bitcast.place, bf16[576,2048]{1,0:T(8,128)(2,1)S(1)} %get-tuple-element.95.qt_ref.kt_ref.vt_ref, bf16[576,2048]{1,0:T(8,128)(2,1)S(1)} %get-tuple-element.95.qt_ref.kt_ref.vt_ref, ...), custom_call_target="tpu_custom_call" | custom-call | flops 2147483648 | bytes 4000000 | tf_op jit(solution)/shard_map/attend/pallas_call | solution.py:612
  68.5 6.7 %attend.4 = (bf16[4,64,512]{2,1,0:T(8,128)(2,1)S(1)}, f32[1,2048,1]{2,1,0:T(8,128)S(1)}) custom-call(s32[1]{0:T(128)} %bitcast.place, bf16[576,2048]{1,0:T(8,128)(2,1)S(1)} %get-tuple-element.95.qt_ref.kt_ref.vt_ref, bf16[576,2048]{1,0:T(8,128)(2,1)S(1)} %get-tuple-element.95.qt_ref.kt_ref.vt_ref, ...), custom_call_target="tpu_custom_call" | custom-call | flops 2147483648 | bytes 4000000 | tf_op jit(solution)/shard_map/attend/pallas_call | solution.py:612
  78.1 5.2 %collective-permute-done.9.refs_3_ = bf16[192,512]{1,0:T(8,128)(2,1)S(1)} collective-permute-done((bf16[192,512]{1,0:T(8,128)(2,1)S(1)}, bf16[192,512]{1,0:T(8,128)(2,1)S(1)}, u32[]{:S(2)}, u32[]{:S(2)}) %collective-permute-start.9) | collective-permute-done | bytes 196640 | tf_op jit(solution)/shard_map/ppermute | solution.py:430
  84.6 3.1 collective-permute-done.8.refs_2_
  89.6 1.5 collective-permute-done.15.refs_11_
  96.5 32.9 %mlp.1 = (bf16[512,768]{1,0:T(8,128)(2,1)}, bf16[2,192,3072]{2,1,0:T(8,128)(2,1)}, bf16[2,192,3072]{2,1,0:T(8,128)(2,1)}, bf16[2,192,3840]{2,1,0:T(8,128)(2,1)},...) custom-call(s32[1]{0:T(128)} %bitcast.place, ...), custom_call_target="tpu_custom_call" | custom-call | flops 16307453952 | bytes 30000000 | tf_op jit(solution)/shard_map/mlp/pallas_call | solution.py:662
  132.6 1.3 convert_reduce_fusion
  134.1 1.5 collective-permute-start.19
  137.0 3.4 fusion.13
  141.5 2.6 add_convert_fusion
  145.2 1.7 collective-permute-start.24
  147.7 7.9 %attend_back.5.refs_7_ = bf16[3,64,2048]{2,1,0:T(8,128)(2,1)S(1)} custom-call(s32[1]{0:T(128)} %bitcast.place, bf16[576,2048]{1,0:T(8,128)(2,1)S(1)} %get-tuple-element.95.qt_ref.kt_ref.vt_ref, bf16[576,2048]{1,0:T(8,128)(2,1)S(1)} %get-tuple-element.95.qt_ref.kt_ref.vt_ref, bf16[576,2048]{1,0:T(8,128)(2,1)S(1)} %get-tuple-element.95.qt_ref.kt_ref.vt_ref, ...), custom_call_target="tpu_custom_call" | custom-call | flops 5368709120 | bytes 4000000 | tf_op jit(solution)/shard_map/attend_back/pallas_call | solution.py:710
  155.6 8.1 %attend_back.4.refs_6_ = bf16[3,64,2048]{2,1,0:T(8,128)(2,1)S(1)} custom-call(s32[1]{0:T(128)} %bitcast.place, bf16[576,2048]{1,0:T(8,128)(2,1)S(1)} %get-tuple-element.95.qt_ref.kt_ref.vt_ref, bf16[576,2048]{1,0:T(8,128)(2,1)S(1)} %get-tuple-element.95.qt_ref.kt_ref.vt_ref, bf16[576,2048]{1,0:T(8,128)(2,1)S(1)} %get-tuple-element.95.qt_ref.kt_ref.vt_ref, ...), custom_call_target="tpu_custom_call" | custom-call | flops 5368709120 | bytes 4000000 | tf_op jit(solution)/shard_map/attend_back/pallas_call | solution.py:710
  163.7 8.2 %attend_back.3.refs_5_ = bf16[3,64,2048]{2,1,0:T(8,128)(2,1)S(1)} custom-call(s32[1]{0:T(128)} %bitcast.place, bf16[576,2048]{1,0:T(8,128)(2,1)S(1)} %get-tuple-element.95.qt_ref.kt_ref.vt_ref, bf16[576,2048]{1,0:T(8,128)(2,1)S(1)} %get-tuple-element.95.qt_ref.kt_ref.vt_ref, bf16[576,2048]{1,0:T(8,128)(2,1)S(1)} %get-tuple-element.95.qt_ref.kt_ref.vt_ref, ...), custom_call_target="tpu_custom_call" | custom-call | flops 5368709120 | bytes 4000000 | tf_op jit(solution)/shard_map/attend_back/pallas_call | solution.py:710
  171.9 3.0 collective-permute-done.23
  174.8 4.9 %collective-permute-done.24 = bf16[2,96,3840]{2,1,0:T(8,128)(2,1)S(1)} collective-permute-done((bf16[2,96,3840]{2,1,0:T(8,128)(2,1)S(1)}, bf16[2,96,3840]{2,1,0:T(8,128)(2,1)S(1)}, u32[]{:S(2)}, u32[]{:S(2)}) %collective-permute-start.24) | collective-permute-done | bytes 1474592 | tf_op jit(solution)/shard_map/ppermute | solution.py:430
  180.2 1.8 collective-permute-start.28
  183.5 10.1 %projection_back.1 = (bf16[2,512,768]{2,1,0:T(8,128)(2,1)S(1)}, bf16[2,512,768]{2,1,0:T(8,128)(2,1)S(1)}, bf16[4,96,588]{2,1,0:T(8,128)(2,1)S(1)}, bf16[4,96,588]{2,1,0:T(8,128)(2,1)S(1)}) custom-call(s32[1]{0:T(128)} %bitcast.place, s32[1]{0:T(128)} %bitcast.1.half, bf16[512,768]{1,0:T(8,128)(2,1)S(1)} %copy-done.6, ...), custom_call_target="tpu_custom_call" | custom-call | flops 7247757312 | bytes 16000000 | tf_op jit(solution)/shard_map/projection_back/pallas_call | solution.py:745
  195.3 1.8 collective-permute-start.29
  197.1 3.0 collective-permute-done.30
  200.3 1.7 collective-permute-start.33
  202.1 2.6 collective-permute-done.29
  204.8 1.3 collective-permute-done.27
  206.1 2.6 collective-permute-start.32
  208.8 1.6 collective-permute-start.31
  210.5 5.3 %collective-permute-done.33 = bf16[48,3840]{1,0:T(8,128)(2,1)S(1)} collective-permute-done((bf16[48,3840]{1,0:T(8,128)(2,1)S(1)}, bf16[48,3840]{1,0:T(8,128)(2,1)S(1)}, u32[]{:S(2)}, u32[]{:S(2)}) %collective-permute-start.33) | collective-permute-done | bytes 368672 | tf_op jit(solution)/shard_map/ppermute | solution.py:430
  215.9 1.7 collective-permute-start.35
  217.7 4.6 %collective-permute-done.31 = bf16[4,48,588]{2,1,0:T(8,128)(2,1)S(1)} collective-permute-done((bf16[4,48,588]{2,1,0:T(8,128)(2,1)S(1)}, bf16[4,48,588]{2,1,0:T(8,128)(2,1)S(1)}, u32[]{:S(2)}, u32[]{:S(2)}) %collective-permute-start.31) | collective-permute-done | bytes 225824 | tf_op jit(solution)/shard_map/ppermute | solution.py:430
  222.4 1.7 collective-permute-start.34
  224.1 5.0 %collective-permute-done.35 = bf16[24,3840]{1,0:T(8,128)(2,1)S(1)} collective-permute-done((bf16[24,3840]{1,0:T(8,128)(2,1)S(1)}, bf16[24,3840]{1,0:T(8,128)(2,1)S(1)}, u32[]{:S(2)}, u32[]{:S(2)}) %collective-permute-start.35) | collective-permute-done | bytes 184352 | tf_op jit(solution)/shard_map/ppermute | solution.py:430
  235.6 1.9 collective-permute-start.37
  237.9 1.7 collective-permute-done.37
  239.6 1.2 collective-permute-done.38
  246.6 14.2 %collective-permute-done.39 = bf16[1,24,2318]{2,1,0:T(8,128)(2,1)S(1)} collective-permute-done((bf16[1,24,2318]{2,1,0:T(8,128)(2,1)S(1)}, bf16[1,24,2318]{2,1,0:T(8,128)(2,1)S(1)}, u32[]{:S(2)}, u32[]{:S(2)}) %collective-permute-start.39) | collective-permute-done | bytes 111296 | tf_op jit(solution)/shard_map/ppermute | solution.py:430
  261.5 8.6 %collective-permute-done.40 = bf16[2,24,2318]{2,1,0:T(8,128)(2,1)S(1)} collective-permute-done((bf16[2,24,2318]{2,1,0:T(8,128)(2,1)S(1)}, bf16[2,24,2318]{2,1,0:T(8,128)(2,1)S(1)}, u32[]{:S(2)}, u32[]{:S(2)}) %collective-permute-start.40) | collective-permute-done | bytes 222560 | tf_op jit(solution)/shard_map/ppermute | solution.py:430
  270.2 2.0 collective-permute-start.41
  274.0 2.2 fusion.14
  277.4 14.4 %collective-permute-done.41.refs_2_ = bf16[4,24,2318]{2,1,0:T(8,128)(2,1)S(1)} collective-permute-done((bf16[4,24,2318]{2,1,0:T(8,128)(2,1)S(1)}, bf16[4,24,2318]{2,1,0:T(8,128)(2,1)S(1)}, u32[]{:S(2)}, u32[]{:S(2)}) %collective-permute-start.41) | collective-permute-done | bytes 445088 | tf_op jit(solution)/shard_map/ppermute | solution.py:430
  293.6 1.4 multiply_subtract_fusion
  295.8 2.2 fusion.35
  298.0 3.2 fusion.9
  301.2 5.6 %all-gather.3.cloned.1.call-done = bf16[192,6912]{1,0:T(8,128)(2,1)} async-done(((bf16[24,6912]{1,0:T(8,128)(2,1)}), bf16[192,6912]{1,0:T(8,128)(2,1)}) %all-gather.3.cloned.1.call-update) | async-done | bytes 2654224 | tf_op jit(solution)/shard_map/all_gather | solution.py:804
  306.8 2.3 copy-done.4
  309.1 2.3 copy-done.7
  311.5 2.3 copy-done.8
  313.8 1.7 copy-done.10
  315.6 1.7 copy-done.11
  317.2 1.7 copy-done.12
  320.9 10.7 %adam.1 = (f32[8,24,3072]{2,1,0:T(8,128)}, f32[8,24,3072]{2,1,0:T(8,128)}, f32[8,24,3072]{2,1,0:T(8,128)}, f32[8,24,3072]{2,1,0:T(8,128)}, f32[2,8,24,3072]{3,2,...) custom-call(f32[1]{0:T(128)} %bitcast.46.factor_ref, ...), custom_call_target="tpu_custom_call" | custom-call | flops 39813120 | bytes 54000000 | tf_op jit(solution)/shard_map/adam/pallas_call | solution.py:874
  (260 shorter events, 48.5 us)
Async XLA Ops:
  7.2 10.5 %copy-start.61 = (s32[1,4]{1,0:T(1,128)S(1)}, s32[1,4]{1,0:T(1,128)}, u32[]{:S(2)}) copy-start(s32[1,4]{1,0:T(1,128)} %param.16) | copy-start | bytes 52
  7.2 10.8 %copy-start.62 = (s32[1,2]{1,0:T(1,128)S(1)}, s32[1,2]{1,0:T(1,128)}, u32[]{:S(2)}) copy-start(s32[1,2]{1,0:T(1,128)} %param.15) | copy-start | bytes 28
  7.2 299.6 %all-gather.3.cloned.1.call-start = ((), (), s32[]{:S(2)}) async-start(), calls=%async_computation | async-start | bytes 2985984 | tf_op jit(solution)/shard_map/all_gather | solution.py:804
  7.2 21.6 %collective-permute-start.1 = (bf16[512,768]{1,0:T(8,128)(2,1)}, bf16[512,768]{1,0:T(8,128)(2,1)S(1)}, u32[]{:S(2)}, u32[]{:S(2)}) collective-permute-start(bf16[512,768]{1,0:T(8,128)(2,1)} %refs_0_.3), channel_id=1, source_target_pairs={{0,2},{1,3},{2,0},{3,1},{4,6},{5,7},{6,4},{7,5},{8,10},{9,11},{10,... | collective-permute-start | bytes 2359304 | tf_op jit(solution)/shard_map/ppermute | solution.py:430
  10.2 28.5 %collective-permute-start = (bf16[512,768]{1,0:T(8,128)(2,1)}, bf16[512,768]{1,0:T(8,128)(2,1)}, u32[]{:S(2)}, u32[]{:S(2)}) collective-permute-start(bf16[512,768]{1,0:T(8,128)(2,1)} %refs_0_.3), channel_id=1, source_target_pairs={{0,1},{1,0},{2,3},{3,2},{4,5},{5,4},{6,7},{7,6},{8,9},{9,8},{10,11... | collective-permute-start | bytes 2359304 | tf_op jit(solution)/shard_map/ppermute | solution.py:430
  12.6 8.1 %copy-start.1 = (f32[192,3072]{1,0:T(8,128)S(1)}, f32[192,3072]{1,0:T(8,128)}, u32[]{:S(2)}) copy-start(f32[192,3072]{1,0:T(8,128)} %out_ref.1) | copy-start | bytes 7077892
  14.9 14.2 %collective-permute-start.3 = (bf16[208,576]{1,0:T(8,128)(2,1)}, bf16[208,576]{1,0:T(8,128)(2,1)S(1)}, u32[]{:S(2)}, u32[]{:S(2)}) collective-permute-start(bf16[208,576]{1,0:T(8,128)(2,1)} %get-tuple-element.85), channel_id=1, source_target_pairs={{0,1},{1,0},{2,3},{3,2},{4,5},{5,4},{6,7},{7,6},{8,9},{9,8},{10,11... | collective-permute-start | bytes 718856 | tf_op jit(solution)/shard_map/ppermute | solution.py:430
  15.4 19.3 %collective-permute-start.4 = (bf16[208,576]{1,0:T(8,128)(2,1)}, bf16[208,576]{1,0:T(8,128)(2,1)}, u32[]{:S(2)}, u32[]{:S(2)}) collective-permute-start(bf16[208,576]{1,0:T(8,128)(2,1)} %get-tuple-element.86), channel_id=1, source_target_pairs={{0,2},{1,3},{2,0},{3,1},{4,6},{5,7},{6,4},{7,5},{8,10},{9,11},{10,... | collective-permute-start | bytes 718856 | tf_op jit(solution)/shard_map/ppermute | solution.py:430
  15.4 23.3 %collective-permute-start.5 = (bf16[208,576]{1,0:T(8,128)(2,1)}, bf16[208,576]{1,0:T(8,128)(2,1)}, u32[]{:S(2)}, u32[]{:S(2)}) collective-permute-start(bf16[208,576]{1,0:T(8,128)(2,1)} %get-tuple-element.87), channel_id=1, source_target_pairs={{0,3},{1,2},{2,1},{3,0},{4,7},{5,6},{6,5},{7,4},{8,11},{9,10},{10,... | collective-permute-start | bytes 718856 | tf_op jit(solution)/shard_map/ppermute | solution.py:430
  23.1 5.8 %copy-start.51 = (s32[2048,1]{1,0:T(8,128)S(1)}, s32[2048,1]{1,0:T(8,128)}, u32[]{:S(2)}) copy-start(s32[2048,1]{1,0:T(8,128)} %copy.49) | copy-start | bytes 24580
  23.1 5.8 %copy-start.54 = (pred[1,2048]{0,1:T(8,128)(4,1)S(1)}, pred[1,2048]{0,1:T(8,128)(4,1)}, u32[]{:S(2)}) copy-start(pred[1,2048]{0,1:T(8,128)(4,1)} %copy.59) | copy-start | bytes 6148
  25.0 15.9 %copy-start.5 = (bf16[512,768]{1,0:T(8,128)(2,1)S(1)}, bf16[512,768]{1,0:T(8,128)(2,1)}, u32[]{:S(2)}) copy-start(bf16[512,768]{1,0:T(8,128)(2,1)} %refs_0_.3) | copy-start | bytes 2359300
  25.0 15.9 %copy-start.17 = (f32[576,1]{1,0:T(8,128)S(1)}, f32[576,1]{1,0:T(8,128)}, u32[]{:S(2)}) copy-start(f32[576,1]{1,0:T(8,128)} %broadcast_in_dim.54.refs_8_) | copy-start | bytes 6916
  25.0 15.9 %copy-start.33 = (bf16[208,576]{1,0:T(8,128)(2,1)S(1)}, bf16[208,576]{1,0:T(8,128)(2,1)}, u32[]{:S(2)}) copy-start(bf16[208,576]{1,0:T(8,128)(2,1)} %copy-done.32) | copy-start | bytes 718852
  28.8 12.1 %copy-start.27 = (bf16[512,768]{1,0:T(8,128)(2,1)}, bf16[512,768]{1,0:T(8,128)(2,1)S(1)}, u32[]{:S(2)}) copy-start(bf16[512,768]{1,0:T(8,128)(2,1)S(1)} %collective-permute-done.1.refs_2_) | copy-start | bytes 2359300
  28.8 9.9 %collective-permute-start.2 = (bf16[512,768]{1,0:T(8,128)(2,1)S(1)}, bf16[512,768]{1,0:T(8,128)(2,1)S(1)}, u32[]{:S(2)}, u32[]{:S(2)}) collective-permute-start(bf16[512,768]{1,0:T(8,128)(2,1)S(1)} %collective-permute-done.1.refs_2_), channel_id=1, source_target_pairs={{0,1},{1,0},{2,3},{3,2},{4,5},{5,4},{6,7},{7,6},{8,9},{9,8},{10,11... | collective-permute-start | bytes 2359304 | tf_op jit(solution)/shard_map/ppermute | solution.py:430
  38.8 10.8 %copy-start.30 = (bf16[512,768]{1,0:T(8,128)(2,1)}, bf16[512,768]{1,0:T(8,128)(2,1)S(1)}, u32[]{:S(2)}) copy-start(bf16[512,768]{1,0:T(8,128)(2,1)S(1)} %collective-permute-done.2.refs_3_) | copy-start | bytes 2359300
  38.8 20.5 %collective-permute-start.6 = (bf16[96,3840]{1,0:T(8,128)(2,1)S(1)}, bf16[96,3840]{1,0:T(8,128)(2,1)}, u32[]{:S(2)}, u32[]{:S(2)}) collective-permute-start(bf16[96,3840]{1,0:T(8,128)(2,1)S(1)} %get-tuple-element.94), channel_id=1, source_target_pairs={{0,2},{1,3},{2,0},{3,1},{4,6},{5,7},{6,4},{7,5},{8,10},{9,11},{10,... | collective-permute-start | bytes 2211848 | tf_op jit(solution)/shard_map/ppermute | solution.py:430
  40.2 34.9 %collective-permute-start.14 = (bf16[96,3072]{1,0:T(8,128)(2,1)S(1)}, bf16[96,3072]{1,0:T(8,128)(2,1)}, u32[]{:S(2)}, u32[]{:S(2)}) collective-permute-start(bf16[96,3072]{1,0:T(8,128)(2,1)S(1)} %get-tuple-element.100), channel_id=1, source_target_pairs={{0,2},{1,3},{2,0},{3,1},{4,6},{5,7},{6,4},{7,5},{8,10},{9,11},{10,... | collective-permute-start | bytes 1769480 | tf_op jit(solution)/shard_map/ppermute | solution.py:430
  40.9 52.8 %collective-permute-start.10 = (bf16[192,6912]{1,0:T(8,128)(2,1)}, bf16[192,6912]{1,0:T(8,128)(2,1)}, u32[]{:S(2)}, u32[]{:S(2)}) collective-permute-start(bf16[192,6912]{1,0:T(8,128)(2,1)} %get-tuple-element.98.refs_4_), channel_id=1, source_target_pairs={{0,1},{1,0},{2,3},{3,2},{4,5},{5,4},{6,7},{7,6},{8,9},{9,8},{10,11... | collective-permute-start | bytes 7962632 | tf_op jit(solution)/shard_map/ppermute | solution.py:430
  51.2 6.4 %copy-start.47 = (bf16[576,768]{1,0:T(8,128)(2,1)}, bf16[576,768]{1,0:T(8,128)(2,1)S(1)}, u32[]{:S(2)}) copy-start(bf16[576,768]{1,0:T(8,128)(2,1)S(1)} %get-tuple-element.130.refs_8_) | copy-start | bytes 2654212
  59.3 29.1 %collective-permute-start.11 = (bf16[96,3840]{1,0:T(8,128)(2,1)}, bf16[96,3840]{1,0:T(8,128)(2,1)}, u32[]{:S(2)}, u32[]{:S(2)}) collective-permute-start(bf16[96,3840]{1,0:T(8,128)(2,1)} %collective-permute-done.6.refs_6_), channel_id=1, source_target_pairs={{0,4},{4,0},{8,12},{12,8},{16,20},{20,16},{24,28},{28,24},{1,5},{5... | collective-permute-start | bytes 2211848 | tf_op jit(solution)/shard_map/ppermute | solution.py:430
  75.1 16.0 %collective-permute-start.15 = (bf16[96,3072]{1,0:T(8,128)(2,1)}, bf16[96,3072]{1,0:T(8,128)(2,1)}, u32[]{:S(2)}, u32[]{:S(2)}) collective-permute-start(bf16[96,3072]{1,0:T(8,128)(2,1)} %collective-permute-done.14.refs_10_), channel_id=1, source_target_pairs={{0,4},{4,0},{8,12},{12,8},{16,20},{20,16},{24,28},{28,24},{1,5},{5... | collective-permute-start | bytes 1769480 | tf_op jit(solution)/shard_map/ppermute | solution.py:430
  76.2 7.0 %collective-permute-start.9 = (bf16[192,512]{1,0:T(8,128)(2,1)S(1)}, bf16[192,512]{1,0:T(8,128)(2,1)S(1)}, u32[]{:S(2)}, u32[]{:S(2)}) collective-permute-start(bf16[192,512]{1,0:T(8,128)(2,1)S(1)} %pad_maximum_fusion.6), channel_id=1, source_target_pairs={{0,3},{1,2},{2,1},{3,0},{4,7},{5,6},{6,5},{7,4},{8,11},{9,10},{10,... | collective-permute-start | bytes 589832 | tf_op jit(solution)/shard_map/ppermute | solution.py:430
  77.2 10.5 %collective-permute-start.8 = (bf16[192,512]{1,0:T(8,128)(2,1)S(1)}, bf16[192,512]{1,0:T(8,128)(2,1)S(1)}, u32[]{:S(2)}, u32[]{:S(2)}) collective-permute-start(bf16[192,512]{1,0:T(8,128)(2,1)S(1)} %pad_maximum_fusion.5), channel_id=1, source_target_pairs={{0,2},{1,3},{2,0},{3,1},{4,6},{5,7},{6,4},{7,5},{8,10},{9,11},{10,... | collective-permute-start | bytes 589832 | tf_op jit(solution)/shard_map/ppermute | solution.py:430
  83.9 5.0 %collective-permute-start.7 = (bf16[192,512]{1,0:T(8,128)(2,1)S(1)}, bf16[192,512]{1,0:T(8,128)(2,1)S(1)}, u32[]{:S(2)}, u32[]{:S(2)}) collective-permute-start(bf16[192,512]{1,0:T(8,128)(2,1)S(1)} %pad_maximum_fusion.4), channel_id=1, source_target_pairs={{0,1},{1,0},{2,3},{3,2},{4,5},{5,4},{6,7},{7,6},{8,9},{9,8},{10,11... | collective-permute-start | bytes 589832 | tf_op jit(solution)/shard_map/ppermute | solution.py:430
  88.4 4.5 %collective-permute-start.12 = (bf16[96,3840]{1,0:T(8,128)(2,1)}, bf16[96,3840]{1,0:T(8,128)(2,1)}, u32[]{:S(2)}, u32[]{:S(2)}) collective-permute-start(bf16[96,3840]{1,0:T(8,128)(2,1)} %collective-permute-done.6.refs_6_), channel_id=1, source_target_pairs={{0,1},{1,0},{2,3},{3,2},{4,5},{5,4},{6,7},{7,6},{8,9},{9,8},{10,11... | collective-permute-start | bytes 2211848 | tf_op jit(solution)/shard_map/ppermute | solution.py:430
  88.4 5.3 %collective-permute-start.13 = (bf16[96,3840]{1,0:T(8,128)(2,1)}, bf16[96,3840]{1,0:T(8,128)(2,1)}, u32[]{:S(2)}, u32[]{:S(2)}) collective-permute-start(bf16[96,3840]{1,0:T(8,128)(2,1)} %collective-permute-done.11.refs_7_), channel_id=1, source_target_pairs={{0,1},{1,0},{2,3},{3,2},{4,5},{5,4},{6,7},{7,6},{8,9},{9,8},{10,11... | collective-permute-start | bytes 2211848 | tf_op jit(solution)/shard_map/ppermute | solution.py:430
  89.6 3.3 collective-permute-start.16
  91.1 2.5 collective-permute-start.17
  132.1 4.9 %collective-permute-start.21 = (bf16[2,192,3072]{2,1,0:T(8,128)(2,1)}, bf16[2,192,3072]{2,1,0:T(8,128)(2,1)}, u32[]{:S(2)}, u32[]{:S(2)}) collective-permute-start(bf16[2,192,3072]{2,1,0:T(8,128)(2,1)} %get-tuple-element.111), channel_id=1, source_target_pairs={{0,1},{1,0},{2,3},{3,2},{4,5},{5,4},{6,7},{7,6},{8,9},{9,8},{10,11... | collective-permute-start | bytes 7077896 | tf_op jit(solution)/shard_map/ppermute | solution.py:430
  132.2 9.2 %collective-permute-start.22 = (bf16[2,192,3840]{2,1,0:T(8,128)(2,1)}, bf16[2,192,3840]{2,1,0:T(8,128)(2,1)}, u32[]{:S(2)}, u32[]{:S(2)}) collective-permute-start(bf16[2,192,3840]{2,1,0:T(8,128)(2,1)} %get-tuple-element.113), channel_id=1, source_target_pairs={{0,1},{1,0},{2,3},{3,2},{4,5},{5,4},{6,7},{7,6},{8,9},{9,8},{10,11... | collective-permute-start | bytes 8847368 | tf_op jit(solution)/shard_map/ppermute | solution.py:430
  133.9 10.4 %collective-permute-start.18 = (bf16[192,512]{1,0:T(8,128)(2,1)}, bf16[192,512]{1,0:T(8,128)(2,1)S(1)}, u32[]{:S(2)}, u32[]{:S(2)}) collective-permute-start(bf16[192,512]{1,0:T(8,128)(2,1)} %copy-done.38), channel_id=1, source_target_pairs={{0,1},{1,0},{2,3},{3,2},{4,5},{5,4},{6,7},{7,6},{8,9},{9,8},{10,11... | collective-permute-start | bytes 589832 | tf_op jit(solution)/shard_map/ppermute | solution.py:430
  134.1 10.2 %collective-permute-start.19 = (bf16[192,512]{1,0:T(8,128)(2,1)}, bf16[192,512]{1,0:T(8,128)(2,1)S(1)}, u32[]{:S(2)}, u32[]{:S(2)}) collective-permute-start(bf16[192,512]{1,0:T(8,128)(2,1)} %copy-done.37), channel_id=1, source_target_pairs={{0,2},{1,3},{2,0},{3,1},{4,6},{5,7},{6,4},{7,5},{8,10},{9,11},{10,... | collective-permute-start | bytes 589832 | tf_op jit(solution)/shard_map/ppermute | solution.py:430
  135.6 9.5 %collective-permute-start.20 = (bf16[192,512]{1,0:T(8,128)(2,1)}, bf16[192,512]{1,0:T(8,128)(2,1)S(1)}, u32[]{:S(2)}, u32[]{:S(2)}) collective-permute-start(bf16[192,512]{1,0:T(8,128)(2,1)} %copy-done.36), channel_id=1, source_target_pairs={{0,3},{1,2},{2,1},{3,0},{4,7},{5,6},{6,5},{7,4},{8,11},{9,10},{10,... | collective-permute-start | bytes 589832 | tf_op jit(solution)/shard_map/ppermute | solution.py:430
  137.0 4.5 %copy-start.52 = (bf16[2,192,3840]{2,1,0:T(8,128)(2,1)S(1)}, bf16[2,192,3840]{2,1,0:T(8,128)(2,1)}, u32[]{:S(2)}) copy-start(bf16[2,192,3840]{2,1,0:T(8,128)(2,1)} %get-tuple-element.112) | copy-start | bytes 8847364
  145.2 34.6 %collective-permute-start.24 = (bf16[2,96,3840]{2,1,0:T(8,128)(2,1)S(1)}, bf16[2,96,3840]{2,1,0:T(8,128)(2,1)S(1)}, u32[]{:S(2)}, u32[]{:S(2)}) collective-permute-start(bf16[2,96,3840]{2,1,0:T(8,128)(2,1)S(1)} %get-tuple-element.121), channel_id=1, source_target_pairs={{0,4},{4,0},{8,12},{12,8},{16,20},{20,16},{24,28},{28,24},{1,5},{5... | collective-permute-start | bytes 4423688 | tf_op jit(solution)/shard_map/ppermute | solution.py:430
  146.9 28.0 %collective-permute-start.23 = (bf16[192,3072]{1,0:T(8,128)(2,1)S(1)}, bf16[192,3072]{1,0:T(8,128)(2,1)S(1)}, u32[]{:S(2)}, u32[]{:S(2)}) collective-permute-start(bf16[192,3072]{1,0:T(8,128)(2,1)S(1)} %get-tuple-element.120), channel_id=1, source_target_pairs={{0,2},{1,3},{2,0},{3,1},{4,6},{5,7},{6,4},{7,5},{8,10},{9,11},{10,... | collective-permute-start | bytes 3538952 | tf_op jit(solution)/shard_map/ppermute | solution.py:430
  147.7 7.9 %copy-start.26 = (f32[1,2048,1]{2,1,0:T(8,128)S(1)}, f32[1,2048,1]{2,1,0:T(8,128)}, u32[]{:S(2)}) copy-start(f32[1,2048,1]{2,1,0:T(8,128)} %copy-done.25) | copy-start | bytes 24580
  155.6 8.1 %copy-start.22 = (f32[1,2048,1]{2,1,0:T(8,128)S(1)}, f32[1,2048,1]{2,1,0:T(8,128)}, u32[]{:S(2)}) copy-start(f32[1,2048,1]{2,1,0:T(8,128)} %copy-done.21) | copy-start | bytes 24580
  180.2 14.9 %collective-permute-start.28 = (bf16[96,3072]{1,0:T(8,128)(2,1)S(1)}, bf16[96,3072]{1,0:T(8,128)(2,1)S(1)}, u32[]{:S(2)}, u32[]{:S(2)}) collective-permute-start(bf16[96,3072]{1,0:T(8,128)(2,1)S(1)} %constant_dynamic-slice_fusion.11), channel_id=1, source_target_pairs={{0,4},{4,0},{8,12},{12,8},{16,20},{20,16},{24,28},{28,24},{1,5},{5... | collective-permute-start | bytes 1769480 | tf_op jit(solution)/shard_map/ppermute | solution.py:430
  182.3 17.7 %collective-permute-start.30 = (bf16[96,3840]{1,0:T(8,128)(2,1)S(1)}, bf16[96,3840]{1,0:T(8,128)(2,1)S(1)}, u32[]{:S(2)}, u32[]{:S(2)}) collective-permute-start(bf16[96,3840]{1,0:T(8,128)(2,1)S(1)} %get-tuple-element.162), channel_id=1, source_target_pairs={{0,2},{1,3},{2,0},{3,1},{4,6},{5,7},{6,4},{7,5},{8,10},{9,11},{10,... | collective-permute-start | bytes 2211848 | tf_op jit(solution)/shard_map/ppermute | solution.py:430
  193.6 6.7 %copy-start.20 = (bf16[2,512,768]{2,1,0:T(8,128)(2,1)}, bf16[2,512,768]{2,1,0:T(8,128)(2,1)S(1)}, u32[]{:S(2)}) copy-start(bf16[2,512,768]{2,1,0:T(8,128)(2,1)S(1)} %get-tuple-element.133) | copy-start | bytes 4718596
  193.6 102.1 %copy-start.9 = (bf16[2,512,768]{2,1,0:T(8,128)(2,1)}, bf16[2,512,768]{2,1,0:T(8,128)(2,1)S(1)}, u32[]{:S(2)}) copy-start(bf16[2,512,768]{2,1,0:T(8,128)(2,1)S(1)} %get-tuple-element.132) | copy-start | bytes 4718596
  193.6 12.4 %collective-permute-start.27 = (bf16[4,96,588]{2,1,0:T(8,128)(2,1)S(1)}, bf16[4,96,588]{2,1,0:T(8,128)(2,1)S(1)}, u32[]{:S(2)}, u32[]{:S(2)}) collective-permute-start(bf16[4,96,588]{2,1,0:T(8,128)(2,1)S(1)} %get-tuple-element.135), channel_id=1, source_target_pairs={{0,4},{4,0},{8,12},{12,8},{16,20},{20,16},{24,28},{28,24},{1,5},{5... | collective-permute-start | bytes 1354760 | tf_op jit(solution)/shard_map/ppermute | solution.py:430
  195.3 9.4 %collective-permute-start.29 = (bf16[48,3072]{1,0:T(8,128)(2,1)S(1)}, bf16[48,3072]{1,0:T(8,128)(2,1)S(1)}, u32[]{:S(2)}, u32[]{:S(2)}) collective-permute-start(bf16[48,3072]{1,0:T(8,128)(2,1)S(1)} %constant_dynamic-slice_fusion.10), channel_id=1, source_target_pairs={{0,8},{4,12},{8,0},{12,4},{16,24},{20,28},{24,16},{28,20},{1,9},{5... | collective-permute-start | bytes 884744 | tf_op jit(solution)/shard_map/ppermute | solution.py:430
  200.3 15.5 %collective-permute-start.33 = (bf16[48,3840]{1,0:T(8,128)(2,1)S(1)}, bf16[48,3840]{1,0:T(8,128)(2,1)S(1)}, u32[]{:S(2)}, u32[]{:S(2)}) collective-permute-start(bf16[48,3840]{1,0:T(8,128)(2,1)S(1)} %constant_dynamic-slice_fusion.7), channel_id=1, source_target_pairs={{0,8},{4,12},{8,0},{12,4},{16,24},{20,28},{24,16},{28,20},{1,9},{5... | collective-permute-start | bytes 1105928 | tf_op jit(solution)/shard_map/ppermute | solution.py:430
  206.1 11.6 %collective-permute-start.32 = (bf16[24,3072]{1,0:T(8,128)(2,1)S(1)}, bf16[24,3072]{1,0:T(8,128)(2,1)S(1)}, u32[]{:S(2)}, u32[]{:S(2)}) collective-permute-start(bf16[24,3072]{1,0:T(8,128)(2,1)S(1)} %constant_dynamic-slice_fusion.8), channel_id=1, source_target_pairs={{0,16},{4,20},{8,24},{12,28},{16,0},{20,4},{24,8},{28,12},{1,17},{... | collective-permute-start | bytes 442376 | tf_op jit(solution)/shard_map/ppermute | solution.py:430
  208.8 13.5 %collective-permute-start.31 = (bf16[4,48,588]{2,1,0:T(8,128)(2,1)S(1)}, bf16[4,48,588]{2,1,0:T(8,128)(2,1)S(1)}, u32[]{:S(2)}, u32[]{:S(2)}) collective-permute-start(bf16[4,48,588]{2,1,0:T(8,128)(2,1)S(1)} %constant_dynamic-slice_fusion.9), channel_id=1, source_target_pairs={{0,8},{4,12},{8,0},{12,4},{16,24},{20,28},{24,16},{28,20},{1,9},{5... | collective-permute-start | bytes 677384 | tf_op jit(solution)/shard_map/ppermute | solution.py:430
  215.9 13.2 %collective-permute-start.35 = (bf16[24,3840]{1,0:T(8,128)(2,1)S(1)}, bf16[24,3840]{1,0:T(8,128)(2,1)S(1)}, u32[]{:S(2)}, u32[]{:S(2)}) collective-permute-start(bf16[24,3840]{1,0:T(8,128)(2,1)S(1)} %constant_dynamic-slice_fusion.5), channel_id=1, source_target_pairs={{0,16},{4,20},{8,24},{12,28},{16,0},{20,4},{24,8},{28,12},{1,17},{... | collective-permute-start | bytes 552968 | tf_op jit(solution)/shard_map/ppermute | solution.py:430
  222.4 9.0 %collective-permute-start.34 = (bf16[4,24,588]{2,1,0:T(8,128)(2,1)S(1)}, bf16[4,24,588]{2,1,0:T(8,128)(2,1)S(1)}, u32[]{:S(2)}, u32[]{:S(2)}) collective-permute-start(bf16[4,24,588]{2,1,0:T(8,128)(2,1)S(1)} %constant_dynamic-slice_fusion.6), channel_id=1, source_target_pairs={{0,16},{4,20},{8,24},{12,28},{16,0},{20,4},{24,8},{28,12},{1,17},{... | collective-permute-start | bytes 338696 | tf_op jit(solution)/shard_map/ppermute | solution.py:430
  235.6 2.3 collective-permute-start.36
  235.6 4.0 %collective-permute-start.37 = (bf16[24,626]{1,0:T(8,128)(2,1)S(1)}, bf16[24,626]{1,0:T(8,128)(2,1)S(1)}, u32[]{:S(2)}, u32[]{:S(2)}) collective-permute-start(bf16[24,626]{1,0:T(8,128)(2,1)S(1)} %get-tuple-element.180), channel_id=1, source_target_pairs={{0,2},{1,3},{2,0},{3,1},{4,6},{5,7},{6,4},{7,5},{8,10},{9,11},{10,... | collective-permute-start | bytes 90152 | tf_op jit(solution)/shard_map/ppermute | solution.py:430
  237.5 3.3 collective-permute-start.38
  237.6 9.0 %copy-start.57 = (f32[512]{0:T(512)}, f32[512]{0:T(512)S(1)}, u32[]{:S(2)}) copy-start(f32[512]{0:T(512)S(1)} %broadcast_multiply_fusion.2) | copy-start | bytes 6148
  237.6 36.4 %collective-permute-start.25 = (bf16[2,512,768]{2,1,0:T(8,128)(2,1)}, bf16[2,512,768]{2,1,0:T(8,128)(2,1)}, u32[]{:S(2)}, u32[]{:S(2)}) collective-permute-start(bf16[2,512,768]{2,1,0:T(8,128)(2,1)} %copy-done.20), channel_id=1, source_target_pairs={{0,1},{1,0},{2,3},{3,2},{4,5},{5,4},{6,7},{7,6},{8,9},{9,8},{10,11... | collective-permute-start | bytes 4718600 | tf_op jit(solution)/shard_map/ppermute | solution.py:430
  246.2 14.6 %collective-permute-start.39 = (bf16[1,24,2318]{2,1,0:T(8,128)(2,1)S(1)}, bf16[1,24,2318]{2,1,0:T(8,128)(2,1)S(1)}, u32[]{:S(2)}, u32[]{:S(2)}) collective-permute-start(bf16[1,24,2318]{2,1,0:T(8,128)(2,1)S(1)} %bitcast.124), channel_id=1, source_target_pairs={{0,16},{4,20},{8,24},{12,28},{16,0},{20,4},{24,8},{28,12},{1,17},{... | collective-permute-start | bytes 333800 | tf_op jit(solution)/shard_map/ppermute | solution.py:430
  260.8 9.3 %collective-permute-start.40 = (bf16[2,24,2318]{2,1,0:T(8,128)(2,1)S(1)}, bf16[2,24,2318]{2,1,0:T(8,128)(2,1)S(1)}, u32[]{:S(2)}, u32[]{:S(2)}) collective-permute-start(bf16[2,24,2318]{2,1,0:T(8,128)(2,1)S(1)} %pad_maximum_fusion.2), channel_id=1, source_target_pairs={{0,8},{4,12},{8,0},{12,4},{16,24},{20,28},{24,16},{28,20},{1,9},{5... | collective-permute-start | bytes 667592 | tf_op jit(solution)/shard_map/ppermute | solution.py:430
  270.2 23.3 %copy-start.13 = (bf16[4,24,2318]{2,1,0:T(8,128)(2,1)}, bf16[4,24,2318]{2,1,0:T(8,128)(2,1)S(1)}, u32[]{:S(2)}) copy-start(bf16[4,24,2318]{2,1,0:T(8,128)(2,1)S(1)} %pad_maximum_fusion.refs_1_) | copy-start | bytes 1335172
  270.2 21.6 %collective-permute-start.41 = (bf16[4,24,2318]{2,1,0:T(8,128)(2,1)S(1)}, bf16[4,24,2318]{2,1,0:T(8,128)(2,1)S(1)}, u32[]{:S(2)}, u32[]{:S(2)}) collective-permute-start(bf16[4,24,2318]{2,1,0:T(8,128)(2,1)S(1)} %pad_maximum_fusion.refs_1_), channel_id=1, source_target_pairs={{0,4},{4,0},{8,12},{12,8},{16,20},{20,16},{24,28},{28,24},{1,5},{5... | collective-permute-start | bytes 1335176 | tf_op jit(solution)/shard_map/ppermute | solution.py:430
  276.2 19.6 %collective-permute-start.26 = (bf16[512,768]{1,0:T(8,128)(2,1)}, bf16[512,768]{1,0:T(8,128)(2,1)}, u32[]{:S(2)}, u32[]{:S(2)}) collective-permute-start(bf16[512,768]{1,0:T(8,128)(2,1)} %fusion.14), channel_id=1, source_target_pairs={{0,2},{1,3},{2,0},{3,1},{4,6},{5,7},{6,4},{7,5},{8,10},{9,11},{10,... | collective-permute-start | bytes 2359304 | tf_op jit(solution)/shard_map/ppermute | solution.py:430
  291.8 6.1 %copy-start.15 = (bf16[4,24,2318]{2,1,0:T(8,128)(2,1)}, bf16[4,24,2318]{2,1,0:T(8,128)(2,1)S(1)}, u32[]{:S(2)}) copy-start(bf16[4,24,2318]{2,1,0:T(8,128)(2,1)S(1)} %collective-permute-done.41.refs_2_) | copy-start | bytes 1335172
  293.6 4.3 %copy-start.55 = (f32[192,12]{0,1:T(8,128)}, f32[192,12]{0,1:T(8,128)S(1)}, u32[]{:S(2)}) copy-start(f32[192,12]{0,1:T(8,128)S(1)} %copy.55) | copy-start | bytes 27652
  298.0 8.8 %copy-start.2 = (f32[192,3072]{1,0:T(8,128)S(1)}, f32[192,3072]{1,0:T(8,128)}, u32[]{:S(2)}) copy-start(f32[192,3072]{1,0:T(8,128)} %out_ref.1) | copy-start | bytes 7077892
  (42 other events, 77.8 us)
Sparse Core Ops, SparseCore 0:
  238.0 68.7 all-gather.2

commit v6 on v5

--- a/solution.py
+++ b/solution.py
@@ -689,7 +689,7 @@
             + [jax.ShapeDtypeStruct((parts // 2, rows, c), LOW) for c in grad_columns for _ in range(2)]
             + [jax.ShapeDtypeStruct((slots, width), HIGH), jax.ShapeDtypeStruct((16, width), HIGH)]
             + [jax.ShapeDtypeStruct((own_cols, slots), LOW)] * parts,
-            compiler_params=params(50),
+            compiler_params=params(44),
             cost_estimate=cost(2 * slots * width * (6 * hidden + 3 * width), 30e6, slots * hidden),
             name="mlp",
         )(prefetch, side, live_own, tokens, cotangent, vectors, *mixed_own, *wide)
@@ -725,19 +725,11 @@
                 ),
                 out_shape=jax.ShapeDtypeStruct((3, head_size, total), LOW),
                 compiler_params=params(28),
-                cost_estimate=cost(
-                    5 * pair_flops, 4e6, total * total // 2
-                ),
+                cost_estimate=cost(pair_flops // 4, 4e5),
                 name="attend_back",
             )(prefetch, qkv, qkv, qkv, seg_col, seg_row, lse[h], *do_own)
 
         dqkv = [attend_back(h, qkv) for h in range(own_heads)]
-        *dqkv, got_a, got_b = lax.optimization_barrier((*dqkv, got_a, got_b))
-        own_a, other_a = halve(add_low(own_a, got_a), half, 0)
-        got_a = swap(other_a, "dp", 1, replicas)
-        own_b, other_b = [add_low(own_b[n], got_b[n]) for n in range(2)]
-        got_b = swap(other_b, "shard", parts // 2, parts)
-        dqkv[0] = after(dqkv[0], other_a, own_b, other_b)
 
         q_cols = 3 * own_cols
         extra = vec_w.shape[0]
@@ -768,7 +760,7 @@
             out_shape=[jax.ShapeDtypeStruct((parts // 2, slots, width), LOW)] * 2
             + [jax.ShapeDtypeStruct((parts, half_rows, q_cols + extra), LOW)] * 2,
             compiler_params=params(28),
-            cost_estimate=cost(4 * total * width * 3 * own_cols * 2, 16e6),
+            cost_estimate=cost(total * width * own_cols // 4, 1e6),
             name="projection_back",
         )(prefetch, side, *x_all, a1, *dqkv, w_t, vectors, mid_grads)
 
@@ -788,6 +780,11 @@
             return scatter_half(array, dim, bit, replica, replicas)
 
         got_q = swap(other_q, "dp", 1, replicas)
+        own_a, other_a = halve(event(add_low(own_a, seen(got_a))), half, 0)
+        got_a = swap(other_a, "dp", 1, replicas)
+        got_b = seen(got_b)
+        own_b, other_b = [event(add_low(own_b[n], got_b[n])) for n in range(2)]
+        got_b = swap(other_b, "shard", parts // 2, parts)
         da1_got = swap(da1_send, "shard", 1, parts)
         state_a = next_half(own_a, got_a, z_bits[0], 0)
         state_b = next_half(own_b, got_b, z_bits[0], 0)
@@ -887,7 +884,7 @@
             ),
             out_shape=[jax.ShapeDtypeStruct(attn_shape, HIGH)] * 4
             + [jax.ShapeDtypeStruct(mlp_shape, HIGH)] * 4,
-            compiler_params=params(20),
+            compiler_params=params(50),
             cost_estimate=cost(30 * 9 * rows * width, 54e6),
             name="adam",
         )(

time: 345 us -> 364 us (1.055)
  waiting for transfers between devices: 104 us -> 118 us
  Pallas kernels: 107 us -> 115 us
  starting transfers between devices: 37.7 us -> 33.9 us
    ppermute x42, waiting for transfers between devices: 98.6 us -> 110 us  [swap(): return lax.ppermute(array, axis, [(i, i ^ bit) for i in range(count)])]
    pallas_call x1, Pallas kernels: 10.7 us -> 19.1 us  [on_device(): pl.pallas_call(functools.partial(adam_kernel, fc_rows), grid_spec=pltpu.P...]
    convert_element_type x14, other arithmetic: 9.7 us -> 14.7 us  [add_low(): return (a.astype(HIGH) + b.astype(HIGH)).astype(LOW)]
    unnamed x129 -> x151, local copies, waits for them, and re-layouts: 34.7 us -> 29.9 us
    ppermute x42, starting transfers between devices: 37.7 us -> 33.8 us  [swap(): return lax.ppermute(array, axis, [(i, i ^ bit) for i in range(count)])]
  transfers between devices with their start and end apart: 43 -> 43, of which waited for: 28 -> 19; matrix products, arithmetic and copies ran while one was open for 9% -> 11% of each run, Pallas kernels for 19% -> 18%
where the time goes in v6:
time: 364 us; the launch traced here: 359 us
  waiting for transfers between devices  118 us (32%)
  Pallas kernels  115 us (32%)
  local copies, waits for them, and re-layouts  39.2 us (11%)
  starting transfers between devices  33.9 us (9%)
  other arithmetic  29.5 us (8%)
  between operations  23.5 us (6%)
    ppermute x42, waiting for transfers between devices, swap(): return lax.ppermute(array, axis, [(i, i ^ bit) for i in range(count)])  110 us
    ppermute x42, starting transfers between devices, swap(): return lax.ppermute(array, axis, [(i, i ^ bit) for i in range(count)])  33.8 us
    pallas_call x1, Pallas kernels, on_device(): pl.pallas_call(functools.partial(mlp_kernel, parts, first_blocks), grid_s...  31.4 us
    unnamed x151, local copies, waits for them, and re-layouts  29.9 us
    pallas_call x3, Pallas kernels, attend_back(): pl.pallas_call(functools.partial(attend_back_kernel, scale), grid_spec=pl...  24 us
    pallas_call x3, Pallas kernels, attend(): pl.pallas_call(functools.partial(attend_kernel, scale), grid_spec=pltpu.P...  19.5 us
    pallas_call x1, Pallas kernels, on_device(): pl.pallas_call(functools.partial(adam_kernel, fc_rows), grid_spec=pltpu.P...  19.1 us
    convert_element_type x14, other arithmetic, add_low(): return (a.astype(HIGH) + b.astype(HIGH)).astype(LOW)  14.7 us
  transfers between devices with their start and end apart: 43, of which 19 were waited for; matrix products, arithmetic and copies ran while one was open for 11% of the time, Pallas kernels for 18%

profile of v6, /device:TPU:0, one launch (start us, length us, event | category | flops | bytes accessed | tf_op | source)
XLA Modules:
  0.0 358.9 jit_solution(17841212019255214534)
XLA Ops:
  7.2 3.0 collective-permute-start.1
  10.3 1.7 copy-done
  12.6 1.5 cut.1
  15.4 1.3 collective-permute-start.5
  18.2 1.3 copy.49
  20.2 2.3 copy-done.8
  22.5 1.9 widen.1
  24.4 4.4 %collective-permute-done.1.refs_2_ = bf16[512,768]{1,0:T(8,128)(2,1)S(1)} collective-permute-done((bf16[512,768]{1,0:T(8,128)(2,1)}, bf16[512,768]{1,0:T(8,128)(2,1)S(1)}, u32[]{:S(2)}, u32[]{:S(2)}) %collective-permute-start.1) | collective-permute-done | bytes 786464 | tf_op jit(solution)/shard_map/ppermute | solution.py:430
  29.1 5.6 %collective-permute-done.4.refs_6_ = bf16[208,576]{1,0:T(8,128)(2,1)} collective-permute-done((bf16[208,576]{1,0:T(8,128)(2,1)}, bf16[208,576]{1,0:T(8,128)(2,1)}, u32[]{:S(2)}, u32[]{:S(2)}) %collective-permute-start.4) | collective-permute-done | bytes 239648 | tf_op jit(solution)/shard_map/ppermute | solution.py:430
  34.6 4.1 %collective-permute-done.5.refs_7_ = bf16[208,576]{1,0:T(8,128)(2,1)} collective-permute-done((bf16[208,576]{1,0:T(8,128)(2,1)}, bf16[208,576]{1,0:T(8,128)(2,1)}, u32[]{:S(2)}, u32[]{:S(2)}) %collective-permute-start.5) | collective-permute-done | bytes 239648 | tf_op jit(solution)/shard_map/ppermute | solution.py:430
  38.8 1.4 collective-permute-start.6
  41.0 1.1 copy-done.37
  42.1 6.6 %project.1 = (bf16[2048,768]{1,0:T(8,128)(2,1)S(1)}, bf16[576,2048]{1,0:T(8,128)(2,1)S(1)}, bf16[576,768]{1,0:T(8,128)(2,1)S(1)}, f32[16,768]{1,0:T(8,128)S(1)}) custom-call(s32[1]{0:T(128)} %bitcast.place, bf16[512,768]{1,0:T(8,128)(2,1)S(1)} %copy-done.3, bf16[512,768]{1,0:T(8,128)(2,1)} %collective-permute-done.refs_1_, bf16[512,768]{1,0:T(8,128)(2,1)S(1)} %copy-done.37, ...), custom_call_target="tpu_custom_call" | custom-call | flops 5435817984 | bytes 12000000 | tf_op jit(solution)/shard_map/project/pallas_call | solution.py:570
  48.7 1.7 copy-done.10
  50.4 6.4 %attend.3 = (bf16[4,64,512]{2,1,0:T(8,128)(2,1)S(1)}, f32[1,2048,1]{2,1,0:T(8,128)S(1)}) custom-call(s32[1]{0:T(128)} %bitcast.place, bf16[576,2048]{1,0:T(8,128)(2,1)S(1)} %get-tuple-element.91.qt_ref.kt_ref.vt_ref, bf16[576,2048]{1,0:T(8,128)(2,1)S(1)} %get-tuple-element.91.qt_ref.kt_ref.vt_ref, ...), custom_call_target="tpu_custom_call" | custom-call | flops 2147483648 | bytes 4000000 | tf_op jit(solution)/shard_map/attend/pallas_call | solution.py:612
  58.5 1.7 collective-permute-start.11
  60.1 6.4 %attend.5 = (bf16[4,64,512]{2,1,0:T(8,128)(2,1)S(1)}, f32[1,2048,1]{2,1,0:T(8,128)S(1)}) custom-call(s32[1]{0:T(128)} %bitcast.place, bf16[576,2048]{1,0:T(8,128)(2,1)S(1)} %get-tuple-element.91.qt_ref.kt_ref.vt_ref, bf16[576,2048]{1,0:T(8,128)(2,1)S(1)} %get-tuple-element.91.qt_ref.kt_ref.vt_ref, ...), custom_call_target="tpu_custom_call" | custom-call | flops 2147483648 | bytes 4000000 | tf_op jit(solution)/shard_map/attend/pallas_call | solution.py:612
  67.6 6.7 %attend.4 = (bf16[4,64,512]{2,1,0:T(8,128)(2,1)S(1)}, f32[1,2048,1]{2,1,0:T(8,128)S(1)}) custom-call(s32[1]{0:T(128)} %bitcast.place, bf16[576,2048]{1,0:T(8,128)(2,1)S(1)} %get-tuple-element.91.qt_ref.kt_ref.vt_ref, bf16[576,2048]{1,0:T(8,128)(2,1)S(1)} %get-tuple-element.91.qt_ref.kt_ref.vt_ref, ...), custom_call_target="tpu_custom_call" | custom-call | flops 2147483648 | bytes 4000000 | tf_op jit(solution)/shard_map/attend/pallas_call | solution.py:612
  78.1 5.2 %collective-permute-done.9.refs_3_ = bf16[192,512]{1,0:T(8,128)(2,1)S(1)} collective-permute-done((bf16[192,512]{1,0:T(8,128)(2,1)S(1)}, bf16[192,512]{1,0:T(8,128)(2,1)S(1)}, u32[]{:S(2)}, u32[]{:S(2)}) %collective-permute-start.9) | collective-permute-done | bytes 196640 | tf_op jit(solution)/shard_map/ppermute | solution.py:430
  84.7 3.1 collective-permute-done.8.refs_2_
  89.6 1.2 collective-permute-done.15.refs_11_
  93.7 1.1 copy-done.4
  94.9 1.1 copy-done.46
  98.8 31.4 %mlp.1 = (bf16[512,768]{1,0:T(8,128)(2,1)}, bf16[2,192,3072]{2,1,0:T(8,128)(2,1)}, bf16[2,192,3072]{2,1,0:T(8,128)(2,1)}, bf16[2,192,3840]{2,1,0:T(8,128)(2,1)},...) custom-call(s32[1]{0:T(128)} %bitcast.place, ...), custom_call_target="tpu_custom_call" | custom-call | flops 16307453952 | bytes 30000000 | tf_op jit(solution)/shard_map/mlp/pallas_call | solution.py:662
  130.9 1.1 copy-done.26
  134.1 1.5 collective-permute-start.19
  135.8 2.5 collective-permute-done.21
  138.3 4.8 %fusion.14 = (bf16[192,3072]{1,0:T(8,128)(2,1)}, bf16[192,3072]{1,0:T(8,128)(2,1)}) fusion(bf16[2,192,3072]{2,1,0:T(8,128)(2,1)} %collective-permute-done.21, bf16[2,192,3072]{2,1,0:T(8,128)(2,1)} %get-tuple-element.106), kind=kLoop, calls=%fused_computation.25 | loop fusion | flops 4718592 | bytes 7077888 | tf_op jit(solution)/shard_map/convert_element_type | solution.py:462
  143.1 2.6 add_convert_fusion
  145.8 1.8 constant_dynamic-slice_fusion.12
  147.6 1.3 collective-permute-start.26
  149.5 1.6 collective-permute-start.28
  151.6 1.2 iota_compare_fusion.1
  157.2 1.2 copy-done.31
  158.4 7.8 %attend_back.5.refs_7_ = bf16[3,64,2048]{2,1,0:T(8,128)(2,1)S(1)} custom-call(s32[1]{0:T(128)} %bitcast.place, bf16[576,2048]{1,0:T(8,128)(2,1)S(1)} %get-tuple-element.91.qt_ref.kt_ref.vt_ref, bf16[576,2048]{1,0:T(8,128)(2,1)S(1)} %get-tuple-element.91.qt_ref.kt_ref.vt_ref, bf16[576,2048]{1,0:T(8,128)(2,1)S(1)} %get-tuple-element.91.qt_ref.kt_ref.vt_ref, ...), custom_call_target="tpu_custom_call" | custom-call | flops 268435456 | bytes 400000 | tf_op jit(solution)/shard_map/attend_back/pallas_call | solution.py:710
  166.3 8.1 %attend_back.4.refs_6_ = bf16[3,64,2048]{2,1,0:T(8,128)(2,1)S(1)} custom-call(s32[1]{0:T(128)} %bitcast.place, bf16[576,2048]{1,0:T(8,128)(2,1)S(1)} %get-tuple-element.91.qt_ref.kt_ref.vt_ref, bf16[576,2048]{1,0:T(8,128)(2,1)S(1)} %get-tuple-element.91.qt_ref.kt_ref.vt_ref, bf16[576,2048]{1,0:T(8,128)(2,1)S(1)} %get-tuple-element.91.qt_ref.kt_ref.vt_ref, ...), custom_call_target="tpu_custom_call" | custom-call | flops 268435456 | bytes 400000 | tf_op jit(solution)/shard_map/attend_back/pallas_call | solution.py:710
  174.5 8.1 %attend_back.3.refs_5_ = bf16[3,64,2048]{2,1,0:T(8,128)(2,1)S(1)} custom-call(s32[1]{0:T(128)} %bitcast.place, bf16[576,2048]{1,0:T(8,128)(2,1)S(1)} %get-tuple-element.91.qt_ref.kt_ref.vt_ref, bf16[576,2048]{1,0:T(8,128)(2,1)S(1)} %get-tuple-element.91.qt_ref.kt_ref.vt_ref, bf16[576,2048]{1,0:T(8,128)(2,1)S(1)} %get-tuple-element.91.qt_ref.kt_ref.vt_ref, ...), custom_call_target="tpu_custom_call" | custom-call | flops 268435456 | bytes 400000 | tf_op jit(solution)/shard_map/attend_back/pallas_call | solution.py:710
  182.6 11.1 %projection_back.1 = (bf16[2,512,768]{2,1,0:T(8,128)(2,1)S(1)}, bf16[2,512,768]{2,1,0:T(8,128)(2,1)}, bf16[4,96,588]{2,1,0:T(8,128)(2,1)S(1)}, bf16[4,96,588]{2,1,0:T(8,128)(2,1)S(1)}) custom-call(s32[1]{0:T(128)} %bitcast.place, s32[1]{0:T(128)} %bitcast.1.half, bf16[512,768]{1,0:T(8,128)(2,1)S(1)} %copy-done.6, ...), custom_call_target="tpu_custom_call" | custom-call | flops 75497472 | bytes 1000000 | tf_op jit(solution)/shard_map/projection_back/pallas_call | solution.py:737
  194.4 1.8 add_convert_fusion.1
  196.2 1.6 collective-permute-start.27
  197.8 1.3 fusion.16
  199.1 1.0 collective-permute-start.30
  200.1 19.3 %collective-permute-done.27 = bf16[96,3072]{1,0:T(8,128)(2,1)S(1)} collective-permute-done((bf16[96,3072]{1,0:T(8,128)(2,1)S(1)}, bf16[96,3072]{1,0:T(8,128)(2,1)S(1)}, u32[]{:S(2)}, u32[]{:S(2)}) %collective-permute-start.27) | collective-permute-done | bytes 589856 | tf_op jit(solution)/shard_map/ppermute | solution.py:430
  219.6 1.6 collective-permute-start.29
  221.2 1.4 fusion.12
  223.2 8.0 %collective-permute-done.29 = bf16[48,3072]{1,0:T(8,128)(2,1)S(1)} collective-permute-done((bf16[48,3072]{1,0:T(8,128)(2,1)S(1)}, bf16[48,3072]{1,0:T(8,128)(2,1)S(1)}, u32[]{:S(2)}, u32[]{:S(2)}) %collective-permute-start.29) | collective-permute-done | bytes 294944 | tf_op jit(solution)/shard_map/ppermute | solution.py:430
  231.3 1.1 collective-permute-start.32
  232.5 3.2 collective-permute-start.31
  235.7 6.9 %collective-permute-done.33 = bf16[48,3840]{1,0:T(8,128)(2,1)S(1)} collective-permute-done((bf16[48,3840]{1,0:T(8,128)(2,1)S(1)}, bf16[48,3840]{1,0:T(8,128)(2,1)S(1)}, u32[]{:S(2)}, u32[]{:S(2)}) %collective-permute-start.33) | collective-permute-done | bytes 368672 | tf_op jit(solution)/shard_map/ppermute | solution.py:430
  242.8 1.7 collective-permute-start.35
  244.5 1.3 collective-permute-done.31
  245.9 2.6 collective-permute-start.34
  248.5 6.8 %collective-permute-done.35 = bf16[24,3840]{1,0:T(8,128)(2,1)S(1)} collective-permute-done((bf16[24,3840]{1,0:T(8,128)(2,1)S(1)}, bf16[24,3840]{1,0:T(8,128)(2,1)S(1)}, u32[]{:S(2)}, u32[]{:S(2)}) %collective-permute-start.35) | collective-permute-done | bytes 184352 | tf_op jit(solution)/shard_map/ppermute | solution.py:430
  262.2 1.4 collective-permute-start.38
  263.6 2.2 fusion.15
  272.0 1.1 reshape.295
  273.3 12.5 %collective-permute-done.24 = bf16[512,768]{1,0:T(8,128)(2,1)S(1)} collective-permute-done((bf16[512,768]{1,0:T(8,128)(2,1)}, bf16[512,768]{1,0:T(8,128)(2,1)S(1)}, u32[]{:S(2)}, u32[]{:S(2)}) %collective-permute-start.24) | collective-permute-done | bytes 786464 | tf_op jit(solution)/shard_map/ppermute | solution.py:430
  285.9 2.2 fusion.36
  288.2 11.1 %collective-permute-done.40 = bf16[2,24,2318]{2,1,0:T(8,128)(2,1)S(1)} collective-permute-done((bf16[2,24,2318]{2,1,0:T(8,128)(2,1)S(1)}, bf16[2,24,2318]{2,1,0:T(8,128)(2,1)S(1)}, u32[]{:S(2)}, u32[]{:S(2)}) %collective-permute-start.40) | collective-permute-done | bytes 222560 | tf_op jit(solution)/shard_map/ppermute | solution.py:430
  299.6 3.0 fusion.9
  302.6 16.1 %collective-permute-done.41.refs_2_ = bf16[4,24,2318]{2,1,0:T(8,128)(2,1)S(1)} collective-permute-done((bf16[4,24,2318]{2,1,0:T(8,128)(2,1)S(1)}, bf16[4,24,2318]{2,1,0:T(8,128)(2,1)S(1)}, u32[]{:S(2)}, u32[]{:S(2)}) %collective-permute-start.41) | collective-permute-done | bytes 445088 | tf_op jit(solution)/shard_map/ppermute | solution.py:430
  321.9 7.4 %all-gather.3.cloned.1.call-done = bf16[192,6912]{1,0:T(8,128)(2,1)} async-done(((bf16[24,6912]{1,0:T(8,128)(2,1)}), bf16[192,6912]{1,0:T(8,128)(2,1)}) %all-gather.3.cloned.1.call-update) | async-done | bytes 2654224 | tf_op jit(solution)/shard_map/all_gather | solution.py:801
  329.3 1.0 copy-done.13
  331.4 19.1 %adam.1 = (f32[8,24,3072]{2,1,0:T(8,128)}, f32[8,24,3072]{2,1,0:T(8,128)}, f32[8,24,3072]{2,1,0:T(8,128)}, f32[8,24,3072]{2,1,0:T(8,128)}, f32[2,8,24,3072]{3,2,...) custom-call(f32[1]{0:T(128)} %bitcast.46.factor_ref, ...), custom_call_target="tpu_custom_call" | custom-call | flops 39813120 | bytes 54000000 | tf_op jit(solution)/shard_map/adam/pallas_call | solution.py:871
  (282 shorter events, 41.5 us)
Async XLA Ops:
  7.2 10.5 %copy-start.72 = (s32[1,4]{1,0:T(1,128)S(1)}, s32[1,4]{1,0:T(1,128)}, u32[]{:S(2)}) copy-start(s32[1,4]{1,0:T(1,128)} %param.16) | copy-start | bytes 52
  7.2 10.8 %copy-start.73 = (s32[1,2]{1,0:T(1,128)S(1)}, s32[1,2]{1,0:T(1,128)}, u32[]{:S(2)}) copy-start(s32[1,2]{1,0:T(1,128)} %param.15) | copy-start | bytes 28
  7.2 322.1 %all-gather.3.cloned.1.call-start = ((), (), s32[]{:S(2)}) async-start(), calls=%async_computation | async-start | bytes 2985984 | tf_op jit(solution)/shard_map/all_gather | solution.py:801
  7.2 21.6 %collective-permute-start.1 = (bf16[512,768]{1,0:T(8,128)(2,1)}, bf16[512,768]{1,0:T(8,128)(2,1)S(1)}, u32[]{:S(2)}, u32[]{:S(2)}) collective-permute-start(bf16[512,768]{1,0:T(8,128)(2,1)} %refs_0_.3), channel_id=1, source_target_pairs={{0,2},{1,3},{2,0},{3,1},{4,6},{5,7},{6,4},{7,5},{8,10},{9,11},{10,... | collective-permute-start | bytes 2359304 | tf_op jit(solution)/shard_map/ppermute | solution.py:430
  10.2 28.5 %collective-permute-start = (bf16[512,768]{1,0:T(8,128)(2,1)}, bf16[512,768]{1,0:T(8,128)(2,1)}, u32[]{:S(2)}, u32[]{:S(2)}) collective-permute-start(bf16[512,768]{1,0:T(8,128)(2,1)} %refs_0_.3), channel_id=1, source_target_pairs={{0,1},{1,0},{2,3},{3,2},{4,5},{5,4},{6,7},{7,6},{8,9},{9,8},{10,11... | collective-permute-start | bytes 2359304 | tf_op jit(solution)/shard_map/ppermute | solution.py:430
  14.9 14.2 %collective-permute-start.3 = (bf16[208,576]{1,0:T(8,128)(2,1)}, bf16[208,576]{1,0:T(8,128)(2,1)}, u32[]{:S(2)}, u32[]{:S(2)}) collective-permute-start(bf16[208,576]{1,0:T(8,128)(2,1)} %get-tuple-element.81), channel_id=1, source_target_pairs={{0,1},{1,0},{2,3},{3,2},{4,5},{5,4},{6,7},{7,6},{8,9},{9,8},{10,11... | collective-permute-start | bytes 718856 | tf_op jit(solution)/shard_map/ppermute | solution.py:430
  15.4 19.3 %collective-permute-start.4 = (bf16[208,576]{1,0:T(8,128)(2,1)}, bf16[208,576]{1,0:T(8,128)(2,1)}, u32[]{:S(2)}, u32[]{:S(2)}) collective-permute-start(bf16[208,576]{1,0:T(8,128)(2,1)} %get-tuple-element.82), channel_id=1, source_target_pairs={{0,2},{1,3},{2,0},{3,1},{4,6},{5,7},{6,4},{7,5},{8,10},{9,11},{10,... | collective-permute-start | bytes 718856 | tf_op jit(solution)/shard_map/ppermute | solution.py:430
  15.4 23.3 %collective-permute-start.5 = (bf16[208,576]{1,0:T(8,128)(2,1)}, bf16[208,576]{1,0:T(8,128)(2,1)}, u32[]{:S(2)}, u32[]{:S(2)}) collective-permute-start(bf16[208,576]{1,0:T(8,128)(2,1)} %get-tuple-element.83), channel_id=1, source_target_pairs={{0,3},{1,2},{2,1},{3,0},{4,7},{5,6},{6,5},{7,4},{8,11},{9,10},{10,... | collective-permute-start | bytes 718856 | tf_op jit(solution)/shard_map/ppermute | solution.py:430
  24.4 16.5 %copy-start.3 = (bf16[512,768]{1,0:T(8,128)(2,1)S(1)}, bf16[512,768]{1,0:T(8,128)(2,1)}, u32[]{:S(2)}) copy-start(bf16[512,768]{1,0:T(8,128)(2,1)} %refs_0_.3) | copy-start | bytes 2359300
  24.4 16.5 %copy-start.43 = (f32[576,1]{1,0:T(8,128)S(1)}, f32[576,1]{1,0:T(8,128)}, u32[]{:S(2)}) copy-start(f32[576,1]{1,0:T(8,128)} %broadcast_in_dim.54.refs_8_) | copy-start | bytes 6916
  24.4 16.5 %copy-start.48 = (bf16[208,576]{1,0:T(8,128)(2,1)S(1)}, bf16[208,576]{1,0:T(8,128)(2,1)}, u32[]{:S(2)}) copy-start(bf16[208,576]{1,0:T(8,128)(2,1)} %copy-done.47) | copy-start | bytes 718852
  28.8 12.1 %copy-start.36 = (bf16[512,768]{1,0:T(8,128)(2,1)}, bf16[512,768]{1,0:T(8,128)(2,1)S(1)}, u32[]{:S(2)}) copy-start(bf16[512,768]{1,0:T(8,128)(2,1)S(1)} %collective-permute-done.1.refs_2_) | copy-start | bytes 2359300
  28.8 9.9 %collective-permute-start.2 = (bf16[512,768]{1,0:T(8,128)(2,1)S(1)}, bf16[512,768]{1,0:T(8,128)(2,1)S(1)}, u32[]{:S(2)}, u32[]{:S(2)}) collective-permute-start(bf16[512,768]{1,0:T(8,128)(2,1)S(1)} %collective-permute-done.1.refs_2_), channel_id=1, source_target_pairs={{0,1},{1,0},{2,3},{3,2},{4,5},{5,4},{6,7},{7,6},{8,9},{9,8},{10,11... | collective-permute-start | bytes 2359304 | tf_op jit(solution)/shard_map/ppermute | solution.py:430
  38.8 9.9 %copy-start.39 = (bf16[512,768]{1,0:T(8,128)(2,1)}, bf16[512,768]{1,0:T(8,128)(2,1)S(1)}, u32[]{:S(2)}) copy-start(bf16[512,768]{1,0:T(8,128)(2,1)S(1)} %collective-permute-done.2.refs_3_) | copy-start | bytes 2359300
  38.8 19.7 %collective-permute-start.6 = (bf16[96,3840]{1,0:T(8,128)(2,1)S(1)}, bf16[96,3840]{1,0:T(8,128)(2,1)}, u32[]{:S(2)}, u32[]{:S(2)}) collective-permute-start(bf16[96,3840]{1,0:T(8,128)(2,1)S(1)} %get-tuple-element.90), channel_id=1, source_target_pairs={{0,2},{1,3},{2,0},{3,1},{4,6},{5,7},{6,4},{7,5},{8,10},{9,11},{10,... | collective-permute-start | bytes 2211848 | tf_op jit(solution)/shard_map/ppermute | solution.py:430
  40.2 35.1 %collective-permute-start.14 = (bf16[96,3072]{1,0:T(8,128)(2,1)S(1)}, bf16[96,3072]{1,0:T(8,128)(2,1)}, u32[]{:S(2)}, u32[]{:S(2)}) collective-permute-start(bf16[96,3072]{1,0:T(8,128)(2,1)S(1)} %get-tuple-element.96), channel_id=1, source_target_pairs={{0,2},{1,3},{2,0},{3,1},{4,6},{5,7},{6,4},{7,5},{8,10},{9,11},{10,... | collective-permute-start | bytes 1769480 | tf_op jit(solution)/shard_map/ppermute | solution.py:430
  40.9 52.8 %collective-permute-start.10 = (bf16[192,6912]{1,0:T(8,128)(2,1)}, bf16[192,6912]{1,0:T(8,128)(2,1)}, u32[]{:S(2)}, u32[]{:S(2)}) collective-permute-start(bf16[192,6912]{1,0:T(8,128)(2,1)} %get-tuple-element.94.refs_4_), channel_id=1, source_target_pairs={{0,1},{1,0},{2,3},{3,2},{4,5},{5,4},{6,7},{7,6},{8,9},{9,8},{10,11... | collective-permute-start | bytes 7962632 | tf_op jit(solution)/shard_map/ppermute | solution.py:430
  58.5 30.0 %collective-permute-start.11 = (bf16[96,3840]{1,0:T(8,128)(2,1)}, bf16[96,3840]{1,0:T(8,128)(2,1)}, u32[]{:S(2)}, u32[]{:S(2)}) collective-permute-start(bf16[96,3840]{1,0:T(8,128)(2,1)} %collective-permute-done.6.refs_6_), channel_id=1, source_target_pairs={{0,4},{4,0},{8,12},{12,8},{16,20},{20,16},{24,28},{28,24},{1,5},{5... | collective-permute-start | bytes 2211848 | tf_op jit(solution)/shard_map/ppermute | solution.py:430
  75.3 15.5 %collective-permute-start.15 = (bf16[96,3072]{1,0:T(8,128)(2,1)}, bf16[96,3072]{1,0:T(8,128)(2,1)}, u32[]{:S(2)}, u32[]{:S(2)}) collective-permute-start(bf16[96,3072]{1,0:T(8,128)(2,1)} %collective-permute-done.14.refs_10_), channel_id=1, source_target_pairs={{0,4},{4,0},{8,12},{12,8},{16,20},{20,16},{24,28},{28,24},{1,5},{5... | collective-permute-start | bytes 1769480 | tf_op jit(solution)/shard_map/ppermute | solution.py:430
  76.3 7.0 %collective-permute-start.9 = (bf16[192,512]{1,0:T(8,128)(2,1)S(1)}, bf16[192,512]{1,0:T(8,128)(2,1)S(1)}, u32[]{:S(2)}, u32[]{:S(2)}) collective-permute-start(bf16[192,512]{1,0:T(8,128)(2,1)S(1)} %pad_maximum_fusion.6), channel_id=1, source_target_pairs={{0,3},{1,2},{2,1},{3,0},{4,7},{5,6},{6,5},{7,4},{8,11},{9,10},{10,... | collective-permute-start | bytes 589832 | tf_op jit(solution)/shard_map/ppermute | solution.py:430
  77.2 10.6 %collective-permute-start.8 = (bf16[192,512]{1,0:T(8,128)(2,1)S(1)}, bf16[192,512]{1,0:T(8,128)(2,1)S(1)}, u32[]{:S(2)}, u32[]{:S(2)}) collective-permute-start(bf16[192,512]{1,0:T(8,128)(2,1)S(1)} %pad_maximum_fusion.5), channel_id=1, source_target_pairs={{0,2},{1,3},{2,0},{3,1},{4,6},{5,7},{6,4},{7,5},{8,10},{9,11},{10,... | collective-permute-start | bytes 589832 | tf_op jit(solution)/shard_map/ppermute | solution.py:430
  84.0 5.0 %collective-permute-start.7 = (bf16[192,512]{1,0:T(8,128)(2,1)S(1)}, bf16[192,512]{1,0:T(8,128)(2,1)S(1)}, u32[]{:S(2)}, u32[]{:S(2)}) collective-permute-start(bf16[192,512]{1,0:T(8,128)(2,1)S(1)} %pad_maximum_fusion.4), channel_id=1, source_target_pairs={{0,1},{1,0},{2,3},{3,2},{4,5},{5,4},{6,7},{7,6},{8,9},{9,8},{10,11... | collective-permute-start | bytes 589832 | tf_op jit(solution)/shard_map/ppermute | solution.py:430
  88.4 4.5 %collective-permute-start.12 = (bf16[96,3840]{1,0:T(8,128)(2,1)}, bf16[96,3840]{1,0:T(8,128)(2,1)}, u32[]{:S(2)}, u32[]{:S(2)}) collective-permute-start(bf16[96,3840]{1,0:T(8,128)(2,1)} %collective-permute-done.6.refs_6_), channel_id=1, source_target_pairs={{0,1},{1,0},{2,3},{3,2},{4,5},{5,4},{6,7},{7,6},{8,9},{9,8},{10,11... | collective-permute-start | bytes 2211848 | tf_op jit(solution)/shard_map/ppermute | solution.py:430
  88.4 5.3 %collective-permute-start.13 = (bf16[96,3840]{1,0:T(8,128)(2,1)}, bf16[96,3840]{1,0:T(8,128)(2,1)}, u32[]{:S(2)}, u32[]{:S(2)}) collective-permute-start(bf16[96,3840]{1,0:T(8,128)(2,1)} %collective-permute-done.11.refs_7_), channel_id=1, source_target_pairs={{0,1},{1,0},{2,3},{3,2},{4,5},{5,4},{6,7},{7,6},{8,9},{9,8},{10,11... | collective-permute-start | bytes 2211848 | tf_op jit(solution)/shard_map/ppermute | solution.py:430
  89.6 3.3 collective-permute-start.16
  90.8 2.9 collective-permute-start.17
  133.4 4.9 %collective-permute-start.21 = (bf16[2,192,3072]{2,1,0:T(8,128)(2,1)}, bf16[2,192,3072]{2,1,0:T(8,128)(2,1)}, u32[]{:S(2)}, u32[]{:S(2)}) collective-permute-start(bf16[2,192,3072]{2,1,0:T(8,128)(2,1)} %get-tuple-element.107), channel_id=1, source_target_pairs={{0,1},{1,0},{2,3},{3,2},{4,5},{5,4},{6,7},{7,6},{8,9},{9,8},{10,11... | collective-permute-start | bytes 7077896 | tf_op jit(solution)/shard_map/ppermute | solution.py:430
  133.6 9.6 %collective-permute-start.22 = (bf16[2,192,3840]{2,1,0:T(8,128)(2,1)}, bf16[2,192,3840]{2,1,0:T(8,128)(2,1)}, u32[]{:S(2)}, u32[]{:S(2)}) collective-permute-start(bf16[2,192,3840]{2,1,0:T(8,128)(2,1)} %get-tuple-element.109), channel_id=1, source_target_pairs={{0,1},{1,0},{2,3},{3,2},{4,5},{5,4},{6,7},{7,6},{8,9},{9,8},{10,11... | collective-permute-start | bytes 8847368 | tf_op jit(solution)/shard_map/ppermute | solution.py:430
  134.0 13.6 %collective-permute-start.18 = (bf16[192,512]{1,0:T(8,128)(2,1)}, bf16[192,512]{1,0:T(8,128)(2,1)S(1)}, u32[]{:S(2)}, u32[]{:S(2)}) collective-permute-start(bf16[192,512]{1,0:T(8,128)(2,1)} %copy-done.55), channel_id=1, source_target_pairs={{0,1},{1,0},{2,3},{3,2},{4,5},{5,4},{6,7},{7,6},{8,9},{9,8},{10,11... | collective-permute-start | bytes 589832 | tf_op jit(solution)/shard_map/ppermute | solution.py:430
  134.1 13.5 %collective-permute-start.19 = (bf16[192,512]{1,0:T(8,128)(2,1)}, bf16[192,512]{1,0:T(8,128)(2,1)S(1)}, u32[]{:S(2)}, u32[]{:S(2)}) collective-permute-start(bf16[192,512]{1,0:T(8,128)(2,1)} %copy-done.54), channel_id=1, source_target_pairs={{0,2},{1,3},{2,0},{3,1},{4,6},{5,7},{6,4},{7,5},{8,10},{9,11},{10,... | collective-permute-start | bytes 589832 | tf_op jit(solution)/shard_map/ppermute | solution.py:430
  135.6 12.0 %collective-permute-start.20 = (bf16[192,512]{1,0:T(8,128)(2,1)}, bf16[192,512]{1,0:T(8,128)(2,1)S(1)}, u32[]{:S(2)}, u32[]{:S(2)}) collective-permute-start(bf16[192,512]{1,0:T(8,128)(2,1)} %copy-done.53), channel_id=1, source_target_pairs={{0,3},{1,2},{2,1},{3,0},{4,7},{5,6},{6,5},{7,4},{8,11},{9,10},{10,... | collective-permute-start | bytes 589832 | tf_op jit(solution)/shard_map/ppermute | solution.py:430
  147.6 46.7 %collective-permute-start.26 = (bf16[192,3072]{1,0:T(8,128)(2,1)}, bf16[192,3072]{1,0:T(8,128)(2,1)}, u32[]{:S(2)}, u32[]{:S(2)}) collective-permute-start(bf16[192,3072]{1,0:T(8,128)(2,1)} %get-tuple-element.123), channel_id=1, source_target_pairs={{0,2},{1,3},{2,0},{3,1},{4,6},{5,7},{6,4},{7,5},{8,10},{9,11},{10,... | collective-permute-start | bytes 3538952 | tf_op jit(solution)/shard_map/ppermute | solution.py:430
  149.5 48.3 %collective-permute-start.28 = (bf16[2,96,3840]{2,1,0:T(8,128)(2,1)}, bf16[2,96,3840]{2,1,0:T(8,128)(2,1)}, u32[]{:S(2)}, u32[]{:S(2)}) collective-permute-start(bf16[2,96,3840]{2,1,0:T(8,128)(2,1)} %get-tuple-element.126), channel_id=1, source_target_pairs={{0,4},{4,0},{8,12},{12,8},{16,20},{20,16},{24,28},{28,24},{1,5},{5... | collective-permute-start | bytes 4423688 | tf_op jit(solution)/shard_map/ppermute | solution.py:430
  174.4 8.2 %copy-start.6 = (bf16[512,768]{1,0:T(8,128)(2,1)S(1)}, bf16[512,768]{1,0:T(8,128)(2,1)}, u32[]{:S(2)}) copy-start(bf16[512,768]{1,0:T(8,128)(2,1)} %refs_0_.3) | copy-start | bytes 2359300
  182.6 11.7 %copy-start.59 = (bf16[192,3072]{1,0:T(8,128)(2,1)S(1)}, bf16[192,3072]{1,0:T(8,128)(2,1)}, u32[]{:S(2)}) copy-start(bf16[192,3072]{1,0:T(8,128)(2,1)} %get-tuple-element.122) | copy-start | bytes 3538948
  193.8 92.1 %copy-start.9 = (bf16[2,512,768]{2,1,0:T(8,128)(2,1)}, bf16[2,512,768]{2,1,0:T(8,128)(2,1)S(1)}, u32[]{:S(2)}) copy-start(bf16[2,512,768]{2,1,0:T(8,128)(2,1)S(1)} %get-tuple-element.118) | copy-start | bytes 4718596
  193.8 37.5 %collective-permute-start.25 = (bf16[4,96,588]{2,1,0:T(8,128)(2,1)S(1)}, bf16[4,96,588]{2,1,0:T(8,128)(2,1)S(1)}, u32[]{:S(2)}, u32[]{:S(2)}) collective-permute-start(bf16[4,96,588]{2,1,0:T(8,128)(2,1)S(1)} %get-tuple-element.121), channel_id=1, source_target_pairs={{0,4},{4,0},{8,12},{12,8},{16,20},{20,16},{24,28},{28,24},{1,5},{5... | collective-permute-start | bytes 1354760 | tf_op jit(solution)/shard_map/ppermute | solution.py:430
  194.3 69.3 %collective-permute-start.23 = (bf16[2,512,768]{2,1,0:T(8,128)(2,1)}, bf16[2,512,768]{2,1,0:T(8,128)(2,1)}, u32[]{:S(2)}, u32[]{:S(2)}) collective-permute-start(bf16[2,512,768]{2,1,0:T(8,128)(2,1)} %get-tuple-element.119), channel_id=1, source_target_pairs={{0,1},{1,0},{2,3},{3,2},{4,5},{5,4},{6,7},{7,6},{8,9},{9,8},{10,11... | collective-permute-start | bytes 4718600 | tf_op jit(solution)/shard_map/ppermute | solution.py:430
  196.2 23.2 %collective-permute-start.27 = (bf16[96,3072]{1,0:T(8,128)(2,1)S(1)}, bf16[96,3072]{1,0:T(8,128)(2,1)S(1)}, u32[]{:S(2)}, u32[]{:S(2)}) collective-permute-start(bf16[96,3072]{1,0:T(8,128)(2,1)S(1)} %constant_dynamic-slice_fusion.11), channel_id=1, source_target_pairs={{0,4},{4,0},{8,12},{12,8},{16,20},{20,16},{24,28},{28,24},{1,5},{5... | collective-permute-start | bytes 1769480 | tf_op jit(solution)/shard_map/ppermute | solution.py:430
  199.1 22.1 %collective-permute-start.30 = (bf16[96,3840]{1,0:T(8,128)(2,1)S(1)}, bf16[96,3840]{1,0:T(8,128)(2,1)S(1)}, u32[]{:S(2)}, u32[]{:S(2)}) collective-permute-start(bf16[96,3840]{1,0:T(8,128)(2,1)S(1)} %fusion.16), channel_id=1, source_target_pairs={{0,2},{1,3},{2,0},{3,1},{4,6},{5,7},{6,4},{7,5},{8,10},{9,11},{10,... | collective-permute-start | bytes 2211848 | tf_op jit(solution)/shard_map/ppermute | solution.py:430
  219.6 11.6 %collective-permute-start.29 = (bf16[48,3072]{1,0:T(8,128)(2,1)S(1)}, bf16[48,3072]{1,0:T(8,128)(2,1)S(1)}, u32[]{:S(2)}, u32[]{:S(2)}) collective-permute-start(bf16[48,3072]{1,0:T(8,128)(2,1)S(1)} %constant_dynamic-slice_fusion.10), channel_id=1, source_target_pairs={{0,8},{4,12},{8,0},{12,4},{16,24},{20,28},{24,16},{28,20},{1,9},{5... | collective-permute-start | bytes 884744 | tf_op jit(solution)/shard_map/ppermute | solution.py:430
  222.7 20.0 %collective-permute-start.33 = (bf16[48,3840]{1,0:T(8,128)(2,1)S(1)}, bf16[48,3840]{1,0:T(8,128)(2,1)S(1)}, u32[]{:S(2)}, u32[]{:S(2)}) collective-permute-start(bf16[48,3840]{1,0:T(8,128)(2,1)S(1)} %constant_dynamic-slice_fusion.7), channel_id=1, source_target_pairs={{0,8},{4,12},{8,0},{12,4},{16,24},{20,28},{24,16},{28,20},{1,9},{5... | collective-permute-start | bytes 1105928 | tf_op jit(solution)/shard_map/ppermute | solution.py:430
  231.3 13.2 %collective-permute-start.32 = (bf16[24,3072]{1,0:T(8,128)(2,1)S(1)}, bf16[24,3072]{1,0:T(8,128)(2,1)S(1)}, u32[]{:S(2)}, u32[]{:S(2)}) collective-permute-start(bf16[24,3072]{1,0:T(8,128)(2,1)S(1)} %constant_dynamic-slice_fusion.8), channel_id=1, source_target_pairs={{0,16},{4,20},{8,24},{12,28},{16,0},{20,4},{24,8},{28,12},{1,17},{... | collective-permute-start | bytes 442376 | tf_op jit(solution)/shard_map/ppermute | solution.py:430
  232.5 13.3 %collective-permute-start.31 = (bf16[4,48,588]{2,1,0:T(8,128)(2,1)S(1)}, bf16[4,48,588]{2,1,0:T(8,128)(2,1)S(1)}, u32[]{:S(2)}, u32[]{:S(2)}) collective-permute-start(bf16[4,48,588]{2,1,0:T(8,128)(2,1)S(1)} %constant_dynamic-slice_fusion.9), channel_id=1, source_target_pairs={{0,8},{4,12},{8,0},{12,4},{16,24},{20,28},{24,16},{28,20},{1,9},{5... | collective-permute-start | bytes 677384 | tf_op jit(solution)/shard_map/ppermute | solution.py:430
  242.8 12.6 %collective-permute-start.35 = (bf16[24,3840]{1,0:T(8,128)(2,1)S(1)}, bf16[24,3840]{1,0:T(8,128)(2,1)S(1)}, u32[]{:S(2)}, u32[]{:S(2)}) collective-permute-start(bf16[24,3840]{1,0:T(8,128)(2,1)S(1)} %constant_dynamic-slice_fusion.5), channel_id=1, source_target_pairs={{0,16},{4,20},{8,24},{12,28},{16,0},{20,4},{24,8},{28,12},{1,17},{... | collective-permute-start | bytes 552968 | tf_op jit(solution)/shard_map/ppermute | solution.py:430
  245.9 10.8 %collective-permute-start.34 = (bf16[4,24,588]{2,1,0:T(8,128)(2,1)S(1)}, bf16[4,24,588]{2,1,0:T(8,128)(2,1)S(1)}, u32[]{:S(2)}, u32[]{:S(2)}) collective-permute-start(bf16[4,24,588]{2,1,0:T(8,128)(2,1)S(1)} %constant_dynamic-slice_fusion.6), channel_id=1, source_target_pairs={{0,16},{4,20},{8,24},{12,28},{16,0},{20,4},{24,8},{28,12},{1,17},{... | collective-permute-start | bytes 338696 | tf_op jit(solution)/shard_map/ppermute | solution.py:430
  261.7 4.5 %collective-permute-start.36 = (bf16[24,626]{1,0:T(8,128)(2,1)S(1)}, bf16[24,626]{1,0:T(8,128)(2,1)S(1)}, u32[]{:S(2)}, u32[]{:S(2)}) collective-permute-start(bf16[24,626]{1,0:T(8,128)(2,1)S(1)} %get-tuple-element.169), channel_id=1, source_target_pairs={{0,1},{1,0},{2,3},{3,2},{4,5},{5,4},{6,7},{7,6},{8,9},{9,8},{10,11... | collective-permute-start | bytes 90152 | tf_op jit(solution)/shard_map/ppermute | solution.py:430
  261.8 4.4 %collective-permute-start.37 = (bf16[24,626]{1,0:T(8,128)(2,1)S(1)}, bf16[24,626]{1,0:T(8,128)(2,1)S(1)}, u32[]{:S(2)}, u32[]{:S(2)}) collective-permute-start(bf16[24,626]{1,0:T(8,128)(2,1)S(1)} %get-tuple-element.170), channel_id=1, source_target_pairs={{0,2},{1,3},{2,0},{3,1},{4,6},{5,7},{6,4},{7,5},{8,10},{9,11},{10,... | collective-permute-start | bytes 90152 | tf_op jit(solution)/shard_map/ppermute | solution.py:430
  262.2 4.0 %collective-permute-start.38 = (bf16[24,626]{1,0:T(8,128)(2,1)S(1)}, bf16[24,626]{1,0:T(8,128)(2,1)S(1)}, u32[]{:S(2)}, u32[]{:S(2)}) collective-permute-start(bf16[24,626]{1,0:T(8,128)(2,1)S(1)} %get-tuple-element.171), channel_id=1, source_target_pairs={{0,3},{1,2},{2,1},{3,0},{4,7},{5,6},{6,5},{7,4},{8,11},{9,10},{10,... | collective-permute-start | bytes 90152 | tf_op jit(solution)/shard_map/ppermute | solution.py:430
  265.8 20.0 %copy-start.7 = (bf16[512,768]{1,0:T(8,128)(2,1)S(1)}, bf16[512,768]{1,0:T(8,128)(2,1)}, u32[]{:S(2)}) copy-start(bf16[512,768]{1,0:T(8,128)(2,1)} %refs_0_.3) | copy-start | bytes 2359300
  265.8 20.0 %copy-start.65 = (f32[768]{0:T(1024)S(1)}, f32[768]{0:T(1024)}, u32[]{:S(2)}) copy-start(f32[768]{0:T(1024)} %slice_reduce_fusion.1) | copy-start | bytes 9220
  265.8 20.0 %collective-permute-start.24 = (bf16[512,768]{1,0:T(8,128)(2,1)}, bf16[512,768]{1,0:T(8,128)(2,1)S(1)}, u32[]{:S(2)}, u32[]{:S(2)}) collective-permute-start(bf16[512,768]{1,0:T(8,128)(2,1)} %fusion.15), channel_id=1, source_target_pairs={{0,2},{1,3},{2,0},{3,1},{4,6},{5,7},{6,4},{7,5},{8,10},{9,11},{10,... | collective-permute-start | bytes 2359304 | tf_op jit(solution)/shard_map/ppermute | solution.py:430
  273.2 26.3 %copy-start.27 = (f32[512,768]{1,0:T(8,128)S(1)}, f32[512,768]{1,0:T(8,128)}, u32[]{:S(2)}) copy-start(f32[512,768]{1,0:T(8,128)} %copy-done.26) | copy-start | bytes 4718596
  273.2 26.3 %copy-start.67 = (f32[512]{0:T(512)S(1)}, f32[512]{0:T(512)}, u32[]{:S(2)}) copy-start(f32[512]{0:T(512)} %copy-done.66) | copy-start | bytes 6148
  273.2 26.3 %copy-start.68 = (f32[512]{0:T(512)S(1)}, f32[512]{0:T(512)}, u32[]{:S(2)}) copy-start(f32[512]{0:T(512)} %add_rsqrt_fusion) | copy-start | bytes 6148
  273.2 26.3 %copy-start.71 = (pred[512]{0:T(512)(128)(4,1)S(1)}, pred[512]{0:T(512)(128)(4,1)}, u32[]{:S(2)}) copy-start(pred[512]{0:T(512)(128)(4,1)} %iota_compare_fusion.1) | copy-start | bytes 1540
  273.2 14.8 %collective-permute-start.39 = (bf16[1,24,2318]{2,1,0:T(8,128)(2,1)S(1)}, bf16[1,24,2318]{2,1,0:T(8,128)(2,1)S(1)}, u32[]{:S(2)}, u32[]{:S(2)}) collective-permute-start(bf16[1,24,2318]{2,1,0:T(8,128)(2,1)S(1)} %bitcast.127), channel_id=1, source_target_pairs={{0,16},{4,20},{8,24},{12,28},{16,0},{20,4},{24,8},{28,12},{1,17},{... | collective-permute-start | bytes 333800 | tf_op jit(solution)/shard_map/ppermute | solution.py:430
  288.1 11.5 %copy-start.62 = (bf16[512,768]{1,0:T(8,128)(2,1)S(1)}, bf16[512,768]{1,0:T(8,128)(2,1)}, u32[]{:S(2)}) copy-start(bf16[512,768]{1,0:T(8,128)(2,1)} %copy-done.61) | copy-start | bytes 2359300
  288.1 11.2 %collective-permute-start.40 = (bf16[2,24,2318]{2,1,0:T(8,128)(2,1)S(1)}, bf16[2,24,2318]{2,1,0:T(8,128)(2,1)S(1)}, u32[]{:S(2)}, u32[]{:S(2)}) collective-permute-start(bf16[2,24,2318]{2,1,0:T(8,128)(2,1)S(1)} %pad_maximum_fusion.2), channel_id=1, source_target_pairs={{0,8},{4,12},{8,0},{12,4},{16,24},{20,28},{24,16},{28,20},{1,9},{5... | collective-permute-start | bytes 667592 | tf_op jit(solution)/shard_map/ppermute | solution.py:430
  299.4 19.3 %collective-permute-start.41 = (bf16[4,24,2318]{2,1,0:T(8,128)(2,1)S(1)}, bf16[4,24,2318]{2,1,0:T(8,128)(2,1)S(1)}, u32[]{:S(2)}, u32[]{:S(2)}) collective-permute-start(bf16[4,24,2318]{2,1,0:T(8,128)(2,1)S(1)} %pad_maximum_fusion.refs_1_), channel_id=1, source_target_pairs={{0,4},{4,0},{8,12},{12,8},{16,20},{20,16},{24,28},{28,24},{1,5},{5... | collective-permute-start | bytes 1335176 | tf_op jit(solution)/shard_map/ppermute | solution.py:430
  299.5 21.7 %copy-start.69 = (f32[12,192]{1,0:T(8,128)S(1)}, f32[12,192]{1,0:T(8,128)}, u32[]{:S(2)}) copy-start(f32[12,192]{1,0:T(8,128)} %param.24) | copy-start | bytes 27652
  299.5 21.7 %copy-start.70 = (f32[12,192]{1,0:T(8,128)S(1)}, f32[12,192]{1,0:T(8,128)}, u32[]{:S(2)}) copy-start(f32[12,192]{1,0:T(8,128)} %param.25) | copy-start | bytes 27652
  299.6 29.8 %copy-start.2 = (f32[192,3072]{1,0:T(8,128)S(1)}, f32[192,3072]{1,0:T(8,128)}, u32[]{:S(2)}) copy-start(f32[192,3072]{1,0:T(8,128)} %out_ref.1) | copy-start | bytes 7077892
  321.2 29.3 %copy-start.64 = (f32[192,12]{0,1:T(8,128)}, f32[192,12]{0,1:T(8,128)S(1)}, u32[]{:S(2)}) copy-start(f32[192,12]{0,1:T(8,128)S(1)} %copy.55) | copy-start | bytes 27652
  (53 other events, 163.4 us)
Sparse Core Ops, SparseCore 0:
  261.4 67.8 all-gather.2

commit v7 on v5

--- a/solution.py
+++ b/solution.py
@@ -335,7 +335,7 @@
         y_scr[...] = r1 + bp
         da2_scr[...] = jnp.zeros_like(da2_scr)
 
-    @pl.when(step == first_blocks)
+    @pl.when(step == split // width - 1)
     def _():
         for copy in copies(1):
             copy.wait()
@@ -648,7 +648,7 @@
 
         steps = blocks
         live_own = lax.dynamic_index_in_dim(counts[0], place, 0, keepdims=True)
-        first_blocks = fc_rows // 2 * 2
+        first_blocks = fc_rows // 2 * 2 + 1
 
         def grad_spec(k):
             first, last = ((0, first_blocks - 1), (first_blocks, steps - 1))[k]
@@ -699,11 +699,10 @@
         got_a = swap(send_a, "shard", 1, parts)
         got_b = swap(send_b, "shard", 1, parts)
         own_a, other_a = [add_low(keep_a[n], got_a[n]) for n in range(2)]
+        got_a = swap(other_a, "shard", parts // 2, parts)
+        got_b = after(got_b, own_a, other_a)
         own_b, other_b = halve(add_low(keep_b, got_b), half, 1)
-        *do_own, own_a, other_a, own_b, other_b = lax.optimization_barrier(
-            (*do_own, own_a, other_a, own_b, other_b)
-        )
-        got_a = swap(other_a, "shard", parts // 2, parts)
+        *do_own, own_b, other_b = lax.optimization_barrier((*do_own, own_b, other_b))
         got_b = swap(other_b, "dp", 1, replicas)
 
         def attend_back(h, qkv):
@@ -887,7 +886,7 @@
             ),
             out_shape=[jax.ShapeDtypeStruct(attn_shape, HIGH)] * 4
             + [jax.ShapeDtypeStruct(mlp_shape, HIGH)] * 4,
-            compiler_params=params(20),
+            compiler_params=params(50),
             cost_estimate=cost(30 * 9 * rows * width, 54e6),
             name="adam",
         )(

time: 345 us -> 340 us (0.986)
  local copies, waits for them, and re-layouts: 40.9 us -> 24.8 us
  Pallas kernels: 107 us -> 117 us
  waiting for transfers between devices: 104 us -> 111 us
    unnamed x129 -> x103, local copies, waits for them, and re-layouts: 34.7 us -> 18.5 us
    pallas_call x1, Pallas kernels: 10.7 us -> 19.2 us  [on_device(): pl.pallas_call(functools.partial(adam_kernel, fc_rows), grid_spec=pltpu.P...]
    ppermute x42, waiting for transfers between devices: 98.6 us -> 104 us  [swap(): return lax.ppermute(array, axis, [(i, i ^ bit) for i in range(count)])]
  transfers between devices with their start and end apart: 43 -> 43, of which waited for: 28 -> 24; matrix products, arithmetic and copies ran while one was open for 9% -> 9% of each run, Pallas kernels for 19% -> 19%
where the time goes in v7:
time: 340 us; the launch traced here: 335 us
  Pallas kernels  117 us (34%)
  waiting for transfers between devices  111 us (33%)
  starting transfers between devices  34.4 us (10%)
  other arithmetic  24.9 us (7%)
  local copies, waits for them, and re-layouts  24.8 us (7%)
  between operations  23.5 us (7%)
    ppermute x42, waiting for transfers between devices, swap(): return lax.ppermute(array, axis, [(i, i ^ bit) for i in range(count)])  104 us
    ppermute x42, starting transfers between devices, swap(): return lax.ppermute(array, axis, [(i, i ^ bit) for i in range(count)])  34.4 us
    pallas_call x1, Pallas kernels, on_device(): pl.pallas_call(functools.partial(mlp_kernel, parts, first_blocks), grid_s...  33 us
    pallas_call x3, Pallas kernels, attend_back(): pl.pallas_call(functools.partial(attend_back_kernel, scale), grid_spec=pl...  24 us
    pallas_call x3, Pallas kernels, attend(): pl.pallas_call(functools.partial(attend_kernel, scale), grid_spec=pltpu.P...  19.5 us
    pallas_call x1, Pallas kernels, on_device(): pl.pallas_call(functools.partial(adam_kernel, fc_rows), grid_spec=pltpu.P...  19.2 us
    unnamed x103, local copies, waits for them, and re-layouts  18.5 us
    pallas_call x1, Pallas kernels, on_device(): pl.pallas_call(functools.partial(projection_back_kernel, own_heads, parts...  11 us
  transfers between devices with their start and end apart: 43, of which 24 were waited for; matrix products, arithmetic and copies ran while one was open for 9% of the time, Pallas kernels for 19%

profile of v7, /device:TPU:0, one launch (start us, length us, event | category | flops | bytes accessed | tf_op | source)
XLA Modules:
  0.0 335.5 jit_solution(17911194551634729821)
XLA Ops:
  7.2 3.0 collective-permute-start.1
  10.3 1.7 copy-done
  12.6 1.5 cut.1
  14.7 1.3 collective-permute-start.5
  17.5 1.3 copy.49
  19.5 2.3 copy-done.3
  21.8 1.9 widen.1
  23.7 5.2 %collective-permute-done.1.refs_2_ = bf16[512,768]{1,0:T(8,128)(2,1)} collective-permute-done((bf16[512,768]{1,0:T(8,128)(2,1)}, bf16[512,768]{1,0:T(8,128)(2,1)}, u32[]{:S(2)}, u32[]{:S(2)}) %collective-permute-start.1) | collective-permute-done | bytes 786464 | tf_op jit(solution)/shard_map/ppermute | solution.py:430
  29.9 4.8 %collective-permute-done.4.refs_6_ = bf16[208,576]{1,0:T(8,128)(2,1)} collective-permute-done((bf16[208,576]{1,0:T(8,128)(2,1)}, bf16[208,576]{1,0:T(8,128)(2,1)}, u32[]{:S(2)}, u32[]{:S(2)}) %collective-permute-start.4) | collective-permute-done | bytes 239648 | tf_op jit(solution)/shard_map/ppermute | solution.py:430
  34.6 4.1 %collective-permute-done.5.refs_7_ = bf16[208,576]{1,0:T(8,128)(2,1)} collective-permute-done((bf16[208,576]{1,0:T(8,128)(2,1)}, bf16[208,576]{1,0:T(8,128)(2,1)}, u32[]{:S(2)}, u32[]{:S(2)}) %collective-permute-start.5) | collective-permute-done | bytes 239648 | tf_op jit(solution)/shard_map/ppermute | solution.py:430
  38.8 1.4 collective-permute-start.6
  41.0 0.9 copy-done.26
  41.9 6.5 %project.1 = (bf16[2048,768]{1,0:T(8,128)(2,1)S(1)}, bf16[576,2048]{1,0:T(8,128)(2,1)S(1)}, bf16[576,768]{1,0:T(8,128)(2,1)S(1)}, f32[16,768]{1,0:T(8,128)S(1)}) custom-call(s32[1]{0:T(128)} %bitcast.place, bf16[512,768]{1,0:T(8,128)(2,1)S(1)} %copy-done.4, bf16[512,768]{1,0:T(8,128)(2,1)} %collective-permute-done.refs_1_, ...), custom_call_target="tpu_custom_call" | custom-call | flops 5435817984 | bytes 12000000 | tf_op jit(solution)/shard_map/project/pallas_call | solution.py:570
  48.4 1.7 copy-done.36
  50.1 6.4 %attend.3 = (bf16[4,64,512]{2,1,0:T(8,128)(2,1)S(1)}, f32[1,2048,1]{2,1,0:T(8,128)S(1)}) custom-call(s32[1]{0:T(128)} %bitcast.place, bf16[576,2048]{1,0:T(8,128)(2,1)S(1)} %get-tuple-element.94.qt_ref.kt_ref.vt_ref, bf16[576,2048]{1,0:T(8,128)(2,1)S(1)} %get-tuple-element.94.qt_ref.kt_ref.vt_ref, ...), custom_call_target="tpu_custom_call" | custom-call | flops 2147483648 | bytes 4000000 | tf_op jit(solution)/shard_map/attend/pallas_call | solution.py:612
  56.5 1.0 copy-done.15
  58.2 1.6 collective-permute-start.11
  59.8 6.4 %attend.5 = (bf16[4,64,512]{2,1,0:T(8,128)(2,1)S(1)}, f32[1,2048,1]{2,1,0:T(8,128)S(1)}) custom-call(s32[1]{0:T(128)} %bitcast.place, bf16[576,2048]{1,0:T(8,128)(2,1)S(1)} %get-tuple-element.94.qt_ref.kt_ref.vt_ref, bf16[576,2048]{1,0:T(8,128)(2,1)S(1)} %get-tuple-element.94.qt_ref.kt_ref.vt_ref, ...), custom_call_target="tpu_custom_call" | custom-call | flops 2147483648 | bytes 4000000 | tf_op jit(solution)/shard_map/attend/pallas_call | solution.py:612
  66.3 1.0 copy-done.17
  67.3 6.7 %attend.4 = (bf16[4,64,512]{2,1,0:T(8,128)(2,1)S(1)}, f32[1,2048,1]{2,1,0:T(8,128)S(1)}) custom-call(s32[1]{0:T(128)} %bitcast.place, bf16[576,2048]{1,0:T(8,128)(2,1)S(1)} %get-tuple-element.94.qt_ref.kt_ref.vt_ref, bf16[576,2048]{1,0:T(8,128)(2,1)S(1)} %get-tuple-element.94.qt_ref.kt_ref.vt_ref, ...), custom_call_target="tpu_custom_call" | custom-call | flops 2147483648 | bytes 4000000 | tf_op jit(solution)/shard_map/attend/pallas_call | solution.py:612
  75.9 0.9 collective-permute-start.8
  76.9 5.4 %collective-permute-done.9.refs_3_ = bf16[192,512]{1,0:T(8,128)(2,1)S(1)} collective-permute-done((bf16[192,512]{1,0:T(8,128)(2,1)S(1)}, bf16[192,512]{1,0:T(8,128)(2,1)S(1)}, u32[]{:S(2)}, u32[]{:S(2)}) %collective-permute-start.9) | collective-permute-done | bytes 196640 | tf_op jit(solution)/shard_map/ppermute | solution.py:430
  83.4 3.2 collective-permute-done.8.refs_2_
  88.6 1.3 collective-permute-done.15.refs_11_
  92.6 0.9 copy-done.31
  93.5 0.9 copy-done.33
  95.4 33.0 %mlp.1 = (bf16[512,768]{1,0:T(8,128)(2,1)}, bf16[2,192,3840]{2,1,0:T(8,128)(2,1)}, bf16[2,192,3840]{2,1,0:T(8,128)(2,1)}, bf16[2,192,3072]{2,1,0:T(8,128)(2,1)},...) custom-call(s32[1]{0:T(128)} %bitcast.place, ...), custom_call_target="tpu_custom_call" | custom-call | flops 16307453952 | bytes 30000000 | tf_op jit(solution)/shard_map/mlp/pallas_call | solution.py:662
  131.0 1.3 convert_reduce_fusion
  132.5 1.4 collective-permute-start.19
  134.2 2.0 collective-permute-done.22
  136.2 3.5 %fusion.13 = (bf16[192,3840]{1,0:T(8,128)(2,1)S(1)}, bf16[192,3840]{1,0:T(8,128)(2,1)S(1)}) fusion(bf16[2,192,3840]{2,1,0:T(8,128)(2,1)} %collective-permute-done.22, bf16[2,192,3840]{2,1,0:T(8,128)(2,1)} %get-tuple-element.111), kind=kLoop, calls=%fused_computation.21 | loop fusion | flops 5898240 | bytes 8847360 | tf_op jit(solution)/shard_map/convert_element_type | solution.py:462
  139.7 1.2 collective-permute-start.23
  140.9 2.5 add_convert_fusion
  143.7 1.6 collective-permute-start.24
  145.3 7.8 %attend_back.5.refs_7_ = bf16[3,64,2048]{2,1,0:T(8,128)(2,1)S(1)} custom-call(s32[1]{0:T(128)} %bitcast.place, bf16[576,2048]{1,0:T(8,128)(2,1)S(1)} %get-tuple-element.94.qt_ref.kt_ref.vt_ref, bf16[576,2048]{1,0:T(8,128)(2,1)S(1)} %get-tuple-element.94.qt_ref.kt_ref.vt_ref, bf16[576,2048]{1,0:T(8,128)(2,1)S(1)} %get-tuple-element.94.qt_ref.kt_ref.vt_ref, ...), custom_call_target="tpu_custom_call" | custom-call | flops 5368709120 | bytes 4000000 | tf_op jit(solution)/shard_map/attend_back/pallas_call | solution.py:709
  153.1 8.1 %attend_back.4.refs_6_ = bf16[3,64,2048]{2,1,0:T(8,128)(2,1)S(1)} custom-call(s32[1]{0:T(128)} %bitcast.place, bf16[576,2048]{1,0:T(8,128)(2,1)S(1)} %get-tuple-element.94.qt_ref.kt_ref.vt_ref, bf16[576,2048]{1,0:T(8,128)(2,1)S(1)} %get-tuple-element.94.qt_ref.kt_ref.vt_ref, bf16[576,2048]{1,0:T(8,128)(2,1)S(1)} %get-tuple-element.94.qt_ref.kt_ref.vt_ref, ...), custom_call_target="tpu_custom_call" | custom-call | flops 5368709120 | bytes 4000000 | tf_op jit(solution)/shard_map/attend_back/pallas_call | solution.py:709
  161.2 8.1 %attend_back.3.refs_5_ = bf16[3,64,2048]{2,1,0:T(8,128)(2,1)S(1)} custom-call(s32[1]{0:T(128)} %bitcast.place, bf16[576,2048]{1,0:T(8,128)(2,1)S(1)} %get-tuple-element.94.qt_ref.kt_ref.vt_ref, bf16[576,2048]{1,0:T(8,128)(2,1)S(1)} %get-tuple-element.94.qt_ref.kt_ref.vt_ref, bf16[576,2048]{1,0:T(8,128)(2,1)S(1)} %get-tuple-element.94.qt_ref.kt_ref.vt_ref, ...), custom_call_target="tpu_custom_call" | custom-call | flops 5368709120 | bytes 4000000 | tf_op jit(solution)/shard_map/attend_back/pallas_call | solution.py:709
  169.3 3.0 collective-permute-done.24
  172.3 3.4 %collective-permute-done.23 = bf16[192,3840]{1,0:T(8,128)(2,1)S(1)} collective-permute-done((bf16[192,3840]{1,0:T(8,128)(2,1)S(1)}, bf16[192,3840]{1,0:T(8,128)(2,1)S(1)}, u32[]{:S(2)}, u32[]{:S(2)}) %collective-permute-start.23) | collective-permute-done | bytes 1474592 | tf_op jit(solution)/shard_map/ppermute | solution.py:430
  176.1 1.7 collective-permute-start.28
  178.2 1.1 collective-permute-start.30
  179.3 11.0 %projection_back.1 = (bf16[2,512,768]{2,1,0:T(8,128)(2,1)S(1)}, bf16[2,512,768]{2,1,0:T(8,128)(2,1)}, bf16[4,96,588]{2,1,0:T(8,128)(2,1)S(1)}, bf16[4,96,588]{2,1,0:T(8,128)(2,1)S(1)}) custom-call(s32[1]{0:T(128)} %bitcast.place, s32[1]{0:T(128)} %bitcast.1.half, bf16[512,768]{1,0:T(8,128)(2,1)S(1)} %copy-done.5, ...), custom_call_target="tpu_custom_call" | custom-call | flops 7247757312 | bytes 16000000 | tf_op jit(solution)/shard_map/projection_back/pallas_call | solution.py:744
  191.0 4.6 %collective-permute-done.28 = bf16[96,3840]{1,0:T(8,128)(2,1)S(1)} collective-permute-done((bf16[96,3840]{1,0:T(8,128)(2,1)S(1)}, bf16[96,3840]{1,0:T(8,128)(2,1)S(1)}, u32[]{:S(2)}, u32[]{:S(2)}) %collective-permute-start.28) | collective-permute-done | bytes 737312 | tf_op jit(solution)/shard_map/ppermute | solution.py:430
  195.8 1.7 collective-permute-start.29
  198.2 8.6 %collective-permute-done.29 = bf16[48,3840]{1,0:T(8,128)(2,1)S(1)} collective-permute-done((bf16[48,3840]{1,0:T(8,128)(2,1)S(1)}, bf16[48,3840]{1,0:T(8,128)(2,1)S(1)}, u32[]{:S(2)}, u32[]{:S(2)}) %collective-permute-start.29) | collective-permute-done | bytes 368672 | tf_op jit(solution)/shard_map/ppermute | solution.py:430
  207.0 2.9 collective-permute-done.33
  210.0 3.9 %collective-permute-start.32 = (bf16[24,3840]{1,0:T(8,128)(2,1)S(1)}, bf16[24,3840]{1,0:T(8,128)(2,1)S(1)}, u32[]{:S(2)}, u32[]{:S(2)}) collective-permute-start(bf16[24,3840]{1,0:T(8,128)(2,1)S(1)} %constant_dynamic-slice_fusion.8), channel_id=1, source_target_pairs={{0,16},{4,20},{8,24},{12,28},{16,0},{20,4},{24,8},{28,12},{1,17},{... | collective-permute-start | bytes 552968 | tf_op jit(solution)/shard_map/ppermute | solution.py:430
  214.7 7.8 %collective-permute-done.32 = bf16[24,3840]{1,0:T(8,128)(2,1)S(1)} collective-permute-done((bf16[24,3840]{1,0:T(8,128)(2,1)S(1)}, bf16[24,3840]{1,0:T(8,128)(2,1)S(1)}, u32[]{:S(2)}, u32[]{:S(2)}) %collective-permute-start.32) | collective-permute-done | bytes 184352 | tf_op jit(solution)/shard_map/ppermute | solution.py:430
  222.6 1.5 collective-permute-done.31
  226.7 3.5 %collective-permute-done.34 = bf16[4,24,588]{2,1,0:T(8,128)(2,1)S(1)} collective-permute-done((bf16[4,24,588]{2,1,0:T(8,128)(2,1)S(1)}, bf16[4,24,588]{2,1,0:T(8,128)(2,1)S(1)}, u32[]{:S(2)}, u32[]{:S(2)}) %collective-permute-start.34) | collective-permute-done | bytes 112928 | tf_op jit(solution)/shard_map/ppermute | solution.py:430
  234.4 3.1 collective-permute-start.37
  237.8 1.7 collective-permute-done.37
  239.5 1.4 collective-permute-done.38
  246.7 13.7 %collective-permute-done.39 = bf16[1,24,2318]{2,1,0:T(8,128)(2,1)S(1)} collective-permute-done((bf16[1,24,2318]{2,1,0:T(8,128)(2,1)S(1)}, bf16[1,24,2318]{2,1,0:T(8,128)(2,1)S(1)}, u32[]{:S(2)}, u32[]{:S(2)}) %collective-permute-start.39) | collective-permute-done | bytes 111296 | tf_op jit(solution)/shard_map/ppermute | solution.py:430
  260.6 9.3 %collective-permute-done.40 = bf16[2,24,2318]{2,1,0:T(8,128)(2,1)S(1)} collective-permute-done((bf16[2,24,2318]{2,1,0:T(8,128)(2,1)S(1)}, bf16[2,24,2318]{2,1,0:T(8,128)(2,1)S(1)}, u32[]{:S(2)}, u32[]{:S(2)}) %collective-permute-start.40) | collective-permute-done | bytes 222560 | tf_op jit(solution)/shard_map/ppermute | solution.py:430
  269.9 1.5 collective-permute-start.41
  272.2 2.3 fusion.14
  274.5 1.1 collective-permute-start.26
  275.6 15.5 %collective-permute-done.41.refs_2_ = bf16[4,24,2318]{2,1,0:T(8,128)(2,1)} collective-permute-done((bf16[4,24,2318]{2,1,0:T(8,128)(2,1)S(1)}, bf16[4,24,2318]{2,1,0:T(8,128)(2,1)}, u32[]{:S(2)}, u32[]{:S(2)}) %collective-permute-start.41) | collective-permute-done | bytes 445088 | tf_op jit(solution)/shard_map/ppermute | solution.py:430
  294.2 2.3 fusion.35
  296.6 3.1 fusion.9
  299.6 7.2 %all-gather.3.cloned.1.call-done = bf16[192,6912]{1,0:T(8,128)(2,1)} async-done(((bf16[24,6912]{1,0:T(8,128)(2,1)}), bf16[192,6912]{1,0:T(8,128)(2,1)}) %all-gather.3.cloned.1.call-update) | async-done | bytes 2654224 | tf_op jit(solution)/shard_map/all_gather | solution.py:803
  306.9 1.0 copy-done.11
  307.9 19.2 %adam.1 = (f32[8,24,3072]{2,1,0:T(8,128)}, f32[8,24,3072]{2,1,0:T(8,128)}, f32[8,24,3072]{2,1,0:T(8,128)}, f32[8,24,3072]{2,1,0:T(8,128)}, f32[2,8,24,3072]{3,2,...) custom-call(f32[1]{0:T(128)} %bitcast.46.factor_ref, ...), custom_call_target="tpu_custom_call" | custom-call | flops 39813120 | bytes 54000000 | tf_op jit(solution)/shard_map/adam/pallas_call | solution.py:873
  (234 shorter events, 31.2 us)
Async XLA Ops:
  7.2 9.8 %copy-start.48 = (s32[1,4]{1,0:T(1,128)S(1)}, s32[1,4]{1,0:T(1,128)}, u32[]{:S(2)}) copy-start(s32[1,4]{1,0:T(1,128)} %param.16) | copy-start | bytes 52
  7.2 10.0 %copy-start.49 = (s32[1,2]{1,0:T(1,128)S(1)}, s32[1,2]{1,0:T(1,128)}, u32[]{:S(2)}) copy-start(s32[1,2]{1,0:T(1,128)} %param.15) | copy-start | bytes 28
  7.2 299.6 %all-gather.3.cloned.1.call-start = ((), (), s32[]{:S(2)}) async-start(), calls=%async_computation | async-start | bytes 2985984 | tf_op jit(solution)/shard_map/all_gather | solution.py:803
  7.2 21.7 %collective-permute-start.1 = (bf16[512,768]{1,0:T(8,128)(2,1)}, bf16[512,768]{1,0:T(8,128)(2,1)}, u32[]{:S(2)}, u32[]{:S(2)}) collective-permute-start(bf16[512,768]{1,0:T(8,128)(2,1)} %refs_0_.3), channel_id=1, source_target_pairs={{0,2},{1,3},{2,0},{3,1},{4,6},{5,7},{6,4},{7,5},{8,10},{9,11},{10,... | collective-permute-start | bytes 2359304 | tf_op jit(solution)/shard_map/ppermute | solution.py:430
  10.3 28.5 %collective-permute-start = (bf16[512,768]{1,0:T(8,128)(2,1)}, bf16[512,768]{1,0:T(8,128)(2,1)}, u32[]{:S(2)}, u32[]{:S(2)}) collective-permute-start(bf16[512,768]{1,0:T(8,128)(2,1)} %refs_0_.3), channel_id=1, source_target_pairs={{0,1},{1,0},{2,3},{3,2},{4,5},{5,4},{6,7},{7,6},{8,9},{9,8},{10,11... | collective-permute-start | bytes 2359304 | tf_op jit(solution)/shard_map/ppermute | solution.py:430
  12.6 6.8 %copy-start.1 = (f32[192,3072]{1,0:T(8,128)S(1)}, f32[192,3072]{1,0:T(8,128)}, u32[]{:S(2)}) copy-start(f32[192,3072]{1,0:T(8,128)} %out_ref.1) | copy-start | bytes 7077892
  14.1 9.6 %copy-start.23 = (bf16[208,576]{1,0:T(8,128)(2,1)}, bf16[208,576]{1,0:T(8,128)(2,1)S(1)}, u32[]{:S(2)}) copy-start(bf16[208,576]{1,0:T(8,128)(2,1)S(1)} %get-tuple-element.83.refs_4_) | copy-start | bytes 718852
  14.2 15.0 %collective-permute-start.3 = (bf16[208,576]{1,0:T(8,128)(2,1)}, bf16[208,576]{1,0:T(8,128)(2,1)S(1)}, u32[]{:S(2)}, u32[]{:S(2)}) collective-permute-start(bf16[208,576]{1,0:T(8,128)(2,1)} %get-tuple-element.84), channel_id=1, source_target_pairs={{0,1},{1,0},{2,3},{3,2},{4,5},{5,4},{6,7},{7,6},{8,9},{9,8},{10,11... | collective-permute-start | bytes 718856 | tf_op jit(solution)/shard_map/ppermute | solution.py:430
  14.7 20.0 %collective-permute-start.4 = (bf16[208,576]{1,0:T(8,128)(2,1)}, bf16[208,576]{1,0:T(8,128)(2,1)}, u32[]{:S(2)}, u32[]{:S(2)}) collective-permute-start(bf16[208,576]{1,0:T(8,128)(2,1)} %get-tuple-element.85), channel_id=1, source_target_pairs={{0,2},{1,3},{2,0},{3,1},{4,6},{5,7},{6,4},{7,5},{8,10},{9,11},{10,... | collective-permute-start | bytes 718856 | tf_op jit(solution)/shard_map/ppermute | solution.py:430
  14.7 24.0 %collective-permute-start.5 = (bf16[208,576]{1,0:T(8,128)(2,1)}, bf16[208,576]{1,0:T(8,128)(2,1)}, u32[]{:S(2)}, u32[]{:S(2)}) collective-permute-start(bf16[208,576]{1,0:T(8,128)(2,1)} %get-tuple-element.86), channel_id=1, source_target_pairs={{0,3},{1,2},{2,1},{3,0},{4,7},{5,6},{6,5},{7,4},{8,11},{9,10},{10,... | collective-permute-start | bytes 718856 | tf_op jit(solution)/shard_map/ppermute | solution.py:430
  21.8 7.2 %copy-start.42 = (s32[2048,1]{1,0:T(8,128)S(1)}, s32[2048,1]{1,0:T(8,128)}, u32[]{:S(2)}) copy-start(s32[2048,1]{1,0:T(8,128)} %copy.49) | copy-start | bytes 24580
  23.7 17.2 %copy-start.4 = (bf16[512,768]{1,0:T(8,128)(2,1)S(1)}, bf16[512,768]{1,0:T(8,128)(2,1)}, u32[]{:S(2)}) copy-start(bf16[512,768]{1,0:T(8,128)(2,1)} %refs_0_.3) | copy-start | bytes 2359300
  23.7 17.2 %copy-start.12 = (f32[576,1]{1,0:T(8,128)S(1)}, f32[576,1]{1,0:T(8,128)}, u32[]{:S(2)}) copy-start(f32[576,1]{1,0:T(8,128)} %broadcast_in_dim.54.refs_8_) | copy-start | bytes 6916
  28.9 12.0 %copy-start.24 = (bf16[208,576]{1,0:T(8,128)(2,1)S(1)}, bf16[208,576]{1,0:T(8,128)(2,1)}, u32[]{:S(2)}) copy-start(bf16[208,576]{1,0:T(8,128)(2,1)} %copy-done.23) | copy-start | bytes 718852
  28.9 9.8 %collective-permute-start.2 = (bf16[512,768]{1,0:T(8,128)(2,1)}, bf16[512,768]{1,0:T(8,128)(2,1)S(1)}, u32[]{:S(2)}, u32[]{:S(2)}) collective-permute-start(bf16[512,768]{1,0:T(8,128)(2,1)} %collective-permute-done.1.refs_2_), channel_id=1, source_target_pairs={{0,1},{1,0},{2,3},{3,2},{4,5},{5,4},{6,7},{7,6},{8,9},{9,8},{10,11... | collective-permute-start | bytes 2359304 | tf_op jit(solution)/shard_map/ppermute | solution.py:430
  38.8 9.6 %copy-start.21 = (bf16[512,768]{1,0:T(8,128)(2,1)}, bf16[512,768]{1,0:T(8,128)(2,1)S(1)}, u32[]{:S(2)}) copy-start(bf16[512,768]{1,0:T(8,128)(2,1)S(1)} %collective-permute-done.2.refs_3_) | copy-start | bytes 2359300
  38.8 19.4 %collective-permute-start.6 = (bf16[96,3840]{1,0:T(8,128)(2,1)S(1)}, bf16[96,3840]{1,0:T(8,128)(2,1)}, u32[]{:S(2)}, u32[]{:S(2)}) collective-permute-start(bf16[96,3840]{1,0:T(8,128)(2,1)S(1)} %get-tuple-element.93), channel_id=1, source_target_pairs={{0,2},{1,3},{2,0},{3,1},{4,6},{5,7},{6,4},{7,5},{8,10},{9,11},{10,... | collective-permute-start | bytes 2211848 | tf_op jit(solution)/shard_map/ppermute | solution.py:430
  40.2 33.8 %collective-permute-start.14 = (bf16[96,3072]{1,0:T(8,128)(2,1)S(1)}, bf16[96,3072]{1,0:T(8,128)(2,1)}, u32[]{:S(2)}, u32[]{:S(2)}) collective-permute-start(bf16[96,3072]{1,0:T(8,128)(2,1)S(1)} %get-tuple-element.99), channel_id=1, source_target_pairs={{0,2},{1,3},{2,0},{3,1},{4,6},{5,7},{6,4},{7,5},{8,10},{9,11},{10,... | collective-permute-start | bytes 1769480 | tf_op jit(solution)/shard_map/ppermute | solution.py:430
  40.9 51.7 %collective-permute-start.10 = (bf16[192,6912]{1,0:T(8,128)(2,1)}, bf16[192,6912]{1,0:T(8,128)(2,1)}, u32[]{:S(2)}, u32[]{:S(2)}) collective-permute-start(bf16[192,6912]{1,0:T(8,128)(2,1)} %get-tuple-element.97.refs_4_), channel_id=1, source_target_pairs={{0,1},{1,0},{2,3},{3,2},{4,5},{5,4},{6,7},{7,6},{8,9},{9,8},{10,11... | collective-permute-start | bytes 7962632 | tf_op jit(solution)/shard_map/ppermute | solution.py:430
  50.1 6.4 %copy-start.38 = (bf16[576,768]{1,0:T(8,128)(2,1)}, bf16[576,768]{1,0:T(8,128)(2,1)S(1)}, u32[]{:S(2)}) copy-start(bf16[576,768]{1,0:T(8,128)(2,1)S(1)} %get-tuple-element.128.refs_8_) | copy-start | bytes 2654212
  58.2 29.2 %collective-permute-start.11 = (bf16[96,3840]{1,0:T(8,128)(2,1)}, bf16[96,3840]{1,0:T(8,128)(2,1)}, u32[]{:S(2)}, u32[]{:S(2)}) collective-permute-start(bf16[96,3840]{1,0:T(8,128)(2,1)} %collective-permute-done.6.refs_6_), channel_id=1, source_target_pairs={{0,4},{4,0},{8,12},{12,8},{16,20},{20,16},{24,28},{28,24},{1,5},{5... | collective-permute-start | bytes 2211848 | tf_op jit(solution)/shard_map/ppermute | solution.py:430
  74.0 15.9 %collective-permute-start.15 = (bf16[96,3072]{1,0:T(8,128)(2,1)}, bf16[96,3072]{1,0:T(8,128)(2,1)}, u32[]{:S(2)}, u32[]{:S(2)}) collective-permute-start(bf16[96,3072]{1,0:T(8,128)(2,1)} %collective-permute-done.14.refs_10_), channel_id=1, source_target_pairs={{0,4},{4,0},{8,12},{12,8},{16,20},{20,16},{24,28},{28,24},{1,5},{5... | collective-permute-start | bytes 1769480 | tf_op jit(solution)/shard_map/ppermute | solution.py:430
  75.1 7.1 %collective-permute-start.9 = (bf16[192,512]{1,0:T(8,128)(2,1)S(1)}, bf16[192,512]{1,0:T(8,128)(2,1)S(1)}, u32[]{:S(2)}, u32[]{:S(2)}) collective-permute-start(bf16[192,512]{1,0:T(8,128)(2,1)S(1)} %pad_maximum_fusion.6), channel_id=1, source_target_pairs={{0,3},{1,2},{2,1},{3,0},{4,7},{5,6},{6,5},{7,4},{8,11},{9,10},{10,... | collective-permute-start | bytes 589832 | tf_op jit(solution)/shard_map/ppermute | solution.py:430
  75.9 10.7 %collective-permute-start.8 = (bf16[192,512]{1,0:T(8,128)(2,1)S(1)}, bf16[192,512]{1,0:T(8,128)(2,1)S(1)}, u32[]{:S(2)}, u32[]{:S(2)}) collective-permute-start(bf16[192,512]{1,0:T(8,128)(2,1)S(1)} %pad_maximum_fusion.5), channel_id=1, source_target_pairs={{0,2},{1,3},{2,0},{3,1},{4,6},{5,7},{6,4},{7,5},{8,10},{9,11},{10,... | collective-permute-start | bytes 589832 | tf_op jit(solution)/shard_map/ppermute | solution.py:430
  83.0 4.9 %collective-permute-start.7 = (bf16[192,512]{1,0:T(8,128)(2,1)S(1)}, bf16[192,512]{1,0:T(8,128)(2,1)S(1)}, u32[]{:S(2)}, u32[]{:S(2)}) collective-permute-start(bf16[192,512]{1,0:T(8,128)(2,1)S(1)} %pad_maximum_fusion.4), channel_id=1, source_target_pairs={{0,1},{1,0},{2,3},{3,2},{4,5},{5,4},{6,7},{7,6},{8,9},{9,8},{10,11... | collective-permute-start | bytes 589832 | tf_op jit(solution)/shard_map/ppermute | solution.py:430
  87.3 4.5 %collective-permute-start.12 = (bf16[96,3840]{1,0:T(8,128)(2,1)}, bf16[96,3840]{1,0:T(8,128)(2,1)}, u32[]{:S(2)}, u32[]{:S(2)}) collective-permute-start(bf16[96,3840]{1,0:T(8,128)(2,1)} %collective-permute-done.6.refs_6_), channel_id=1, source_target_pairs={{0,1},{1,0},{2,3},{3,2},{4,5},{5,4},{6,7},{7,6},{8,9},{9,8},{10,11... | collective-permute-start | bytes 2211848 | tf_op jit(solution)/shard_map/ppermute | solution.py:430
  87.4 5.2 %collective-permute-start.13 = (bf16[96,3840]{1,0:T(8,128)(2,1)}, bf16[96,3840]{1,0:T(8,128)(2,1)}, u32[]{:S(2)}, u32[]{:S(2)}) collective-permute-start(bf16[96,3840]{1,0:T(8,128)(2,1)} %collective-permute-done.11.refs_7_), channel_id=1, source_target_pairs={{0,1},{1,0},{2,3},{3,2},{4,5},{5,4},{6,7},{7,6},{8,9},{9,8},{10,11... | collective-permute-start | bytes 2211848 | tf_op jit(solution)/shard_map/ppermute | solution.py:430
  88.5 3.3 collective-permute-start.16
  89.9 2.7 collective-permute-start.17
  130.4 5.7 %collective-permute-start.22 = (bf16[2,192,3840]{2,1,0:T(8,128)(2,1)}, bf16[2,192,3840]{2,1,0:T(8,128)(2,1)}, u32[]{:S(2)}, u32[]{:S(2)}) collective-permute-start(bf16[2,192,3840]{2,1,0:T(8,128)(2,1)} %get-tuple-element.112), channel_id=1, source_target_pairs={{0,1},{1,0},{2,3},{3,2},{4,5},{5,4},{6,7},{7,6},{8,9},{9,8},{10,11... | collective-permute-start | bytes 8847368 | tf_op jit(solution)/shard_map/ppermute | solution.py:430
  130.6 10.3 %collective-permute-start.21 = (bf16[2,192,3072]{2,1,0:T(8,128)(2,1)}, bf16[2,192,3072]{2,1,0:T(8,128)(2,1)}, u32[]{:S(2)}, u32[]{:S(2)}) collective-permute-start(bf16[2,192,3072]{2,1,0:T(8,128)(2,1)} %get-tuple-element.110), channel_id=1, source_target_pairs={{0,1},{1,0},{2,3},{3,2},{4,5},{5,4},{6,7},{7,6},{8,9},{9,8},{10,11... | collective-permute-start | bytes 7077896 | tf_op jit(solution)/shard_map/ppermute | solution.py:430
  132.3 11.4 %collective-permute-start.18 = (bf16[192,512]{1,0:T(8,128)(2,1)}, bf16[192,512]{1,0:T(8,128)(2,1)S(1)}, u32[]{:S(2)}, u32[]{:S(2)}) collective-permute-start(bf16[192,512]{1,0:T(8,128)(2,1)} %copy-done.29), channel_id=1, source_target_pairs={{0,1},{1,0},{2,3},{3,2},{4,5},{5,4},{6,7},{7,6},{8,9},{9,8},{10,11... | collective-permute-start | bytes 589832 | tf_op jit(solution)/shard_map/ppermute | solution.py:430
  132.5 11.2 %collective-permute-start.19 = (bf16[192,512]{1,0:T(8,128)(2,1)}, bf16[192,512]{1,0:T(8,128)(2,1)S(1)}, u32[]{:S(2)}, u32[]{:S(2)}) collective-permute-start(bf16[192,512]{1,0:T(8,128)(2,1)} %copy-done.28), channel_id=1, source_target_pairs={{0,2},{1,3},{2,0},{3,1},{4,6},{5,7},{6,4},{7,5},{8,10},{9,11},{10,... | collective-permute-start | bytes 589832 | tf_op jit(solution)/shard_map/ppermute | solution.py:430
  133.8 9.9 %collective-permute-start.20 = (bf16[192,512]{1,0:T(8,128)(2,1)}, bf16[192,512]{1,0:T(8,128)(2,1)S(1)}, u32[]{:S(2)}, u32[]{:S(2)}) collective-permute-start(bf16[192,512]{1,0:T(8,128)(2,1)} %copy-done.27), channel_id=1, source_target_pairs={{0,3},{1,2},{2,1},{3,0},{4,7},{5,6},{6,5},{7,4},{8,11},{9,10},{10,... | collective-permute-start | bytes 589832 | tf_op jit(solution)/shard_map/ppermute | solution.py:430
  136.2 4.7 %copy-start.43 = (bf16[2,192,3072]{2,1,0:T(8,128)(2,1)S(1)}, bf16[2,192,3072]{2,1,0:T(8,128)(2,1)}, u32[]{:S(2)}) copy-start(bf16[2,192,3072]{2,1,0:T(8,128)(2,1)} %get-tuple-element.109) | copy-start | bytes 7077892
  139.7 36.0 %collective-permute-start.23 = (bf16[192,3840]{1,0:T(8,128)(2,1)S(1)}, bf16[192,3840]{1,0:T(8,128)(2,1)S(1)}, u32[]{:S(2)}, u32[]{:S(2)}) collective-permute-start(bf16[192,3840]{1,0:T(8,128)(2,1)S(1)} %get-tuple-element.158), channel_id=1, source_target_pairs={{0,2},{1,3},{2,0},{3,1},{4,6},{5,7},{6,4},{7,5},{8,10},{9,11},{10,... | collective-permute-start | bytes 4423688 | tf_op jit(solution)/shard_map/ppermute | solution.py:430
  143.7 28.6 %collective-permute-start.24 = (bf16[2,96,3072]{2,1,0:T(8,128)(2,1)S(1)}, bf16[2,96,3072]{2,1,0:T(8,128)(2,1)S(1)}, u32[]{:S(2)}, u32[]{:S(2)}) collective-permute-start(bf16[2,96,3072]{2,1,0:T(8,128)(2,1)S(1)} %get-tuple-element.120), channel_id=1, source_target_pairs={{0,4},{4,0},{8,12},{12,8},{16,20},{20,16},{24,28},{28,24},{1,5},{5... | collective-permute-start | bytes 3538952 | tf_op jit(solution)/shard_map/ppermute | solution.py:430
  145.3 7.8 %copy-start.20 = (f32[1,2048,1]{2,1,0:T(8,128)S(1)}, f32[1,2048,1]{2,1,0:T(8,128)}, u32[]{:S(2)}) copy-start(f32[1,2048,1]{2,1,0:T(8,128)} %copy-done.19) | copy-start | bytes 24580
  153.1 8.1 %copy-start.16 = (f32[1,2048,1]{2,1,0:T(8,128)S(1)}, f32[1,2048,1]{2,1,0:T(8,128)}, u32[]{:S(2)}) copy-start(f32[1,2048,1]{2,1,0:T(8,128)} %copy-done.15) | copy-start | bytes 24580
  176.1 19.5 %collective-permute-start.28 = (bf16[96,3840]{1,0:T(8,128)(2,1)S(1)}, bf16[96,3840]{1,0:T(8,128)(2,1)S(1)}, u32[]{:S(2)}, u32[]{:S(2)}) collective-permute-start(bf16[96,3840]{1,0:T(8,128)(2,1)S(1)} %constant_dynamic-slice_fusion.11), channel_id=1, source_target_pairs={{0,4},{4,0},{8,12},{12,8},{16,20},{20,16},{24,28},{28,24},{1,5},{5... | collective-permute-start | bytes 2211848 | tf_op jit(solution)/shard_map/ppermute | solution.py:430
  178.2 17.6 %collective-permute-start.30 = (bf16[96,3072]{1,0:T(8,128)(2,1)S(1)}, bf16[96,3072]{1,0:T(8,128)(2,1)S(1)}, u32[]{:S(2)}, u32[]{:S(2)}) collective-permute-start(bf16[96,3072]{1,0:T(8,128)(2,1)S(1)} %get-tuple-element.160), channel_id=1, source_target_pairs={{0,2},{1,3},{2,0},{3,1},{4,6},{5,7},{6,4},{7,5},{8,10},{9,11},{10,... | collective-permute-start | bytes 1769480 | tf_op jit(solution)/shard_map/ppermute | solution.py:430
  190.3 7.4 %copy-start.7 = (bf16[2,512,768]{2,1,0:T(8,128)(2,1)}, bf16[2,512,768]{2,1,0:T(8,128)(2,1)S(1)}, u32[]{:S(2)}) copy-start(bf16[2,512,768]{2,1,0:T(8,128)(2,1)S(1)} %get-tuple-element.130) | copy-start | bytes 4718596
  190.3 16.5 %collective-permute-start.27 = (bf16[4,96,588]{2,1,0:T(8,128)(2,1)S(1)}, bf16[4,96,588]{2,1,0:T(8,128)(2,1)S(1)}, u32[]{:S(2)}, u32[]{:S(2)}) collective-permute-start(bf16[4,96,588]{2,1,0:T(8,128)(2,1)S(1)} %get-tuple-element.133), channel_id=1, source_target_pairs={{0,4},{4,0},{8,12},{12,8},{16,20},{20,16},{24,28},{28,24},{1,5},{5... | collective-permute-start | bytes 1354760 | tf_op jit(solution)/shard_map/ppermute | solution.py:430
  195.8 10.9 %collective-permute-start.29 = (bf16[48,3840]{1,0:T(8,128)(2,1)S(1)}, bf16[48,3840]{1,0:T(8,128)(2,1)S(1)}, u32[]{:S(2)}, u32[]{:S(2)}) collective-permute-start(bf16[48,3840]{1,0:T(8,128)(2,1)S(1)} %constant_dynamic-slice_fusion.10), channel_id=1, source_target_pairs={{0,8},{4,12},{8,0},{12,4},{16,24},{20,28},{24,16},{28,20},{1,9},{5... | collective-permute-start | bytes 1105928 | tf_op jit(solution)/shard_map/ppermute | solution.py:430
  197.8 12.1 %collective-permute-start.33 = (bf16[48,3072]{1,0:T(8,128)(2,1)S(1)}, bf16[48,3072]{1,0:T(8,128)(2,1)S(1)}, u32[]{:S(2)}, u32[]{:S(2)}) collective-permute-start(bf16[48,3072]{1,0:T(8,128)(2,1)S(1)} %constant_dynamic-slice_fusion.7), channel_id=1, source_target_pairs={{0,8},{4,12},{8,0},{12,4},{16,24},{20,28},{24,16},{28,20},{1,9},{5... | collective-permute-start | bytes 884744 | tf_op jit(solution)/shard_map/ppermute | solution.py:430
  210.0 12.6 %collective-permute-start.32 = (bf16[24,3840]{1,0:T(8,128)(2,1)S(1)}, bf16[24,3840]{1,0:T(8,128)(2,1)S(1)}, u32[]{:S(2)}, u32[]{:S(2)}) collective-permute-start(bf16[24,3840]{1,0:T(8,128)(2,1)S(1)} %constant_dynamic-slice_fusion.8), channel_id=1, source_target_pairs={{0,16},{4,20},{8,24},{12,28},{16,0},{20,4},{24,8},{28,12},{1,17},{... | collective-permute-start | bytes 552968 | tf_op jit(solution)/shard_map/ppermute | solution.py:430
  213.9 10.4 %collective-permute-start.35 = (bf16[24,3072]{1,0:T(8,128)(2,1)S(1)}, bf16[24,3072]{1,0:T(8,128)(2,1)S(1)}, u32[]{:S(2)}, u32[]{:S(2)}) collective-permute-start(bf16[24,3072]{1,0:T(8,128)(2,1)S(1)} %constant_dynamic-slice_fusion.5), channel_id=1, source_target_pairs={{0,16},{4,20},{8,24},{12,28},{16,0},{20,4},{24,8},{28,12},{1,17},{... | collective-permute-start | bytes 442376 | tf_op jit(solution)/shard_map/ppermute | solution.py:430
  214.0 10.1 %collective-permute-start.31 = (bf16[4,48,588]{2,1,0:T(8,128)(2,1)S(1)}, bf16[4,48,588]{2,1,0:T(8,128)(2,1)S(1)}, u32[]{:S(2)}, u32[]{:S(2)}) collective-permute-start(bf16[4,48,588]{2,1,0:T(8,128)(2,1)S(1)} %constant_dynamic-slice_fusion.9), channel_id=1, source_target_pairs={{0,8},{4,12},{8,0},{12,4},{16,24},{20,28},{24,16},{28,20},{1,9},{5... | collective-permute-start | bytes 677384 | tf_op jit(solution)/shard_map/ppermute | solution.py:430
  224.3 5.8 %collective-permute-start.34 = (bf16[4,24,588]{2,1,0:T(8,128)(2,1)S(1)}, bf16[4,24,588]{2,1,0:T(8,128)(2,1)S(1)}, u32[]{:S(2)}, u32[]{:S(2)}) collective-permute-start(bf16[4,24,588]{2,1,0:T(8,128)(2,1)S(1)} %constant_dynamic-slice_fusion.6), channel_id=1, source_target_pairs={{0,16},{4,20},{8,24},{12,28},{16,0},{20,4},{24,8},{28,12},{1,17},{... | collective-permute-start | bytes 338696 | tf_op jit(solution)/shard_map/ppermute | solution.py:430
  230.2 16.1 %copy-start.6 = (bf16[512,768]{1,0:T(8,128)(2,1)S(1)}, bf16[512,768]{1,0:T(8,128)(2,1)}, u32[]{:S(2)}) copy-start(bf16[512,768]{1,0:T(8,128)(2,1)} %refs_0_.3) | copy-start | bytes 2359300
  234.4 3.4 %collective-permute-start.36 = (bf16[24,626]{1,0:T(8,128)(2,1)S(1)}, bf16[24,626]{1,0:T(8,128)(2,1)S(1)}, u32[]{:S(2)}, u32[]{:S(2)}) collective-permute-start(bf16[24,626]{1,0:T(8,128)(2,1)S(1)} %get-tuple-element.177), channel_id=1, source_target_pairs={{0,1},{1,0},{2,3},{3,2},{4,5},{5,4},{6,7},{7,6},{8,9},{9,8},{10,11... | collective-permute-start | bytes 90152 | tf_op jit(solution)/shard_map/ppermute | solution.py:430
  234.4 5.1 %collective-permute-start.37 = (bf16[24,626]{1,0:T(8,128)(2,1)S(1)}, bf16[24,626]{1,0:T(8,128)(2,1)S(1)}, u32[]{:S(2)}, u32[]{:S(2)}) collective-permute-start(bf16[24,626]{1,0:T(8,128)(2,1)S(1)} %get-tuple-element.178), channel_id=1, source_target_pairs={{0,2},{1,3},{2,0},{3,1},{4,6},{5,7},{6,4},{7,5},{8,10},{9,11},{10,... | collective-permute-start | bytes 90152 | tf_op jit(solution)/shard_map/ppermute | solution.py:430
  237.6 3.3 collective-permute-start.38
  237.7 34.5 %collective-permute-start.25 = (bf16[2,512,768]{2,1,0:T(8,128)(2,1)}, bf16[2,512,768]{2,1,0:T(8,128)(2,1)}, u32[]{:S(2)}, u32[]{:S(2)}) collective-permute-start(bf16[2,512,768]{2,1,0:T(8,128)(2,1)} %get-tuple-element.131), channel_id=1, source_target_pairs={{0,1},{1,0},{2,3},{3,2},{4,5},{5,4},{6,7},{7,6},{8,9},{9,8},{10,11... | collective-permute-start | bytes 4718600 | tf_op jit(solution)/shard_map/ppermute | solution.py:430
  245.8 26.3 %copy-start.8 = (bf16[2,512,768]{2,1,0:T(8,128)(2,1)S(1)}, bf16[2,512,768]{2,1,0:T(8,128)(2,1)}, u32[]{:S(2)}) copy-start(bf16[2,512,768]{2,1,0:T(8,128)(2,1)} %copy-done.7) | copy-start | bytes 4718596
  246.3 14.1 %collective-permute-start.39 = (bf16[1,24,2318]{2,1,0:T(8,128)(2,1)S(1)}, bf16[1,24,2318]{2,1,0:T(8,128)(2,1)S(1)}, u32[]{:S(2)}, u32[]{:S(2)}) collective-permute-start(bf16[1,24,2318]{2,1,0:T(8,128)(2,1)S(1)} %bitcast.124), channel_id=1, source_target_pairs={{0,16},{4,20},{8,24},{12,28},{16,0},{20,4},{24,8},{28,12},{1,17},{... | collective-permute-start | bytes 333800 | tf_op jit(solution)/shard_map/ppermute | solution.py:430
  260.5 9.4 %collective-permute-start.40 = (bf16[2,24,2318]{2,1,0:T(8,128)(2,1)S(1)}, bf16[2,24,2318]{2,1,0:T(8,128)(2,1)S(1)}, u32[]{:S(2)}, u32[]{:S(2)}) collective-permute-start(bf16[2,24,2318]{2,1,0:T(8,128)(2,1)S(1)} %pad_maximum_fusion.2), channel_id=1, source_target_pairs={{0,8},{4,12},{8,0},{12,4},{16,24},{20,28},{24,16},{28,20},{1,9},{5... | collective-permute-start | bytes 667592 | tf_op jit(solution)/shard_map/ppermute | solution.py:430
  269.9 23.6 %copy-start.10 = (bf16[4,24,2318]{2,1,0:T(8,128)(2,1)}, bf16[4,24,2318]{2,1,0:T(8,128)(2,1)S(1)}, u32[]{:S(2)}) copy-start(bf16[4,24,2318]{2,1,0:T(8,128)(2,1)S(1)} %pad_maximum_fusion.refs_1_) | copy-start | bytes 1335172
  269.9 21.1 %collective-permute-start.41 = (bf16[4,24,2318]{2,1,0:T(8,128)(2,1)S(1)}, bf16[4,24,2318]{2,1,0:T(8,128)(2,1)}, u32[]{:S(2)}, u32[]{:S(2)}) collective-permute-start(bf16[4,24,2318]{2,1,0:T(8,128)(2,1)S(1)} %pad_maximum_fusion.refs_1_), channel_id=1, source_target_pairs={{0,4},{4,0},{8,12},{12,8},{16,20},{20,16},{24,28},{28,24},{1,5},{5... | collective-permute-start | bytes 1335176 | tf_op jit(solution)/shard_map/ppermute | solution.py:430
  272.1 21.4 %copy-start.14 = (f32[12,192]{1,0:T(8,128)S(1)}, f32[12,192]{1,0:T(8,128)}, u32[]{:S(2)}) copy-start(f32[12,192]{1,0:T(8,128)} %vec_ref.1) | copy-start | bytes 27652
  272.1 21.4 %copy-start.46 = (f32[12,192]{1,0:T(8,128)S(1)}, f32[12,192]{1,0:T(8,128)}, u32[]{:S(2)}) copy-start(f32[12,192]{1,0:T(8,128)} %param.24) | copy-start | bytes 27652
  272.2 21.4 %copy-start.47 = (f32[12,192]{1,0:T(8,128)S(1)}, f32[12,192]{1,0:T(8,128)}, u32[]{:S(2)}) copy-start(f32[12,192]{1,0:T(8,128)} %param.25) | copy-start | bytes 27652
  274.5 19.7 %collective-permute-start.26 = (bf16[512,768]{1,0:T(8,128)(2,1)}, bf16[512,768]{1,0:T(8,128)(2,1)}, u32[]{:S(2)}, u32[]{:S(2)}) collective-permute-start(bf16[512,768]{1,0:T(8,128)(2,1)} %fusion.14), channel_id=1, source_target_pairs={{0,2},{1,3},{2,0},{3,1},{4,6},{5,7},{6,4},{7,5},{8,10},{9,11},{10,... | collective-permute-start | bytes 2359304 | tf_op jit(solution)/shard_map/ppermute | solution.py:430
  296.6 10.3 %copy-start.2 = (f32[192,3072]{1,0:T(8,128)S(1)}, f32[192,3072]{1,0:T(8,128)}, u32[]{:S(2)}) copy-start(f32[192,3072]{1,0:T(8,128)} %out_ref.1) | copy-start | bytes 7077892
  (29 other events, 44.3 us)
Sparse Core Ops, SparseCore 0:
  237.9 68.8 all-gather.2

commit v8 on v7

--- a/solution.py
+++ b/solution.py
@@ -790,11 +790,20 @@
         da1_got = swap(da1_send, "shard", 1, parts)
         state_a = next_half(own_a, got_a, z_bits[0], 0)
         state_b = next_half(own_b, got_b, z_bits[0], 0)
+        da1_got = seen(da1_got)
+        own_da1 = da1_keep[0].astype(HIGH) + da1_got[0].astype(HIGH)
+        other_da1 = event(add_low(da1_keep[1], da1_got[1]))
+        got_da1 = swap(other_da1, "shard", 2, parts)
         for bit in z_bits[1:]:
             state_a = next_half(*state_a, bit, 0)
         state_q = next_half(own_q, got_q, z_bits[0], 1)
         for bit in z_bits[1:]:
             state_b = next_half(*state_b, bit, 0)
+        da1 = own_da1 + seen(got_da1).astype(HIGH)
+        unit, inverse = normalize(seen(tokens).astype(HIGH))
+        grad_input = grad_resid + normalize_back(unit, inverse, da1 * vectors[0:1])
+        live_rows = jnp.arange(slots, dtype=jnp.int32) < live_own[0]
+        grad_in = event(jnp.where(live_rows[:, None], grad_input, 0.0).astype(LOW))
         part_a = event(add_low(state_a[0], seen(state_a[1])))
         for bit in z_bits[1:]:
             state_q = next_half(*state_q, bit, 1)
@@ -850,13 +859,6 @@
         small = jnp.stack([pick(small, turn ^ r) for r in range(replicas)]).astype(HIGH)
         summed_vec = small[:, :, :extra].reshape(rows, extra).T
         squares = jnp.sum(small[:, 0, extra:])
-
-        own_da1 = da1_keep[0].astype(HIGH) + da1_got[0].astype(HIGH)
-        da1 = own_da1 + swap(add_low(da1_keep[1], da1_got[1]), "shard", 2, parts).astype(HIGH)
-        unit, inverse = normalize(tokens.astype(HIGH))
-        grad_input = grad_resid + normalize_back(unit, inverse, da1 * vectors[0:1])
-        live_rows = jnp.arange(slots, dtype=jnp.int32) < live_own[0]
-        grad_in = jnp.where(live_rows[:, None], grad_input, 0.0).astype(LOW)
 
         norm_total = jnp.sqrt(squares)
         factor = jnp.minimum(1.0, CLIP_LIMIT / (norm_total + 1e-06))

time: 340 us -> 325 us (0.956)
  other arithmetic: 24.9 us -> 18.9 us
  local copies, waits for them, and re-layouts: 24.8 us -> 20.3 us
    unnamed x103 -> x87, local copies, waits for them, and re-layouts: 18.5 us -> 15.8 us
  transfers between devices with their start and end apart: 43 -> 43, of which waited for: 24 -> 21; matrix products, arithmetic and copies ran while one was open for 9% -> 8% of each run, Pallas kernels for 19% -> 20%
where the time goes in v8:
time: 325 us; the launch traced here: 321 us
  Pallas kernels  116 us (36%)
  waiting for transfers between devices  108 us (33%)
  starting transfers between devices  34.5 us (11%)
  between operations  23.4 us (7%)
  local copies, waits for them, and re-layouts  20.3 us (6%)
  other arithmetic  18.9 us (6%)
    ppermute x42, waiting for transfers between devices, swap(): return lax.ppermute(array, axis, [(i, i ^ bit) for i in range(count)])  102 us
    ppermute x42, starting transfers between devices, swap(): return lax.ppermute(array, axis, [(i, i ^ bit) for i in range(count)])  34.4 us
    pallas_call x1, Pallas kernels, on_device(): pl.pallas_call(functools.partial(mlp_kernel, parts, first_blocks), grid_s...  32.9 us
    pallas_call x3, Pallas kernels, attend_back(): pl.pallas_call(functools.partial(attend_back_kernel, scale), grid_spec=pl...  24.2 us
    pallas_call x3, Pallas kernels, attend(): pl.pallas_call(functools.partial(attend_kernel, scale), grid_spec=pltpu.P...  19.6 us
    pallas_call x1, Pallas kernels, on_device(): pl.pallas_call(functools.partial(adam_kernel, fc_rows), grid_spec=pltpu.P...  19.1 us
    unnamed x87, local copies, waits for them, and re-layouts  15.8 us
    pallas_call x1, Pallas kernels, on_device(): pl.pallas_call(functools.partial(projection_back_kernel, own_heads, parts...  10.1 us
  transfers between devices with their start and end apart: 43, of which 21 were waited for; matrix products, arithmetic and copies ran while one was open for 8% of the time, Pallas kernels for 20%

profile of v8, /device:TPU:0, one launch (start us, length us, event | category | flops | bytes accessed | tf_op | source)
XLA Modules:
  0.0 320.6 jit_solution(4722541219626585420)
XLA Ops:
  7.2 3.0 collective-permute-start.1
  10.3 1.7 copy-done
  12.6 1.5 cut.1
  15.4 1.3 collective-permute-start.5
  16.8 0.9 broadcast_in_dim.54.refs_8_
  18.7 1.1 copy.59
  19.8 2.3 copy-done.3
  22.1 1.9 widen.1
  24.1 4.9 %collective-permute-done.1.refs_2_ = bf16[512,768]{1,0:T(8,128)(2,1)} collective-permute-done((bf16[512,768]{1,0:T(8,128)(2,1)}, bf16[512,768]{1,0:T(8,128)(2,1)}, u32[]{:S(2)}, u32[]{:S(2)}) %collective-permute-start.1) | collective-permute-done | bytes 786464 | tf_op jit(solution)/shard_map/ppermute | solution.py:430
  29.2 5.5 %collective-permute-done.4.refs_6_ = bf16[208,576]{1,0:T(8,128)(2,1)} collective-permute-done((bf16[208,576]{1,0:T(8,128)(2,1)}, bf16[208,576]{1,0:T(8,128)(2,1)}, u32[]{:S(2)}, u32[]{:S(2)}) %collective-permute-start.4) | collective-permute-done | bytes 239648 | tf_op jit(solution)/shard_map/ppermute | solution.py:430
  34.6 4.1 %collective-permute-done.5.refs_7_ = bf16[208,576]{1,0:T(8,128)(2,1)} collective-permute-done((bf16[208,576]{1,0:T(8,128)(2,1)}, bf16[208,576]{1,0:T(8,128)(2,1)}, u32[]{:S(2)}, u32[]{:S(2)}) %collective-permute-start.5) | collective-permute-done | bytes 239648 | tf_op jit(solution)/shard_map/ppermute | solution.py:430
  38.8 1.4 collective-permute-start.6
  41.0 6.6 %project.1 = (bf16[2048,768]{1,0:T(8,128)(2,1)S(1)}, bf16[576,2048]{1,0:T(8,128)(2,1)S(1)}, bf16[576,768]{1,0:T(8,128)(2,1)S(1)}, f32[16,768]{1,0:T(8,128)S(1)}) custom-call(s32[1]{0:T(128)} %bitcast.place, bf16[512,768]{1,0:T(8,128)(2,1)S(1)} %copy-done.4, bf16[512,768]{1,0:T(8,128)(2,1)} %collective-permute-done.refs_1_, ...), custom_call_target="tpu_custom_call" | custom-call | flops 5435817984 | bytes 12000000 | tf_op jit(solution)/shard_map/project/pallas_call | solution.py:570
  47.6 6.5 %attend.3 = (bf16[4,64,512]{2,1,0:T(8,128)(2,1)S(1)}, f32[1,2048,1]{2,1,0:T(8,128)S(1)}) custom-call(s32[1]{0:T(128)} %bitcast.place, bf16[576,2048]{1,0:T(8,128)(2,1)S(1)} %get-tuple-element.97.qt_ref.kt_ref.vt_ref, bf16[576,2048]{1,0:T(8,128)(2,1)S(1)} %get-tuple-element.97.qt_ref.kt_ref.vt_ref, ...), custom_call_target="tpu_custom_call" | custom-call | flops 2147483648 | bytes 4000000 | tf_op jit(solution)/shard_map/attend/pallas_call | solution.py:612
  54.1 1.0 copy-done.9
  55.7 2.5 collective-permute-done.6.refs_6_
  58.2 1.6 collective-permute-start.11
  59.8 6.4 %attend.5 = (bf16[4,64,512]{2,1,0:T(8,128)(2,1)S(1)}, f32[1,2048,1]{2,1,0:T(8,128)S(1)}) custom-call(s32[1]{0:T(128)} %bitcast.place, bf16[576,2048]{1,0:T(8,128)(2,1)S(1)} %get-tuple-element.97.qt_ref.kt_ref.vt_ref, bf16[576,2048]{1,0:T(8,128)(2,1)S(1)} %get-tuple-element.97.qt_ref.kt_ref.vt_ref, ...), custom_call_target="tpu_custom_call" | custom-call | flops 2147483648 | bytes 4000000 | tf_op jit(solution)/shard_map/attend/pallas_call | solution.py:612
  66.3 6.7 %attend.4 = (bf16[4,64,512]{2,1,0:T(8,128)(2,1)S(1)}, f32[1,2048,1]{2,1,0:T(8,128)S(1)}) custom-call(s32[1]{0:T(128)} %bitcast.place, bf16[576,2048]{1,0:T(8,128)(2,1)S(1)} %get-tuple-element.97.qt_ref.kt_ref.vt_ref, bf16[576,2048]{1,0:T(8,128)(2,1)S(1)} %get-tuple-element.97.qt_ref.kt_ref.vt_ref, ...), custom_call_target="tpu_custom_call" | custom-call | flops 2147483648 | bytes 4000000 | tf_op jit(solution)/shard_map/attend/pallas_call | solution.py:612
  74.8 0.9 collective-permute-start.8
  75.7 5.7 %collective-permute-done.9.refs_3_ = bf16[192,512]{1,0:T(8,128)(2,1)S(1)} collective-permute-done((bf16[192,512]{1,0:T(8,128)(2,1)S(1)}, bf16[192,512]{1,0:T(8,128)(2,1)S(1)}, u32[]{:S(2)}, u32[]{:S(2)}) %collective-permute-start.9) | collective-permute-done | bytes 196640 | tf_op jit(solution)/shard_map/ppermute | solution.py:430
  82.3 3.3 %collective-permute-done.8.refs_2_ = bf16[192,512]{1,0:T(8,128)(2,1)S(1)} collective-permute-done((bf16[192,512]{1,0:T(8,128)(2,1)S(1)}, bf16[192,512]{1,0:T(8,128)(2,1)S(1)}, u32[]{:S(2)}, u32[]{:S(2)}) %collective-permute-start.8) | collective-permute-done | bytes 196640 | tf_op jit(solution)/shard_map/ppermute | solution.py:430
  87.7 1.6 collective-permute-done.15.refs_11_
  89.8 0.9 pad_maximum_fusion.3.refs_0_
  90.7 0.9 collective-permute-done.17.refs_13_
  91.6 0.9 copy-done.23
  92.5 0.9 copy-done.25
  93.5 0.9 copy-done.27
  94.4 32.9 %mlp.1 = (bf16[512,768]{1,0:T(8,128)(2,1)}, bf16[2,192,3840]{2,1,0:T(8,128)(2,1)}, bf16[2,192,3840]{2,1,0:T(8,128)(2,1)}, bf16[2,192,3072]{2,1,0:T(8,128)(2,1)},...) custom-call(s32[1]{0:T(128)} %bitcast.place, ...), custom_call_target="tpu_custom_call" | custom-call | flops 16307453952 | bytes 30000000 | tf_op jit(solution)/shard_map/mlp/pallas_call | solution.py:662
  131.5 1.8 collective-permute-start.19
  133.4 2.4 collective-permute-done.22
  135.8 3.5 %fusion.13 = (bf16[192,3840]{1,0:T(8,128)(2,1)S(1)}, bf16[192,3840]{1,0:T(8,128)(2,1)S(1)}) fusion(bf16[2,192,3840]{2,1,0:T(8,128)(2,1)} %collective-permute-done.22, bf16[2,192,3840]{2,1,0:T(8,128)(2,1)} %get-tuple-element.112), kind=kLoop, calls=%fused_computation.21 | loop fusion | flops 5898240 | bytes 8847360 | tf_op jit(solution)/shard_map/convert_element_type | solution.py:462
  139.3 1.9 collective-permute-start.23
  141.3 2.5 add_convert_fusion
  144.0 1.6 collective-permute-start.24
  145.6 7.9 %attend_back.5.refs_7_ = bf16[3,64,2048]{2,1,0:T(8,128)(2,1)S(1)} custom-call(s32[1]{0:T(128)} %bitcast.place, bf16[576,2048]{1,0:T(8,128)(2,1)S(1)} %get-tuple-element.97.qt_ref.kt_ref.vt_ref, bf16[576,2048]{1,0:T(8,128)(2,1)S(1)} %get-tuple-element.97.qt_ref.kt_ref.vt_ref, bf16[576,2048]{1,0:T(8,128)(2,1)S(1)} %get-tuple-element.97.qt_ref.kt_ref.vt_ref, ...), custom_call_target="tpu_custom_call" | custom-call | flops 5368709120 | bytes 4000000 | tf_op jit(solution)/shard_map/attend_back/pallas_call | solution.py:709
  153.5 8.1 %attend_back.4.refs_6_ = bf16[3,64,2048]{2,1,0:T(8,128)(2,1)S(1)} custom-call(s32[1]{0:T(128)} %bitcast.place, bf16[576,2048]{1,0:T(8,128)(2,1)S(1)} %get-tuple-element.97.qt_ref.kt_ref.vt_ref, bf16[576,2048]{1,0:T(8,128)(2,1)S(1)} %get-tuple-element.97.qt_ref.kt_ref.vt_ref, bf16[576,2048]{1,0:T(8,128)(2,1)S(1)} %get-tuple-element.97.qt_ref.kt_ref.vt_ref, ...), custom_call_target="tpu_custom_call" | custom-call | flops 5368709120 | bytes 4000000 | tf_op jit(solution)/shard_map/attend_back/pallas_call | solution.py:709
  161.7 8.2 %attend_back.3.refs_5_ = bf16[3,64,2048]{2,1,0:T(8,128)(2,1)S(1)} custom-call(s32[1]{0:T(128)} %bitcast.place, bf16[576,2048]{1,0:T(8,128)(2,1)S(1)} %get-tuple-element.97.qt_ref.kt_ref.vt_ref, bf16[576,2048]{1,0:T(8,128)(2,1)S(1)} %get-tuple-element.97.qt_ref.kt_ref.vt_ref, bf16[576,2048]{1,0:T(8,128)(2,1)S(1)} %get-tuple-element.97.qt_ref.kt_ref.vt_ref, ...), custom_call_target="tpu_custom_call" | custom-call | flops 5368709120 | bytes 4000000 | tf_op jit(solution)/shard_map/attend_back/pallas_call | solution.py:709
  169.9 2.0 collective-permute-done.24
  171.8 3.0 collective-permute-done.23
  175.2 1.7 collective-permute-start.26
  177.3 1.7 collective-permute-start.25
  179.0 10.1 %projection_back.1 = (bf16[2,512,768]{2,1,0:T(8,128)(2,1)S(1)}, bf16[2,512,768]{2,1,0:T(8,128)(2,1)S(1)}, bf16[4,96,588]{2,1,0:T(8,128)(2,1)S(1)}, bf16[4,96,588]{2,1,0:T(8,128)(2,1)S(1)}) custom-call(s32[1]{0:T(128)} %bitcast.place, s32[1]{0:T(128)} %bitcast.1.half, bf16[512,768]{1,0:T(8,128)(2,1)S(1)} %copy-done.5, ...), custom_call_target="tpu_custom_call" | custom-call | flops 7247757312 | bytes 16000000 | tf_op jit(solution)/shard_map/projection_back/pallas_call | solution.py:744
  189.8 4.6 %collective-permute-done.26 = bf16[96,3840]{1,0:T(8,128)(2,1)S(1)} collective-permute-done((bf16[96,3840]{1,0:T(8,128)(2,1)S(1)}, bf16[96,3840]{1,0:T(8,128)(2,1)S(1)}, u32[]{:S(2)}, u32[]{:S(2)}) %collective-permute-start.26) | collective-permute-done | bytes 737312 | tf_op jit(solution)/shard_map/ppermute | solution.py:430
  194.5 1.7 collective-permute-start.29
  197.1 2.2 collective-permute-start.31
  199.3 6.7 %collective-permute-done.29 = bf16[48,3840]{1,0:T(8,128)(2,1)S(1)} collective-permute-done((bf16[48,3840]{1,0:T(8,128)(2,1)S(1)}, bf16[48,3840]{1,0:T(8,128)(2,1)S(1)}, u32[]{:S(2)}, u32[]{:S(2)}) %collective-permute-start.29) | collective-permute-done | bytes 368672 | tf_op jit(solution)/shard_map/ppermute | solution.py:430
  206.3 2.9 collective-permute-done.27
  209.4 3.1 collective-permute-start.35
  212.5 1.4 collective-permute-start.32
  214.4 0.8 fusion.35
  215.8 1.8 fusion.9
  217.6 6.4 %collective-permute-done.33 = bf16[24,3840]{1,0:T(8,128)(2,1)S(1)} collective-permute-done((bf16[24,3840]{1,0:T(8,128)(2,1)S(1)}, bf16[24,3840]{1,0:T(8,128)(2,1)S(1)}, u32[]{:S(2)}, u32[]{:S(2)}) %collective-permute-start.33) | collective-permute-done | bytes 184352 | tf_op jit(solution)/shard_map/ppermute | solution.py:430
  224.5 0.7 pad_maximum_fusion.1
  225.3 0.8 multiply_reduce_fusion
  226.0 5.6 %collective-permute-done.34 = bf16[4,24,588]{2,1,0:T(8,128)(2,1)S(1)} collective-permute-done((bf16[4,24,588]{2,1,0:T(8,128)(2,1)S(1)}, bf16[4,24,588]{2,1,0:T(8,128)(2,1)S(1)}, u32[]{:S(2)}, u32[]{:S(2)}) %collective-permute-start.34) | collective-permute-done | bytes 112928 | tf_op jit(solution)/shard_map/ppermute | solution.py:430
  236.0 1.8 collective-permute-start.38
  237.8 2.2 collective-permute-done.37
  245.5 10.4 %collective-permute-done.39 = bf16[1,24,2318]{2,1,0:T(8,128)(2,1)S(1)} collective-permute-done((bf16[1,24,2318]{2,1,0:T(8,128)(2,1)S(1)}, bf16[1,24,2318]{2,1,0:T(8,128)(2,1)S(1)}, u32[]{:S(2)}, u32[]{:S(2)}) %collective-permute-start.39) | collective-permute-done | bytes 111296 | tf_op jit(solution)/shard_map/ppermute | solution.py:430
  256.1 16.5 %collective-permute-done.40 = bf16[2,24,2318]{2,1,0:T(8,128)(2,1)S(1)} collective-permute-done((bf16[2,24,2318]{2,1,0:T(8,128)(2,1)S(1)}, bf16[2,24,2318]{2,1,0:T(8,128)(2,1)S(1)}, u32[]{:S(2)}, u32[]{:S(2)}) %collective-permute-start.40) | collective-permute-done | bytes 222560 | tf_op jit(solution)/shard_map/ppermute | solution.py:430
  272.6 1.5 collective-permute-start.41
  274.1 11.2 %collective-permute-done.41.refs_2_ = bf16[4,24,2318]{2,1,0:T(8,128)(2,1)S(1)} collective-permute-done((bf16[4,24,2318]{2,1,0:T(8,128)(2,1)S(1)}, bf16[4,24,2318]{2,1,0:T(8,128)(2,1)S(1)}, u32[]{:S(2)}, u32[]{:S(2)}) %collective-permute-start.41) | collective-permute-done | bytes 445088 | tf_op jit(solution)/shard_map/ppermute | solution.py:430
  287.7 5.4 %all-gather.3.cloned.1.call-done = bf16[192,6912]{1,0:T(8,128)(2,1)} async-done(((bf16[24,6912]{1,0:T(8,128)(2,1)}), bf16[192,6912]{1,0:T(8,128)(2,1)}) %all-gather.3.cloned.1.call-update) | async-done | bytes 2654224 | tf_op jit(solution)/shard_map/all_gather | solution.py:812
  293.0 19.1 %adam.1 = (f32[8,24,3072]{2,1,0:T(8,128)}, f32[8,24,3072]{2,1,0:T(8,128)}, f32[8,24,3072]{2,1,0:T(8,128)}, f32[8,24,3072]{2,1,0:T(8,128)}, f32[2,8,24,3072]{3,2,...) custom-call(f32[1]{0:T(128)} %bitcast.46.factor_ref, ...), custom_call_target="tpu_custom_call" | custom-call | flops 39813120 | bytes 54000000 | tf_op jit(solution)/shard_map/adam/pallas_call | solution.py:875
  (218 shorter events, 24.5 us)
Async XLA Ops:
  7.2 10.5 %copy-start.40 = (s32[1,4]{1,0:T(1,128)S(1)}, s32[1,4]{1,0:T(1,128)}, u32[]{:S(2)}) copy-start(s32[1,4]{1,0:T(1,128)} %param.16) | copy-start | bytes 52
  7.2 10.8 %copy-start.41 = (s32[1,2]{1,0:T(1,128)S(1)}, s32[1,2]{1,0:T(1,128)}, u32[]{:S(2)}) copy-start(s32[1,2]{1,0:T(1,128)} %param.15) | copy-start | bytes 28
  7.2 285.8 %all-gather.3.cloned.1.call-start = ((), (), s32[]{:S(2)}) async-start(), calls=%async_computation | async-start | bytes 2985984 | tf_op jit(solution)/shard_map/all_gather | solution.py:812
  7.2 21.7 %collective-permute-start.1 = (bf16[512,768]{1,0:T(8,128)(2,1)}, bf16[512,768]{1,0:T(8,128)(2,1)}, u32[]{:S(2)}, u32[]{:S(2)}) collective-permute-start(bf16[512,768]{1,0:T(8,128)(2,1)} %refs_0_.3), channel_id=1, source_target_pairs={{0,2},{1,3},{2,0},{3,1},{4,6},{5,7},{6,4},{7,5},{8,10},{9,11},{10,... | collective-permute-start | bytes 2359304 | tf_op jit(solution)/shard_map/ppermute | solution.py:430
  10.2 28.5 %collective-permute-start = (bf16[512,768]{1,0:T(8,128)(2,1)}, bf16[512,768]{1,0:T(8,128)(2,1)}, u32[]{:S(2)}, u32[]{:S(2)}) collective-permute-start(bf16[512,768]{1,0:T(8,128)(2,1)} %refs_0_.3), channel_id=1, source_target_pairs={{0,1},{1,0},{2,3},{3,2},{4,5},{5,4},{6,7},{7,6},{8,9},{9,8},{10,11... | collective-permute-start | bytes 2359304 | tf_op jit(solution)/shard_map/ppermute | solution.py:430
  12.6 4.1 %copy-start.8 = (f32[12,192]{1,0:T(8,128)S(1)}, f32[12,192]{1,0:T(8,128)}, u32[]{:S(2)}) copy-start(f32[12,192]{1,0:T(8,128)} %vec_ref.1) | copy-start | bytes 27652
  12.6 7.1 %copy-start.1 = (f32[192,3072]{1,0:T(8,128)S(1)}, f32[192,3072]{1,0:T(8,128)}, u32[]{:S(2)}) copy-start(f32[192,3072]{1,0:T(8,128)} %out_ref.1) | copy-start | bytes 7077892
  14.9 14.3 %collective-permute-start.3 = (bf16[208,576]{1,0:T(8,128)(2,1)}, bf16[208,576]{1,0:T(8,128)(2,1)}, u32[]{:S(2)}, u32[]{:S(2)}) collective-permute-start(bf16[208,576]{1,0:T(8,128)(2,1)} %get-tuple-element.87), channel_id=1, source_target_pairs={{0,1},{1,0},{2,3},{3,2},{4,5},{5,4},{6,7},{7,6},{8,9},{9,8},{10,11... | collective-permute-start | bytes 718856 | tf_op jit(solution)/shard_map/ppermute | solution.py:430
  15.4 19.3 %collective-permute-start.4 = (bf16[208,576]{1,0:T(8,128)(2,1)}, bf16[208,576]{1,0:T(8,128)(2,1)}, u32[]{:S(2)}, u32[]{:S(2)}) collective-permute-start(bf16[208,576]{1,0:T(8,128)(2,1)} %get-tuple-element.88), channel_id=1, source_target_pairs={{0,2},{1,3},{2,0},{3,1},{4,6},{5,7},{6,4},{7,5},{8,10},{9,11},{10,... | collective-permute-start | bytes 718856 | tf_op jit(solution)/shard_map/ppermute | solution.py:430
  15.4 23.3 %collective-permute-start.5 = (bf16[208,576]{1,0:T(8,128)(2,1)}, bf16[208,576]{1,0:T(8,128)(2,1)}, u32[]{:S(2)}, u32[]{:S(2)}) collective-permute-start(bf16[208,576]{1,0:T(8,128)(2,1)} %get-tuple-element.89), channel_id=1, source_target_pairs={{0,3},{1,2},{2,1},{3,0},{4,7},{5,6},{6,5},{7,4},{8,11},{9,10},{10,... | collective-permute-start | bytes 718856 | tf_op jit(solution)/shard_map/ppermute | solution.py:430
  22.1 6.8 %copy-start.36 = (pred[1,2048]{0,1:T(8,128)(4,1)S(1)}, pred[1,2048]{0,1:T(8,128)(4,1)}, u32[]{:S(2)}) copy-start(pred[1,2048]{0,1:T(8,128)(4,1)} %copy.59) | copy-start | bytes 6148
  24.1 16.9 %copy-start.4 = (bf16[512,768]{1,0:T(8,128)(2,1)S(1)}, bf16[512,768]{1,0:T(8,128)(2,1)}, u32[]{:S(2)}) copy-start(bf16[512,768]{1,0:T(8,128)(2,1)} %refs_0_.3) | copy-start | bytes 2359300
  24.1 16.9 %copy-start.6 = (f32[576,1]{1,0:T(8,128)S(1)}, f32[576,1]{1,0:T(8,128)}, u32[]{:S(2)}) copy-start(f32[576,1]{1,0:T(8,128)} %broadcast_in_dim.54.refs_8_) | copy-start | bytes 6916
  24.1 16.9 %copy-start.18 = (bf16[208,576]{1,0:T(8,128)(2,1)S(1)}, bf16[208,576]{1,0:T(8,128)(2,1)}, u32[]{:S(2)}) copy-start(bf16[208,576]{1,0:T(8,128)(2,1)} %copy-done.17) | copy-start | bytes 718852
  28.9 9.8 %collective-permute-start.2 = (bf16[512,768]{1,0:T(8,128)(2,1)}, bf16[512,768]{1,0:T(8,128)(2,1)S(1)}, u32[]{:S(2)}, u32[]{:S(2)}) collective-permute-start(bf16[512,768]{1,0:T(8,128)(2,1)} %collective-permute-done.1.refs_2_), channel_id=1, source_target_pairs={{0,1},{1,0},{2,3},{3,2},{4,5},{5,4},{6,7},{7,6},{8,9},{9,8},{10,11... | collective-permute-start | bytes 2359304 | tf_op jit(solution)/shard_map/ppermute | solution.py:430
  38.8 8.8 %copy-start.15 = (bf16[512,768]{1,0:T(8,128)(2,1)}, bf16[512,768]{1,0:T(8,128)(2,1)S(1)}, u32[]{:S(2)}) copy-start(bf16[512,768]{1,0:T(8,128)(2,1)S(1)} %collective-permute-done.2.refs_3_) | copy-start | bytes 2359300
  38.8 19.4 %collective-permute-start.6 = (bf16[96,3840]{1,0:T(8,128)(2,1)S(1)}, bf16[96,3840]{1,0:T(8,128)(2,1)}, u32[]{:S(2)}, u32[]{:S(2)}) collective-permute-start(bf16[96,3840]{1,0:T(8,128)(2,1)S(1)} %get-tuple-element.96), channel_id=1, source_target_pairs={{0,2},{1,3},{2,0},{3,1},{4,6},{5,7},{6,4},{7,5},{8,10},{9,11},{10,... | collective-permute-start | bytes 2211848 | tf_op jit(solution)/shard_map/ppermute | solution.py:430
  40.2 32.8 %collective-permute-start.14 = (bf16[96,3072]{1,0:T(8,128)(2,1)S(1)}, bf16[96,3072]{1,0:T(8,128)(2,1)}, u32[]{:S(2)}, u32[]{:S(2)}) collective-permute-start(bf16[96,3072]{1,0:T(8,128)(2,1)S(1)} %get-tuple-element.102), channel_id=1, source_target_pairs={{0,2},{1,3},{2,0},{3,1},{4,6},{5,7},{6,4},{7,5},{8,10},{9,11},{10,... | collective-permute-start | bytes 1769480 | tf_op jit(solution)/shard_map/ppermute | solution.py:430
  40.9 50.7 %collective-permute-start.10 = (bf16[192,6912]{1,0:T(8,128)(2,1)}, bf16[192,6912]{1,0:T(8,128)(2,1)}, u32[]{:S(2)}, u32[]{:S(2)}) collective-permute-start(bf16[192,6912]{1,0:T(8,128)(2,1)} %get-tuple-element.100.refs_4_), channel_id=1, source_target_pairs={{0,1},{1,0},{2,3},{3,2},{4,5},{5,4},{6,7},{7,6},{8,9},{9,8},{10,11... | collective-permute-start | bytes 7962632 | tf_op jit(solution)/shard_map/ppermute | solution.py:430
  47.6 6.5 %copy-start.28 = (bf16[2048,768]{1,0:T(8,128)(2,1)}, bf16[2048,768]{1,0:T(8,128)(2,1)S(1)}, u32[]{:S(2)}) copy-start(bf16[2048,768]{1,0:T(8,128)(2,1)S(1)} %get-tuple-element.126.refs_4_) | copy-start | bytes 9437188
  47.6 6.5 %copy-start.30 = (bf16[576,768]{1,0:T(8,128)(2,1)}, bf16[576,768]{1,0:T(8,128)(2,1)S(1)}, u32[]{:S(2)}) copy-start(bf16[576,768]{1,0:T(8,128)(2,1)S(1)} %get-tuple-element.131.refs_8_) | copy-start | bytes 2654212
  58.2 28.3 %collective-permute-start.11 = (bf16[96,3840]{1,0:T(8,128)(2,1)}, bf16[96,3840]{1,0:T(8,128)(2,1)}, u32[]{:S(2)}, u32[]{:S(2)}) collective-permute-start(bf16[96,3840]{1,0:T(8,128)(2,1)} %collective-permute-done.6.refs_6_), channel_id=1, source_target_pairs={{0,4},{4,0},{8,12},{12,8},{16,20},{20,16},{24,28},{28,24},{1,5},{5... | collective-permute-start | bytes 2211848 | tf_op jit(solution)/shard_map/ppermute | solution.py:430
  66.3 6.7 %copy-start.11 = (f32[1,2048,1]{2,1,0:T(8,128)}, f32[1,2048,1]{2,1,0:T(8,128)S(1)}, u32[]{:S(2)}) copy-start(f32[1,2048,1]{2,1,0:T(8,128)S(1)} %get-tuple-element.122.lse_ref) | copy-start | bytes 24580
  73.0 16.3 %collective-permute-start.15 = (bf16[96,3072]{1,0:T(8,128)(2,1)}, bf16[96,3072]{1,0:T(8,128)(2,1)}, u32[]{:S(2)}, u32[]{:S(2)}) collective-permute-start(bf16[96,3072]{1,0:T(8,128)(2,1)} %collective-permute-done.14.refs_10_), channel_id=1, source_target_pairs={{0,4},{4,0},{8,12},{12,8},{16,20},{20,16},{24,28},{28,24},{1,5},{5... | collective-permute-start | bytes 1769480 | tf_op jit(solution)/shard_map/ppermute | solution.py:430
  74.1 7.3 %collective-permute-start.9 = (bf16[192,512]{1,0:T(8,128)(2,1)S(1)}, bf16[192,512]{1,0:T(8,128)(2,1)S(1)}, u32[]{:S(2)}, u32[]{:S(2)}) collective-permute-start(bf16[192,512]{1,0:T(8,128)(2,1)S(1)} %pad_maximum_fusion.6), channel_id=1, source_target_pairs={{0,3},{1,2},{2,1},{3,0},{4,7},{5,6},{6,5},{7,4},{8,11},{9,10},{10,... | collective-permute-start | bytes 589832 | tf_op jit(solution)/shard_map/ppermute | solution.py:430
  74.8 10.7 %collective-permute-start.8 = (bf16[192,512]{1,0:T(8,128)(2,1)S(1)}, bf16[192,512]{1,0:T(8,128)(2,1)S(1)}, u32[]{:S(2)}, u32[]{:S(2)}) collective-permute-start(bf16[192,512]{1,0:T(8,128)(2,1)S(1)} %pad_maximum_fusion.5), channel_id=1, source_target_pairs={{0,2},{1,3},{2,0},{3,1},{4,6},{5,7},{6,4},{7,5},{8,10},{9,11},{10,... | collective-permute-start | bytes 589832 | tf_op jit(solution)/shard_map/ppermute | solution.py:430
  82.1 4.7 %collective-permute-start.7 = (bf16[192,512]{1,0:T(8,128)(2,1)S(1)}, bf16[192,512]{1,0:T(8,128)(2,1)S(1)}, u32[]{:S(2)}, u32[]{:S(2)}) collective-permute-start(bf16[192,512]{1,0:T(8,128)(2,1)S(1)} %pad_maximum_fusion.4), channel_id=1, source_target_pairs={{0,1},{1,0},{2,3},{3,2},{4,5},{5,4},{6,7},{7,6},{8,9},{9,8},{10,11... | collective-permute-start | bytes 589832 | tf_op jit(solution)/shard_map/ppermute | solution.py:430
  86.3 4.5 %collective-permute-start.12 = (bf16[96,3840]{1,0:T(8,128)(2,1)}, bf16[96,3840]{1,0:T(8,128)(2,1)}, u32[]{:S(2)}, u32[]{:S(2)}) collective-permute-start(bf16[96,3840]{1,0:T(8,128)(2,1)} %collective-permute-done.6.refs_6_), channel_id=1, source_target_pairs={{0,1},{1,0},{2,3},{3,2},{4,5},{5,4},{6,7},{7,6},{8,9},{9,8},{10,11... | collective-permute-start | bytes 2211848 | tf_op jit(solution)/shard_map/ppermute | solution.py:430
  86.5 5.1 %collective-permute-start.13 = (bf16[96,3840]{1,0:T(8,128)(2,1)}, bf16[96,3840]{1,0:T(8,128)(2,1)}, u32[]{:S(2)}, u32[]{:S(2)}) collective-permute-start(bf16[96,3840]{1,0:T(8,128)(2,1)} %collective-permute-done.11.refs_7_), channel_id=1, source_target_pairs={{0,1},{1,0},{2,3},{3,2},{4,5},{5,4},{6,7},{7,6},{8,9},{9,8},{10,11... | collective-permute-start | bytes 2211848 | tf_op jit(solution)/shard_map/ppermute | solution.py:430
  87.4 3.3 %collective-permute-start.16 = (bf16[96,3072]{1,0:T(8,128)(2,1)}, bf16[96,3072]{1,0:T(8,128)(2,1)}, u32[]{:S(2)}, u32[]{:S(2)}) collective-permute-start(bf16[96,3072]{1,0:T(8,128)(2,1)} %collective-permute-done.14.refs_10_), channel_id=1, source_target_pairs={{0,1},{1,0},{2,3},{3,2},{4,5},{5,4},{6,7},{7,6},{8,9},{9,8},{10,11... | collective-permute-start | bytes 1769480 | tf_op jit(solution)/shard_map/ppermute | solution.py:430
  89.3 2.3 collective-permute-start.17
  130.1 5.7 %collective-permute-start.22 = (bf16[2,192,3840]{2,1,0:T(8,128)(2,1)}, bf16[2,192,3840]{2,1,0:T(8,128)(2,1)}, u32[]{:S(2)}, u32[]{:S(2)}) collective-permute-start(bf16[2,192,3840]{2,1,0:T(8,128)(2,1)} %get-tuple-element.113), channel_id=1, source_target_pairs={{0,1},{1,0},{2,3},{3,2},{4,5},{5,4},{6,7},{7,6},{8,9},{9,8},{10,11... | collective-permute-start | bytes 8847368 | tf_op jit(solution)/shard_map/ppermute | solution.py:430
  130.3 11.0 %collective-permute-start.21 = (bf16[2,192,3072]{2,1,0:T(8,128)(2,1)}, bf16[2,192,3072]{2,1,0:T(8,128)(2,1)}, u32[]{:S(2)}, u32[]{:S(2)}) collective-permute-start(bf16[2,192,3072]{2,1,0:T(8,128)(2,1)} %get-tuple-element.111), channel_id=1, source_target_pairs={{0,1},{1,0},{2,3},{3,2},{4,5},{5,4},{6,7},{7,6},{8,9},{9,8},{10,11... | collective-permute-start | bytes 7077896 | tf_op jit(solution)/shard_map/ppermute | solution.py:430
  131.3 12.7 %collective-permute-start.18 = (bf16[192,512]{1,0:T(8,128)(2,1)}, bf16[192,512]{1,0:T(8,128)(2,1)S(1)}, u32[]{:S(2)}, u32[]{:S(2)}) collective-permute-start(bf16[192,512]{1,0:T(8,128)(2,1)} %copy-done.21), channel_id=1, source_target_pairs={{0,1},{1,0},{2,3},{3,2},{4,5},{5,4},{6,7},{7,6},{8,9},{9,8},{10,11... | collective-permute-start | bytes 589832 | tf_op jit(solution)/shard_map/ppermute | solution.py:430
  131.5 12.5 %collective-permute-start.19 = (bf16[192,512]{1,0:T(8,128)(2,1)}, bf16[192,512]{1,0:T(8,128)(2,1)S(1)}, u32[]{:S(2)}, u32[]{:S(2)}) collective-permute-start(bf16[192,512]{1,0:T(8,128)(2,1)} %copy-done.20), channel_id=1, source_target_pairs={{0,2},{1,3},{2,0},{3,1},{4,6},{5,7},{6,4},{7,5},{8,10},{9,11},{10,... | collective-permute-start | bytes 589832 | tf_op jit(solution)/shard_map/ppermute | solution.py:430
  133.4 10.7 %collective-permute-start.20 = (bf16[192,512]{1,0:T(8,128)(2,1)}, bf16[192,512]{1,0:T(8,128)(2,1)S(1)}, u32[]{:S(2)}, u32[]{:S(2)}) collective-permute-start(bf16[192,512]{1,0:T(8,128)(2,1)} %copy-done.19), channel_id=1, source_target_pairs={{0,3},{1,2},{2,1},{3,0},{4,7},{5,6},{6,5},{7,4},{8,11},{9,10},{10,... | collective-permute-start | bytes 589832 | tf_op jit(solution)/shard_map/ppermute | solution.py:430
  135.8 5.5 %copy-start.34 = (bf16[2,192,3072]{2,1,0:T(8,128)(2,1)S(1)}, bf16[2,192,3072]{2,1,0:T(8,128)(2,1)}, u32[]{:S(2)}) copy-start(bf16[2,192,3072]{2,1,0:T(8,128)(2,1)} %get-tuple-element.110) | copy-start | bytes 7077892
  139.3 35.5 %collective-permute-start.23 = (bf16[192,3840]{1,0:T(8,128)(2,1)S(1)}, bf16[192,3840]{1,0:T(8,128)(2,1)S(1)}, u32[]{:S(2)}, u32[]{:S(2)}) collective-permute-start(bf16[192,3840]{1,0:T(8,128)(2,1)S(1)} %get-tuple-element.164), channel_id=1, source_target_pairs={{0,2},{1,3},{2,0},{3,1},{4,6},{5,7},{6,4},{7,5},{8,10},{9,11},{10,... | collective-permute-start | bytes 4423688 | tf_op jit(solution)/shard_map/ppermute | solution.py:430
  144.0 27.8 %collective-permute-start.24 = (bf16[2,96,3072]{2,1,0:T(8,128)(2,1)S(1)}, bf16[2,96,3072]{2,1,0:T(8,128)(2,1)S(1)}, u32[]{:S(2)}, u32[]{:S(2)}) collective-permute-start(bf16[2,96,3072]{2,1,0:T(8,128)(2,1)S(1)} %get-tuple-element.123), channel_id=1, source_target_pairs={{0,4},{4,0},{8,12},{12,8},{16,20},{20,16},{24,28},{28,24},{1,5},{5... | collective-permute-start | bytes 3538952 | tf_op jit(solution)/shard_map/ppermute | solution.py:430
  145.6 7.9 %copy-start.14 = (f32[1,2048,1]{2,1,0:T(8,128)S(1)}, f32[1,2048,1]{2,1,0:T(8,128)}, u32[]{:S(2)}) copy-start(f32[1,2048,1]{2,1,0:T(8,128)} %copy-done.13) | copy-start | bytes 24580
  153.5 8.2 %copy-start.10 = (f32[1,2048,1]{2,1,0:T(8,128)S(1)}, f32[1,2048,1]{2,1,0:T(8,128)}, u32[]{:S(2)}) copy-start(f32[1,2048,1]{2,1,0:T(8,128)} %copy-done.9) | copy-start | bytes 24580
  174.8 4.2 %copy-start.31 = (bf16[576,768]{1,0:T(8,128)(2,1)S(1)}, bf16[576,768]{1,0:T(8,128)(2,1)}, u32[]{:S(2)}) copy-start(bf16[576,768]{1,0:T(8,128)(2,1)} %copy-done.30) | copy-start | bytes 2654212
  175.1 3.9 %copy-start.29 = (bf16[2048,768]{1,0:T(8,128)(2,1)S(1)}, bf16[2048,768]{1,0:T(8,128)(2,1)}, u32[]{:S(2)}) copy-start(bf16[2048,768]{1,0:T(8,128)(2,1)} %copy-done.28) | copy-start | bytes 9437188
  175.2 19.1 %collective-permute-start.26 = (bf16[96,3840]{1,0:T(8,128)(2,1)S(1)}, bf16[96,3840]{1,0:T(8,128)(2,1)S(1)}, u32[]{:S(2)}, u32[]{:S(2)}) collective-permute-start(bf16[96,3840]{1,0:T(8,128)(2,1)S(1)} %constant_dynamic-slice_fusion.11), channel_id=1, source_target_pairs={{0,4},{4,0},{8,12},{12,8},{16,20},{20,16},{24,28},{28,24},{1,5},{5... | collective-permute-start | bytes 2211848 | tf_op jit(solution)/shard_map/ppermute | solution.py:430
  177.3 17.2 %collective-permute-start.25 = (bf16[96,3072]{1,0:T(8,128)(2,1)S(1)}, bf16[96,3072]{1,0:T(8,128)(2,1)S(1)}, u32[]{:S(2)}, u32[]{:S(2)}) collective-permute-start(bf16[96,3072]{1,0:T(8,128)(2,1)S(1)} %get-tuple-element.167), channel_id=1, source_target_pairs={{0,2},{1,3},{2,0},{3,1},{4,6},{5,7},{6,4},{7,5},{8,10},{9,11},{10,... | collective-permute-start | bytes 1769480 | tf_op jit(solution)/shard_map/ppermute | solution.py:430
  189.1 7.8 %collective-permute-start.30 = (bf16[2,512,768]{2,1,0:T(8,128)(2,1)S(1)}, bf16[2,512,768]{2,1,0:T(8,128)(2,1)S(1)}, u32[]{:S(2)}, u32[]{:S(2)}) collective-permute-start(bf16[2,512,768]{2,1,0:T(8,128)(2,1)S(1)} %get-tuple-element.138), channel_id=1, source_target_pairs={{0,1},{1,0},{2,3},{3,2},{4,5},{5,4},{6,7},{7,6},{8,9},{9,8},{10,11... | collective-permute-start | bytes 4718600 | tf_op jit(solution)/shard_map/ppermute | solution.py:430
  189.2 16.9 %collective-permute-start.28 = (bf16[4,96,588]{2,1,0:T(8,128)(2,1)S(1)}, bf16[4,96,588]{2,1,0:T(8,128)(2,1)S(1)}, u32[]{:S(2)}, u32[]{:S(2)}) collective-permute-start(bf16[4,96,588]{2,1,0:T(8,128)(2,1)S(1)} %get-tuple-element.136), channel_id=1, source_target_pairs={{0,4},{4,0},{8,12},{12,8},{16,20},{20,16},{24,28},{28,24},{1,5},{5... | collective-permute-start | bytes 1354760 | tf_op jit(solution)/shard_map/ppermute | solution.py:430
  194.5 11.5 %collective-permute-start.29 = (bf16[48,3840]{1,0:T(8,128)(2,1)S(1)}, bf16[48,3840]{1,0:T(8,128)(2,1)S(1)}, u32[]{:S(2)}, u32[]{:S(2)}) collective-permute-start(bf16[48,3840]{1,0:T(8,128)(2,1)S(1)} %constant_dynamic-slice_fusion.9), channel_id=1, source_target_pairs={{0,8},{4,12},{8,0},{12,4},{16,24},{20,28},{24,16},{28,20},{1,9},{5... | collective-permute-start | bytes 1105928 | tf_op jit(solution)/shard_map/ppermute | solution.py:430
  196.4 12.7 %collective-permute-start.27 = (bf16[48,3072]{1,0:T(8,128)(2,1)S(1)}, bf16[48,3072]{1,0:T(8,128)(2,1)S(1)}, u32[]{:S(2)}, u32[]{:S(2)}) collective-permute-start(bf16[48,3072]{1,0:T(8,128)(2,1)S(1)} %constant_dynamic-slice_fusion.10), channel_id=1, source_target_pairs={{0,8},{4,12},{8,0},{12,4},{16,24},{20,28},{24,16},{28,20},{1,9},{5... | collective-permute-start | bytes 884744 | tf_op jit(solution)/shard_map/ppermute | solution.py:430
  197.1 17.3 %collective-permute-start.31 = (bf16[512,768]{1,0:T(8,128)(2,1)S(1)}, bf16[512,768]{1,0:T(8,128)(2,1)S(1)}, u32[]{:S(2)}, u32[]{:S(2)}) collective-permute-start(bf16[512,768]{1,0:T(8,128)(2,1)S(1)} %fusion.14), channel_id=1, source_target_pairs={{0,2},{1,3},{2,0},{3,1},{4,6},{5,7},{6,4},{7,5},{8,10},{9,11},{10,... | collective-permute-start | bytes 2359304 | tf_op jit(solution)/shard_map/ppermute | solution.py:430
  209.4 14.8 %collective-permute-start.35 = (bf16[24,3072]{1,0:T(8,128)(2,1)S(1)}, bf16[24,3072]{1,0:T(8,128)(2,1)S(1)}, u32[]{:S(2)}, u32[]{:S(2)}) collective-permute-start(bf16[24,3072]{1,0:T(8,128)(2,1)S(1)} %constant_dynamic-slice_fusion.5), channel_id=1, source_target_pairs={{0,16},{4,20},{8,24},{12,28},{16,0},{20,4},{24,8},{28,12},{1,17},{... | collective-permute-start | bytes 442376 | tf_op jit(solution)/shard_map/ppermute | solution.py:430
  212.4 11.5 %collective-permute-start.33 = (bf16[24,3840]{1,0:T(8,128)(2,1)S(1)}, bf16[24,3840]{1,0:T(8,128)(2,1)S(1)}, u32[]{:S(2)}, u32[]{:S(2)}) collective-permute-start(bf16[24,3840]{1,0:T(8,128)(2,1)S(1)} %constant_dynamic-slice_fusion.7), channel_id=1, source_target_pairs={{0,16},{4,20},{8,24},{12,28},{16,0},{20,4},{24,8},{28,12},{1,17},{... | collective-permute-start | bytes 552968 | tf_op jit(solution)/shard_map/ppermute | solution.py:430
  212.5 11.5 %collective-permute-start.32 = (bf16[4,48,588]{2,1,0:T(8,128)(2,1)S(1)}, bf16[4,48,588]{2,1,0:T(8,128)(2,1)S(1)}, u32[]{:S(2)}, u32[]{:S(2)}) collective-permute-start(bf16[4,48,588]{2,1,0:T(8,128)(2,1)S(1)} %constant_dynamic-slice_fusion.8), channel_id=1, source_target_pairs={{0,8},{4,12},{8,0},{12,4},{16,24},{20,28},{24,16},{28,20},{1,9},{5... | collective-permute-start | bytes 677384 | tf_op jit(solution)/shard_map/ppermute | solution.py:430
  224.2 7.4 %collective-permute-start.34 = (bf16[4,24,588]{2,1,0:T(8,128)(2,1)S(1)}, bf16[4,24,588]{2,1,0:T(8,128)(2,1)S(1)}, u32[]{:S(2)}, u32[]{:S(2)}) collective-permute-start(bf16[4,24,588]{2,1,0:T(8,128)(2,1)S(1)} %constant_dynamic-slice_fusion.6), channel_id=1, source_target_pairs={{0,16},{4,20},{8,24},{12,28},{16,0},{20,4},{24,8},{28,12},{1,17},{... | collective-permute-start | bytes 338696 | tf_op jit(solution)/shard_map/ppermute | solution.py:430
  235.8 1.9 collective-permute-start.36
  235.9 4.1 %collective-permute-start.37 = (bf16[24,626]{1,0:T(8,128)(2,1)S(1)}, bf16[24,626]{1,0:T(8,128)(2,1)S(1)}, u32[]{:S(2)}, u32[]{:S(2)}) collective-permute-start(bf16[24,626]{1,0:T(8,128)(2,1)S(1)} %get-tuple-element.184), channel_id=1, source_target_pairs={{0,2},{1,3},{2,0},{3,1},{4,6},{5,7},{6,4},{7,5},{8,10},{9,11},{10,... | collective-permute-start | bytes 90152 | tf_op jit(solution)/shard_map/ppermute | solution.py:430
  236.0 4.0 %collective-permute-start.38 = (bf16[24,626]{1,0:T(8,128)(2,1)S(1)}, bf16[24,626]{1,0:T(8,128)(2,1)S(1)}, u32[]{:S(2)}, u32[]{:S(2)}) collective-permute-start(bf16[24,626]{1,0:T(8,128)(2,1)S(1)} %get-tuple-element.185), channel_id=1, source_target_pairs={{0,3},{1,2},{2,1},{3,0},{4,7},{5,6},{6,5},{7,4},{8,11},{9,10},{10,... | collective-permute-start | bytes 90152 | tf_op jit(solution)/shard_map/ppermute | solution.py:430
  245.1 41.9 %copy-start.38 = (f32[12,192]{1,0:T(8,128)S(1)}, f32[12,192]{1,0:T(8,128)}, u32[]{:S(2)}) copy-start(f32[12,192]{1,0:T(8,128)} %param.24) | copy-start | bytes 27652
  245.1 41.9 %copy-start.39 = (f32[12,192]{1,0:T(8,128)S(1)}, f32[12,192]{1,0:T(8,128)}, u32[]{:S(2)}) copy-start(f32[12,192]{1,0:T(8,128)} %param.25) | copy-start | bytes 27652
  245.1 47.9 %copy-start.2 = (f32[192,3072]{1,0:T(8,128)S(1)}, f32[192,3072]{1,0:T(8,128)}, u32[]{:S(2)}) copy-start(f32[192,3072]{1,0:T(8,128)} %out_ref.1) | copy-start | bytes 7077892
  245.5 10.5 %collective-permute-start.39 = (bf16[1,24,2318]{2,1,0:T(8,128)(2,1)S(1)}, bf16[1,24,2318]{2,1,0:T(8,128)(2,1)S(1)}, u32[]{:S(2)}, u32[]{:S(2)}) collective-permute-start(bf16[1,24,2318]{2,1,0:T(8,128)(2,1)S(1)} %bitcast.124), channel_id=1, source_target_pairs={{0,16},{4,20},{8,24},{12,28},{16,0},{20,4},{24,8},{28,12},{1,17},{... | collective-permute-start | bytes 333800 | tf_op jit(solution)/shard_map/ppermute | solution.py:430
  256.0 16.6 %collective-permute-start.40 = (bf16[2,24,2318]{2,1,0:T(8,128)(2,1)S(1)}, bf16[2,24,2318]{2,1,0:T(8,128)(2,1)S(1)}, u32[]{:S(2)}, u32[]{:S(2)}) collective-permute-start(bf16[2,24,2318]{2,1,0:T(8,128)(2,1)S(1)} %pad_maximum_fusion.2), channel_id=1, source_target_pairs={{0,8},{4,12},{8,0},{12,4},{16,24},{20,28},{24,16},{28,20},{1,9},{5... | collective-permute-start | bytes 667592 | tf_op jit(solution)/shard_map/ppermute | solution.py:430
  272.6 12.6 %collective-permute-start.41 = (bf16[4,24,2318]{2,1,0:T(8,128)(2,1)S(1)}, bf16[4,24,2318]{2,1,0:T(8,128)(2,1)S(1)}, u32[]{:S(2)}, u32[]{:S(2)}) collective-permute-start(bf16[4,24,2318]{2,1,0:T(8,128)(2,1)S(1)} %pad_maximum_fusion.refs_1_), channel_id=1, source_target_pairs={{0,4},{4,0},{8,12},{12,8},{16,20},{20,16},{24,28},{28,24},{1,5},{5... | collective-permute-start | bytes 1335176 | tf_op jit(solution)/shard_map/ppermute | solution.py:430
  287.0 25.1 %copy-start.37 = (f32[192,12]{0,1:T(8,128)}, f32[192,12]{0,1:T(8,128)S(1)}, u32[]{:S(2)}) copy-start(f32[192,12]{0,1:T(8,128)S(1)} %copy.55) | copy-start | bytes 27652
  (21 other events, 27.7 us)
Sparse Core Ops, SparseCore 0:
  225.4 67.6 all-gather.2
